TPU v7x, 32 devices: a whole 2x2x4 slice. The times are simulated.
32 devices in a mesh: pipe: 8 (over y, x, core), dp: 4 (over z).
Axes of the slice: x: 2, y: 2, z: 4, core: 2. Of those that a mesh axis runs over, the one named last changes fastest.
Arguments:
- section_inputs: bfloat16 [8, 2, 256, 4096], P('pipe', None, 'dp'), may hold values from -6 to 6
- arriving: bfloat16 [8, 256, 4096], P('pipe', 'dp'), may hold values from -2.5 to 2.5
- top_grads: bfloat16 [1, 256, 4096], P(None, 'dp', 'pipe'), may hold values from -2.5 to 2.5
- project_weights: bfloat16 [8, 4096, 384], P('pipe', 'dp'), may hold values from -0.09375 to 0.09375
- output_weights: bfloat16 [8, 4096, 128], P('pipe', 'dp'), may hold values from -0.5 to 0.5
Outputs:
- project_grads: float32 [8, 4096, 384], P('pipe', 'dp')
- output_grads: float32 [8, 4096, 128], P('pipe', 'dp')
- passed_back: bfloat16 [8, 256, 4096], P('pipe', 'dp')
All inputs are finite; a program needn't handle non-finite values.
Results may differ from a plain program's by a relative error of at most 0.015.
Values may be sent and summed in bfloat16 or wider, within the bound.
No kernel may reach another device: no remote copies, remote signals or barrier semaphores. Data moves between devices by JAX's collectives and lax.ppermute only.
A program may use at most 64 MiB of HBM per device.

v0:
```python
import math

import jax
import jax.numpy as jnp
from jax import lax
from jax.sharding import PartitionSpec as P

EPSILON = 1e-06
CONTRACT_FIRST = (((0,), (0,)), ((), ()))
CONTRACT_LAST = (((1,), (1,)), ((), ()))


def passed_along(value, axis, steps):
    count = lax.axis_size(axis)
    leading, last = (max(0, -steps), min(count, count - steps))
    return lax.ppermute(value, axis, [(source, source + steps) for source in range(leading, last)])


def normalize(values):
    centered = values - jnp.mean(values, axis=-1, keepdims=True)
    inverse = lax.rsqrt(jnp.mean(centered * centered, axis=-1, keepdims=True) + EPSILON)
    return (centered * inverse, inverse)


def norm_back(gradient, normed, inverse):
    centered = gradient - jnp.mean(gradient, axis=-1, keepdims=True)
    return inverse * (centered - normed * jnp.mean(gradient * normed, axis=-1, keepdims=True))


def shards(section_inputs, arriving, top_grads, project_weights, output_weights):
    tick_count = section_inputs.shape[1]
    seq_len = section_inputs.shape[2]
    width = section_inputs.shape[3]
    head_size = output_weights.shape[2]
    root_size = math.sqrt(head_size)
    total_rows = tick_count * seq_len
    normed, inverse = normalize(section_inputs[0].reshape(total_rows, width).astype(jnp.float32))
    hidden = normed.astype(jnp.bfloat16)
    full_project, full_output = (
        lax.all_gather(project_weights[0], "dp", axis=0, tiled=True),
        lax.all_gather(output_weights[0], "dp", axis=0, tiled=True),
    )
    projected = jnp.dot(hidden, full_project, preferred_element_type=jnp.float32)
    query, query_scale = normalize(projected[:, :head_size])
    key_normed, key_scale = normalize(projected[:, head_size : 2 * head_size])
    query_half = query.astype(jnp.bfloat16).reshape(tick_count, seq_len, head_size)
    key_half = key_normed.astype(jnp.bfloat16).reshape(tick_count, seq_len, head_size)
    value_half = (
        projected[:, 2 * head_size :].astype(jnp.bfloat16).reshape(tick_count, seq_len, head_size)
    )
    scores = (
        jnp.einsum("ksh,kth->kst", query_half, key_half, preferred_element_type=jnp.float32)
        / root_size
    )
    powered = jnp.exp(scores)
    attention = powered / jnp.sum(powered, axis=-1, keepdims=True)
    attention_half = attention.astype(jnp.bfloat16)
    mixed_half = jnp.einsum(
        "kst,kth->ksh", attention_half, value_half, preferred_element_type=jnp.float32
    ).astype(jnp.bfloat16)
    later_grads = lax.all_gather(top_grads, "pipe", axis=2, tiled=True)
    last_section = lax.axis_index("pipe") == lax.axis_size("pipe") - 1
    incoming = arriving[0]
    received = incoming
    passed = incoming
    sum_project = jnp.zeros((width, 3 * head_size), jnp.float32)
    sum_output = jnp.zeros((width, head_size), jnp.float32)
    for tick_index in range(tick_count):
        if tick_index > 0:
            incoming = jnp.where(last_section, later_grads[tick_index - 1], received)
        lower = tick_index * seq_len
        upper = lower + seq_len
        head_grad = jnp.dot(incoming, full_output, preferred_element_type=jnp.float32).astype(
            jnp.bfloat16
        )
        prob_grad = lax.dot_general(
            head_grad, value_half[tick_index], CONTRACT_LAST, preferred_element_type=jnp.float32
        )
        value_grad = lax.dot_general(
            attention_half[tick_index],
            head_grad,
            CONTRACT_FIRST,
            preferred_element_type=jnp.float32,
        ).astype(jnp.bfloat16)
        weighted = attention[tick_index]
        score_grad = (
            weighted
            * (prob_grad - jnp.sum(weighted * prob_grad, axis=-1, keepdims=True))
            / root_size
        ).astype(jnp.bfloat16)
        query_grad = jnp.dot(score_grad, key_half[tick_index], preferred_element_type=jnp.float32)
        key_grad = lax.dot_general(
            score_grad, query_half[tick_index], CONTRACT_FIRST, preferred_element_type=jnp.float32
        )
        normed_grads = jnp.concatenate(
            [
                norm_back(query_grad, query[lower:upper], query_scale[lower:upper]),
                norm_back(key_grad, key_normed[lower:upper], key_scale[lower:upper]),
            ],
            axis=1,
        ).astype(jnp.bfloat16)
        proj_grad = jnp.concatenate([normed_grads, value_grad], axis=1)
        hidden_grad = lax.dot_general(
            proj_grad, full_project, CONTRACT_LAST, preferred_element_type=jnp.float32
        )
        passed = (
            incoming.astype(jnp.float32)
            + norm_back(hidden_grad, normed[lower:upper], inverse[lower:upper])
        ).astype(jnp.bfloat16)
        if tick_index + 1 < tick_count:
            received = passed_along(passed, "pipe", -1)
        sum_project = sum_project + lax.dot_general(
            hidden[lower:upper], proj_grad, CONTRACT_FIRST, preferred_element_type=jnp.float32
        )
        sum_output = sum_output + lax.dot_general(
            incoming, mixed_half[tick_index], CONTRACT_FIRST, preferred_element_type=jnp.float32
        )
    summed = lax.psum_scatter(
        jnp.concatenate([sum_project, sum_output], axis=1).astype(jnp.bfloat16),
        "dp",
        scatter_dimension=0,
        tiled=True,
    ).astype(jnp.float32)
    return (summed[None, :, : 3 * head_size], summed[None, :, 3 * head_size :], passed[None])


def solution(mesh):
    in_specs = (
        P("pipe", None, "dp", None),
        P("pipe", "dp", None),
        P(None, "dp", "pipe"),
        P("pipe", "dp", None),
        P("pipe", "dp", None),
    )
    out_specs = (P("pipe", "dp", None), P("pipe", "dp", None), P("pipe", "dp", None))
    return jax.shard_map(shards, mesh=mesh, in_specs=in_specs, out_specs=out_specs, check_vma=False)
```

profile of v0, /device:TPU:0, one launch (start us, length us, event | category | flops | bytes accessed | tf_op | source)
XLA Modules:
  0.0 215.8 jit_solution(9222207081711706463)
XLA Ops:
  7.2 0.7 all-gather.7.cloned.1.call-update
  8.0 0.7 all-gather.5.cloned.1.call-update
  8.7 1.5 convert_reduce_fusion
  10.2 0.1 div.77
  10.3 0.4 multiply_reduce_fusion
  10.7 0.1 rsqrt.43
  10.8 12.4 %all_gather.11 = bf16[1,64,4096]{2,1,0:T(8,128)(2,1)} all-gather(bf16[1,64,512]{2,1,0:T(8,128)(2,1)S(1)} %copy-done.11), channel_id=1, replica_groups=mesh['pipe'=8,'dp'=4] {'pipe'}, dimensions={2}, use_global_device_ids=true | all-gather | bytes 589824 | tf_op jit(solution)/shard_map/all_gather | solution.py:61
  23.2 2.1 fusion.7
  25.3 14.9 %all-gather.7.cloned.1.call-done = bf16[1,4096,128]{2,1,0:T(8,128)(2,1)} async-done(((bf16[1,1024,128]{2,1,0:T(8,128)(2,1)}), bf16[1,4096,128]{2,1,0:T(8,128)(2,1)}) %all-gather.7.cloned.1.call-update) | async-done | bytes 1048592 | tf_op jit(solution)/shard_map/all_gather | solution.py:41
  40.3 1.5 convolution_convert_fusion.2
  41.8 63.1 %all-gather.5.cloned.1.call-done = bf16[1,4096,384]{2,1,0:T(8,128)(2,1)} async-done(((bf16[1,1024,384]{2,1,0:T(8,128)(2,1)}), bf16[1,4096,384]{2,1,0:T(8,128)(2,1)}) %all-gather.5.cloned.1.call-update) | async-done | bytes 3145744 | tf_op jit(solution)/shard_map/all_gather | solution.py:40
  104.9 3.1 %fusion.50 = (bf16[128,384]{1,0:T(8,128)(2,1)S(1)}, f32[128,384]{1,0:T(8,128)S(1)}) fusion(bf16[128,4096]{1,0:T(8,128)(2,1)} %get-tuple-element.29, bf16[1,4096,384]{2,1,0:T(8,128)(2,1)} %all-gather.5.cloned.1.call-done), kind=kOutput, calls=%fused_computation.115 | convolution fusion | flops 402702336 | bytes 4489216 | tf_op jit(solution)/shard_map/dot_general | solution.py:43
  107.9 0.1 slice_reduce_fusion
  108.0 0.2 multiply_reduce_fusion.3
  108.3 0.1 fusion.47
  108.3 0.1 fusion.43
  108.5 0.1 fusion.48
  108.6 0.2 fusion.49
  108.7 0.1 multiply_reduce_fusion.10
  108.9 0.3 fusion.40
  109.2 0.2 fusion.41
  109.5 0.1 convolution_convert_fusion.4
  109.6 0.1 multiply_convert_fusion.4
  109.7 0.1 multiply_convert_fusion.3
  109.8 1.2 fusion.37
  111.1 0.3 add_convert_fusion.2
  111.4 1.4 collective-permute-start
  112.8 0.2 convolution_convert_fusion
  113.0 0.5 convolution_bitcast_fusion
  113.5 1.0 fusion.13
  114.5 0.8 collective-permute-done
  115.4 0.3 convolution_convert_fusion.1
  115.8 0.1 multiply_reduce_fusion.7
  115.9 0.3 fusion.38
  116.2 0.2 fusion.39
  116.5 0.1 convolution_convert_fusion.3
  116.6 0.5 fusion
  117.1 0.1 multiply_convert_fusion.1
  117.2 0.1 multiply_convert_fusion
  117.3 1.0 add_convert_fusion
  118.3 2.2 %pad_maximum_fusion = bf16[4096,512]{0,1:T(8,128)(2,1)} fusion(bf16[4096,128]{0,1:T(8,128)(2,1)S(1)} %fusion, bf16[4096,384]{0,1:T(8,128)(2,1)S(1)} %add_convert_fusion), kind=kLoop, calls=%fused_computation.4 | loop fusion | flops 8388608 | bytes 8388608 | tf_op jit(solution)/shard_map/concatenate | solution.py:119
  120.6 2.6 %fusion.36 = (f32[64]{0:T(128)S(1)}, f32[64]{0:T(128)S(1)}, f32[64,4096]{1,0:T(8,128)S(1)}) fusion(f32[128,4096]{1,0:T(8,128)} %get-tuple-element.28, bf16[1,4096,384]{2,1,0:T(8,128)(2,1)S(1)} %copy-done, bf16[64,128]{1,0:T(8,128)(2,1)S(1)} %convolution_convert_fusion.3, bf16[64,128]{1,0:T(8,128)(2,1)S(1)} %multiply_convert_fusion, ...), kind=kOutput, calls=%fused_computation.103 | convolution fusion | flops 202260352 | bytes 5292544 | tf_op jit(solution)/shard_map/dot_general | solution.py:103
  123.2 1.1 fusion.11
  124.3 78.1 %reduce-scatter.2.cloned.1.call-done = bf16[1024,512]{0,1:T(8,128)(2,1)} async-done(((bf16[4096,512]{0,1:T(8,128)(2,1)}), bf16[1024,512]{0,1:T(8,128)(2,1)}) %reduce-scatter.2.cloned.1.call-update) | async-done | bytes 1048592 | tf_op jit(solution)/shard_map/reduce_scatter | solution.py:118
  202.4 1.5 convert_element_type.78
  203.9 1.3 slice_bitcast_fusion
  205.2 3.0 %copy.9 = f32[1,1024,384]{2,1,0:T(8,128)} copy(f32[1,1024,384]{1,2,0:T(8,128)} %slice_bitcast_fusion) | data formatting | bytes 3145728
  208.3 1.0 copy.10
  (52 shorter events, 0.4 us)
Async XLA Ops:
  7.2 3.1 %copy-start.4 = (bf16[1,2,64,4096]{3,2,1,0:T(8,128)(2,1)S(1)}, bf16[1,2,64,4096]{3,2,1,0:T(8,128)(2,1)}, u32[]{:S(2)}) copy-start(bf16[1,2,64,4096]{3,2,1,0:T(8,128)(2,1)} %param.5) | copy-start | bytes 3145732
  7.2 3.6 %copy-start.11 = (bf16[1,64,512]{2,1,0:T(8,128)(2,1)S(1)}, bf16[1,64,512]{2,1,0:T(8,128)(2,1)}, u32[]{:S(2)}) copy-start(bf16[1,64,512]{2,1,0:T(8,128)(2,1)} %param.7) | copy-start | bytes 196612
  7.2 33.1 %all-gather.7.cloned.1.call-start = ((), (), s32[]{:S(2)}) async-start(), calls=%async_computation.3 | async-start | bytes 1310720 | tf_op jit(solution)/shard_map/all_gather | solution.py:41
  7.9 96.9 %all-gather.5.cloned.1.call-start = ((), (), s32[]{:S(2)}) async-start(), calls=%async_computation.2 | async-start | bytes 3932160 | tf_op jit(solution)/shard_map/all_gather | solution.py:40
  8.7 193.7 %reduce-scatter.2.cloned.1.call-start = ((), (), s32[]{:S(2)}) async-start(), calls=%async_computation.1 | async-start | bytes 5242880 | tf_op jit(solution)/shard_map/reduce_scatter | solution.py:118
  23.2 17.1 %copy-start.7 = (bf16[1,64,4096]{2,1,0:T(8,128)(2,1)S(1)}, bf16[1,64,4096]{2,1,0:T(8,128)(2,1)}, u32[]{:S(2)}) copy-start(bf16[1,64,4096]{2,1,0:T(8,128)(2,1)} %param.6) | copy-start | bytes 1572868
  104.9 4.9 %copy-start = (bf16[1,4096,384]{2,1,0:T(8,128)(2,1)S(1)}, bf16[1,4096,384]{2,1,0:T(8,128)(2,1)}, u32[]{:S(2)}) copy-start(bf16[1,4096,384]{2,1,0:T(8,128)(2,1)} %all-gather.5.cloned.1.call-done) | copy-start | bytes 9437188
  104.9 5.0 %copy-start.1 = (f32[128,4096]{1,0:T(8,128)S(1)}, f32[128,4096]{1,0:T(8,128)}, u32[]{:S(2)}) copy-start(f32[128,4096]{1,0:T(8,128)} %get-tuple-element.28) | copy-start | bytes 6291460
  109.8 1.3 copy-start.8
  111.4 2.1 copy-start.3
  111.4 3.9 %collective-permute-start = (bf16[64,4096]{1,0:T(8,128)(2,1)S(1)}, bf16[64,4096]{1,0:T(8,128)(2,1)S(1)}, u32[]{:S(2)}, u32[]{:S(2)}) collective-permute-start(bf16[64,4096]{1,0:T(8,128)(2,1)S(1)} %add_convert_fusion.2), channel_id=1, source_target_pairs={{4,0},{8,4},{12,8},{16,12},{20,16},{24,20},{28,24},{5,1},{9,5},{13... | collective-permute-start | bytes 1572872 | tf_op jit(solution)/shard_map/ppermute | solution.py:16
  113.5 1.8 copy-start.10
  113.5 1.9 copy-start.9
  115.4 1.7 copy-start.5
  120.5 2.6 %copy-start.2 = (f32[128,4096]{1,0:T(8,128)S(1)}, f32[128,4096]{1,0:T(8,128)}, u32[]{:S(2)}) copy-start(f32[128,4096]{1,0:T(8,128)} %get-tuple-element.28) | copy-start | bytes 6291460
  120.6 2.6 %copy-start.6 = (bf16[64,4096]{1,0:T(8,128)(2,1)S(1)}, bf16[64,4096]{1,0:T(8,128)(2,1)}, u32[]{:S(2)}) copy-start(bf16[64,4096]{1,0:T(8,128)(2,1)} %copy-done.5) | copy-start | bytes 1572868
Sparse Core Ops, SparseCore 0:
  9.6 30.6 all-gather.6
  41.8 62.9 all-gather.4
  120.7 81.6 reduce-scatter.1
where the time goes:
time: 216 us
  waiting for transfers between devices  158 us (73%)
  between operations  14.1 us (7%)
  matrix products  13.6 us (6%)
  blocking collectives  12.4 us (6%)
  other arithmetic  10 us (5%)
  local copies, waits for them, and re-layouts  5.77 us (3%)
    reduce_scatter x1, waiting for transfers between devices, shards(): lax.psum_scatter(jnp.concatenate([sum_project, sum_output], axis=1).astyp...  78.1 us
    all_gather x1, waiting for transfers between devices, shards(): lax.all_gather(project_weights[0], 'dp', axis=0, tiled=True)  63.1 us
    all_gather x1, waiting for transfers between devices, shards(): lax.all_gather(output_weights[0], 'dp', axis=0, tiled=True)  14.9 us
    all_gather x1, blocking collectives, shards(): later_grads = lax.all_gather(top_grads, 'pipe', axis=2, tiled=True)  12.4 us
  transfers between devices with their start and end apart: 4, of which 4 were waited for; matrix products, arithmetic and copies ran while one was open for 5% of the time, Pallas kernels for 0%

commit v1 on v0

v1 whole, which is shorter than its diff:
```python
import math

import jax
import jax.numpy as jnp
from jax import lax
from jax.sharding import PartitionSpec as P

EPSILON = 1e-06
CONTRACT_FIRST = (((0,), (0,)), ((), ()))
CONTRACT_LAST = (((1,), (1,)), ((), ()))
F32 = jnp.float32
BF16 = jnp.bfloat16


def normalize(values):
    centered = values - jnp.mean(values, axis=-1, keepdims=True)
    inverse = lax.rsqrt(jnp.mean(centered * centered, axis=-1, keepdims=True) + EPSILON)
    return (centered * inverse, inverse)


def norm_back(gradient, normed, inverse):
    centered = gradient - jnp.mean(gradient, axis=-1, keepdims=True)
    return inverse * (centered - normed * jnp.mean(gradient * normed, axis=-1, keepdims=True))


def shift(value, steps):
    count = lax.axis_size("dp")
    if steps % count == 0:
        return value
    return lax.ppermute(value, "dp", [(i, (i + steps) % count) for i in range(count)])


def split_two(value):
    high = value.astype(BF16)
    return high, (value - high.astype(F32)).astype(BF16)


def shards(section_inputs, arriving, top_grads, project_weights, output_weights):
    count = lax.axis_size("dp")
    pipe = lax.axis_size("pipe")
    me = lax.axis_index("dp")
    ticks = section_inputs.shape[1]
    seq = section_inputs.shape[2]
    width = section_inputs.shape[3]
    head = output_weights.shape[2]
    part = width // count
    root = math.sqrt(head)
    others = range(count)
    project, output = project_weights[0], output_weights[0]

    def scatter_features(value):
        return [
            shift(lax.dynamic_slice_in_dim(value, (me + j) % count * part, part, 1), j)
            for j in others
        ]

    def sum_at_owner(pieces):
        return sum(shift(pieces[j], -j).astype(F32) for j in others)

    normed, inverse = normalize(section_inputs[0].astype(F32))
    hidden_rows = normed.astype(BF16)
    hidden = [scatter_features(hidden_rows[0])]
    incoming = scatter_features(arriving[0])
    hidden += [scatter_features(hidden_rows[t]) for t in range(1, ticks)]

    per_owner = pipe // count
    gathered = []
    for j in others:
        pairs = [
            (q * count + (q // per_owner - j) % count, q * count + q // per_owner)
            for q in range(pipe)
        ]
        gathered.append(lax.ppermute(top_grads, ("pipe", "dp"), pairs) if j else top_grads)
    gathered = jnp.stack(gathered)
    top = jnp.concatenate(
        [
            lax.ppermute(
                gathered,
                ("pipe", "dp"),
                [((per_owner * s + a) * count + s, (pipe - 1) * count + s) for s in range(count)],
            )
            for a in range(per_owner)
        ],
        axis=3,
    )

    row_mean = jnp.sum(project.astype(F32), axis=0, keepdims=True) / width
    row_mean = jnp.broadcast_to(row_mean, (16, 3 * head)).astype(BF16)
    row_mean = sum(shift(row_mean, j).astype(F32) for j in others)[:1]

    project_sums = [jnp.zeros((part, 3 * head), F32) for _ in others]
    output_sums = [jnp.zeros((part, head), F32) for _ in others]
    for t in range(ticks):
        mine = [
            jnp.dot(hidden[t][j], project, preferred_element_type=F32).astype(BF16) for j in others
        ]
        heads = [
            jnp.dot(incoming[j], output, preferred_element_type=F32).astype(BF16) for j in others
        ]
        projected = sum_at_owner(mine)
        query, query_scale = normalize(projected[:, :head])
        key, key_scale = normalize(projected[:, head : 2 * head])
        query_half, key_half = query.astype(BF16), key.astype(BF16)
        value_half = projected[:, 2 * head :].astype(BF16)
        scores = lax.dot_general(query_half, key_half, CONTRACT_LAST, preferred_element_type=F32)
        powered = jnp.exp(scores / root)
        attention = powered / jnp.sum(powered, axis=-1, keepdims=True)
        attention_half = attention.astype(BF16)
        mixed = jnp.dot(attention_half, value_half, preferred_element_type=F32).astype(BF16)

        head_grad = sum_at_owner(heads).astype(BF16)
        prob_grad = lax.dot_general(
            head_grad, value_half, CONTRACT_LAST, preferred_element_type=F32
        )
        value_grad = lax.dot_general(
            attention_half, head_grad, CONTRACT_FIRST, preferred_element_type=F32
        ).astype(BF16)
        score_grad = (
            attention
            * (prob_grad - jnp.sum(attention * prob_grad, axis=-1, keepdims=True))
            / root
        ).astype(BF16)
        query_grad = jnp.dot(score_grad, key_half, preferred_element_type=F32)
        key_grad = lax.dot_general(
            score_grad, query_half, CONTRACT_FIRST, preferred_element_type=F32
        )
        proj_grad = jnp.concatenate(
            [
                norm_back(query_grad, query, query_scale).astype(BF16),
                norm_back(key_grad, key, key_scale).astype(BF16),
                value_grad,
            ],
            axis=1,
        )
        wide = proj_grad.astype(F32)
        scale = inverse[t]
        offset = scale * jnp.sum(wide * row_mean, axis=-1, keepdims=True)
        slope = scale * (jnp.sum(wide * projected, axis=-1, keepdims=True) / width)
        facts = [*split_two(scale), *split_two(offset), *split_two(slope)]
        facts.append(jnp.zeros((seq, head - len(facts)), BF16))
        message = jnp.concatenate([proj_grad, mixed, *facts], axis=1)
        messages = [shift(message, j) for j in others]

        passed = []
        for j in others:
            grad = messages[j][:, : 3 * head]
            mix = messages[j][:, 3 * head : 4 * head]
            numbers = messages[j][:, 4 * head :].astype(F32)
            scale, offset, slope = (
                numbers[:, i : i + 1] + numbers[:, i + 1 : i + 2] for i in (0, 2, 4)
            )
            hidden_grad = lax.dot_general(
                grad, project, CONTRACT_LAST, preferred_element_type=F32
            )
            passed.append(
                (
                    incoming[j].astype(F32)
                    + (scale * hidden_grad - offset - slope * hidden[t][j].astype(F32))
                ).astype(BF16)
            )
            project_sums[j] = project_sums[j] + lax.dot_general(
                hidden[t][j], grad, CONTRACT_FIRST, preferred_element_type=F32
            )
            output_sums[j] = output_sums[j] + lax.dot_general(
                incoming[j], mix, CONTRACT_FIRST, preferred_element_type=F32
            )
        if t + 1 < ticks:
            received = lax.ppermute(
                jnp.stack(passed), "pipe", [(p, (p - 1) % pipe) for p in range(pipe)]
            )
            last = lax.axis_index("pipe") == pipe - 1
            received = jnp.where(last, top[:, t], received)
            incoming = [received[j] for j in others]
    back = [shift(passed[j], -j) for j in others]
    passed_back = jnp.zeros((seq, width), BF16)
    for j in others:
        passed_back = lax.dynamic_update_slice_in_dim(
            passed_back, back[j], (me + j) % count * part, 1
        )
    project_grads = sum(value.astype(BF16).astype(F32) for value in project_sums)
    output_grads = sum(value.astype(BF16).astype(F32) for value in output_sums)
    return (project_grads[None], output_grads[None], passed_back[None])


def solution(mesh):
    in_specs = (
        P("pipe", None, "dp", None),
        P("pipe", "dp", None),
        P(None, "dp", "pipe"),
        P("pipe", "dp", None),
        P("pipe", "dp", None),
    )
    out_specs = (P("pipe", "dp", None), P("pipe", "dp", None), P("pipe", "dp", None))
    return jax.shard_map(shards, mesh=mesh, in_specs=in_specs, out_specs=out_specs, check_vma=False)
```

time: 216 us -> 149 us (0.69)
  waiting for transfers between devices: 158 us -> 14 us
  starting transfers between devices: 1.54 us -> 71 us
  matrix products: 13.6 us -> 29.2 us
  blocking collectives: 12.4 us -> 0 us
  local copies, waits for them, and re-layouts: 5.77 us -> 18.1 us
  between operations: 14.1 us -> 1.8 us
  other arithmetic: 10 us -> 13.3 us
    reduce_scatter x1 -> x0, waiting for transfers between devices: 78.1 us -> none  [shards(): lax.psum_scatter(jnp.concatenate([sum_project, sum_output], axis=1).astyp...]
    all_gather x2 -> x0, waiting for transfers between devices: 78 us -> none  [the longest x1 63.1 us: shards(): lax.all_gather(project_weights[0], 'dp', axis=0, tiled=True)]
    ppermute x1 -> x39, starting transfers between devices: 1.42 us -> 71 us  [the longest x33 63.7 us: shift(): lax.ppermute(value, 'dp', [(i, (i + steps) % count) for i in range(count)])]
    dot_general x19 -> x52, matrix products: 13.6 us -> 29.2 us  [the longest x8 8.69 us: shards(): lax.dot_general(hidden[t][j], grad, CONTRACT_FIRST, preferred_element_typ...]
    ppermute x1 -> x39, waiting for transfers between devices: 0.8 us -> 14 us  [the longest x33 9.37 us: shift(): lax.ppermute(value, 'dp', [(i, (i + steps) % count) for i in range(count)])]
    all_gather x1 -> x0, blocking collectives: 12.4 us -> none  [shards(): later_grads = lax.all_gather(top_grads, 'pipe', axis=2, tiled=True)]
    convert_element_type x0 -> x13, local copies, waits for them, and re-layouts: none -> 7.99 us  [the longest x6 4.31 us: split_two(): return (high, (value - high.astype(F32)).astype(BF16))]
    concatenate x0 -> x4, local copies, waits for them, and re-layouts: none -> 3.35 us  [shards(): message = jnp.concatenate([proj_grad, mixed, *facts], axis=1)]
  transfers between devices with their start and end apart: 4 -> 39, of which waited for: 4 -> 10; matrix products, arithmetic and copies ran while one was open for 5% -> 29% of each run, Pallas kernels for 0% -> 0%
where the time goes in v1:
time: 149 us; the launch traced here: 147 us
  starting transfers between devices  71 us (48%)
  matrix products  29.2 us (20%)
  local copies, waits for them, and re-layouts  18.1 us (12%)
  waiting for transfers between devices  14 us (9%)
  other arithmetic  13.3 us (9%)
  between operations  1.8 us (1%)
    ppermute x33, starting transfers between devices, shift(): lax.ppermute(value, 'dp', [(i, (i + steps) % count) for i in range(count)])  63.7 us
    ppermute x33, waiting for transfers between devices, shift(): lax.ppermute(value, 'dp', [(i, (i + steps) % count) for i in range(count)])  9.37 us
    dot_general x8, matrix products, shards(): lax.dot_general(hidden[t][j], grad, CONTRACT_FIRST, preferred_element_typ...  8.69 us
    dot_general x8, matrix products, shards(): lax.dot_general(grad, project, CONTRACT_LAST, preferred_element_type=F32)  6.32 us
    dot_general x8, matrix products, shards(): lax.dot_general(incoming[j], mix, CONTRACT_FIRST, preferred_element_type=...  5.86 us
    ppermute x1, waiting for transfers between devices, shards(): lax.ppermute(jnp.stack(passed), 'pipe', [(p, (p - 1) % pipe) for p in ran...  4.59 us
    unnamed x94, local copies, waits for them, and re-layouts  4.32 us
    convert_element_type x6, local copies, waits for them, and re-layouts, split_two(): return (high, (value - high.astype(F32)).astype(BF16))  4.31 us
  transfers between devices with their start and end apart: 39, of which 10 were waited for; matrix products, arithmetic and copies ran while one was open for 29% of the time, Pallas kernels for 0%

profile of v1, /device:TPU:0, one launch (start us, length us, event | category | flops | bytes accessed | tf_op | source)
XLA Modules:
  0.0 147.4 jit_solution(2078078118156291861)
XLA Ops:
  0.7 1.4 convert_reduce_fusion.1
  2.1 5.1 %collective-permute-start.25 = (bf16[16,384]{1,0:T(8,128)(2,1)S(1)}, bf16[16,384]{1,0:T(8,128)(2,1)S(1)}, u32[]{:S(2)}, u32[]{:S(2)}) collective-permute-start(bf16[16,384]{1,0:T(8,128)(2,1)S(1)} %broadcast_in_dim.19), channel_id=1, source_target_pairs={{0,3},{1,0},{2,1},{3,2},{4,7},{5,4},{6,5},{7,6},{8,11},{9,8},{10,9... | collective-permute-start | bytes 36872 | tf_op jit(solution)/shard_map/ppermute | solution.py:30
  8.2 1.3 collective-permute-start.20
  9.5 1.3 collective-permute-start.19
  10.8 1.5 convert_reduce_fusion
  18.1 1.3 collective-permute-start.18
  19.4 3.0 %collective-permute-start.14 = (bf16[64,1024]{1,0:T(8,128)(2,1)}, bf16[64,1024]{1,0:T(8,128)(2,1)S(1)}, u32[]{:S(2)}, u32[]{:S(2)}) collective-permute-start(bf16[64,1024]{1,0:T(8,128)(2,1)} %get-tuple-element.53), channel_id=1, source_target_pairs={{0,2},{1,3},{2,0},{3,1},{4,6},{5,7},{6,4},{7,5},{8,10},{9,11},{10,... | collective-permute-start | bytes 393224 | tf_op jit(solution)/shard_map/ppermute | solution.py:30
  22.4 1.6 %collective-permute-start.16 = (bf16[64,1024]{1,0:T(8,128)(2,1)}, bf16[64,1024]{1,0:T(8,128)(2,1)S(1)}, u32[]{:S(2)}, u32[]{:S(2)}) collective-permute-start(bf16[64,1024]{1,0:T(8,128)(2,1)} %get-tuple-element.52), channel_id=1, source_target_pairs={{0,3},{1,0},{2,1},{3,2},{4,7},{5,4},{6,5},{7,6},{8,11},{9,8},{10,9... | collective-permute-start | bytes 393224 | tf_op jit(solution)/shard_map/ppermute | solution.py:30
  25.7 3.3 %collective-permute-start.10 = (bf16[64,1024]{1,0:T(8,128)(2,1)}, bf16[64,1024]{1,0:T(8,128)(2,1)S(1)}, u32[]{:S(2)}, u32[]{:S(2)}) collective-permute-start(bf16[64,1024]{1,0:T(8,128)(2,1)} %get-tuple-element.58), channel_id=1, source_target_pairs={{0,3},{1,0},{2,1},{3,2},{4,7},{5,4},{6,5},{7,6},{8,11},{9,8},{10,9... | collective-permute-start | bytes 393224 | tf_op jit(solution)/shard_map/ppermute | solution.py:30
  29.1 1.6 %pad_maximum_fusion.1 = bf16[4,1,64,512]{3,2,0,1:T(8,128)(2,1)} fusion(bf16[1,1,64,512]{3,2,0,1:T(8,128)(2,1)} %bitcast.263, bf16[1,1,64,512]{3,2,0,1:T(8,128)(2,1)} %bitcast.264, bf16[1,1,64,512]{3,2,0,1:T(8,128)(2,1)S(1)} %bitcast.265, bf16[1,1,64,512]{3,2,0,1:T(8,128)(2,1)} %bitcast.15), kind=kLoop, calls=%fused_computation.107 | loop fusion | flops 393216 | bytes 524288 | tf_op jit(solution)/shard_map/stack | solution.py:74
  30.7 1.2 collective-permute-done.16
  32.0 3.7 %collective-permute-start.2 = (bf16[64,1024]{1,0:T(8,128)(2,1)}, bf16[64,1024]{1,0:T(8,128)(2,1)S(1)}, u32[]{:S(2)}, u32[]{:S(2)}) collective-permute-start(bf16[64,1024]{1,0:T(8,128)(2,1)} %get-tuple-element.56), channel_id=1, source_target_pairs={{0,2},{1,3},{2,0},{3,1},{4,6},{5,7},{6,4},{7,5},{8,10},{9,11},{10,... | collective-permute-start | bytes 393224 | tf_op jit(solution)/shard_map/ppermute | solution.py:30
  38.5 6.2 %collective-permute-start.8 = (bf16[64,1024]{1,0:T(8,128)(2,1)}, bf16[64,1024]{1,0:T(8,128)(2,1)S(1)}, u32[]{:S(2)}, u32[]{:S(2)}) collective-permute-start(bf16[64,1024]{1,0:T(8,128)(2,1)} %get-tuple-element.59), channel_id=1, source_target_pairs={{0,2},{1,3},{2,0},{3,1},{4,6},{5,7},{6,4},{7,5},{8,10},{9,11},{10,... | collective-permute-start | bytes 393224 | tf_op jit(solution)/shard_map/ppermute | solution.py:30
  45.5 8.0 %collective-permute-start.6 = (bf16[64,1024]{1,0:T(8,128)(2,1)S(1)}, bf16[64,1024]{1,0:T(8,128)(2,1)S(1)}, u32[]{:S(2)}, u32[]{:S(2)}) collective-permute-start(bf16[64,1024]{1,0:T(8,128)(2,1)S(1)} %copy-done.35), channel_id=1, source_target_pairs={{0,1},{1,2},{2,3},{3,0},{4,5},{5,6},{6,7},{7,4},{8,9},{9,10},{10,1... | collective-permute-start | bytes 393224 | tf_op jit(solution)/shard_map/ppermute | solution.py:30
  53.8 2.0 %collective-permute-done.2 = bf16[64,1024]{1,0:T(8,128)(2,1)S(1)} collective-permute-done((bf16[64,1024]{1,0:T(8,128)(2,1)}, bf16[64,1024]{1,0:T(8,128)(2,1)S(1)}, u32[]{:S(2)}, u32[]{:S(2)}) %collective-permute-start.2) | collective-permute-done | bytes 131104 | tf_op jit(solution)/shard_map/ppermute | solution.py:30
  55.8 1.4 collective-permute-start.22
  57.4 2.0 %collective-permute-start.21 = (bf16[4,1,64,512]{3,2,0,1:T(8,128)(2,1)}, bf16[4,1,64,512]{3,2,0,1:T(8,128)(2,1)}, u32[]{:S(2)}, u32[]{:S(2)}) collective-permute-start(bf16[4,1,64,512]{3,2,0,1:T(8,128)(2,1)} %pad_maximum_fusion.1), channel_id=1, source_target_pairs={{0,28},{9,29},{18,30},{27,31}} | collective-permute-start | bytes 786440 | tf_op jit(solution)/shard_map/ppermute | solution.py:77
  60.2 3.9 %collective-permute-start.7 = (bf16[64,128]{1,0:T(8,128)(2,1)S(1)}, bf16[64,128]{1,0:T(8,128)(2,1)S(1)}, u32[]{:S(2)}, u32[]{:S(2)}) collective-permute-start(bf16[64,128]{1,0:T(8,128)(2,1)S(1)} %convolution_convert_fusion.18), channel_id=1, source_target_pairs={{0,3},{1,0},{2,1},{3,2},{4,7},{5,4},{6,5},{7,6},{8,11},{9,8},{10,9... | collective-permute-start | bytes 49160 | tf_op jit(solution)/shard_map/ppermute | solution.py:30
  66.4 3.2 %collective-permute-start.1 = (bf16[64,384]{1,0:T(8,128)(2,1)S(1)}, bf16[64,384]{1,0:T(8,128)(2,1)S(1)}, u32[]{:S(2)}, u32[]{:S(2)}) collective-permute-start(bf16[64,384]{1,0:T(8,128)(2,1)S(1)} %convolution_convert_fusion.6), channel_id=1, source_target_pairs={{0,3},{1,0},{2,1},{3,2},{4,7},{5,4},{6,5},{7,6},{8,11},{9,8},{10,9... | collective-permute-start | bytes 147464 | tf_op jit(solution)/shard_map/ppermute | solution.py:30
  69.7 1.7 %collective-permute-done.5 = bf16[64,384]{1,0:T(8,128)(2,1)S(1)} collective-permute-done((bf16[64,384]{1,0:T(8,128)(2,1)S(1)}, bf16[64,384]{1,0:T(8,128)(2,1)S(1)}, u32[]{:S(2)}, u32[]{:S(2)}) %collective-permute-start.5) | collective-permute-done | bytes 49184 | tf_op jit(solution)/shard_map/ppermute | solution.py:30
  71.9 3.8 %collective-permute-start.13 = (bf16[64,384]{1,0:T(8,128)(2,1)}, bf16[64,384]{1,0:T(8,128)(2,1)}, u32[]{:S(2)}, u32[]{:S(2)}) collective-permute-start(bf16[64,384]{1,0:T(8,128)(2,1)} %convolution_convert_fusion.2), channel_id=1, source_target_pairs={{0,3},{1,0},{2,1},{3,2},{4,7},{5,4},{6,5},{7,6},{8,11},{9,8},{10,9... | collective-permute-start | bytes 147464 | tf_op jit(solution)/shard_map/ppermute | solution.py:30
  78.7 1.5 %collective-permute-start.27 = (bf16[64,640]{1,0:T(8,128)(2,1)S(1)}, bf16[64,640]{1,0:T(8,128)(2,1)S(1)}, u32[]{:S(2)}, u32[]{:S(2)}) collective-permute-start(bf16[64,640]{1,0:T(8,128)(2,1)S(1)} %concatenate.26), channel_id=1, source_target_pairs={{0,2},{1,3},{2,0},{3,1},{4,6},{5,7},{6,4},{7,5},{8,10},{9,11},{10,... | collective-permute-start | bytes 245768 | tf_op jit(solution)/shard_map/ppermute | solution.py:30
  80.2 1.9 %collective-permute-start.26 = (bf16[64,640]{1,0:T(8,128)(2,1)S(1)}, bf16[64,640]{1,0:T(8,128)(2,1)S(1)}, u32[]{:S(2)}, u32[]{:S(2)}) collective-permute-start(bf16[64,640]{1,0:T(8,128)(2,1)S(1)} %concatenate.26), channel_id=1, source_target_pairs={{0,1},{1,2},{2,3},{3,0},{4,5},{5,6},{6,7},{7,4},{8,9},{9,10},{10,1... | collective-permute-start | bytes 245768 | tf_op jit(solution)/shard_map/ppermute | solution.py:30
  84.5 1.9 %collective-permute-done.26 = bf16[64,640]{1,0:T(8,128)(2,1)S(1)} collective-permute-done((bf16[64,640]{1,0:T(8,128)(2,1)S(1)}, bf16[64,640]{1,0:T(8,128)(2,1)S(1)}, u32[]{:S(2)}, u32[]{:S(2)}) %collective-permute-start.26) | collective-permute-done | bytes 81952 | tf_op jit(solution)/shard_map/ppermute | solution.py:30
  90.2 4.6 %collective-permute-done.29 = bf16[4,64,1024]{2,1,0:T(8,128)(2,1)S(1)} collective-permute-done((bf16[4,64,1024]{2,1,0:T(8,128)(2,1)S(1)}, bf16[4,64,1024]{2,1,0:T(8,128)(2,1)S(1)}, u32[]{:S(2)}, u32[]{:S(2)}) %collective-permute-start.29) | collective-permute-done | bytes 524320 | tf_op jit(solution)/shard_map/ppermute | solution.py:168
  94.8 1.2 fusion.62
  96.7 2.2 %collective-permute-start.31 = (bf16[64,128]{1,0:T(8,128)(2,1)S(1)}, bf16[64,128]{1,0:T(8,128)(2,1)S(1)}, u32[]{:S(2)}, u32[]{:S(2)}) collective-permute-start(bf16[64,128]{1,0:T(8,128)(2,1)S(1)} %convolution_convert_fusion.13), channel_id=1, source_target_pairs={{0,2},{1,3},{2,0},{3,1},{4,6},{5,7},{6,4},{7,5},{8,10},{9,11},{10,... | collective-permute-start | bytes 49160 | tf_op jit(solution)/shard_map/ppermute | solution.py:30
  98.9 1.5 %collective-permute-start.30 = (bf16[64,128]{1,0:T(8,128)(2,1)S(1)}, bf16[64,128]{1,0:T(8,128)(2,1)S(1)}, u32[]{:S(2)}, u32[]{:S(2)}) collective-permute-start(bf16[64,128]{1,0:T(8,128)(2,1)S(1)} %convolution_convert_fusion.14), channel_id=1, source_target_pairs={{0,3},{1,0},{2,1},{3,2},{4,7},{5,4},{6,5},{7,6},{8,11},{9,8},{10,9... | collective-permute-start | bytes 49160 | tf_op jit(solution)/shard_map/ppermute | solution.py:30
  100.4 1.3 fusion.83
  105.1 1.3 copy.45
  106.4 1.3 copy.46
  107.7 1.4 copy.47
  109.1 1.3 copy.48
  110.4 1.4 copy.49
  111.7 1.6 %concatenate.28 = bf16[64,640]{1,0:T(8,128)(2,1)} concatenate(bf16[64,128]{1,0:T(8,128)(2,1)} %copy-done.25, bf16[64,128]{1,0:T(8,128)(2,1)S(1)} %get-tuple-element.60, bf16[64,128]{1,0:T(8,128)(2,1)} %copy-done.33, bf16[64,128]{1,0:T(8,128)(2,1)} %convolution_convert_fusion.8, bf16[64,1]{1,0:T(8,128)(2,1)} %copy.44, bf16[64,1]{1,0:T(8,128)(2,1)} %copy.45, bf16[64,1]{1,0:T(8,128)(2,1)} %copy.46, ...), dimensions={1} | concatenate | bytes 163840 | tf_op jit(solution)/shard_map/concatenate | solution.py:141
  113.3 1.2 collective-permute-start.34
  114.5 2.6 %collective-permute-start.33 = (bf16[64,640]{1,0:T(8,128)(2,1)}, bf16[64,640]{1,0:T(8,128)(2,1)}, u32[]{:S(2)}, u32[]{:S(2)}) collective-permute-start(bf16[64,640]{1,0:T(8,128)(2,1)} %concatenate.28), channel_id=1, source_target_pairs={{0,1},{1,2},{2,3},{3,0},{4,5},{5,6},{6,7},{7,4},{8,9},{9,10},{10,1... | collective-permute-start | bytes 245768 | tf_op jit(solution)/shard_map/ppermute | solution.py:30
  117.2 1.2 collective-permute-start.35
  118.4 1.5 %concatenate.29 = bf16[64,128]{1,0:T(8,128)(2,1)} concatenate(bf16[64,1]{1,0:T(8,128)(2,1)} %copy.44, bf16[64,1]{1,0:T(8,128)(2,1)} %copy.45, bf16[64,1]{1,0:T(8,128)(2,1)} %copy.46, bf16[64,1]{1,0:T(8,128)(2,1)} %copy.47, bf16[64,1]{1,0:T(8,128)(2,1)} %copy.48, bf16[64,1]{1,0:T(8,128)(2,1)} %copy.49, bf16[64,122]{1,0:T(8,128)(2,1)} %copy-done.22), dimensions={1} | concatenate | bytes 32768 | tf_op jit(solution)/shard_map/concatenate | solution.py:141
  119.9 1.4 add_convert_fusion.3
  121.6 1.3 fusion.75
  124.0 1.2 add_convert_fusion.6
  125.1 3.0 %collective-permute-start.36 = (bf16[64,1024]{1,0:T(8,128)(2,1)S(1)}, bf16[64,1024]{1,0:T(8,128)(2,1)S(1)}, u32[]{:S(2)}, u32[]{:S(2)}) collective-permute-start(bf16[64,1024]{1,0:T(8,128)(2,1)S(1)} %add_convert_fusion.6), channel_id=1, source_target_pairs={{0,3},{1,0},{2,1},{3,2},{4,7},{5,4},{6,5},{7,6},{8,11},{9,8},{10,9... | collective-permute-start | bytes 393224 | tf_op jit(solution)/shard_map/ppermute | solution.py:30
  132.8 2.1 %collective-permute-start.38 = (bf16[64,1024]{1,0:T(8,128)(2,1)S(1)}, bf16[64,1024]{1,0:T(8,128)(2,1)S(1)}, u32[]{:S(2)}, u32[]{:S(2)}) collective-permute-start(bf16[64,1024]{1,0:T(8,128)(2,1)S(1)} %add_convert_fusion.4), channel_id=1, source_target_pairs={{0,1},{1,2},{2,3},{3,0},{4,5},{5,6},{6,7},{7,4},{8,9},{9,10},{10,1... | collective-permute-start | bytes 393224 | tf_op jit(solution)/shard_map/ppermute | solution.py:30
  134.9 1.2 fusion.115
  136.1 1.2 fusion.118
  137.3 1.2 fusion.112
  143.8 1.6 %add_bitcast_fusion = f32[1,1024,384]{2,1,0:T(8,128)} fusion(bf16[1024,384]{1,0:T(8,128)(2,1)S(1)} %add_convert_fusion.1, bf16[1024,384]{1,0:T(8,128)(2,1)S(1)} %add_convert_fusion.2, bf16[1024,384]{1,0:T(8,128)(2,1)S(1)} %add_convert_fusion.3, f32[1024,384]{1,0:T(8,128)S(1)} %fusion.112, bf16[64,1024]{1,0:T(8,128)(2,1)S(1)} %copy-done.8, ...), kind=kOutput, calls=%fused_computation.7 | convolution fusion | flops 53870592 | bytes 5685248 | tf_op jit(solution)/shard_map/dot_general | solution.py:161
  (259 shorter events, 42.2 us)
Async XLA Ops:
  0.6 15.7 %copy-start = (bf16[1,1024,128]{2,1,0:T(8,128)(2,1)S(1)}, bf16[1,1024,128]{2,1,0:T(8,128)(2,1)}, u32[]{:S(2)}) copy-start(bf16[1,1024,128]{2,1,0:T(8,128)(2,1)} %param.9) | copy-start | bytes 786436
  2.1 16.0 %collective-permute-start.25 = (bf16[16,384]{1,0:T(8,128)(2,1)S(1)}, bf16[16,384]{1,0:T(8,128)(2,1)S(1)}, u32[]{:S(2)}, u32[]{:S(2)}) collective-permute-start(bf16[16,384]{1,0:T(8,128)(2,1)S(1)} %broadcast_in_dim.19), channel_id=1, source_target_pairs={{0,3},{1,0},{2,1},{3,2},{4,7},{5,4},{6,5},{7,6},{8,11},{9,8},{10,9... | collective-permute-start | bytes 36872 | tf_op jit(solution)/shard_map/ppermute | solution.py:30
  7.2 12.2 %collective-permute-start.24 = (bf16[16,384]{1,0:T(8,128)(2,1)S(1)}, bf16[16,384]{1,0:T(8,128)(2,1)S(1)}, u32[]{:S(2)}, u32[]{:S(2)}) collective-permute-start(bf16[16,384]{1,0:T(8,128)(2,1)S(1)} %broadcast_in_dim.19), channel_id=1, source_target_pairs={{0,2},{1,3},{2,0},{3,1},{4,6},{5,7},{6,4},{7,5},{8,10},{9,11},{10,... | collective-permute-start | bytes 36872 | tf_op jit(solution)/shard_map/ppermute | solution.py:30
  7.2 15.2 %collective-permute-start.23 = (bf16[16,384]{1,0:T(8,128)(2,1)S(1)}, bf16[16,384]{1,0:T(8,128)(2,1)S(1)}, u32[]{:S(2)}, u32[]{:S(2)}) collective-permute-start(bf16[16,384]{1,0:T(8,128)(2,1)S(1)} %broadcast_in_dim.19), channel_id=1, source_target_pairs={{0,1},{1,2},{2,3},{3,0},{4,5},{5,6},{6,7},{7,4},{8,9},{9,10},{10,1... | collective-permute-start | bytes 36872 | tf_op jit(solution)/shard_map/ppermute | solution.py:30
  8.2 15.8 %collective-permute-start.20 = (bf16[1,64,512]{2,1,0:T(8,128)(2,1)}, bf16[1,64,512]{2,1,0:T(8,128)(2,1)S(1)}, u32[]{:S(2)}, u32[]{:S(2)}) collective-permute-start(bf16[1,64,512]{2,1,0:T(8,128)(2,1)} %param.7), channel_id=1, source_target_pairs={{1,0},{5,4},{10,9},{14,13},{19,18},{23,22},{24,27},{28,31}} | collective-permute-start | bytes 196616 | tf_op jit(solution)/shard_map/ppermute | solution.py:73
  9.5 15.6 %collective-permute-start.19 = (bf16[1,64,512]{2,1,0:T(8,128)(2,1)}, bf16[1,64,512]{2,1,0:T(8,128)(2,1)S(1)}, u32[]{:S(2)}, u32[]{:S(2)}) collective-permute-start(bf16[1,64,512]{2,1,0:T(8,128)(2,1)} %param.7), channel_id=1, source_target_pairs={{2,0},{6,4},{11,9},{15,13},{16,18},{20,22},{25,27},{29,31}} | collective-permute-start | bytes 196616 | tf_op jit(solution)/shard_map/ppermute | solution.py:73
  13.3 70.3 %copy-start.3 = (bf16[1,64,4096]{2,1,0:T(8,128)(2,1)}, bf16[1,64,4096]{2,1,0:T(8,128)(2,1)S(1)}, u32[]{:S(2)}) copy-start(bf16[1,64,4096]{2,1,0:T(8,128)(2,1)S(1)} %get-tuple-element.49) | copy-start | bytes 1572868
  18.1 11.0 %collective-permute-start.18 = (bf16[1,64,512]{2,1,0:T(8,128)(2,1)}, bf16[1,64,512]{2,1,0:T(8,128)(2,1)S(1)}, u32[]{:S(2)}, u32[]{:S(2)}) collective-permute-start(bf16[1,64,512]{2,1,0:T(8,128)(2,1)} %param.7), channel_id=1, source_target_pairs={{3,0},{7,4},{8,9},{12,13},{17,18},{21,22},{26,27},{30,31}} | collective-permute-start | bytes 196616 | tf_op jit(solution)/shard_map/ppermute | solution.py:73
  19.4 17.1 %collective-permute-start.14 = (bf16[64,1024]{1,0:T(8,128)(2,1)}, bf16[64,1024]{1,0:T(8,128)(2,1)S(1)}, u32[]{:S(2)}, u32[]{:S(2)}) collective-permute-start(bf16[64,1024]{1,0:T(8,128)(2,1)} %get-tuple-element.53), channel_id=1, source_target_pairs={{0,2},{1,3},{2,0},{3,1},{4,6},{5,7},{6,4},{7,5},{8,10},{9,11},{10,... | collective-permute-start | bytes 393224 | tf_op jit(solution)/shard_map/ppermute | solution.py:30
  22.4 9.6 %collective-permute-start.16 = (bf16[64,1024]{1,0:T(8,128)(2,1)}, bf16[64,1024]{1,0:T(8,128)(2,1)S(1)}, u32[]{:S(2)}, u32[]{:S(2)}) collective-permute-start(bf16[64,1024]{1,0:T(8,128)(2,1)} %get-tuple-element.52), channel_id=1, source_target_pairs={{0,3},{1,0},{2,1},{3,2},{4,7},{5,4},{6,5},{7,6},{8,11},{9,8},{10,9... | collective-permute-start | bytes 393224 | tf_op jit(solution)/shard_map/ppermute | solution.py:30
  24.0 53.5 %copy-start.42 = (f32[384]{0:T(512)}, f32[384]{0:T(512)S(1)}, u32[]{:S(2)}) copy-start(f32[384]{0:T(512)S(1)} %fusion.177) | copy-start | bytes 4612
  24.6 13.8 %collective-permute-start.12 = (bf16[64,1024]{1,0:T(8,128)(2,1)S(1)}, bf16[64,1024]{1,0:T(8,128)(2,1)S(1)}, u32[]{:S(2)}, u32[]{:S(2)}) collective-permute-start(bf16[64,1024]{1,0:T(8,128)(2,1)S(1)} %get-tuple-element.51), channel_id=1, source_target_pairs={{0,1},{1,2},{2,3},{3,0},{4,5},{5,6},{6,7},{7,4},{8,9},{9,10},{10,1... | collective-permute-start | bytes 393224 | tf_op jit(solution)/shard_map/ppermute | solution.py:30
  25.7 31.7 %collective-permute-start.10 = (bf16[64,1024]{1,0:T(8,128)(2,1)}, bf16[64,1024]{1,0:T(8,128)(2,1)S(1)}, u32[]{:S(2)}, u32[]{:S(2)}) collective-permute-start(bf16[64,1024]{1,0:T(8,128)(2,1)} %get-tuple-element.58), channel_id=1, source_target_pairs={{0,3},{1,0},{2,1},{3,2},{4,7},{5,4},{6,5},{7,6},{8,11},{9,8},{10,9... | collective-permute-start | bytes 393224 | tf_op jit(solution)/shard_map/ppermute | solution.py:30
  29.1 16.4 %collective-permute-start.4 = (bf16[64,1024]{1,0:T(8,128)(2,1)S(1)}, bf16[64,1024]{1,0:T(8,128)(2,1)S(1)}, u32[]{:S(2)}, u32[]{:S(2)}) collective-permute-start(bf16[64,1024]{1,0:T(8,128)(2,1)S(1)} %get-tuple-element.55), channel_id=1, source_target_pairs={{0,3},{1,0},{2,1},{3,2},{4,7},{5,4},{6,5},{7,6},{8,11},{9,8},{10,9... | collective-permute-start | bytes 393224 | tf_op jit(solution)/shard_map/ppermute | solution.py:30
  32.0 23.8 %collective-permute-start.2 = (bf16[64,1024]{1,0:T(8,128)(2,1)}, bf16[64,1024]{1,0:T(8,128)(2,1)S(1)}, u32[]{:S(2)}, u32[]{:S(2)}) collective-permute-start(bf16[64,1024]{1,0:T(8,128)(2,1)} %get-tuple-element.56), channel_id=1, source_target_pairs={{0,2},{1,3},{2,0},{3,1},{4,6},{5,7},{6,4},{7,5},{8,10},{9,11},{10,... | collective-permute-start | bytes 393224 | tf_op jit(solution)/shard_map/ppermute | solution.py:30
  36.5 20.9 %copy-start.13 = (bf16[64,1024]{1,0:T(8,128)(2,1)}, bf16[64,1024]{1,0:T(8,128)(2,1)S(1)}, u32[]{:S(2)}) copy-start(bf16[64,1024]{1,0:T(8,128)(2,1)S(1)} %collective-permute-done.14) | copy-start | bytes 393220
  36.5 23.7 %collective-permute-start = (bf16[64,1024]{1,0:T(8,128)(2,1)S(1)}, bf16[64,1024]{1,0:T(8,128)(2,1)S(1)}, u32[]{:S(2)}, u32[]{:S(2)}) collective-permute-start(bf16[64,1024]{1,0:T(8,128)(2,1)S(1)} %get-tuple-element.54), channel_id=1, source_target_pairs={{0,1},{1,2},{2,3},{3,0},{4,5},{5,6},{6,7},{7,4},{8,9},{9,10},{10,1... | collective-permute-start | bytes 393224 | tf_op jit(solution)/shard_map/ppermute | solution.py:30
  38.5 21.1 %copy-start.17 = (bf16[64,1024]{1,0:T(8,128)(2,1)}, bf16[64,1024]{1,0:T(8,128)(2,1)S(1)}, u32[]{:S(2)}) copy-start(bf16[64,1024]{1,0:T(8,128)(2,1)S(1)} %collective-permute-done.12) | copy-start | bytes 393220
  38.5 21.1 %collective-permute-start.8 = (bf16[64,1024]{1,0:T(8,128)(2,1)}, bf16[64,1024]{1,0:T(8,128)(2,1)S(1)}, u32[]{:S(2)}, u32[]{:S(2)}) collective-permute-start(bf16[64,1024]{1,0:T(8,128)(2,1)} %get-tuple-element.59), channel_id=1, source_target_pairs={{0,2},{1,3},{2,0},{3,1},{4,6},{5,7},{6,4},{7,5},{8,10},{9,11},{10,... | collective-permute-start | bytes 393224 | tf_op jit(solution)/shard_map/ppermute | solution.py:30
  45.5 41.2 %copy-start.7 = (bf16[64,1024]{1,0:T(8,128)(2,1)}, bf16[64,1024]{1,0:T(8,128)(2,1)S(1)}, u32[]{:S(2)}) copy-start(bf16[64,1024]{1,0:T(8,128)(2,1)S(1)} %collective-permute-done.4) | copy-start | bytes 393220
  45.5 14.3 %collective-permute-start.6 = (bf16[64,1024]{1,0:T(8,128)(2,1)S(1)}, bf16[64,1024]{1,0:T(8,128)(2,1)S(1)}, u32[]{:S(2)}, u32[]{:S(2)}) collective-permute-start(bf16[64,1024]{1,0:T(8,128)(2,1)S(1)} %copy-done.35), channel_id=1, source_target_pairs={{0,1},{1,2},{2,3},{3,0},{4,5},{5,6},{6,7},{7,4},{8,9},{9,10},{10,1... | collective-permute-start | bytes 393224 | tf_op jit(solution)/shard_map/ppermute | solution.py:30
  55.8 31.3 %copy-start.9 = (bf16[64,1024]{1,0:T(8,128)(2,1)}, bf16[64,1024]{1,0:T(8,128)(2,1)S(1)}, u32[]{:S(2)}) copy-start(bf16[64,1024]{1,0:T(8,128)(2,1)S(1)} %collective-permute-done.2) | copy-start | bytes 393220
  55.8 34.4 %collective-permute-start.22 = (bf16[4,1,64,512]{3,2,0,1:T(8,128)(2,1)}, bf16[4,1,64,512]{3,2,0,1:T(8,128)(2,1)}, u32[]{:S(2)}, u32[]{:S(2)}) collective-permute-start(bf16[4,1,64,512]{3,2,0,1:T(8,128)(2,1)} %pad_maximum_fusion.1), channel_id=1, source_target_pairs={{4,28},{13,29},{22,30},{31,31}} | collective-permute-start | bytes 786440 | tf_op jit(solution)/shard_map/ppermute | solution.py:77
  57.4 32.8 %collective-permute-start.21 = (bf16[4,1,64,512]{3,2,0,1:T(8,128)(2,1)}, bf16[4,1,64,512]{3,2,0,1:T(8,128)(2,1)}, u32[]{:S(2)}, u32[]{:S(2)}) collective-permute-start(bf16[4,1,64,512]{3,2,0,1:T(8,128)(2,1)} %pad_maximum_fusion.1), channel_id=1, source_target_pairs={{0,28},{9,29},{18,30},{27,31}} | collective-permute-start | bytes 786440 | tf_op jit(solution)/shard_map/ppermute | solution.py:77
  59.6 5.8 %collective-permute-start.11 = (bf16[64,128]{1,0:T(8,128)(2,1)S(1)}, bf16[64,128]{1,0:T(8,128)(2,1)S(1)}, u32[]{:S(2)}, u32[]{:S(2)}) collective-permute-start(bf16[64,128]{1,0:T(8,128)(2,1)S(1)} %convolution_convert_fusion.16), channel_id=1, source_target_pairs={{0,1},{1,2},{2,3},{3,0},{4,5},{5,6},{6,7},{7,4},{8,9},{9,10},{10,1... | collective-permute-start | bytes 49160 | tf_op jit(solution)/shard_map/ppermute | solution.py:30
  59.9 5.5 %collective-permute-start.9 = (bf16[64,128]{1,0:T(8,128)(2,1)S(1)}, bf16[64,128]{1,0:T(8,128)(2,1)S(1)}, u32[]{:S(2)}, u32[]{:S(2)}) collective-permute-start(bf16[64,128]{1,0:T(8,128)(2,1)S(1)} %convolution_convert_fusion.17), channel_id=1, source_target_pairs={{0,2},{1,3},{2,0},{3,1},{4,6},{5,7},{6,4},{7,5},{8,10},{9,11},{10,... | collective-permute-start | bytes 49160 | tf_op jit(solution)/shard_map/ppermute | solution.py:30
  60.1 17.5 %copy-start.45 = (f32[2,64]{1,0:T(2,128)S(1)}, f32[2,64]{1,0:T(2,128)}, u32[]{:S(2)}) copy-start(f32[2,64]{1,0:T(2,128)} %copy-done.44) | copy-start | bytes 1540
  60.2 27.4 %copy-start.11 = (bf16[64,1024]{1,0:T(8,128)(2,1)}, bf16[64,1024]{1,0:T(8,128)(2,1)S(1)}, u32[]{:S(2)}) copy-start(bf16[64,1024]{1,0:T(8,128)(2,1)S(1)} %collective-permute-done) | copy-start | bytes 393220
  60.2 6.3 %collective-permute-start.7 = (bf16[64,128]{1,0:T(8,128)(2,1)S(1)}, bf16[64,128]{1,0:T(8,128)(2,1)S(1)}, u32[]{:S(2)}, u32[]{:S(2)}) collective-permute-start(bf16[64,128]{1,0:T(8,128)(2,1)S(1)} %convolution_convert_fusion.18), channel_id=1, source_target_pairs={{0,3},{1,0},{2,1},{3,2},{4,7},{5,4},{6,5},{7,6},{8,11},{9,8},{10,9... | collective-permute-start | bytes 49160 | tf_op jit(solution)/shard_map/ppermute | solution.py:30
  65.4 6.0 %collective-permute-start.5 = (bf16[64,384]{1,0:T(8,128)(2,1)S(1)}, bf16[64,384]{1,0:T(8,128)(2,1)S(1)}, u32[]{:S(2)}, u32[]{:S(2)}) collective-permute-start(bf16[64,384]{1,0:T(8,128)(2,1)S(1)} %convolution_convert_fusion.4), channel_id=1, source_target_pairs={{0,1},{1,2},{2,3},{3,0},{4,5},{5,6},{6,7},{7,4},{8,9},{9,10},{10,1... | collective-permute-start | bytes 147464 | tf_op jit(solution)/shard_map/ppermute | solution.py:30
  65.4 6.0 %collective-permute-start.3 = (bf16[64,384]{1,0:T(8,128)(2,1)S(1)}, bf16[64,384]{1,0:T(8,128)(2,1)S(1)}, u32[]{:S(2)}, u32[]{:S(2)}) collective-permute-start(bf16[64,384]{1,0:T(8,128)(2,1)S(1)} %convolution_convert_fusion.5), channel_id=1, source_target_pairs={{0,2},{1,3},{2,0},{3,1},{4,6},{5,7},{6,4},{7,5},{8,10},{9,11},{10,... | collective-permute-start | bytes 147464 | tf_op jit(solution)/shard_map/ppermute | solution.py:30
  66.4 5.4 %collective-permute-start.1 = (bf16[64,384]{1,0:T(8,128)(2,1)S(1)}, bf16[64,384]{1,0:T(8,128)(2,1)S(1)}, u32[]{:S(2)}, u32[]{:S(2)}) collective-permute-start(bf16[64,384]{1,0:T(8,128)(2,1)S(1)} %convolution_convert_fusion.6), channel_id=1, source_target_pairs={{0,3},{1,0},{2,1},{3,2},{4,7},{5,4},{6,5},{7,6},{8,11},{9,8},{10,9... | collective-permute-start | bytes 147464 | tf_op jit(solution)/shard_map/ppermute | solution.py:30
  71.4 7.2 %collective-permute-start.17 = (bf16[64,384]{1,0:T(8,128)(2,1)}, bf16[64,384]{1,0:T(8,128)(2,1)S(1)}, u32[]{:S(2)}, u32[]{:S(2)}) collective-permute-start(bf16[64,384]{1,0:T(8,128)(2,1)} %convolution_convert_fusion), channel_id=1, source_target_pairs={{0,1},{1,2},{2,3},{3,0},{4,5},{5,6},{6,7},{7,4},{8,9},{9,10},{10,1... | collective-permute-start | bytes 147464 | tf_op jit(solution)/shard_map/ppermute | solution.py:30
  71.4 7.3 %collective-permute-start.15 = (bf16[64,384]{1,0:T(8,128)(2,1)}, bf16[64,384]{1,0:T(8,128)(2,1)S(1)}, u32[]{:S(2)}, u32[]{:S(2)}) collective-permute-start(bf16[64,384]{1,0:T(8,128)(2,1)} %convolution_convert_fusion.1), channel_id=1, source_target_pairs={{0,2},{1,3},{2,0},{3,1},{4,6},{5,7},{6,4},{7,5},{8,10},{9,11},{10,... | collective-permute-start | bytes 147464 | tf_op jit(solution)/shard_map/ppermute | solution.py:30
  71.9 8.3 %collective-permute-start.13 = (bf16[64,384]{1,0:T(8,128)(2,1)}, bf16[64,384]{1,0:T(8,128)(2,1)}, u32[]{:S(2)}, u32[]{:S(2)}) collective-permute-start(bf16[64,384]{1,0:T(8,128)(2,1)} %convolution_convert_fusion.2), channel_id=1, source_target_pairs={{0,3},{1,0},{2,1},{3,2},{4,7},{5,4},{6,5},{7,6},{8,11},{9,8},{10,9... | collective-permute-start | bytes 147464 | tf_op jit(solution)/shard_map/ppermute | solution.py:30
  78.5 5.5 %collective-permute-start.28 = (bf16[64,640]{1,0:T(8,128)(2,1)S(1)}, bf16[64,640]{1,0:T(8,128)(2,1)S(1)}, u32[]{:S(2)}, u32[]{:S(2)}) collective-permute-start(bf16[64,640]{1,0:T(8,128)(2,1)S(1)} %concatenate.26), channel_id=1, source_target_pairs={{0,3},{1,0},{2,1},{3,2},{4,7},{5,4},{6,5},{7,6},{8,11},{9,8},{10,9... | collective-permute-start | bytes 245768 | tf_op jit(solution)/shard_map/ppermute | solution.py:30
  78.7 5.6 %collective-permute-start.27 = (bf16[64,640]{1,0:T(8,128)(2,1)S(1)}, bf16[64,640]{1,0:T(8,128)(2,1)S(1)}, u32[]{:S(2)}, u32[]{:S(2)}) collective-permute-start(bf16[64,640]{1,0:T(8,128)(2,1)S(1)} %concatenate.26), channel_id=1, source_target_pairs={{0,2},{1,3},{2,0},{3,1},{4,6},{5,7},{6,4},{7,5},{8,10},{9,11},{10,... | collective-permute-start | bytes 245768 | tf_op jit(solution)/shard_map/ppermute | solution.py:30
  80.2 6.2 %collective-permute-start.26 = (bf16[64,640]{1,0:T(8,128)(2,1)S(1)}, bf16[64,640]{1,0:T(8,128)(2,1)S(1)}, u32[]{:S(2)}, u32[]{:S(2)}) collective-permute-start(bf16[64,640]{1,0:T(8,128)(2,1)S(1)} %concatenate.26), channel_id=1, source_target_pairs={{0,1},{1,2},{2,3},{3,0},{4,5},{5,6},{6,7},{7,4},{8,9},{9,10},{10,1... | collective-permute-start | bytes 245768 | tf_op jit(solution)/shard_map/ppermute | solution.py:30
  88.0 6.8 %collective-permute-start.29 = (bf16[4,64,1024]{2,1,0:T(8,128)(2,1)S(1)}, bf16[4,64,1024]{2,1,0:T(8,128)(2,1)S(1)}, u32[]{:S(2)}, u32[]{:S(2)}) collective-permute-start(bf16[4,64,1024]{2,1,0:T(8,128)(2,1)S(1)} %pad_maximum_fusion), channel_id=1, source_target_pairs={{0,28},{4,0},{8,4},{12,8},{16,12},{20,16},{24,20},{28,24},{1,29},{... | collective-permute-start | bytes 1572872 | tf_op jit(solution)/shard_map/ppermute | solution.py:168
  96.5 5.6 %collective-permute-start.32 = (bf16[64,128]{1,0:T(8,128)(2,1)S(1)}, bf16[64,128]{1,0:T(8,128)(2,1)S(1)}, u32[]{:S(2)}, u32[]{:S(2)}) collective-permute-start(bf16[64,128]{1,0:T(8,128)(2,1)S(1)} %convolution_convert_fusion.12), channel_id=1, source_target_pairs={{0,1},{1,2},{2,3},{3,0},{4,5},{5,6},{6,7},{7,4},{8,9},{9,10},{10,1... | collective-permute-start | bytes 49160 | tf_op jit(solution)/shard_map/ppermute | solution.py:30
  96.7 5.4 %collective-permute-start.31 = (bf16[64,128]{1,0:T(8,128)(2,1)S(1)}, bf16[64,128]{1,0:T(8,128)(2,1)S(1)}, u32[]{:S(2)}, u32[]{:S(2)}) collective-permute-start(bf16[64,128]{1,0:T(8,128)(2,1)S(1)} %convolution_convert_fusion.13), channel_id=1, source_target_pairs={{0,2},{1,3},{2,0},{3,1},{4,6},{5,7},{6,4},{7,5},{8,10},{9,11},{10,... | collective-permute-start | bytes 49160 | tf_op jit(solution)/shard_map/ppermute | solution.py:30
  98.9 3.8 %collective-permute-start.30 = (bf16[64,128]{1,0:T(8,128)(2,1)S(1)}, bf16[64,128]{1,0:T(8,128)(2,1)S(1)}, u32[]{:S(2)}, u32[]{:S(2)}) collective-permute-start(bf16[64,128]{1,0:T(8,128)(2,1)S(1)} %convolution_convert_fusion.14), channel_id=1, source_target_pairs={{0,3},{1,0},{2,1},{3,2},{4,7},{5,4},{6,5},{7,6},{8,11},{9,8},{10,9... | collective-permute-start | bytes 49160 | tf_op jit(solution)/shard_map/ppermute | solution.py:30
  113.3 14.8 %collective-permute-start.34 = (bf16[64,640]{1,0:T(8,128)(2,1)}, bf16[64,640]{1,0:T(8,128)(2,1)}, u32[]{:S(2)}, u32[]{:S(2)}) collective-permute-start(bf16[64,640]{1,0:T(8,128)(2,1)} %concatenate.28), channel_id=1, source_target_pairs={{0,2},{1,3},{2,0},{3,1},{4,6},{5,7},{6,4},{7,5},{8,10},{9,11},{10,... | collective-permute-start | bytes 245768 | tf_op jit(solution)/shard_map/ppermute | solution.py:30
  114.5 8.5 %collective-permute-start.33 = (bf16[64,640]{1,0:T(8,128)(2,1)}, bf16[64,640]{1,0:T(8,128)(2,1)}, u32[]{:S(2)}, u32[]{:S(2)}) collective-permute-start(bf16[64,640]{1,0:T(8,128)(2,1)} %concatenate.28), channel_id=1, source_target_pairs={{0,1},{1,2},{2,3},{3,0},{4,5},{5,6},{6,7},{7,4},{8,9},{9,10},{10,1... | collective-permute-start | bytes 245768 | tf_op jit(solution)/shard_map/ppermute | solution.py:30
  117.2 13.5 %collective-permute-start.35 = (bf16[64,640]{1,0:T(8,128)(2,1)}, bf16[64,640]{1,0:T(8,128)(2,1)}, u32[]{:S(2)}, u32[]{:S(2)}) collective-permute-start(bf16[64,640]{1,0:T(8,128)(2,1)} %concatenate.28), channel_id=1, source_target_pairs={{0,3},{1,0},{2,1},{3,2},{4,7},{5,4},{6,5},{7,6},{8,11},{9,8},{10,9... | collective-permute-start | bytes 245768 | tf_op jit(solution)/shard_map/ppermute | solution.py:30
  125.1 21.3 %collective-permute-start.36 = (bf16[64,1024]{1,0:T(8,128)(2,1)S(1)}, bf16[64,1024]{1,0:T(8,128)(2,1)S(1)}, u32[]{:S(2)}, u32[]{:S(2)}) collective-permute-start(bf16[64,1024]{1,0:T(8,128)(2,1)S(1)} %add_convert_fusion.6), channel_id=1, source_target_pairs={{0,3},{1,0},{2,1},{3,2},{4,7},{5,4},{6,5},{7,6},{8,11},{9,8},{10,9... | collective-permute-start | bytes 393224 | tf_op jit(solution)/shard_map/ppermute | solution.py:30
  130.3 16.3 %collective-permute-start.37 = (bf16[64,1024]{1,0:T(8,128)(2,1)S(1)}, bf16[64,1024]{1,0:T(8,128)(2,1)S(1)}, u32[]{:S(2)}, u32[]{:S(2)}) collective-permute-start(bf16[64,1024]{1,0:T(8,128)(2,1)S(1)} %add_convert_fusion.5), channel_id=1, source_target_pairs={{0,2},{1,3},{2,0},{3,1},{4,6},{5,7},{6,4},{7,5},{8,10},{9,11},{10,... | collective-permute-start | bytes 393224 | tf_op jit(solution)/shard_map/ppermute | solution.py:30
  132.8 13.7 %collective-permute-start.38 = (bf16[64,1024]{1,0:T(8,128)(2,1)S(1)}, bf16[64,1024]{1,0:T(8,128)(2,1)S(1)}, u32[]{:S(2)}, u32[]{:S(2)}) collective-permute-start(bf16[64,1024]{1,0:T(8,128)(2,1)S(1)} %add_convert_fusion.4), channel_id=1, source_target_pairs={{0,1},{1,2},{2,3},{3,0},{4,5},{5,6},{6,7},{7,4},{8,9},{9,10},{10,1... | collective-permute-start | bytes 393224 | tf_op jit(solution)/shard_map/ppermute | solution.py:30
  (38 other events, 157.8 us)

commit v2 on v0

v2 whole, which is shorter than its diff:
```python
import functools
import math

import jax
import jax.numpy as jnp
from jax import lax
from jax.experimental import pallas as pl
from jax.experimental.pallas import tpu as pltpu
from jax.sharding import PartitionSpec as P

EPSILON = 1e-06
CONTRACT_FIRST = (((0,), (0,)), ((), ()))
CONTRACT_LAST = (((1,), (1,)), ((), ()))
F32 = jnp.float32
BF16 = jnp.bfloat16
ROW_TILE = 16
LANES = 128
BOTH = ("pipe", "dp")


def shape(*dims, kind=BF16):
    return jax.ShapeDtypeStruct(dims, kind)


def kernel_call(body, outs, scalars, arrays, scratch=(), flops=0):
    moved = sum(math.prod(a.shape) * a.dtype.itemsize for a in [*arrays, *outs])
    return pl.pallas_call(
        body,
        out_shape=tuple(outs),
        in_specs=[pl.BlockSpec(memory_space=pltpu.SMEM)] * len(scalars)
        + [pl.BlockSpec(memory_space=pltpu.VMEM)] * len(arrays),
        out_specs=tuple(pl.BlockSpec(memory_space=pltpu.VMEM) for _ in outs),
        scratch_shapes=list(scratch),
        compiler_params=pltpu.CompilerParams(vmem_limit_bytes=24 * 1024 * 1024),
        cost_estimate=pl.CostEstimate(flops=flops, bytes_accessed=moved, transcendentals=0),
    )(*[s.reshape(1).astype(jnp.int32) for s in scalars], *arrays)


def dot(left, right, contract=(((1,), (0,)), ((), ()))):
    return lax.dot_general(left, right, contract, preferred_element_type=F32)


def normalize(values):
    centered = values - jnp.mean(values, axis=-1, keepdims=True)
    inverse = lax.rsqrt(jnp.mean(centered * centered, axis=-1, keepdims=True) + EPSILON)
    return (centered * inverse, inverse)


def norm_back(gradient, normed, inverse):
    centered = gradient - jnp.mean(gradient, axis=-1, keepdims=True)
    return inverse * (centered - normed * jnp.mean(gradient * normed, axis=-1, keepdims=True))


def hidden_pieces(inputs, extra, me, count):
    ticks, seq, width = inputs.shape
    part = width // count
    extras = [] if extra is None else [extra]
    slots = ticks + len(extras)

    def body(me_ref, x_ref, *refs):
        extra_refs, refs = refs[: len(extras)], refs[len(extras) :]
        outs, scale_ref, hidden_ref = refs[:count], refs[count], refs[count + 1]
        for t in range(ticks):
            for row in range(0, seq, ROW_TILE):
                rows = slice(row, row + ROW_TILE)
                normed, inverse = normalize(x_ref[t, rows, :].astype(F32))
                hidden_ref[t, rows, :] = normed.astype(BF16)
                scale_ref[t, rows, :] = jnp.broadcast_to(inverse, (ROW_TILE, LANES))
        for j in range(count):
            owner = lax.rem(me_ref[0] + j, count)
            columns = pl.ds(pl.multiple_of(owner * part, LANES), part)
            for t in range(ticks):
                outs[j][t] = hidden_ref[t, :, columns]
            for extra_ref in extra_refs:
                outs[j][ticks] = extra_ref[:, columns]

    outs = [shape(slots, seq, part) for _ in range(count)]
    outs.append(shape(ticks, seq, LANES, kind=F32))
    result = kernel_call(
        body, outs, [me], [inputs, *extras], [pltpu.VMEM((ticks, seq, width), BF16)]
    )
    return list(result[:count]), result[count]


def first_partials(pieces, project, output, width):
    count = len(pieces)
    seq = pieces[0].shape[1]
    wide, head = project.shape[1], output.shape[1]

    def body(*refs):
        piece_refs, project_ref, output_ref = refs[:count], refs[count], refs[count + 1]
        outs = refs[count + 2 :]
        project, output = project_ref[...], output_ref[...]
        sums = jnp.sum(project.astype(F32), axis=0, keepdims=True) / width
        sums = jnp.broadcast_to(sums, (ROW_TILE, wide)).astype(BF16)
        for j in range(count):
            outs[j][:seq, :wide] = dot(piece_refs[j][0], project).astype(BF16)
            outs[j][:seq, wide:] = dot(piece_refs[j][1], output).astype(BF16)
            outs[j][seq:, :wide] = sums
            outs[j][seq:, wide:] = jnp.zeros((ROW_TILE, head), BF16)

    outs = [shape(seq + ROW_TILE, wide + head) for _ in range(count)]
    return list(kernel_call(body, outs, [], [*pieces, project, output]))


def later_partials(pieces, tick, project):
    count = len(pieces)
    seq = pieces[0].shape[1]
    wide = project.shape[1]

    def body(*refs):
        project = refs[count][...]
        for j in range(count):
            refs[count + 1 + j][...] = dot(refs[j][tick], project).astype(BF16)

    return list(kernel_call(body, [shape(seq, wide)] * count, [], [*pieces, project]))


def split_two(value):
    high = value.astype(BF16).astype(F32)
    return high, value - high


def attention_message(projected_parts, head_parts, mean_parts, scales, tick, width):
    seq = scales.shape[1]
    head = head_parts[0].shape[1]
    lists = (projected_parts, head_parts, mean_parts)
    sizes = [len(part) for part in lists]
    root = math.sqrt(head)
    wide = 3 * head

    def body(*refs):
        refs = list(refs)
        projected, head_grad, row_mean = (
            sum(refs.pop(0)[...].astype(F32) for _ in range(size)) for size in sizes
        )
        scale_ref, out_ref = refs
        query, query_scale = normalize(projected[:, :head])
        key, key_scale = normalize(projected[:, head : 2 * head])
        query_half, key_half = query.astype(BF16), key.astype(BF16)
        value_half = projected[:, 2 * head :].astype(BF16)
        powered = jnp.exp(dot(query_half, key_half, CONTRACT_LAST) / root)
        attention = powered / jnp.sum(powered, axis=-1, keepdims=True)
        attention_half = attention.astype(BF16)
        out_ref[:, wide : wide + head] = dot(attention_half, value_half).astype(BF16)
        head_half = head_grad.astype(BF16)
        prob_grad = dot(head_half, value_half, CONTRACT_LAST)
        value_grad = dot(attention_half, head_half, CONTRACT_FIRST).astype(BF16)
        score_grad = (
            attention
            * (prob_grad - jnp.sum(attention * prob_grad, axis=-1, keepdims=True))
            / root
        ).astype(BF16)
        query_grad = norm_back(dot(score_grad, key_half), query, query_scale).astype(BF16)
        key_grad = norm_back(
            dot(score_grad, query_half, CONTRACT_FIRST), key, key_scale
        ).astype(BF16)
        out_ref[:, :head] = query_grad
        out_ref[:, head : 2 * head] = key_grad
        out_ref[:, 2 * head : wide] = value_grad
        proj_grad = jnp.concatenate([query_grad, key_grad, value_grad], axis=1).astype(F32)
        scale = scale_ref[tick, :, :1]
        offset = scale * jnp.sum(proj_grad * row_mean[:1], axis=-1, keepdims=True)
        slope = scale * (jnp.sum(proj_grad * projected, axis=-1, keepdims=True) / width)
        lane = lax.broadcasted_iota(jnp.int32, (seq, LANES), 1)
        numbers = jnp.zeros((seq, LANES), F32)
        facts = [*split_two(scale), *split_two(offset), *split_two(slope)]
        for place, fact in enumerate(facts):
            numbers = jnp.where(lane == place, fact, numbers)
        out_ref[:, wide + head :] = numbers.astype(BF16)

    arrays = [part for group in lists for part in group]
    return kernel_call(body, [shape(seq, wide + head + LANES)], [], [*arrays, scales])[0]


def input_gradient(message_ref, incoming, hidden, project, wide, head):
    numbers = message_ref[:, wide + head :].astype(F32)
    scale, offset, slope = (numbers[:, i : i + 1] + numbers[:, i + 1 : i + 2] for i in (0, 2, 4))
    hidden_grad = dot(message_ref[:, :wide], project, CONTRACT_LAST)
    change = scale * hidden_grad - offset - slope * hidden.astype(F32)
    return (incoming.astype(F32) + change).astype(BF16)


def middle_step(messages, incoming, inc_slot, hidden, hid_slot, tops, tick, first, project, below):
    count, (_, seq, part) = len(messages), hidden[0].shape
    wide, head = project.shape[1], below.shape[1]
    runs = len(tops)
    run = part // runs

    def body(first_ref, *refs):
        refs = list(refs)
        message_refs, inc_refs, hid_refs = (
            [refs.pop(0) for _ in range(count)] for _ in range(3)
        )
        top_refs = [refs.pop(0) for _ in range(runs)]
        project_ref, below_ref, passed_ref, *head_refs = refs
        is_first = first_ref[0] == 1

        @pl.when(is_first)
        def _():
            for j in range(count):
                for a in range(runs):
                    passed_ref[j, :, a * run : (a + 1) * run] = top_refs[a][j, tick]

        @pl.when(jnp.logical_not(is_first))
        def _():
            for j in range(count):
                passed_ref[j] = input_gradient(
                    message_refs[j],
                    inc_refs[j][inc_slot],
                    hid_refs[j][hid_slot],
                    project_ref[...],
                    wide,
                    head,
                )

        for j in range(count):
            head_refs[j][...] = dot(passed_ref[j], below_ref[...]).astype(BF16)

    outs = [shape(count, seq, part)] + [shape(seq, head)] * count
    arrays = [*messages, *incoming, *hidden, *tops, project, below]
    passed, *heads = kernel_call(body, outs, [first], arrays)
    return passed, heads


def last_step(messages, incoming, hidden, hid_slot, project, head):
    count, (_, seq, part) = len(messages), hidden[0].shape
    wide = project.shape[1]

    def body(*refs):
        incoming_ref, project_ref = refs[2 * count], refs[2 * count + 1]
        for j in range(count):
            refs[2 * count + 2 + j][...] = input_gradient(
                refs[j], incoming_ref[j], refs[count + j][hid_slot], project_ref[...], wide, head
            )

    arrays = [*messages, *hidden, incoming, project]
    return list(kernel_call(body, [shape(seq, part)] * count, [], arrays))


def weight_gradients(hidden, incoming, messages, head):
    ticks, count = len(messages), len(messages[0])
    arrays, places = [], []
    for group in (hidden, incoming):
        for t in range(ticks):
            for j in range(count):
                array, index = group[t][j]
                spots = [i for i, other in enumerate(arrays) if other is array]
                if not spots:
                    arrays.append(array)
                    spots = [len(arrays) - 1]
                places.append((spots[0], index))
    base = len(arrays)
    for t in range(ticks):
        arrays += messages[t]
    seq, part = arrays[0].shape[-2:]
    wide = 3 * head
    block = min(part, 256)

    def body(*refs):
        project_ref, output_ref = refs[len(arrays) :]

        def rows(group, t, j, columns):
            spot, index = places[(group * ticks + t) * count + j]
            return refs[spot][index, :, columns]

        for start in range(0, part, block):
            columns = slice(start, start + block)
            project_sum, output_sum = 0.0, 0.0
            for j in range(count):
                project_part, output_part = 0.0, 0.0
                for t in range(ticks):
                    message = refs[base + t * count + j]
                    project_part += dot(
                        rows(0, t, j, columns), message[:, :wide], CONTRACT_FIRST
                    )
                    output_part += dot(
                        rows(1, t, j, columns), message[:, wide : wide + head], CONTRACT_FIRST
                    )
                project_sum += project_part.astype(BF16).astype(F32)
                output_sum += output_part.astype(BF16).astype(F32)
            project_ref[columns, :] = project_sum
            output_ref[columns, :] = output_sum

    outs = [shape(part, wide, kind=F32), shape(part, head, kind=F32)]
    return kernel_call(body, outs, [], arrays)


def join_features(pieces, me):
    count = len(pieces)
    seq, part = pieces[0].shape

    def body(me_ref, *refs):
        for j in range(count):
            owner = lax.rem(me_ref[0] + j, count)
            columns = pl.ds(pl.multiple_of(owner * part, LANES), part)
            refs[count][:, columns] = refs[j][...]

    return kernel_call(body, [shape(seq, part * count)], [me], pieces)[0]


def shift(value, steps):
    count = lax.axis_size("dp")
    if steps % count == 0:
        return value
    return lax.ppermute(value, "dp", [(i, (i + steps) % count) for i in range(count)])


def down(value, steps=0):
    pipe, count = lax.axis_size("pipe"), lax.axis_size("dp")
    pairs = [
        (p * count + r, (p - 1) % pipe * count + (r + steps) % count)
        for p in range(pipe)
        for r in range(count)
    ]
    return lax.ppermute(value, BOTH, pairs)


def top_to_first(top_grads):
    pipe, count = lax.axis_size("pipe"), lax.axis_size("dp")
    runs = pipe // count
    gathered = [top_grads]
    for j in range(1, count):
        pairs = [(q * count + (q // runs - j) % count, q * count + q // runs) for q in range(pipe)]
        gathered.append(lax.ppermute(top_grads, BOTH, pairs))
    gathered = jnp.stack(gathered)
    return [
        lax.ppermute(gathered, BOTH, [((runs * s + a) * count + s, s) for s in range(count)])
        for a in range(runs)
    ]


def shards(section_inputs, arriving, top_grads, project_weights, output_weights):
    count = lax.axis_size("dp")
    pipe = lax.axis_size("pipe")
    me = lax.axis_index("dp")
    first = lax.axis_index("pipe") == 0
    _, ticks, seq, width = section_inputs.shape
    head = output_weights.shape[2]
    project, output = project_weights[0], output_weights[0]
    others = range(count)

    pieces, first_scale = hidden_pieces(section_inputs[0, :1], arriving[0], me, count)
    first_pieces = [shift(pieces[j], j) for j in others]
    pieces, later_scale = hidden_pieces(section_inputs[0, 1:], None, me, count)
    later_pieces = [shift(pieces[j], j) for j in others]
    below = lax.ppermute(output, "pipe", [(p, (p + 1) % pipe) for p in range(pipe)])
    tops = top_to_first(top_grads)

    partials = first_partials(first_pieces, project, output, width)
    partials = [shift(partials[j], -j) for j in others]
    projected = [value[:seq, : 3 * head] for value in partials]
    heads = [value[:seq, 3 * head :] for value in partials]
    means = [value[seq:, : 3 * head] for value in partials]

    hidden = [[(first_pieces[j], 0) for j in others]]
    incoming = [[(first_pieces[j], 1) for j in others]]
    messages = []
    for t in range(ticks):
        scales, slot = (first_scale, 0) if t == 0 else (later_scale, t - 1)
        message = attention_message(projected, heads, means, scales, slot, width)
        messages.append([shift(message, j) for j in others])
        hidden_now = [array for array, _ in hidden[t]]
        incoming_now = [array for array, _ in incoming[t]]
        if t + 1 < ticks:
            if t > 0:
                incoming_now = [passed[j][None] for j in others]
            passed, heads = middle_step(
                messages[t],
                incoming_now,
                1 if t == 0 else 0,
                hidden_now,
                slot,
                tops,
                t,
                first,
                project,
                below,
            )
            heads = [down(heads[j], -j) for j in others]
            passed = down(passed)
            projected = later_partials(later_pieces, t, project)
            projected = [shift(projected[j], -j) for j in others]
            hidden.append([(later_pieces[j], t) for j in others])
            incoming.append([(passed, j) for j in others])
    back = last_step(messages[-1], passed, hidden_now, slot, project, head)
    back = [shift(back[j], -j) for j in others]
    project_grads, output_grads = weight_gradients(hidden, incoming, messages, head)
    passed_back = join_features(back, me)
    return (project_grads[None], output_grads[None], passed_back[None])


def solution(mesh):
    in_specs = (
        P("pipe", None, "dp", None),
        P("pipe", "dp", None),
        P(None, "dp", "pipe"),
        P("pipe", "dp", None),
        P("pipe", "dp", None),
    )
    out_specs = (P("pipe", "dp", None), P("pipe", "dp", None), P("pipe", "dp", None))
    return jax.shard_map(shards, mesh=mesh, in_specs=in_specs, out_specs=out_specs, check_vma=False)
```

time: 216 us -> 120 us (0.56)
  waiting for transfers between devices: 158 us -> 69.4 us
  starting transfers between devices: 1.54 us -> 36.5 us
  matrix products: 13.6 us -> 0 us
  between operations: 14.1 us -> 0.92 us
  blocking collectives: 12.4 us -> 0 us
  Pallas kernels: 0 us -> 10.3 us
  other arithmetic: 10 us -> 0.74 us
  local copies, waits for them, and re-layouts: 5.77 us -> 1.46 us
    reduce_scatter x1 -> x0, waiting for transfers between devices: 78.1 us -> none  [shards(): lax.psum_scatter(jnp.concatenate([sum_project, sum_output], axis=1).astyp...]
    all_gather x2 -> x0, waiting for transfers between devices: 78 us -> none  [the longest x1 63.1 us: shards(): lax.all_gather(project_weights[0], 'dp', axis=0, tiled=True)]
    ppermute x1 -> x32, waiting for transfers between devices: 0.8 us -> 69.4 us  [the longest x21 45.2 us: shift(): lax.ppermute(value, 'dp', [(i, (i + steps) % count) for i in range(count)])]
    ppermute x1 -> x32, starting transfers between devices: 1.42 us -> 36.5 us  [the longest x21 27.8 us: shift(): lax.ppermute(value, 'dp', [(i, (i + steps) % count) for i in range(count)])]
    dot_general x19 -> x0, matrix products: 13.6 us -> none  [the longest x2 3.8 us: shards(): lax.dot_general(proj_grad, full_project, CONTRACT_LAST, preferred_element...]
    all_gather x1 -> x0, blocking collectives: 12.4 us -> none  [shards(): later_grads = lax.all_gather(top_grads, 'pipe', axis=2, tiled=True)]
    pallas_call x0 -> x10, Pallas kernels: none -> 10.3 us  [kernel_call(): pl.pallas_call(body, out_shape=tuple(outs), in_specs=[pl.BlockSpec(memory...]
    unnamed x26 -> x8, local copies, waits for them, and re-layouts: 4.07 us -> 0.02 us
  transfers between devices with their start and end apart: 4 -> 32, of which waited for: 4 -> 17; matrix products, arithmetic and copies ran while one was open for 5% -> 1% of each run, Pallas kernels for 0% -> 6%
where the time goes in v2:
time: 120 us; the launch traced here: 119 us
  waiting for transfers between devices  69.4 us (58%)
  starting transfers between devices  36.5 us (30%)
  Pallas kernels  10.3 us (9%)
  local copies, waits for them, and re-layouts  1.46 us (1%)
    ppermute x21, waiting for transfers between devices, shift(): lax.ppermute(value, 'dp', [(i, (i + steps) % count) for i in range(count)])  45.2 us
    ppermute x21, starting transfers between devices, shift(): lax.ppermute(value, 'dp', [(i, (i + steps) % count) for i in range(count)])  27.8 us
    ppermute x3, waiting for transfers between devices, top_to_first(): gathered.append(lax.ppermute(top_grads, BOTH, pairs))  19.2 us
    pallas_call x10, Pallas kernels, kernel_call(): pl.pallas_call(body, out_shape=tuple(outs), in_specs=[pl.BlockSpec(memory...  10.3 us
    ppermute x5, waiting for transfers between devices, down(): return lax.ppermute(value, BOTH, pairs)  4.96 us
    ppermute x3, starting transfers between devices, top_to_first(): gathered.append(lax.ppermute(top_grads, BOTH, pairs))  3.84 us
    ppermute x2, starting transfers between devices, top_to_first(): lax.ppermute(gathered, BOTH, [((runs * s + a) * count + s, s) for s in ra...  2.88 us
  transfers between devices with their start and end apart: 32, of which 17 were waited for; matrix products, arithmetic and copies ran while one was open for 1% of the time, Pallas kernels for 6%

profile of v2, /device:TPU:0, one launch (start us, length us, event | category | flops | bytes accessed | tf_op | source)
XLA Modules:
  0.0 119.3 jit_solution(13131855644433598492)
XLA Ops:
  0.7 1.4 %slice_bitcast_fusion = (bf16[1,64,4096]{2,1,0:T(8,128)(2,1)S(1)}, bf16[1,64,4096]{2,1,0:T(8,128)(2,1)S(1)}) fusion(bf16[1,2,64,4096]{3,2,1,0:T(8,128)(2,1)} %param.5), kind=kLoop, calls=%fused_computation | loop fusion | bytes 2097152 | tf_op jit(solution)/shard_map/squeeze | solution.py:345
  2.1 0.4 shard_map.76
  2.5 3.1 %collective-permute-start = (bf16[2,64,1024]{2,1,0:T(8,128)(2,1)S(1)}, bf16[2,64,1024]{2,1,0:T(8,128)(2,1)S(1)}, u32[]{:S(2)}, u32[]{:S(2)}) collective-permute-start(bf16[2,64,1024]{2,1,0:T(8,128)(2,1)S(1)} %get-tuple-element.33), channel_id=1, source_target_pairs={{0,1},{1,2},{2,3},{3,0},{4,5},{5,6},{6,7},{7,4},{8,9},{9,10},{10,1... | collective-permute-start | bytes 786440 | tf_op jit(solution)/shard_map/ppermute | solution.py:306
  5.6 1.3 %collective-permute-start.14 = (bf16[1,64,512]{2,1,0:T(8,128)(2,1)S(1)}, bf16[1,64,512]{2,1,0:T(8,128)(2,1)S(1)}, u32[]{:S(2)}, u32[]{:S(2)}) collective-permute-start(bf16[1,64,512]{2,1,0:T(8,128)(2,1)S(1)} %copy-done.3), channel_id=1, source_target_pairs={{1,0},{5,4},{10,9},{14,13},{19,18},{23,22},{24,27},{28,31}} | collective-permute-start | bytes 196616 | tf_op jit(solution)/shard_map/ppermute | solution.py:325
  6.9 2.0 %collective-permute-start.1 = (bf16[2,64,1024]{2,1,0:T(8,128)(2,1)S(1)}, bf16[2,64,1024]{2,1,0:T(8,128)(2,1)S(1)}, u32[]{:S(2)}, u32[]{:S(2)}) collective-permute-start(bf16[2,64,1024]{2,1,0:T(8,128)(2,1)S(1)} %get-tuple-element.34), channel_id=1, source_target_pairs={{0,2},{1,3},{2,0},{3,1},{4,6},{5,7},{6,4},{7,5},{8,10},{9,11},{10,... | collective-permute-start | bytes 786440 | tf_op jit(solution)/shard_map/ppermute | solution.py:306
  8.9 3.0 %collective-permute-start.2 = (bf16[2,64,1024]{2,1,0:T(8,128)(2,1)S(1)}, bf16[2,64,1024]{2,1,0:T(8,128)(2,1)S(1)}, u32[]{:S(2)}, u32[]{:S(2)}) collective-permute-start(bf16[2,64,1024]{2,1,0:T(8,128)(2,1)S(1)} %get-tuple-element.35), channel_id=1, source_target_pairs={{0,3},{1,0},{2,1},{3,2},{4,7},{5,4},{6,5},{7,6},{8,11},{9,8},{10,9... | collective-permute-start | bytes 786440 | tf_op jit(solution)/shard_map/ppermute | solution.py:306
  11.9 1.3 %collective-permute-start.13 = (bf16[1,64,512]{2,1,0:T(8,128)(2,1)S(1)}, bf16[1,64,512]{2,1,0:T(8,128)(2,1)S(1)}, u32[]{:S(2)}, u32[]{:S(2)}) collective-permute-start(bf16[1,64,512]{2,1,0:T(8,128)(2,1)S(1)} %copy-done.3), channel_id=1, source_target_pairs={{2,0},{6,4},{11,9},{15,13},{16,18},{20,22},{25,27},{29,31}} | collective-permute-start | bytes 196616 | tf_op jit(solution)/shard_map/ppermute | solution.py:325
  13.2 2.3 %collective-permute-done.14 = bf16[1,64,512]{2,1,0:T(8,128)(2,1)S(1)} collective-permute-done((bf16[1,64,512]{2,1,0:T(8,128)(2,1)S(1)}, bf16[1,64,512]{2,1,0:T(8,128)(2,1)S(1)}, u32[]{:S(2)}, u32[]{:S(2)}) %collective-permute-start.14) | collective-permute-done | bytes 65568 | tf_op jit(solution)/shard_map/ppermute | solution.py:325
  15.5 1.3 %collective-permute-start.12 = (bf16[1,64,512]{2,1,0:T(8,128)(2,1)S(1)}, bf16[1,64,512]{2,1,0:T(8,128)(2,1)S(1)}, u32[]{:S(2)}, u32[]{:S(2)}) collective-permute-start(bf16[1,64,512]{2,1,0:T(8,128)(2,1)S(1)} %copy-done.3), channel_id=1, source_target_pairs={{3,0},{7,4},{8,9},{12,13},{17,18},{21,22},{26,27},{30,31}} | collective-permute-start | bytes 196616 | tf_op jit(solution)/shard_map/ppermute | solution.py:325
  16.8 16.9 %collective-permute-done.13 = bf16[1,64,512]{2,1,0:T(8,128)(2,1)S(1)} collective-permute-done((bf16[1,64,512]{2,1,0:T(8,128)(2,1)S(1)}, bf16[1,64,512]{2,1,0:T(8,128)(2,1)S(1)}, u32[]{:S(2)}, u32[]{:S(2)}) %collective-permute-start.13) | collective-permute-done | bytes 65568 | tf_op jit(solution)/shard_map/ppermute | solution.py:325
  33.7 0.7 pad_maximum_fusion
  34.4 1.6 %collective-permute-start.15 = (bf16[4,1,64,512]{3,2,1,0:T(8,128)(2,1)}, bf16[4,1,64,512]{3,2,1,0:T(8,128)(2,1)S(1)}, u32[]{:S(2)}, u32[]{:S(2)}) collective-permute-start(bf16[4,1,64,512]{3,2,1,0:T(8,128)(2,1)} %pad_maximum_fusion), channel_id=1, source_target_pairs={{0,0},{9,1},{18,2},{27,3}} | collective-permute-start | bytes 786440 | tf_op jit(solution)/shard_map/ppermute | solution.py:328
  36.0 1.3 %collective-permute-start.16 = (bf16[4,1,64,512]{3,2,1,0:T(8,128)(2,1)}, bf16[4,1,64,512]{3,2,1,0:T(8,128)(2,1)S(1)}, u32[]{:S(2)}, u32[]{:S(2)}) collective-permute-start(bf16[4,1,64,512]{3,2,1,0:T(8,128)(2,1)} %pad_maximum_fusion), channel_id=1, source_target_pairs={{4,0},{13,1},{22,2},{31,3}} | collective-permute-start | bytes 786440 | tf_op jit(solution)/shard_map/ppermute | solution.py:328
  37.4 0.8 shard_map.78
  38.3 6.4 %collective-permute-done.6 = bf16[80,512]{1,0:T(8,128)(2,1)S(1)} collective-permute-done((bf16[80,512]{1,0:T(8,128)(2,1)S(1)}, bf16[80,512]{1,0:T(8,128)(2,1)S(1)}, u32[]{:S(2)}, u32[]{:S(2)}) %collective-permute-start.6) | collective-permute-done | bytes 81952 | tf_op jit(solution)/shard_map/ppermute | solution.py:306
  44.7 1.4 %collective-permute-done.7 = bf16[80,512]{1,0:T(8,128)(2,1)S(1)} collective-permute-done((bf16[80,512]{1,0:T(8,128)(2,1)S(1)}, bf16[80,512]{1,0:T(8,128)(2,1)S(1)}, u32[]{:S(2)}, u32[]{:S(2)}) %collective-permute-start.7) | collective-permute-done | bytes 81952 | tf_op jit(solution)/shard_map/ppermute | solution.py:306
  46.1 5.0 %collective-permute-done.8 = bf16[80,512]{1,0:T(8,128)(2,1)S(1)} collective-permute-done((bf16[80,512]{1,0:T(8,128)(2,1)S(1)}, bf16[80,512]{1,0:T(8,128)(2,1)S(1)}, u32[]{:S(2)}, u32[]{:S(2)}) %collective-permute-start.8) | collective-permute-done | bytes 81952 | tf_op jit(solution)/shard_map/ppermute | solution.py:306
  51.1 1.1 shard_map.79.refs_0_.refs_9_
  52.3 0.1 collective-permute-start.10
  52.4 3.7 %collective-permute-start.11 = (bf16[64,640]{1,0:T(8,128)(2,1)S(1)}, bf16[64,640]{1,0:T(8,128)(2,1)S(1)}, u32[]{:S(2)}, u32[]{:S(2)}) collective-permute-start(bf16[64,640]{1,0:T(8,128)(2,1)S(1)} %shard_map.79.refs_0_.refs_9_), channel_id=1, source_target_pairs={{0,3},{1,0},{2,1},{3,2},{4,7},{5,4},{6,5},{7,6},{8,11},{9,8},{10,9... | collective-permute-start | bytes 245768 | tf_op jit(solution)/shard_map/ppermute | solution.py:306
  56.1 3.4 %collective-permute-done.9.refs_1_.refs_10_ = bf16[64,640]{1,0:T(8,128)(2,1)S(1)} collective-permute-done((bf16[64,640]{1,0:T(8,128)(2,1)S(1)}, bf16[64,640]{1,0:T(8,128)(2,1)S(1)}, u32[]{:S(2)}, u32[]{:S(2)}) %collective-permute-start.9) | collective-permute-done | bytes 81952 | tf_op jit(solution)/shard_map/ppermute | solution.py:306
  59.5 1.9 %collective-permute-done.10.refs_2_.refs_11_ = bf16[64,640]{1,0:T(8,128)(2,1)S(1)} collective-permute-done((bf16[64,640]{1,0:T(8,128)(2,1)S(1)}, bf16[64,640]{1,0:T(8,128)(2,1)S(1)}, u32[]{:S(2)}, u32[]{:S(2)}) %collective-permute-start.10) | collective-permute-done | bytes 81952 | tf_op jit(solution)/shard_map/ppermute | solution.py:306
  61.4 0.3 shard_map.80
  61.8 0.4 shard_map.77
  62.2 1.5 %collective-permute-start.3 = (bf16[1,64,1024]{2,1,0:T(8,128)(2,1)S(1)}, bf16[1,64,1024]{2,1,0:T(8,128)(2,1)S(1)}, u32[]{:S(2)}, u32[]{:S(2)}) collective-permute-start(bf16[1,64,1024]{2,1,0:T(8,128)(2,1)S(1)} %get-tuple-element.37), channel_id=1, source_target_pairs={{0,1},{1,2},{2,3},{3,0},{4,5},{5,6},{6,7},{7,4},{8,9},{9,10},{10,1... | collective-permute-start | bytes 393224 | tf_op jit(solution)/shard_map/ppermute | solution.py:306
  63.7 0.8 collective-permute-start.4
  64.6 1.6 %collective-permute-start.5 = (bf16[1,64,1024]{2,1,0:T(8,128)(2,1)S(1)}, bf16[1,64,1024]{2,1,0:T(8,128)(2,1)S(1)}, u32[]{:S(2)}, u32[]{:S(2)}) collective-permute-start(bf16[1,64,1024]{2,1,0:T(8,128)(2,1)S(1)} %get-tuple-element.39), channel_id=1, source_target_pairs={{0,3},{1,0},{2,1},{3,2},{4,7},{5,4},{6,5},{7,6},{8,11},{9,8},{10,9... | collective-permute-start | bytes 393224 | tf_op jit(solution)/shard_map/ppermute | solution.py:306
  66.2 4.3 %collective-permute-done.3.refs_1_.refs_5_ = bf16[1,64,1024]{2,1,0:T(8,128)(2,1)S(1)} collective-permute-done((bf16[1,64,1024]{2,1,0:T(8,128)(2,1)S(1)}, bf16[1,64,1024]{2,1,0:T(8,128)(2,1)S(1)}, u32[]{:S(2)}, u32[]{:S(2)}) %collective-permute-start.3) | collective-permute-done | bytes 131104 | tf_op jit(solution)/shard_map/ppermute | solution.py:306
  70.5 5.2 %collective-permute-done.4.refs_2_.refs_6_ = bf16[1,64,1024]{2,1,0:T(8,128)(2,1)S(1)} collective-permute-done((bf16[1,64,1024]{2,1,0:T(8,128)(2,1)S(1)}, bf16[1,64,1024]{2,1,0:T(8,128)(2,1)S(1)}, u32[]{:S(2)}, u32[]{:S(2)}) %collective-permute-start.4) | collective-permute-done | bytes 131104 | tf_op jit(solution)/shard_map/ppermute | solution.py:306
  75.7 0.6 shard_map.81
  76.3 3.1 %collective-permute-start.19 = (bf16[64,384]{1,0:T(8,128)(2,1)S(1)}, bf16[64,384]{1,0:T(8,128)(2,1)S(1)}, u32[]{:S(2)}, u32[]{:S(2)}) collective-permute-start(bf16[64,384]{1,0:T(8,128)(2,1)S(1)} %get-tuple-element.47), channel_id=1, source_target_pairs={{0,3},{1,0},{2,1},{3,2},{4,7},{5,4},{6,5},{7,6},{8,11},{9,8},{10,9... | collective-permute-start | bytes 147464 | tf_op jit(solution)/shard_map/ppermute | solution.py:306
  79.4 1.8 %collective-permute-start.20 = (bf16[64,384]{1,0:T(8,128)(2,1)S(1)}, bf16[64,384]{1,0:T(8,128)(2,1)S(1)}, u32[]{:S(2)}, u32[]{:S(2)}) collective-permute-start(bf16[64,384]{1,0:T(8,128)(2,1)S(1)} %get-tuple-element.48), channel_id=1, source_target_pairs={{0,2},{1,3},{2,0},{3,1},{4,6},{5,7},{6,4},{7,5},{8,10},{9,11},{10,... | collective-permute-start | bytes 147464 | tf_op jit(solution)/shard_map/ppermute | solution.py:306
  81.1 0.6 collective-permute-done.19.refs_1_
  81.7 1.9 %collective-permute-start.23 = (bf16[64,128]{1,0:T(8,128)(2,1)S(1)}, bf16[64,128]{1,0:T(8,128)(2,1)S(1)}, u32[]{:S(2)}, u32[]{:S(2)}) collective-permute-start(bf16[64,128]{1,0:T(8,128)(2,1)S(1)} %get-tuple-element.51), channel_id=1, source_target_pairs={{0,31},{1,28},{2,29},{3,30},{4,3},{5,0},{6,1},{7,2},{8,7},{9,4},{1... | collective-permute-start | bytes 49160 | tf_op jit(solution)/shard_map/ppermute | solution.py:316
  83.7 1.3 %collective-permute-done.20.refs_2_ = bf16[64,384]{1,0:T(8,128)(2,1)S(1)} collective-permute-done((bf16[64,384]{1,0:T(8,128)(2,1)S(1)}, bf16[64,384]{1,0:T(8,128)(2,1)S(1)}, u32[]{:S(2)}, u32[]{:S(2)}) %collective-permute-start.20) | collective-permute-done | bytes 49184 | tf_op jit(solution)/shard_map/ppermute | solution.py:306
  85.0 2.2 %collective-permute-done.21.refs_3_ = bf16[64,384]{1,0:T(8,128)(2,1)S(1)} collective-permute-done((bf16[64,384]{1,0:T(8,128)(2,1)S(1)}, bf16[64,384]{1,0:T(8,128)(2,1)S(1)}, u32[]{:S(2)}, u32[]{:S(2)}) %collective-permute-start.21) | collective-permute-done | bytes 49184 | tf_op jit(solution)/shard_map/ppermute | solution.py:306
  87.2 1.8 %collective-permute-done.24.refs_6_ = bf16[64,128]{1,0:T(8,128)(2,1)S(1)} collective-permute-done((bf16[64,128]{1,0:T(8,128)(2,1)S(1)}, bf16[64,128]{1,0:T(8,128)(2,1)S(1)}, u32[]{:S(2)}, u32[]{:S(2)}) %collective-permute-start.24) | collective-permute-done | bytes 16416 | tf_op jit(solution)/shard_map/ppermute | solution.py:316
  89.1 3.1 %collective-permute-done.25.refs_7_ = bf16[64,128]{1,0:T(8,128)(2,1)S(1)} collective-permute-done((bf16[64,128]{1,0:T(8,128)(2,1)S(1)}, bf16[64,128]{1,0:T(8,128)(2,1)S(1)}, u32[]{:S(2)}, u32[]{:S(2)}) %collective-permute-start.25) | collective-permute-done | bytes 16416 | tf_op jit(solution)/shard_map/ppermute | solution.py:316
  92.2 1.1 shard_map.82.refs_13_.refs_0_
  93.4 3.7 %collective-permute-start.28 = (bf16[64,640]{1,0:T(8,128)(2,1)S(1)}, bf16[64,640]{1,0:T(8,128)(2,1)S(1)}, u32[]{:S(2)}, u32[]{:S(2)}) collective-permute-start(bf16[64,640]{1,0:T(8,128)(2,1)S(1)} %shard_map.82.refs_13_.refs_0_), channel_id=1, source_target_pairs={{0,3},{1,0},{2,1},{3,2},{4,7},{5,4},{6,5},{7,6},{8,11},{9,8},{10,9... | collective-permute-start | bytes 245768 | tf_op jit(solution)/shard_map/ppermute | solution.py:306
  97.1 3.3 %collective-permute-done.26.refs_14_.refs_1_ = bf16[64,640]{1,0:T(8,128)(2,1)S(1)} collective-permute-done((bf16[64,640]{1,0:T(8,128)(2,1)S(1)}, bf16[64,640]{1,0:T(8,128)(2,1)S(1)}, u32[]{:S(2)}, u32[]{:S(2)}) %collective-permute-start.26) | collective-permute-done | bytes 81952 | tf_op jit(solution)/shard_map/ppermute | solution.py:306
  100.4 2.5 %collective-permute-done.27.refs_15_.refs_2_ = bf16[64,640]{1,0:T(8,128)(2,1)S(1)} collective-permute-done((bf16[64,640]{1,0:T(8,128)(2,1)S(1)}, bf16[64,640]{1,0:T(8,128)(2,1)S(1)}, u32[]{:S(2)}, u32[]{:S(2)}) %collective-permute-start.27) | collective-permute-done | bytes 81952 | tf_op jit(solution)/shard_map/ppermute | solution.py:306
  103.0 1.1 shard_map.84
  104.1 2.1 %collective-permute-start.29 = (bf16[64,1024]{1,0:T(8,128)(2,1)S(1)}, bf16[64,1024]{1,0:T(8,128)(2,1)S(1)}, u32[]{:S(2)}, u32[]{:S(2)}) collective-permute-start(bf16[64,1024]{1,0:T(8,128)(2,1)S(1)} %get-tuple-element.58), channel_id=1, source_target_pairs={{0,3},{1,0},{2,1},{3,2},{4,7},{5,4},{6,5},{7,6},{8,11},{9,8},{10,9... | collective-permute-start | bytes 393224 | tf_op jit(solution)/shard_map/ppermute | solution.py:306
  106.2 0.9 collective-permute-start.30
  107.1 3.7 %shard_map.83 = (f32[1024,384]{1,0:T(8,128)}, f32[1024,128]{1,0:T(8,128)}) custom-call(bf16[2,64,1024]{2,1,0:T(8,128)(2,1)S(1)} %get-tuple-element.32.refs_0_.refs_4_.refs_8_, bf16[2,64,1024]{2,1,0:T(8,128)(2,1)S(1)} %collective-permute-done.refs_1_.refs_5_.refs_9_, bf16[2,64,1024]{2,1,0:T(8,128)(2,1)S(1)} %collective-permute-done.1.refs_2_.refs_6_.refs_10_, ...), custom_call_target="tpu_custom_call" | custom-call | bytes 4849664 | tf_op jit(solution)/shard_map/pallas_call | solution.py:27
  110.8 7.7 %collective-permute-done.30.refs_2_ = bf16[64,1024]{1,0:T(8,128)(2,1)S(1)} collective-permute-done((bf16[64,1024]{1,0:T(8,128)(2,1)S(1)}, bf16[64,1024]{1,0:T(8,128)(2,1)S(1)}, u32[]{:S(2)}, u32[]{:S(2)}) %collective-permute-start.30) | collective-permute-done | bytes 131104 | tf_op jit(solution)/shard_map/ppermute | solution.py:306
  118.5 0.8 shard_map.85
  (48 shorter events, 0.5 us)
Async XLA Ops:
  0.6 1.4 %copy-start.1 = (bf16[1,64,4096]{2,1,0:T(8,128)(2,1)S(1)}, bf16[1,64,4096]{2,1,0:T(8,128)(2,1)}, u32[]{:S(2)}) copy-start(bf16[1,64,4096]{2,1,0:T(8,128)(2,1)} %param.6) | copy-start | bytes 1572868
  0.6 4.9 %copy-start.3 = (bf16[1,64,512]{2,1,0:T(8,128)(2,1)S(1)}, bf16[1,64,512]{2,1,0:T(8,128)(2,1)}, u32[]{:S(2)}) copy-start(bf16[1,64,512]{2,1,0:T(8,128)(2,1)} %param.7) | copy-start | bytes 196612
  0.7 33.0 %copy-start.2 = (bf16[1,1024,128]{2,1,0:T(8,128)(2,1)S(1)}, bf16[1,1024,128]{2,1,0:T(8,128)(2,1)}, u32[]{:S(2)}) copy-start(bf16[1,1024,128]{2,1,0:T(8,128)(2,1)} %param.9) | copy-start | bytes 786436
  0.7 36.7 %copy-start = (bf16[1,1024,384]{2,1,0:T(8,128)(2,1)S(1)}, bf16[1,1024,384]{2,1,0:T(8,128)(2,1)}, u32[]{:S(2)}) copy-start(bf16[1,1024,384]{2,1,0:T(8,128)(2,1)} %param.8) | copy-start | bytes 2359300
  2.5 33.5 %collective-permute-start = (bf16[2,64,1024]{2,1,0:T(8,128)(2,1)S(1)}, bf16[2,64,1024]{2,1,0:T(8,128)(2,1)S(1)}, u32[]{:S(2)}, u32[]{:S(2)}) collective-permute-start(bf16[2,64,1024]{2,1,0:T(8,128)(2,1)S(1)} %get-tuple-element.33), channel_id=1, source_target_pairs={{0,1},{1,2},{2,3},{3,0},{4,5},{5,6},{6,7},{7,4},{8,9},{9,10},{10,1... | collective-permute-start | bytes 786440 | tf_op jit(solution)/shard_map/ppermute | solution.py:306
  5.6 9.9 %collective-permute-start.14 = (bf16[1,64,512]{2,1,0:T(8,128)(2,1)S(1)}, bf16[1,64,512]{2,1,0:T(8,128)(2,1)S(1)}, u32[]{:S(2)}, u32[]{:S(2)}) collective-permute-start(bf16[1,64,512]{2,1,0:T(8,128)(2,1)S(1)} %copy-done.3), channel_id=1, source_target_pairs={{1,0},{5,4},{10,9},{14,13},{19,18},{23,22},{24,27},{28,31}} | collective-permute-start | bytes 196616 | tf_op jit(solution)/shard_map/ppermute | solution.py:325
  6.9 30.5 %collective-permute-start.1 = (bf16[2,64,1024]{2,1,0:T(8,128)(2,1)S(1)}, bf16[2,64,1024]{2,1,0:T(8,128)(2,1)S(1)}, u32[]{:S(2)}, u32[]{:S(2)}) collective-permute-start(bf16[2,64,1024]{2,1,0:T(8,128)(2,1)S(1)} %get-tuple-element.34), channel_id=1, source_target_pairs={{0,2},{1,3},{2,0},{3,1},{4,6},{5,7},{6,4},{7,5},{8,10},{9,11},{10,... | collective-permute-start | bytes 786440 | tf_op jit(solution)/shard_map/ppermute | solution.py:306
  8.9 28.4 %collective-permute-start.2 = (bf16[2,64,1024]{2,1,0:T(8,128)(2,1)S(1)}, bf16[2,64,1024]{2,1,0:T(8,128)(2,1)S(1)}, u32[]{:S(2)}, u32[]{:S(2)}) collective-permute-start(bf16[2,64,1024]{2,1,0:T(8,128)(2,1)S(1)} %get-tuple-element.35), channel_id=1, source_target_pairs={{0,3},{1,0},{2,1},{3,2},{4,7},{5,4},{6,5},{7,6},{8,11},{9,8},{10,9... | collective-permute-start | bytes 786440 | tf_op jit(solution)/shard_map/ppermute | solution.py:306
  11.9 21.7 %collective-permute-start.13 = (bf16[1,64,512]{2,1,0:T(8,128)(2,1)S(1)}, bf16[1,64,512]{2,1,0:T(8,128)(2,1)S(1)}, u32[]{:S(2)}, u32[]{:S(2)}) collective-permute-start(bf16[1,64,512]{2,1,0:T(8,128)(2,1)S(1)} %copy-done.3), channel_id=1, source_target_pairs={{2,0},{6,4},{11,9},{15,13},{16,18},{20,22},{25,27},{29,31}} | collective-permute-start | bytes 196616 | tf_op jit(solution)/shard_map/ppermute | solution.py:325
  15.5 18.2 %collective-permute-start.12 = (bf16[1,64,512]{2,1,0:T(8,128)(2,1)S(1)}, bf16[1,64,512]{2,1,0:T(8,128)(2,1)S(1)}, u32[]{:S(2)}, u32[]{:S(2)}) collective-permute-start(bf16[1,64,512]{2,1,0:T(8,128)(2,1)S(1)} %copy-done.3), channel_id=1, source_target_pairs={{3,0},{7,4},{8,9},{12,13},{17,18},{21,22},{26,27},{30,31}} | collective-permute-start | bytes 196616 | tf_op jit(solution)/shard_map/ppermute | solution.py:325
  33.7 18.7 %collective-permute-start.17 = (bf16[1024,128]{1,0:T(8,128)(2,1)S(1)}, bf16[1024,128]{1,0:T(8,128)(2,1)S(1)}, u32[]{:S(2)}, u32[]{:S(2)}) collective-permute-start(bf16[1024,128]{1,0:T(8,128)(2,1)S(1)} %bitcast.21), channel_id=1, source_target_pairs={{0,4},{4,8},{8,12},{12,16},{16,20},{20,24},{24,28},{28,0},{1,5},{5... | collective-permute-start | bytes 786440 | tf_op jit(solution)/shard_map/ppermute | solution.py:347
  34.4 21.7 %collective-permute-start.15 = (bf16[4,1,64,512]{3,2,1,0:T(8,128)(2,1)}, bf16[4,1,64,512]{3,2,1,0:T(8,128)(2,1)S(1)}, u32[]{:S(2)}, u32[]{:S(2)}) collective-permute-start(bf16[4,1,64,512]{3,2,1,0:T(8,128)(2,1)} %pad_maximum_fusion), channel_id=1, source_target_pairs={{0,0},{9,1},{18,2},{27,3}} | collective-permute-start | bytes 786440 | tf_op jit(solution)/shard_map/ppermute | solution.py:328
  36.0 20.1 %collective-permute-start.16 = (bf16[4,1,64,512]{3,2,1,0:T(8,128)(2,1)}, bf16[4,1,64,512]{3,2,1,0:T(8,128)(2,1)S(1)}, u32[]{:S(2)}, u32[]{:S(2)}) collective-permute-start(bf16[4,1,64,512]{3,2,1,0:T(8,128)(2,1)} %pad_maximum_fusion), channel_id=1, source_target_pairs={{4,0},{13,1},{22,2},{31,3}} | collective-permute-start | bytes 786440 | tf_op jit(solution)/shard_map/ppermute | solution.py:328
  38.1 6.5 %collective-permute-start.6 = (bf16[80,512]{1,0:T(8,128)(2,1)S(1)}, bf16[80,512]{1,0:T(8,128)(2,1)S(1)}, u32[]{:S(2)}, u32[]{:S(2)}) collective-permute-start(bf16[80,512]{1,0:T(8,128)(2,1)S(1)} %get-tuple-element.41), channel_id=1, source_target_pairs={{0,3},{1,0},{2,1},{3,2},{4,7},{5,4},{6,5},{7,6},{8,11},{9,8},{10,9... | collective-permute-start | bytes 245768 | tf_op jit(solution)/shard_map/ppermute | solution.py:306
  38.2 7.9 %collective-permute-start.7 = (bf16[80,512]{1,0:T(8,128)(2,1)S(1)}, bf16[80,512]{1,0:T(8,128)(2,1)S(1)}, u32[]{:S(2)}, u32[]{:S(2)}) collective-permute-start(bf16[80,512]{1,0:T(8,128)(2,1)S(1)} %get-tuple-element.42), channel_id=1, source_target_pairs={{0,2},{1,3},{2,0},{3,1},{4,6},{5,7},{6,4},{7,5},{8,10},{9,11},{10,... | collective-permute-start | bytes 245768 | tf_op jit(solution)/shard_map/ppermute | solution.py:306
  44.7 6.4 %collective-permute-start.8 = (bf16[80,512]{1,0:T(8,128)(2,1)S(1)}, bf16[80,512]{1,0:T(8,128)(2,1)S(1)}, u32[]{:S(2)}, u32[]{:S(2)}) collective-permute-start(bf16[80,512]{1,0:T(8,128)(2,1)S(1)} %get-tuple-element.43), channel_id=1, source_target_pairs={{0,1},{1,2},{2,3},{3,0},{4,5},{5,6},{6,7},{7,4},{8,9},{9,10},{10,1... | collective-permute-start | bytes 245768 | tf_op jit(solution)/shard_map/ppermute | solution.py:306
  52.2 7.3 %collective-permute-start.9 = (bf16[64,640]{1,0:T(8,128)(2,1)S(1)}, bf16[64,640]{1,0:T(8,128)(2,1)S(1)}, u32[]{:S(2)}, u32[]{:S(2)}) collective-permute-start(bf16[64,640]{1,0:T(8,128)(2,1)S(1)} %shard_map.79.refs_0_.refs_9_), channel_id=1, source_target_pairs={{0,1},{1,2},{2,3},{3,0},{4,5},{5,6},{6,7},{7,4},{8,9},{9,10},{10,1... | collective-permute-start | bytes 245768 | tf_op jit(solution)/shard_map/ppermute | solution.py:306
  52.3 9.1 %collective-permute-start.10 = (bf16[64,640]{1,0:T(8,128)(2,1)S(1)}, bf16[64,640]{1,0:T(8,128)(2,1)S(1)}, u32[]{:S(2)}, u32[]{:S(2)}) collective-permute-start(bf16[64,640]{1,0:T(8,128)(2,1)S(1)} %shard_map.79.refs_0_.refs_9_), channel_id=1, source_target_pairs={{0,2},{1,3},{2,0},{3,1},{4,6},{5,7},{6,4},{7,5},{8,10},{9,11},{10,... | collective-permute-start | bytes 245768 | tf_op jit(solution)/shard_map/ppermute | solution.py:306
  52.4 9.0 %collective-permute-start.11 = (bf16[64,640]{1,0:T(8,128)(2,1)S(1)}, bf16[64,640]{1,0:T(8,128)(2,1)S(1)}, u32[]{:S(2)}, u32[]{:S(2)}) collective-permute-start(bf16[64,640]{1,0:T(8,128)(2,1)S(1)} %shard_map.79.refs_0_.refs_9_), channel_id=1, source_target_pairs={{0,3},{1,0},{2,1},{3,2},{4,7},{5,4},{6,5},{7,6},{8,11},{9,8},{10,9... | collective-permute-start | bytes 245768 | tf_op jit(solution)/shard_map/ppermute | solution.py:306
  61.7 41.2 %collective-permute-start.18 = (bf16[4,64,1024]{2,1,0:T(8,128)(2,1)S(1)}, bf16[4,64,1024]{2,1,0:T(8,128)(2,1)S(1)}, u32[]{:S(2)}, u32[]{:S(2)}) collective-permute-start(bf16[4,64,1024]{2,1,0:T(8,128)(2,1)S(1)} %get-tuple-element.45), channel_id=1, source_target_pairs={{0,28},{1,29},{2,30},{3,31},{4,0},{5,1},{6,2},{7,3},{8,4},{9,5},{1... | collective-permute-start | bytes 1572872 | tf_op jit(solution)/shard_map/ppermute | solution.py:316
  62.2 8.3 %collective-permute-start.3 = (bf16[1,64,1024]{2,1,0:T(8,128)(2,1)S(1)}, bf16[1,64,1024]{2,1,0:T(8,128)(2,1)S(1)}, u32[]{:S(2)}, u32[]{:S(2)}) collective-permute-start(bf16[1,64,1024]{2,1,0:T(8,128)(2,1)S(1)} %get-tuple-element.37), channel_id=1, source_target_pairs={{0,1},{1,2},{2,3},{3,0},{4,5},{5,6},{6,7},{7,4},{8,9},{9,10},{10,1... | collective-permute-start | bytes 393224 | tf_op jit(solution)/shard_map/ppermute | solution.py:306
  63.7 11.9 %collective-permute-start.4 = (bf16[1,64,1024]{2,1,0:T(8,128)(2,1)S(1)}, bf16[1,64,1024]{2,1,0:T(8,128)(2,1)S(1)}, u32[]{:S(2)}, u32[]{:S(2)}) collective-permute-start(bf16[1,64,1024]{2,1,0:T(8,128)(2,1)S(1)} %get-tuple-element.38), channel_id=1, source_target_pairs={{0,2},{1,3},{2,0},{3,1},{4,6},{5,7},{6,4},{7,5},{8,10},{9,11},{10,... | collective-permute-start | bytes 393224 | tf_op jit(solution)/shard_map/ppermute | solution.py:306
  64.6 11.1 %collective-permute-start.5 = (bf16[1,64,1024]{2,1,0:T(8,128)(2,1)S(1)}, bf16[1,64,1024]{2,1,0:T(8,128)(2,1)S(1)}, u32[]{:S(2)}, u32[]{:S(2)}) collective-permute-start(bf16[1,64,1024]{2,1,0:T(8,128)(2,1)S(1)} %get-tuple-element.39), channel_id=1, source_target_pairs={{0,3},{1,0},{2,1},{3,2},{4,7},{5,4},{6,5},{7,6},{8,11},{9,8},{10,9... | collective-permute-start | bytes 393224 | tf_op jit(solution)/shard_map/ppermute | solution.py:306
  76.3 5.4 %collective-permute-start.19 = (bf16[64,384]{1,0:T(8,128)(2,1)S(1)}, bf16[64,384]{1,0:T(8,128)(2,1)S(1)}, u32[]{:S(2)}, u32[]{:S(2)}) collective-permute-start(bf16[64,384]{1,0:T(8,128)(2,1)S(1)} %get-tuple-element.47), channel_id=1, source_target_pairs={{0,3},{1,0},{2,1},{3,2},{4,7},{5,4},{6,5},{7,6},{8,11},{9,8},{10,9... | collective-permute-start | bytes 147464 | tf_op jit(solution)/shard_map/ppermute | solution.py:306
  79.4 5.6 %collective-permute-start.20 = (bf16[64,384]{1,0:T(8,128)(2,1)S(1)}, bf16[64,384]{1,0:T(8,128)(2,1)S(1)}, u32[]{:S(2)}, u32[]{:S(2)}) collective-permute-start(bf16[64,384]{1,0:T(8,128)(2,1)S(1)} %get-tuple-element.48), channel_id=1, source_target_pairs={{0,2},{1,3},{2,0},{3,1},{4,6},{5,7},{6,4},{7,5},{8,10},{9,11},{10,... | collective-permute-start | bytes 147464 | tf_op jit(solution)/shard_map/ppermute | solution.py:306
  81.1 6.1 %collective-permute-start.21 = (bf16[64,384]{1,0:T(8,128)(2,1)S(1)}, bf16[64,384]{1,0:T(8,128)(2,1)S(1)}, u32[]{:S(2)}, u32[]{:S(2)}) collective-permute-start(bf16[64,384]{1,0:T(8,128)(2,1)S(1)} %get-tuple-element.49), channel_id=1, source_target_pairs={{0,1},{1,2},{2,3},{3,0},{4,5},{5,6},{6,7},{7,4},{8,9},{9,10},{10,1... | collective-permute-start | bytes 147464 | tf_op jit(solution)/shard_map/ppermute | solution.py:306
  81.1 6.1 %collective-permute-start.22 = (bf16[64,128]{1,0:T(8,128)(2,1)S(1)}, bf16[64,128]{1,0:T(8,128)(2,1)S(1)}, u32[]{:S(2)}, u32[]{:S(2)}) collective-permute-start(bf16[64,128]{1,0:T(8,128)(2,1)S(1)} %get-tuple-element.50), channel_id=1, source_target_pairs={{0,28},{1,29},{2,30},{3,31},{4,0},{5,1},{6,2},{7,3},{8,4},{9,5},{1... | collective-permute-start | bytes 49160 | tf_op jit(solution)/shard_map/ppermute | solution.py:316
  81.7 5.5 %collective-permute-start.23 = (bf16[64,128]{1,0:T(8,128)(2,1)S(1)}, bf16[64,128]{1,0:T(8,128)(2,1)S(1)}, u32[]{:S(2)}, u32[]{:S(2)}) collective-permute-start(bf16[64,128]{1,0:T(8,128)(2,1)S(1)} %get-tuple-element.51), channel_id=1, source_target_pairs={{0,31},{1,28},{2,29},{3,30},{4,3},{5,0},{6,1},{7,2},{8,7},{9,4},{1... | collective-permute-start | bytes 49160 | tf_op jit(solution)/shard_map/ppermute | solution.py:316
  85.0 4.1 %collective-permute-start.24 = (bf16[64,128]{1,0:T(8,128)(2,1)S(1)}, bf16[64,128]{1,0:T(8,128)(2,1)S(1)}, u32[]{:S(2)}, u32[]{:S(2)}) collective-permute-start(bf16[64,128]{1,0:T(8,128)(2,1)S(1)} %get-tuple-element.52), channel_id=1, source_target_pairs={{0,30},{1,31},{2,28},{3,29},{4,2},{5,3},{6,0},{7,1},{8,6},{9,7},{1... | collective-permute-start | bytes 49160 | tf_op jit(solution)/shard_map/ppermute | solution.py:316
  87.2 5.0 %collective-permute-start.25 = (bf16[64,128]{1,0:T(8,128)(2,1)S(1)}, bf16[64,128]{1,0:T(8,128)(2,1)S(1)}, u32[]{:S(2)}, u32[]{:S(2)}) collective-permute-start(bf16[64,128]{1,0:T(8,128)(2,1)S(1)} %get-tuple-element.53), channel_id=1, source_target_pairs={{0,29},{1,30},{2,31},{3,28},{4,1},{5,2},{6,3},{7,0},{8,5},{9,6},{1... | collective-permute-start | bytes 49160 | tf_op jit(solution)/shard_map/ppermute | solution.py:316
  93.2 7.2 %collective-permute-start.26 = (bf16[64,640]{1,0:T(8,128)(2,1)S(1)}, bf16[64,640]{1,0:T(8,128)(2,1)S(1)}, u32[]{:S(2)}, u32[]{:S(2)}) collective-permute-start(bf16[64,640]{1,0:T(8,128)(2,1)S(1)} %shard_map.82.refs_13_.refs_0_), channel_id=1, source_target_pairs={{0,1},{1,2},{2,3},{3,0},{4,5},{5,6},{6,7},{7,4},{8,9},{9,10},{10,1... | collective-permute-start | bytes 245768 | tf_op jit(solution)/shard_map/ppermute | solution.py:306
  93.3 9.7 %collective-permute-start.27 = (bf16[64,640]{1,0:T(8,128)(2,1)S(1)}, bf16[64,640]{1,0:T(8,128)(2,1)S(1)}, u32[]{:S(2)}, u32[]{:S(2)}) collective-permute-start(bf16[64,640]{1,0:T(8,128)(2,1)S(1)} %shard_map.82.refs_13_.refs_0_), channel_id=1, source_target_pairs={{0,2},{1,3},{2,0},{3,1},{4,6},{5,7},{6,4},{7,5},{8,10},{9,11},{10,... | collective-permute-start | bytes 245768 | tf_op jit(solution)/shard_map/ppermute | solution.py:306
  93.4 9.6 %collective-permute-start.28 = (bf16[64,640]{1,0:T(8,128)(2,1)S(1)}, bf16[64,640]{1,0:T(8,128)(2,1)S(1)}, u32[]{:S(2)}, u32[]{:S(2)}) collective-permute-start(bf16[64,640]{1,0:T(8,128)(2,1)S(1)} %shard_map.82.refs_13_.refs_0_), channel_id=1, source_target_pairs={{0,3},{1,0},{2,1},{3,2},{4,7},{5,4},{6,5},{7,6},{8,11},{9,8},{10,9... | collective-permute-start | bytes 245768 | tf_op jit(solution)/shard_map/ppermute | solution.py:306
  104.1 6.7 %collective-permute-start.29 = (bf16[64,1024]{1,0:T(8,128)(2,1)S(1)}, bf16[64,1024]{1,0:T(8,128)(2,1)S(1)}, u32[]{:S(2)}, u32[]{:S(2)}) collective-permute-start(bf16[64,1024]{1,0:T(8,128)(2,1)S(1)} %get-tuple-element.58), channel_id=1, source_target_pairs={{0,3},{1,0},{2,1},{3,2},{4,7},{5,4},{6,5},{7,6},{8,11},{9,8},{10,9... | collective-permute-start | bytes 393224 | tf_op jit(solution)/shard_map/ppermute | solution.py:306
  106.2 12.3 %collective-permute-start.30 = (bf16[64,1024]{1,0:T(8,128)(2,1)S(1)}, bf16[64,1024]{1,0:T(8,128)(2,1)S(1)}, u32[]{:S(2)}, u32[]{:S(2)}) collective-permute-start(bf16[64,1024]{1,0:T(8,128)(2,1)S(1)} %get-tuple-element.59), channel_id=1, source_target_pairs={{0,2},{1,3},{2,0},{3,1},{4,6},{5,7},{6,4},{7,5},{8,10},{9,11},{10,... | collective-permute-start | bytes 393224 | tf_op jit(solution)/shard_map/ppermute | solution.py:306
  107.1 11.4 %collective-permute-start.31 = (bf16[64,1024]{1,0:T(8,128)(2,1)S(1)}, bf16[64,1024]{1,0:T(8,128)(2,1)S(1)}, u32[]{:S(2)}, u32[]{:S(2)}) collective-permute-start(bf16[64,1024]{1,0:T(8,128)(2,1)S(1)} %get-tuple-element.60), channel_id=1, source_target_pairs={{0,1},{1,2},{2,3},{3,0},{4,5},{5,6},{6,7},{7,4},{8,9},{9,10},{10,1... | collective-permute-start | bytes 393224 | tf_op jit(solution)/shard_map/ppermute | solution.py:306

commit v3 on v0

v3 whole, which is shorter than its diff:
```python
import functools
import math

import jax
import jax.numpy as jnp
from jax import lax
from jax.experimental import pallas as pl
from jax.experimental.pallas import tpu as pltpu
from jax.sharding import PartitionSpec as P

EPSILON = 1e-06
CONTRACT_FIRST = (((0,), (0,)), ((), ()))
CONTRACT_LAST = (((1,), (1,)), ((), ()))
F32 = jnp.float32
BF16 = jnp.bfloat16
ROW_TILE = 16
LANES = 128
BOTH = ("pipe", "dp")


def shape(*dims, kind=BF16):
    return jax.ShapeDtypeStruct(dims, kind)


def kernel_call(body, outs, scalars, arrays, scratch=()):
    return pl.pallas_call(
        body,
        out_shape=tuple(outs),
        in_specs=[pl.BlockSpec(memory_space=pltpu.SMEM)] * len(scalars)
        + [pl.BlockSpec(memory_space=pltpu.VMEM)] * len(arrays),
        out_specs=tuple(pl.BlockSpec(memory_space=pltpu.VMEM) for _ in outs),
        scratch_shapes=list(scratch),
        compiler_params=pltpu.CompilerParams(vmem_limit_bytes=24 * 1024 * 1024),
        cost_estimate=pl.CostEstimate(flops=1, bytes_accessed=1, transcendentals=0),
    )(*[s.reshape(1).astype(jnp.int32) for s in scalars], *arrays)


def dot(left, right, contract=(((1,), (0,)), ((), ()))):
    return lax.dot_general(left, right, contract, preferred_element_type=F32)


def normalize(values):
    centered = values - jnp.mean(values, axis=-1, keepdims=True)
    inverse = lax.rsqrt(jnp.mean(centered * centered, axis=-1, keepdims=True) + EPSILON)
    return (centered * inverse, inverse)


def norm_back(gradient, normed, inverse):
    centered = gradient - jnp.mean(gradient, axis=-1, keepdims=True)
    return inverse * (centered - normed * jnp.mean(gradient * normed, axis=-1, keepdims=True))


def column(row):
    return jnp.broadcast_to(row, (LANES, LANES)).T


def as_row(column):
    seq = column.shape[0]
    if seq < LANES:
        column = jnp.concatenate([column, jnp.zeros((LANES - seq, LANES), F32)], axis=0)
    return column.T[:1]


def split_two(value):
    high = value.astype(BF16).astype(F32)
    return high, value - high


def replica_of(me_ref, j, count):
    return lax.rem(me_ref[0] + count - j, count)


def block_rows(me_ref, j, count, seq):
    block = replica_of(me_ref, j, count) // 2 + (j % 2) * (count // 2)
    return pl.ds(pl.multiple_of(block * seq, seq), seq)


def first_pieces(inputs, arriving, me, count):
    seq, width = arriving.shape
    part = width // count

    def body(me_ref, x_ref, arriving_ref, *refs):
        outs, (scale_ref, hidden_ref) = refs[:count], refs[count:]
        for row in range(0, seq, ROW_TILE):
            rows = slice(row, row + ROW_TILE)
            normed, inverse = normalize(x_ref[0, rows, :].astype(F32))
            hidden_ref[rows, :] = normed.astype(BF16)
            scale_ref[rows, :] = jnp.broadcast_to(inverse, (ROW_TILE, LANES))
        for j in range(count):
            owner = lax.rem(me_ref[0] + j, count)
            columns = pl.ds(pl.multiple_of(owner * part, LANES), part)
            outs[j][0] = hidden_ref[:, columns]
            outs[j][1] = arriving_ref[:, columns]

    outs = [shape(2, seq, part)] * count + [shape(seq, LANES, kind=F32)]
    scratch = [pltpu.VMEM((seq, width), BF16)]
    result = kernel_call(body, outs, [me], [inputs, arriving], scratch)
    return list(result[:count]), result[count]


def later_pieces(inputs, me, count):
    _, seq, width = inputs.shape
    part = width // count

    def body(me_ref, x_ref, *refs):
        outs, (scale_ref, hidden_ref) = refs[:count], refs[count:]
        for row in range(0, seq, ROW_TILE):
            rows = slice(row, row + ROW_TILE)
            normed, inverse = normalize(x_ref[1, rows, :].astype(F32))
            hidden_ref[rows, :] = normed.astype(BF16)
            scale_ref[rows, :] = jnp.broadcast_to(inverse, (ROW_TILE, LANES))
        for j in range(count):
            owner = lax.rem(me_ref[0] + j, count)
            columns = pl.ds(pl.multiple_of(owner * part, LANES), part)
            outs[j][...] = hidden_ref[:, columns]

    outs = [shape(seq, part)] * count + [shape(seq, LANES, kind=F32)]
    scratch = [pltpu.VMEM((seq, width), BF16)]
    result = kernel_call(body, outs, [me], [inputs], scratch)
    return list(result[:count]), result[count]


def first_partials(pieces, scales, project, output, me, width):
    count = len(pieces)
    _, seq, part = pieces[0].shape
    wide, head = project.shape[1], output.shape[1]
    half, ticks = count // 2, len(scales)
    extra = -(-2 * ticks * half // ROW_TILE) * ROW_TILE

    def body(me_ref, *refs):
        piece_refs, refs = refs[:count], refs[count:]
        scale_refs, (project_ref, output_ref, *outs) = refs[:ticks], refs[ticks:]
        project = project_ref[...]
        for j in range(count):
            out_ref, rows = outs[j % 2], half_rows(me_ref, j, count, seq)
            out_ref[rows, :wide] = dot(piece_refs[j][0], project).astype(BF16)
            out_ref[rows, wide:] = dot(piece_refs[j][1], output_ref[...]).astype(BF16)
        sums = jnp.sum(project.astype(F32), axis=0, keepdims=True) / width
        place = lax.broadcasted_iota(jnp.int32, (extra, LANES), 0) - 2 * ticks * (me_ref[0] // 2)
        facts = jnp.zeros((extra, LANES), F32)
        for t in range(ticks):
            for index, value in enumerate(split_two(as_row(scale_refs[t][...]))):
                facts = jnp.where(place == 2 * t + index, value, facts)
        for out_ref, lanes in zip(outs, (facts, jnp.zeros((extra, LANES), F32))):
            out_ref[half * seq :, :LANES] = lanes.astype(BF16)
            out_ref[half * seq :, LANES:] = jnp.broadcast_to(sums, (extra, wide)).astype(BF16)

    outs = [shape(half * seq + extra, wide + head)] * 2
    return kernel_call(body, outs, [me], [*pieces, *scales, project, output])


def half_rows(me_ref, j, count, seq):
    block = replica_of(me_ref, j, count) // 2
    return pl.ds(pl.multiple_of(block * seq, seq), seq)


def later_partials(pieces, project, me):
    count = len(pieces)
    seq = pieces[0].shape[0]
    wide = project.shape[1]

    def body(me_ref, *refs):
        piece_refs, (project_ref, *outs) = refs[:count], refs[count:]
        for j in range(count):
            value = dot(piece_refs[j][...], project_ref[...])
            outs[j % 2][half_rows(me_ref, j, count, seq), :] = value.astype(BF16)

    return kernel_call(body, [shape(count // 2 * seq, wide)] * 2, [me], [*pieces, project])


def add_two(left, right):
    def body(left_ref, right_ref, out_ref):
        out_ref[...] = (left_ref[...].astype(F32) + right_ref[...].astype(F32)).astype(BF16)

    return kernel_call(body, [shape(*left.shape)], [], [left, right])[0]


def attention_back(projected, head_half, row_mean, scale, seq, outs, width):
    grad_ref, mixed_ref, numbers_ref = outs
    rows, head = head_half.shape
    count = rows // seq
    root = math.sqrt(head)
    query, query_scale = normalize(projected[:, :head])
    key, key_scale = normalize(projected[:, head : 2 * head])
    query_half, key_half = query.astype(BF16), key.astype(BF16)
    value_half = projected[:, 2 * head :].astype(BF16)

    def each(function, *values):
        return jnp.concatenate(
            [function(*(v[r * seq : (r + 1) * seq] for v in values)) for r in range(count)], axis=0
        )

    def last(left, right):
        return dot(left, right, CONTRACT_LAST)

    def leading(left, right):
        return dot(left, right, CONTRACT_FIRST)

    powered = jnp.exp(each(last, query_half, key_half) / root)
    attention = powered / jnp.sum(powered, axis=-1, keepdims=True)
    attention_half = attention.astype(BF16)
    mixed_ref[...] = each(dot, attention_half, value_half).astype(BF16)
    prob_grad = each(last, head_half, value_half)
    value_grad = each(leading, attention_half, head_half).astype(BF16)
    score_grad = (
        attention * (prob_grad - jnp.sum(attention * prob_grad, axis=-1, keepdims=True)) / root
    ).astype(BF16)
    query_grad = norm_back(each(dot, score_grad, key_half), query, query_scale)
    key_grad = norm_back(each(leading, score_grad, query_half), key, key_scale)
    proj_grad = jnp.concatenate(
        [query_grad.astype(BF16), key_grad.astype(BF16), value_grad], axis=1
    )
    grad_ref[...] = proj_grad
    spread = proj_grad.astype(F32)
    offset = scale * jnp.sum(spread * row_mean, axis=-1, keepdims=True)
    slope = scale * (jnp.sum(spread * projected, axis=-1, keepdims=True) / width)
    lane = lax.broadcasted_iota(jnp.int32, (rows, LANES), 1)
    numbers_ref[...] = jnp.where(lane == 0, scale, jnp.where(lane == 1, offset, slope))


def all_rows(half_refs, seq, half, columns):
    return jnp.concatenate([ref[: half * seq, columns] for ref in half_refs], axis=0).astype(F32)


def scale_column(half_refs, tick, ticks, seq, half):
    columns = []
    for ref in half_refs:
        facts = ref[half * seq :, :LANES].astype(F32)
        for block in range(half):
            row = 2 * (ticks * block + tick)
            columns.append(column(facts[row : row + 1] + facts[row + 1 : row + 2])[:seq, :1])
    return jnp.concatenate(columns, axis=0)


def attention_outs(rows, head):
    return [shape(rows, 3 * head), shape(rows, head), shape(rows, LANES, kind=F32)]


def first_attention(halves, seq, half, head, ticks, width):
    rows, wide = 2 * half * seq, 3 * head

    def body(*refs):
        mine = refs[:2]
        attention_back(
            all_rows(mine, seq, half, slice(0, wide)),
            all_rows(mine, seq, half, slice(wide, wide + head)).astype(BF16),
            refs[0][half * seq :, LANES:].astype(F32)[:1],
            scale_column(mine, 0, ticks, seq, half),
            seq,
            refs[2:],
            width,
        )

    return kernel_call(body, attention_outs(rows, head), [], halves)


def later_attention(halves, facts, heads, received, seq, half, head, ticks, me, width):
    rows, count = 2 * half * seq, 2 * half
    part = received.shape[2] - head

    def body(me_ref, *refs):
        mine, facts, refs = refs[:2], refs[2:4], refs[4:]
        head_refs, (received_ref, *outs) = refs[: len(heads)], refs[len(heads) :]
        blocks = []
        for parity in range(2):
            for block in range(half):
                replica = 2 * block + lax.rem(me_ref[0] + parity, 2)
                place = pl.ds(pl.multiple_of(replica * seq, seq), seq)
                total = sum(ref[place, :].astype(F32) for ref in head_refs)
                piece = lax.rem(me_ref[0] + count - replica, count)
                blocks.append(total + received_ref[piece, :, part:].astype(F32))
        attention_back(
            all_rows(mine, seq, half, slice(None)),
            jnp.concatenate(blocks, axis=0).astype(BF16),
            facts[0][half * seq :, LANES:].astype(F32)[:1],
            scale_column(facts, 1, ticks, seq, half),
            seq,
            outs,
            width,
        )

    arrays = [*halves, *facts, *heads, received]
    return kernel_call(body, attention_outs(rows, head), [me], arrays)


def input_gradient(grad, numbers, incoming, hidden, project):
    scale, offset, slope = (numbers[:, i : i + 1] for i in range(3))
    hidden_grad = dot(grad, project, CONTRACT_LAST)
    change = scale * hidden_grad - offset - slope * hidden.astype(F32)
    return (incoming.astype(F32) + change).astype(BF16)


def middle_step(grads, pieces, tops, project, below, me, first):
    count, (_, seq, part) = len(pieces), pieces[0].shape
    head, runs = below.shape[1], len(tops)
    run = part // runs

    def body(me_ref, first_ref, *refs):
        refs = list(refs)
        piece_refs = [refs.pop(0) for _ in range(count)]
        top_refs = [refs.pop(0) for _ in range(runs)]
        grad_ref, numbers_ref, project_ref, below_ref, passed_ref, head_ref = refs
        is_first = first_ref[0] == 1

        @pl.when(is_first)
        def _():
            for j in range(count):
                block = lax.bitwise_xor(me_ref[0], replica_of(me_ref, j, count))
                for a in range(runs):
                    passed_ref[j, :, a * run : (a + 1) * run] = top_refs[a][block]

        @pl.when(jnp.logical_not(is_first))
        def _():
            for j in range(count):
                rows = block_rows(me_ref, j, count, seq)
                hidden, incoming = piece_refs[j][0], piece_refs[j][1]
                passed_ref[j, :, :part] = input_gradient(
                    grad_ref[rows, :], numbers_ref[rows, :], incoming, hidden, project_ref[...]
                )

        for j in range(count):
            value = dot(passed_ref[j, :, :part], below_ref[...]).astype(BF16)
            passed_ref[j, :, part:] = value
            replica = replica_of(me_ref, j, count)
            head_ref[pl.ds(pl.multiple_of(replica * seq, seq), seq), :] = value

    outs = [shape(count, seq, part + head), shape(count * seq, head)]
    return kernel_call(body, outs, [me, first], [*pieces, *tops, *grads, project, below])


def last_step(grads, received, pieces, project, me):
    count, (seq, part) = len(pieces), pieces[0].shape

    def body(me_ref, *refs):
        piece_refs, (grad_ref, numbers_ref, received_ref, project_ref, *outs) = (
            refs[:count],
            refs[count:],
        )
        for j in range(count):
            rows = block_rows(me_ref, j, count, seq)
            outs[j][...] = input_gradient(
                grad_ref[rows, :],
                numbers_ref[rows, :],
                received_ref[j, :, :part],
                piece_refs[j][...],
                project_ref[...],
            )

    arrays = [*pieces, *grads, received, project]
    return list(kernel_call(body, [shape(seq, part)] * count, [me], arrays))


def weight_gradients(pieces, later, received, first_grads, later_grads, me):
    count, (_, seq, part) = len(pieces), pieces[0].shape
    wide, head = first_grads[0].shape[1], first_grads[1].shape[1]
    block = min(part, 256)

    def body(me_ref, *refs):
        piece_refs, later_refs, refs = refs[:count], refs[count : 2 * count], refs[2 * count :]
        received_ref, grad0, mixed0, grad1, mixed1, project_ref, output_ref = refs
        for start in range(0, part, block):
            columns = slice(start, start + block)
            project_sum, output_sum = 0.0, 0.0
            for j in range(count):
                rows = block_rows(me_ref, j, count, seq)
                value = dot(piece_refs[j][0, :, columns], grad0[rows, :], CONTRACT_FIRST)
                value += dot(later_refs[j][:, columns], grad1[rows, :], CONTRACT_FIRST)
                project_sum += value.astype(BF16).astype(F32)
                value = dot(piece_refs[j][1, :, columns], mixed0[rows, :], CONTRACT_FIRST)
                value += dot(received_ref[j, :, columns], mixed1[rows, :], CONTRACT_FIRST)
                output_sum += value.astype(BF16).astype(F32)
            project_ref[columns, :] = project_sum
            output_ref[columns, :] = output_sum

    outs = [shape(part, wide, kind=F32), shape(part, head, kind=F32)]
    arrays = [*pieces, *later, received, *first_grads, *later_grads]
    return kernel_call(body, outs, [me], arrays)


def join_features(pieces, me):
    count = len(pieces)
    seq, part = pieces[0].shape

    def body(me_ref, *refs):
        for j in range(count):
            owner = lax.rem(me_ref[0] + j, count)
            columns = pl.ds(pl.multiple_of(owner * part, LANES), part)
            refs[count][:, columns] = refs[j][...]

    return kernel_call(body, [shape(seq, part * count)], [me], pieces)[0]


def shift(value, steps):
    count = lax.axis_size("dp")
    if steps % count == 0:
        return value
    return lax.ppermute(value, "dp", [(i, (i + steps) % count) for i in range(count)])


def after(value, *earlier):
    return lax.optimization_barrier((value, *earlier))[0]


def down(value, steps=0):
    pipe, count = lax.axis_size("pipe"), lax.axis_size("dp")
    pairs = [
        (p * count + r, (p - 1) % pipe * count + (r + steps) % count)
        for p in range(pipe)
        for r in range(count)
    ]
    return lax.ppermute(value, BOTH, pairs)


def join_pieces(left, right):
    size = left.shape[0]

    def body(left_ref, right_ref, out_ref):
        out_ref[:size] = left_ref[...]
        out_ref[size:] = right_ref[...]

    outs = [shape(2 * size, *left.shape[1:])]
    return kernel_call(body, outs, [], [left, right])[0]


def toward_owner(blocks, bit):
    pipe, count = lax.axis_size("pipe"), lax.axis_size("dp")
    runs = pipe // count
    pairs = [
        (q * count + r, q * count + (r ^ bit))
        for q in range(pipe)
        for r in range(count)
        if (r ^ (q // runs)) % (2 * bit) == bit
    ]
    return lax.ppermute(blocks, BOTH, pairs)


def owner_to_first(blocks, run):
    pipe, count = lax.axis_size("pipe"), lax.axis_size("dp")
    runs = pipe // count
    return lax.ppermute(blocks, BOTH, [((runs * s + run) * count + s, s) for s in range(count)])


def exchanged(value, step):
    count = lax.axis_size("dp")
    return lax.ppermute(value, "dp", [(i, i ^ step) for i in range(count)])


def shards(section_inputs, arriving, top_grads, project_weights, output_weights):
    count = lax.axis_size("dp")
    pipe = lax.axis_size("pipe")
    me = lax.axis_index("dp")
    first = lax.axis_index("pipe") == 0
    _, ticks, seq, width = section_inputs.shape
    head = output_weights.shape[2]
    project, output = project_weights[0], output_weights[0]
    others, half = range(count), count // 2

    blocks, moved = top_grads, toward_owner(top_grads, 1)
    sent, scale = first_pieces(section_inputs[0], arriving[0], me, count)
    pieces = [shift(sent[j], j) for j in others]
    later_sent, later_scale = later_pieces(section_inputs[0], me, count)
    blocks = join_pieces(after(blocks, later_scale), moved)
    bit = 2
    while bit < count // 2:
        blocks = join_pieces(blocks, toward_owner(blocks, bit))
        bit *= 2
    moved = toward_owner(blocks, bit) if bit < count else None

    mine, other = first_partials(
        pieces, [scale, later_scale], after(project, blocks), output, me, width
    )
    below = lax.ppermute(
        after(output, other), "pipe", [(p, (p + 1) % pipe) for p in range(pipe)]
    )
    later_sent = after(tuple(later_sent), other)
    later = [shift(later_sent[j], j) for j in others]
    later_mine, later_other = later_partials(later, project, me)
    total = add_two(after(mine, later_other, below), exchanged(other, 1))
    if moved is not None:
        blocks = join_pieces(after(blocks, total), moved)
    tops = [owner_to_first(blocks, run) for run in range(pipe // count)]
    later_total = add_two(after(later_mine, total), exchanged(later_other, 1))
    step = 2
    while step < count:
        received = exchanged(total, step)
        total = add_two(after(total, later_total), received)
        step *= 2
    halves = [total, exchanged(total, 1)]
    step = 2
    while step < count:
        received = exchanged(later_total, step)
        later_total = add_two(after(later_total, total), received)
        step *= 2
    halves[0] = after(halves[0], later_total)
    later_halves = [later_total, exchanged(later_total, 1)]

    first_grads = first_attention(halves, seq, half, head, ticks, width)
    passed, heads = middle_step(
        [first_grads[0], first_grads[2]], pieces, tops, project, below, me, first
    )
    heads = [down(heads, j) for j in others[1:]]
    received = down(passed)
    later_grads = later_attention(
        later_halves, halves, heads, received, seq, half, head, ticks, me, width
    )
    back = last_step([later_grads[0], later_grads[2]], received, later, project, me)
    mixed = after(later_grads[1], back[0])
    back = [shift(back[j], -j) for j in others]
    project_grads, output_grads = weight_gradients(
        pieces, later, received, first_grads[:2], [later_grads[0], mixed], me
    )
    passed_back = join_features(back, me)
    return (project_grads[None], output_grads[None], passed_back[None])


def solution(mesh):
    in_specs = (
        P("pipe", None, "dp", None),
        P("pipe", "dp", None),
        P(None, "dp", "pipe"),
        P("pipe", "dp", None),
        P("pipe", "dp", None),
    )
    out_specs = (P("pipe", "dp", None), P("pipe", "dp", None), P("pipe", "dp", None))
    return jax.shard_map(shards, mesh=mesh, in_specs=in_specs, out_specs=out_specs, check_vma=False)
```

time: 216 us -> 101 us (0.47)
  waiting for transfers between devices: 158 us -> 50 us
  starting transfers between devices: 1.54 us -> 34.8 us
  matrix products: 13.6 us -> 0 us
  between operations: 14.1 us -> 0.89 us
  Pallas kernels: 0 us -> 12.7 us
  blocking collectives: 12.4 us -> 0 us
  other arithmetic: 10 us -> 0 us
  local copies, waits for them, and re-layouts: 5.77 us -> 2.34 us
    reduce_scatter x1 -> x0, waiting for transfers between devices: 78.1 us -> none  [shards(): lax.psum_scatter(jnp.concatenate([sum_project, sum_output], axis=1).astyp...]
    all_gather x2 -> x0, waiting for transfers between devices: 78 us -> none  [the longest x1 63.1 us: shards(): lax.all_gather(project_weights[0], 'dp', axis=0, tiled=True)]
    ppermute x1 -> x24, waiting for transfers between devices: 0.8 us -> 50 us  [the longest x9 17.8 us: shift(): lax.ppermute(value, 'dp', [(i, (i + steps) % count) for i in range(count)])]
    ppermute x1 -> x24, starting transfers between devices: 1.42 us -> 34.8 us  [the longest x9 19.3 us: shift(): lax.ppermute(value, 'dp', [(i, (i + steps) % count) for i in range(count)])]
    dot_general x19 -> x0, matrix products: 13.6 us -> none  [the longest x2 3.8 us: shards(): lax.dot_general(proj_grad, full_project, CONTRACT_LAST, preferred_element...]
    pallas_call x0 -> x16, Pallas kernels: none -> 12.7 us  [kernel_call(): pl.pallas_call(body, out_shape=tuple(outs), in_specs=[pl.BlockSpec(memory...]
    all_gather x1 -> x0, blocking collectives: 12.4 us -> none  [shards(): later_grads = lax.all_gather(top_grads, 'pipe', axis=2, tiled=True)]
    concatenate x1 -> x0, other arithmetic: 2.2 us -> none  [shards(): jnp.concatenate([sum_project, sum_output], axis=1).astype(jnp.bfloat16)]
  transfers between devices with their start and end apart: 4 -> 24, of which waited for: 4 -> 8; matrix products, arithmetic and copies ran while one was open for 5% -> 0% of each run, Pallas kernels for 0% -> 7%
where the time goes in v3:
time: 101 us
  waiting for transfers between devices  50 us (50%)
  starting transfers between devices  34.8 us (34%)
  Pallas kernels  12.7 us (13%)
  local copies, waits for them, and re-layouts  2.34 us (2%)
    ppermute x9, starting transfers between devices, shift(): lax.ppermute(value, 'dp', [(i, (i + steps) % count) for i in range(count)])  19.3 us
    ppermute x9, waiting for transfers between devices, shift(): lax.ppermute(value, 'dp', [(i, (i + steps) % count) for i in range(count)])  17.8 us
    ppermute x2, waiting for transfers between devices, toward_owner(): return lax.ppermute(blocks, BOTH, pairs)  15.3 us
    pallas_call x16, Pallas kernels, kernel_call(): pl.pallas_call(body, out_shape=tuple(outs), in_specs=[pl.BlockSpec(memory...  12.7 us
    ppermute x6, waiting for transfers between devices, exchanged(): return lax.ppermute(value, 'dp', [(i, i ^ step) for i in range(count)])  12.1 us
    ppermute x6, starting transfers between devices, exchanged(): return lax.ppermute(value, 'dp', [(i, i ^ step) for i in range(count)])  5.32 us
    ppermute x4, starting transfers between devices, down(): return lax.ppermute(value, BOTH, pairs)  4.93 us
    ppermute x4, waiting for transfers between devices, down(): return lax.ppermute(value, BOTH, pairs)  4.74 us
  transfers between devices with their start and end apart: 24, of which 8 were waited for; matrix products, arithmetic and copies ran while one was open for 0% of the time, Pallas kernels for 7%

profile of v3, /device:TPU:0, one launch (start us, length us, event | category | flops | bytes accessed | tf_op | source)
XLA Modules:
  0.0 100.7 jit_solution(4608035851782730509)
XLA Ops:
  0.7 1.3 %copy-done.1 = bf16[1,2,64,4096]{3,2,1,0:T(8,128)(2,1)S(1)} copy-done((bf16[1,2,64,4096]{3,2,1,0:T(8,128)(2,1)S(1)}, bf16[1,2,64,4096]{3,2,1,0:T(8,128)(2,1)}, u32[]{:S(2)}) %copy-start.1) | copy-done | bytes 1048600
  1.9 1.0 %copy-done.2 = bf16[1,64,4096]{2,1,0:T(8,128)(2,1)S(1)} copy-done((bf16[1,64,4096]{2,1,0:T(8,128)(2,1)S(1)}, bf16[1,64,4096]{2,1,0:T(8,128)(2,1)}, u32[]{:S(2)}) %copy-start.2) | copy-done | bytes 524312
  3.0 0.4 shard_map.76
  3.4 3.1 %collective-permute-start = (bf16[2,64,1024]{2,1,0:T(8,128)(2,1)S(1)}, bf16[2,64,1024]{2,1,0:T(8,128)(2,1)S(1)}, u32[]{:S(2)}, u32[]{:S(2)}) collective-permute-start(bf16[2,64,1024]{2,1,0:T(8,128)(2,1)S(1)} %get-tuple-element.46), channel_id=1, source_target_pairs={{0,1},{1,2},{2,3},{3,0},{4,5},{5,6},{6,7},{7,4},{8,9},{9,10},{10,1... | collective-permute-start | bytes 786440 | tf_op jit(solution)/shard_map/ppermute | solution.py:397
  6.5 2.6 %collective-permute-start.1 = (bf16[2,64,1024]{2,1,0:T(8,128)(2,1)S(1)}, bf16[2,64,1024]{2,1,0:T(8,128)(2,1)S(1)}, u32[]{:S(2)}, u32[]{:S(2)}) collective-permute-start(bf16[2,64,1024]{2,1,0:T(8,128)(2,1)S(1)} %get-tuple-element.47), channel_id=1, source_target_pairs={{0,2},{1,3},{2,0},{3,1},{4,6},{5,7},{6,4},{7,5},{8,10},{9,11},{10,... | collective-permute-start | bytes 786440 | tf_op jit(solution)/shard_map/ppermute | solution.py:397
  9.1 1.3 %collective-permute-start.2 = (bf16[2,64,1024]{2,1,0:T(8,128)(2,1)S(1)}, bf16[2,64,1024]{2,1,0:T(8,128)(2,1)S(1)}, u32[]{:S(2)}, u32[]{:S(2)}) collective-permute-start(bf16[2,64,1024]{2,1,0:T(8,128)(2,1)S(1)} %get-tuple-element.48), channel_id=1, source_target_pairs={{0,3},{1,0},{2,1},{3,2},{4,7},{5,4},{6,5},{7,6},{8,11},{9,8},{10,9... | collective-permute-start | bytes 786440 | tf_op jit(solution)/shard_map/ppermute | solution.py:397
  10.4 1.3 %collective-permute-start.3 = (bf16[1,64,512]{2,1,0:T(8,128)(2,1)S(1)}, bf16[1,64,512]{2,1,0:T(8,128)(2,1)S(1)}, u32[]{:S(2)}, u32[]{:S(2)}) collective-permute-start(bf16[1,64,512]{2,1,0:T(8,128)(2,1)S(1)} %copy-done.4), channel_id=1, source_target_pairs={{1,0},{3,2},{5,4},{7,6},{8,9},{10,11},{12,13},{14,15},{17,16},{19,... | collective-permute-start | bytes 196616 | tf_op jit(solution)/shard_map/ppermute | solution.py:434
  11.7 0.4 shard_map.77
  12.1 15.3 %collective-permute-done.3.right_ref = bf16[1,64,512]{2,1,0:T(8,128)(2,1)S(1)} collective-permute-done((bf16[1,64,512]{2,1,0:T(8,128)(2,1)S(1)}, bf16[1,64,512]{2,1,0:T(8,128)(2,1)S(1)}, u32[]{:S(2)}, u32[]{:S(2)}) %collective-permute-start.3) | collective-permute-done | bytes 65568 | tf_op jit(solution)/shard_map/ppermute | solution.py:434
  27.5 0.0 collective-permute-done.2.refs_3_
  27.5 0.8 shard_map.79
  28.3 0.1 collective-permute-start.7
  28.4 4.8 %collective-permute-start.4 = (bf16[64,1024]{1,0:T(8,128)(2,1)S(1)}, bf16[64,1024]{1,0:T(8,128)(2,1)S(1)}, u32[]{:S(2)}, u32[]{:S(2)}) collective-permute-start(bf16[64,1024]{1,0:T(8,128)(2,1)S(1)} %get-tuple-element.59), channel_id=1, source_target_pairs={{0,1},{1,2},{2,3},{3,0},{4,5},{5,6},{6,7},{7,4},{8,9},{9,10},{10,1... | collective-permute-start | bytes 393224 | tf_op jit(solution)/shard_map/ppermute | solution.py:397
  33.2 0.1 collective-permute-start.8
  33.3 1.5 %collective-permute-start.5 = (bf16[64,1024]{1,0:T(8,128)(2,1)S(1)}, bf16[64,1024]{1,0:T(8,128)(2,1)S(1)}, u32[]{:S(2)}, u32[]{:S(2)}) collective-permute-start(bf16[64,1024]{1,0:T(8,128)(2,1)S(1)} %get-tuple-element.60), channel_id=1, source_target_pairs={{0,2},{1,3},{2,0},{3,1},{4,6},{5,7},{6,4},{7,5},{8,10},{9,11},{10,... | collective-permute-start | bytes 393224 | tf_op jit(solution)/shard_map/ppermute | solution.py:397
  34.9 2.8 %collective-permute-start.6 = (bf16[64,1024]{1,0:T(8,128)(2,1)S(1)}, bf16[64,1024]{1,0:T(8,128)(2,1)S(1)}, u32[]{:S(2)}, u32[]{:S(2)}) collective-permute-start(bf16[64,1024]{1,0:T(8,128)(2,1)S(1)} %get-tuple-element.61), channel_id=1, source_target_pairs={{0,3},{1,0},{2,1},{3,2},{4,7},{5,4},{6,5},{7,6},{8,11},{9,8},{10,9... | collective-permute-start | bytes 393224 | tf_op jit(solution)/shard_map/ppermute | solution.py:397
  37.6 0.2 collective-permute-done.4.refs_1_.refs_5_
  37.9 1.3 %collective-permute-start.9 = (bf16[2,64,512]{2,1,0:T(8,128)(2,1)S(1)}, bf16[2,64,512]{2,1,0:T(8,128)(2,1)S(1)}, u32[]{:S(2)}, u32[]{:S(2)}) collective-permute-start(bf16[2,64,512]{2,1,0:T(8,128)(2,1)S(1)} %shard_map.78.left_ref), channel_id=1, source_target_pairs={{2,0},{6,4},{11,9},{15,13},{16,18},{20,22},{25,27},{29,31}} | collective-permute-start | bytes 393224 | tf_op jit(solution)/shard_map/ppermute | solution.py:434
  39.1 3.5 %collective-permute-done.5.refs_2_.refs_6_ = bf16[64,1024]{1,0:T(8,128)(2,1)S(1)} collective-permute-done((bf16[64,1024]{1,0:T(8,128)(2,1)S(1)}, bf16[64,1024]{1,0:T(8,128)(2,1)S(1)}, u32[]{:S(2)}, u32[]{:S(2)}) %collective-permute-start.5) | collective-permute-done | bytes 131104 | tf_op jit(solution)/shard_map/ppermute | solution.py:397
  42.6 7.5 %collective-permute-done.6.refs_3_.refs_7_ = bf16[64,1024]{1,0:T(8,128)(2,1)S(1)} collective-permute-done((bf16[64,1024]{1,0:T(8,128)(2,1)S(1)}, bf16[64,1024]{1,0:T(8,128)(2,1)S(1)}, u32[]{:S(2)}, u32[]{:S(2)}) %collective-permute-start.6) | collective-permute-done | bytes 131104 | tf_op jit(solution)/shard_map/ppermute | solution.py:397
  50.2 0.6 shard_map.80
  50.8 0.0 collective-permute-done.7.refs_9_
  50.9 0.1 collective-permute-start.13
  51.0 1.3 %collective-permute-start.11 = (bf16[4,64,512]{2,1,0:T(8,128)(2,1)S(1)}, bf16[4,64,512]{2,1,0:T(8,128)(2,1)S(1)}, u32[]{:S(2)}, u32[]{:S(2)}) collective-permute-start(bf16[4,64,512]{2,1,0:T(8,128)(2,1)S(1)} %shard_map.82), channel_id=1, source_target_pairs={{4,0},{13,1},{22,2},{31,3}} | collective-permute-start | bytes 786440 | tf_op jit(solution)/shard_map/ppermute | solution.py:440
  52.3 1.3 %collective-permute-start.10 = (bf16[4,64,512]{2,1,0:T(8,128)(2,1)S(1)}, bf16[4,64,512]{2,1,0:T(8,128)(2,1)}, u32[]{:S(2)}, u32[]{:S(2)}) collective-permute-start(bf16[4,64,512]{2,1,0:T(8,128)(2,1)S(1)} %shard_map.82), channel_id=1, source_target_pairs={{0,0},{9,1},{18,2},{27,3}} | collective-permute-start | bytes 786440 | tf_op jit(solution)/shard_map/ppermute | solution.py:440
  53.6 0.1 collective-permute-start.12
  53.8 6.3 %collective-permute-done.12.right_ref = bf16[128,384]{1,0:T(8,128)(2,1)S(1)} collective-permute-done((bf16[128,384]{1,0:T(8,128)(2,1)S(1)}, bf16[128,384]{1,0:T(8,128)(2,1)S(1)}, u32[]{:S(2)}, u32[]{:S(2)}) %collective-permute-start.12) | collective-permute-done | bytes 98336 | tf_op jit(solution)/shard_map/ppermute | solution.py:445
  60.1 0.1 collective-permute-start.15
  60.2 2.3 %collective-permute-start.14 = (bf16[128,384]{1,0:T(8,128)(2,1)S(1)}, bf16[128,384]{1,0:T(8,128)(2,1)}, u32[]{:S(2)}, u32[]{:S(2)}) collective-permute-start(bf16[128,384]{1,0:T(8,128)(2,1)S(1)} %shard_map.83.left_ref), channel_id=1, source_target_pairs={{0,2},{1,3},{2,0},{3,1},{4,6},{5,7},{6,4},{7,5},{8,10},{9,11},{10,... | collective-permute-start | bytes 294920 | tf_op jit(solution)/shard_map/ppermute | solution.py:445
  62.5 5.8 %collective-permute-done.14.right_ref = bf16[128,384]{1,0:T(8,128)(2,1)} collective-permute-done((bf16[128,384]{1,0:T(8,128)(2,1)S(1)}, bf16[128,384]{1,0:T(8,128)(2,1)}, u32[]{:S(2)}, u32[]{:S(2)}) %collective-permute-start.14) | collective-permute-done | bytes 98336 | tf_op jit(solution)/shard_map/ppermute | solution.py:445
  68.3 0.9 shard_map.85.refs_0_
  69.2 0.0 collective-permute-done.15.refs_1_.refs_3_
  69.2 1.2 %shard_map.86 = (bf16[256,384]{1,0:T(8,128)(2,1)S(1)}, bf16[256,128]{1,0:T(8,128)(2,1)S(1)}, f32[256,128]{1,0:T(8,128)S(1)}) custom-call(bf16[144,512]{1,0:T(8,128)(2,1)S(1)} %shard_map.84.refs_0_.refs_2_, bf16[144,512]{1,0:T(8,128)(2,1)S(1)} %collective-permute-done.15.refs_1_.refs_3_), custom_call_target="tpu_custom_call" | custom-call | flops 1 | bytes 1 | tf_op jit(solution)/shard_map/pallas_call | solution.py:26
  70.4 1.3 %shard_map.87 = (bf16[4,64,1152]{2,1,0:T(8,128)(2,1)S(1)}, bf16[256,128]{1,0:T(8,128)(2,1)S(1)}) custom-call(s32[1]{0:T(128)} %bitcast.me_ref, s32[1]{0:T(128)} %bitcast.5.first_ref, bf16[2,64,1024]{2,1,0:T(8,128)(2,1)S(1)} %get-tuple-element.45.refs_0_, bf16[2,64,1024]{2,1,0:T(8,128)(2,1)S(1)} %collective-permute-done.refs_1_, ...), custom_call_target="tpu_custom_call" | custom-call | flops 1 | bytes 1 | tf_op jit(solution)/shard_map/pallas_call | solution.py:26
  71.7 0.1 collective-permute-start.16
  71.8 2.7 %collective-permute-start.17 = (bf16[128,384]{1,0:T(8,128)(2,1)S(1)}, bf16[128,384]{1,0:T(8,128)(2,1)S(1)}, u32[]{:S(2)}, u32[]{:S(2)}) collective-permute-start(bf16[128,384]{1,0:T(8,128)(2,1)S(1)} %shard_map.85.refs_0_), channel_id=1, source_target_pairs={{0,1},{1,0},{2,3},{3,2},{4,5},{5,4},{6,7},{7,6},{8,9},{9,8},{10,11... | collective-permute-start | bytes 294920 | tf_op jit(solution)/shard_map/ppermute | solution.py:445
  74.4 1.6 %collective-permute-start.20 = (bf16[256,128]{1,0:T(8,128)(2,1)S(1)}, bf16[256,128]{1,0:T(8,128)(2,1)S(1)}, u32[]{:S(2)}, u32[]{:S(2)}) collective-permute-start(bf16[256,128]{1,0:T(8,128)(2,1)S(1)} %get-tuple-element.76), channel_id=1, source_target_pairs={{0,31},{1,28},{2,29},{3,30},{4,3},{5,0},{6,1},{7,2},{8,7},{9,4},{1... | collective-permute-start | bytes 196616 | tf_op jit(solution)/shard_map/ppermute | solution.py:411
  76.1 0.3 collective-permute-start.19
  76.4 2.9 %collective-permute-start.18 = (bf16[256,128]{1,0:T(8,128)(2,1)S(1)}, bf16[256,128]{1,0:T(8,128)(2,1)S(1)}, u32[]{:S(2)}, u32[]{:S(2)}) collective-permute-start(bf16[256,128]{1,0:T(8,128)(2,1)S(1)} %get-tuple-element.76), channel_id=1, source_target_pairs={{0,29},{1,30},{2,31},{3,28},{4,1},{5,2},{6,3},{7,0},{8,5},{9,6},{1... | collective-permute-start | bytes 196616 | tf_op jit(solution)/shard_map/ppermute | solution.py:411
  79.3 4.7 %collective-permute-done.19.refs_5_ = bf16[256,128]{1,0:T(8,128)(2,1)S(1)} collective-permute-done((bf16[256,128]{1,0:T(8,128)(2,1)S(1)}, bf16[256,128]{1,0:T(8,128)(2,1)S(1)}, u32[]{:S(2)}, u32[]{:S(2)}) %collective-permute-start.19) | collective-permute-done | bytes 65568 | tf_op jit(solution)/shard_map/ppermute | solution.py:411
  84.1 1.2 %shard_map.88 = (bf16[256,384]{1,0:T(8,128)(2,1)S(1)}, bf16[256,128]{1,0:T(8,128)(2,1)S(1)}, f32[256,128]{1,0:T(8,128)S(1)}) custom-call(s32[1]{0:T(128)} %bitcast.me_ref, bf16[128,384]{1,0:T(8,128)(2,1)S(1)} %shard_map.85.refs_0_, bf16[128,384]{1,0:T(8,128)(2,1)S(1)} %collective-permute-done.17.refs_1_, bf16[144,512]{1,0:T(8,128)(2,1)S(1)} %shard_map.84.refs_0_.refs_2_, ...), custom_call_target="tpu_custom_call" | custom-call | flops 1 | bytes 1 | tf_op jit(solution)/shard_map/pallas_call | solution.py:26
  85.3 1.2 %shard_map.89 = (bf16[64,1024]{1,0:T(8,128)(2,1)S(1)}, bf16[64,1024]{1,0:T(8,128)(2,1)S(1)}, bf16[64,1024]{1,0:T(8,128)(2,1)S(1)}, bf16[64,1024]{1,0:T(8,128)(2,1)S(1)}) custom-call(s32[1]{0:T(128)} %bitcast.me_ref, bf16[64,1024]{1,0:T(8,128)(2,1)S(1)} %get-tuple-element.58.refs_0_.refs_4_, bf16[64,1024]{1,0:T(8,128)(2,1)S(1)} %collective-permute-done.4.refs_1_.refs_5_, ...), custom_call_target="tpu_custom_call" | custom-call | flops 1 | bytes 1 | tf_op jit(solution)/shard_map/pallas_call | solution.py:26
  86.4 0.7 collective-permute-start.21
  87.1 0.7 collective-permute-start.22
  87.8 1.7 %collective-permute-start.23 = (bf16[64,1024]{1,0:T(8,128)(2,1)S(1)}, bf16[64,1024]{1,0:T(8,128)(2,1)S(1)}, u32[]{:S(2)}, u32[]{:S(2)}) collective-permute-start(bf16[64,1024]{1,0:T(8,128)(2,1)S(1)} %get-tuple-element.86), channel_id=1, source_target_pairs={{0,1},{1,2},{2,3},{3,0},{4,5},{5,6},{6,7},{7,4},{8,9},{9,10},{10,1... | collective-permute-start | bytes 393224 | tf_op jit(solution)/shard_map/ppermute | solution.py:397
  89.6 3.7 %shard_map.90 = (f32[1024,384]{1,0:T(8,128)}, f32[1024,128]{1,0:T(8,128)}) custom-call(s32[1]{0:T(128)} %bitcast.me_ref, bf16[2,64,1024]{2,1,0:T(8,128)(2,1)S(1)} %get-tuple-element.45.refs_0_, bf16[2,64,1024]{2,1,0:T(8,128)(2,1)S(1)} %collective-permute-done.refs_1_, bf16[2,64,1024]{2,1,0:T(8,128)(2,1)S(1)} %collective-permute-done.1.refs_2_, ...), custom_call_target="tpu_custom_call" | custom-call | flops 1 | bytes 1 | tf_op jit(solution)/shard_map/pallas_call | solution.py:26
  93.3 6.6 %collective-permute-done.22.refs_2_ = bf16[64,1024]{1,0:T(8,128)(2,1)S(1)} collective-permute-done((bf16[64,1024]{1,0:T(8,128)(2,1)S(1)}, bf16[64,1024]{1,0:T(8,128)(2,1)S(1)}, u32[]{:S(2)}, u32[]{:S(2)}) %collective-permute-start.22) | collective-permute-done | bytes 131104 | tf_op jit(solution)/shard_map/ppermute | solution.py:397
  99.8 0.8 shard_map.91
  (26 shorter events, 0.2 us)
Async XLA Ops:
  0.6 26.9 %copy-start = (bf16[1,1024,384]{2,1,0:T(8,128)(2,1)S(1)}, bf16[1,1024,384]{2,1,0:T(8,128)(2,1)}, u32[]{:S(2)}) copy-start(bf16[1,1024,384]{2,1,0:T(8,128)(2,1)} %param.8) | copy-start | bytes 2359300
  0.6 1.3 %copy-start.1 = (bf16[1,2,64,4096]{3,2,1,0:T(8,128)(2,1)S(1)}, bf16[1,2,64,4096]{3,2,1,0:T(8,128)(2,1)}, u32[]{:S(2)}) copy-start(bf16[1,2,64,4096]{3,2,1,0:T(8,128)(2,1)} %param.5) | copy-start | bytes 3145732
  1.9 1.0 %copy-start.2 = (bf16[1,64,4096]{2,1,0:T(8,128)(2,1)S(1)}, bf16[1,64,4096]{2,1,0:T(8,128)(2,1)}, u32[]{:S(2)}) copy-start(bf16[1,64,4096]{2,1,0:T(8,128)(2,1)} %param.6) | copy-start | bytes 1572868
  3.0 7.4 %copy-start.4 = (bf16[1,64,512]{2,1,0:T(8,128)(2,1)S(1)}, bf16[1,64,512]{2,1,0:T(8,128)(2,1)}, u32[]{:S(2)}) copy-start(bf16[1,64,512]{2,1,0:T(8,128)(2,1)} %left_ref) | copy-start | bytes 196612
  3.0 24.5 %copy-start.3 = (bf16[1,1024,128]{2,1,0:T(8,128)(2,1)S(1)}, bf16[1,1024,128]{2,1,0:T(8,128)(2,1)}, u32[]{:S(2)}) copy-start(bf16[1,1024,128]{2,1,0:T(8,128)(2,1)} %param.9) | copy-start | bytes 786436
  3.4 24.1 %collective-permute-start = (bf16[2,64,1024]{2,1,0:T(8,128)(2,1)S(1)}, bf16[2,64,1024]{2,1,0:T(8,128)(2,1)S(1)}, u32[]{:S(2)}, u32[]{:S(2)}) collective-permute-start(bf16[2,64,1024]{2,1,0:T(8,128)(2,1)S(1)} %get-tuple-element.46), channel_id=1, source_target_pairs={{0,1},{1,2},{2,3},{3,0},{4,5},{5,6},{6,7},{7,4},{8,9},{9,10},{10,1... | collective-permute-start | bytes 786440 | tf_op jit(solution)/shard_map/ppermute | solution.py:397
  6.5 21.0 %collective-permute-start.1 = (bf16[2,64,1024]{2,1,0:T(8,128)(2,1)S(1)}, bf16[2,64,1024]{2,1,0:T(8,128)(2,1)S(1)}, u32[]{:S(2)}, u32[]{:S(2)}) collective-permute-start(bf16[2,64,1024]{2,1,0:T(8,128)(2,1)S(1)} %get-tuple-element.47), channel_id=1, source_target_pairs={{0,2},{1,3},{2,0},{3,1},{4,6},{5,7},{6,4},{7,5},{8,10},{9,11},{10,... | collective-permute-start | bytes 786440 | tf_op jit(solution)/shard_map/ppermute | solution.py:397
  9.1 18.4 %collective-permute-start.2 = (bf16[2,64,1024]{2,1,0:T(8,128)(2,1)S(1)}, bf16[2,64,1024]{2,1,0:T(8,128)(2,1)S(1)}, u32[]{:S(2)}, u32[]{:S(2)}) collective-permute-start(bf16[2,64,1024]{2,1,0:T(8,128)(2,1)S(1)} %get-tuple-element.48), channel_id=1, source_target_pairs={{0,3},{1,0},{2,1},{3,2},{4,7},{5,4},{6,5},{7,6},{8,11},{9,8},{10,9... | collective-permute-start | bytes 786440 | tf_op jit(solution)/shard_map/ppermute | solution.py:397
  10.4 17.0 %collective-permute-start.3 = (bf16[1,64,512]{2,1,0:T(8,128)(2,1)S(1)}, bf16[1,64,512]{2,1,0:T(8,128)(2,1)S(1)}, u32[]{:S(2)}, u32[]{:S(2)}) collective-permute-start(bf16[1,64,512]{2,1,0:T(8,128)(2,1)S(1)} %copy-done.4), channel_id=1, source_target_pairs={{1,0},{3,2},{5,4},{7,6},{8,9},{10,11},{12,13},{14,15},{17,16},{19,... | collective-permute-start | bytes 196616 | tf_op jit(solution)/shard_map/ppermute | solution.py:434
  28.3 22.5 %collective-permute-start.7 = (bf16[1024,128]{1,0:T(8,128)(2,1)S(1)}, bf16[1024,128]{1,0:T(8,128)(2,1)S(1)}, u32[]{:S(2)}, u32[]{:S(2)}) collective-permute-start(bf16[1024,128]{1,0:T(8,128)(2,1)S(1)} %bitcast.17), channel_id=1, source_target_pairs={{0,4},{4,8},{8,12},{12,16},{16,20},{20,24},{24,28},{28,0},{1,5},{5... | collective-permute-start | bytes 786440 | tf_op jit(solution)/shard_map/ppermute | solution.py:472
  28.4 9.5 %collective-permute-start.4 = (bf16[64,1024]{1,0:T(8,128)(2,1)S(1)}, bf16[64,1024]{1,0:T(8,128)(2,1)S(1)}, u32[]{:S(2)}, u32[]{:S(2)}) collective-permute-start(bf16[64,1024]{1,0:T(8,128)(2,1)S(1)} %get-tuple-element.59), channel_id=1, source_target_pairs={{0,1},{1,2},{2,3},{3,0},{4,5},{5,6},{6,7},{7,4},{8,9},{9,10},{10,1... | collective-permute-start | bytes 393224 | tf_op jit(solution)/shard_map/ppermute | solution.py:397
  33.2 17.5 %collective-permute-start.8 = (bf16[144,512]{1,0:T(8,128)(2,1)S(1)}, bf16[144,512]{1,0:T(8,128)(2,1)S(1)}, u32[]{:S(2)}, u32[]{:S(2)}) collective-permute-start(bf16[144,512]{1,0:T(8,128)(2,1)S(1)} %get-tuple-element.57), channel_id=1, source_target_pairs={{0,1},{1,0},{2,3},{3,2},{4,5},{5,4},{6,7},{7,6},{8,9},{9,8},{10,11... | collective-permute-start | bytes 442376 | tf_op jit(solution)/shard_map/ppermute | solution.py:445
  33.3 9.3 %collective-permute-start.5 = (bf16[64,1024]{1,0:T(8,128)(2,1)S(1)}, bf16[64,1024]{1,0:T(8,128)(2,1)S(1)}, u32[]{:S(2)}, u32[]{:S(2)}) collective-permute-start(bf16[64,1024]{1,0:T(8,128)(2,1)S(1)} %get-tuple-element.60), channel_id=1, source_target_pairs={{0,2},{1,3},{2,0},{3,1},{4,6},{5,7},{6,4},{7,5},{8,10},{9,11},{10,... | collective-permute-start | bytes 393224 | tf_op jit(solution)/shard_map/ppermute | solution.py:397
  34.9 15.3 %collective-permute-start.6 = (bf16[64,1024]{1,0:T(8,128)(2,1)S(1)}, bf16[64,1024]{1,0:T(8,128)(2,1)S(1)}, u32[]{:S(2)}, u32[]{:S(2)}) collective-permute-start(bf16[64,1024]{1,0:T(8,128)(2,1)S(1)} %get-tuple-element.61), channel_id=1, source_target_pairs={{0,3},{1,0},{2,1},{3,2},{4,7},{5,4},{6,5},{7,6},{8,11},{9,8},{10,9... | collective-permute-start | bytes 393224 | tf_op jit(solution)/shard_map/ppermute | solution.py:397
  37.9 13.1 %collective-permute-start.9 = (bf16[2,64,512]{2,1,0:T(8,128)(2,1)S(1)}, bf16[2,64,512]{2,1,0:T(8,128)(2,1)S(1)}, u32[]{:S(2)}, u32[]{:S(2)}) collective-permute-start(bf16[2,64,512]{2,1,0:T(8,128)(2,1)S(1)} %shard_map.78.left_ref), channel_id=1, source_target_pairs={{2,0},{6,4},{11,9},{15,13},{16,18},{20,22},{25,27},{29,31}} | collective-permute-start | bytes 393224 | tf_op jit(solution)/shard_map/ppermute | solution.py:434
  50.9 9.2 %collective-permute-start.13 = (bf16[144,512]{1,0:T(8,128)(2,1)S(1)}, bf16[144,512]{1,0:T(8,128)(2,1)S(1)}, u32[]{:S(2)}, u32[]{:S(2)}) collective-permute-start(bf16[144,512]{1,0:T(8,128)(2,1)S(1)} %shard_map.81.left_ref), channel_id=1, source_target_pairs={{0,2},{1,3},{2,0},{3,1},{4,6},{5,7},{6,4},{7,5},{8,10},{9,11},{10,... | collective-permute-start | bytes 442376 | tf_op jit(solution)/shard_map/ppermute | solution.py:445
  51.0 19.4 %collective-permute-start.11 = (bf16[4,64,512]{2,1,0:T(8,128)(2,1)S(1)}, bf16[4,64,512]{2,1,0:T(8,128)(2,1)S(1)}, u32[]{:S(2)}, u32[]{:S(2)}) collective-permute-start(bf16[4,64,512]{2,1,0:T(8,128)(2,1)S(1)} %shard_map.82), channel_id=1, source_target_pairs={{4,0},{13,1},{22,2},{31,3}} | collective-permute-start | bytes 786440 | tf_op jit(solution)/shard_map/ppermute | solution.py:440
  52.3 18.2 %collective-permute-start.10 = (bf16[4,64,512]{2,1,0:T(8,128)(2,1)S(1)}, bf16[4,64,512]{2,1,0:T(8,128)(2,1)}, u32[]{:S(2)}, u32[]{:S(2)}) collective-permute-start(bf16[4,64,512]{2,1,0:T(8,128)(2,1)S(1)} %shard_map.82), channel_id=1, source_target_pairs={{0,0},{9,1},{18,2},{27,3}} | collective-permute-start | bytes 786440 | tf_op jit(solution)/shard_map/ppermute | solution.py:440
  53.6 6.4 %collective-permute-start.12 = (bf16[128,384]{1,0:T(8,128)(2,1)S(1)}, bf16[128,384]{1,0:T(8,128)(2,1)S(1)}, u32[]{:S(2)}, u32[]{:S(2)}) collective-permute-start(bf16[128,384]{1,0:T(8,128)(2,1)S(1)} %get-tuple-element.63), channel_id=1, source_target_pairs={{0,1},{1,0},{2,3},{3,2},{4,5},{5,4},{6,7},{7,6},{8,9},{9,8},{10,11... | collective-permute-start | bytes 294920 | tf_op jit(solution)/shard_map/ppermute | solution.py:445
  60.1 9.1 %collective-permute-start.15 = (bf16[144,512]{1,0:T(8,128)(2,1)S(1)}, bf16[144,512]{1,0:T(8,128)(2,1)S(1)}, u32[]{:S(2)}, u32[]{:S(2)}) collective-permute-start(bf16[144,512]{1,0:T(8,128)(2,1)S(1)} %shard_map.84.refs_0_.refs_2_), channel_id=1, source_target_pairs={{0,1},{1,0},{2,3},{3,2},{4,5},{5,4},{6,7},{7,6},{8,9},{9,8},{10,11... | collective-permute-start | bytes 442376 | tf_op jit(solution)/shard_map/ppermute | solution.py:445
  60.2 8.1 %collective-permute-start.14 = (bf16[128,384]{1,0:T(8,128)(2,1)S(1)}, bf16[128,384]{1,0:T(8,128)(2,1)}, u32[]{:S(2)}, u32[]{:S(2)}) collective-permute-start(bf16[128,384]{1,0:T(8,128)(2,1)S(1)} %shard_map.83.left_ref), channel_id=1, source_target_pairs={{0,2},{1,3},{2,0},{3,1},{4,6},{5,7},{6,4},{7,5},{8,10},{9,11},{10,... | collective-permute-start | bytes 294920 | tf_op jit(solution)/shard_map/ppermute | solution.py:445
  71.7 12.3 %collective-permute-start.16 = (bf16[4,64,1152]{2,1,0:T(8,128)(2,1)S(1)}, bf16[4,64,1152]{2,1,0:T(8,128)(2,1)S(1)}, u32[]{:S(2)}, u32[]{:S(2)}) collective-permute-start(bf16[4,64,1152]{2,1,0:T(8,128)(2,1)S(1)} %get-tuple-element.74), channel_id=1, source_target_pairs={{0,28},{1,29},{2,30},{3,31},{4,0},{5,1},{6,2},{7,3},{8,4},{9,5},{1... | collective-permute-start | bytes 1769480 | tf_op jit(solution)/shard_map/ppermute | solution.py:411
  71.8 7.5 %collective-permute-start.17 = (bf16[128,384]{1,0:T(8,128)(2,1)S(1)}, bf16[128,384]{1,0:T(8,128)(2,1)S(1)}, u32[]{:S(2)}, u32[]{:S(2)}) collective-permute-start(bf16[128,384]{1,0:T(8,128)(2,1)S(1)} %shard_map.85.refs_0_), channel_id=1, source_target_pairs={{0,1},{1,0},{2,3},{3,2},{4,5},{5,4},{6,7},{7,6},{8,9},{9,8},{10,11... | collective-permute-start | bytes 294920 | tf_op jit(solution)/shard_map/ppermute | solution.py:445
  74.4 4.9 %collective-permute-start.20 = (bf16[256,128]{1,0:T(8,128)(2,1)S(1)}, bf16[256,128]{1,0:T(8,128)(2,1)S(1)}, u32[]{:S(2)}, u32[]{:S(2)}) collective-permute-start(bf16[256,128]{1,0:T(8,128)(2,1)S(1)} %get-tuple-element.76), channel_id=1, source_target_pairs={{0,31},{1,28},{2,29},{3,30},{4,3},{5,0},{6,1},{7,2},{8,7},{9,4},{1... | collective-permute-start | bytes 196616 | tf_op jit(solution)/shard_map/ppermute | solution.py:411
  76.1 8.0 %collective-permute-start.19 = (bf16[256,128]{1,0:T(8,128)(2,1)S(1)}, bf16[256,128]{1,0:T(8,128)(2,1)S(1)}, u32[]{:S(2)}, u32[]{:S(2)}) collective-permute-start(bf16[256,128]{1,0:T(8,128)(2,1)S(1)} %get-tuple-element.76), channel_id=1, source_target_pairs={{0,30},{1,31},{2,28},{3,29},{4,2},{5,3},{6,0},{7,1},{8,6},{9,7},{1... | collective-permute-start | bytes 196616 | tf_op jit(solution)/shard_map/ppermute | solution.py:411
  76.4 7.7 %collective-permute-start.18 = (bf16[256,128]{1,0:T(8,128)(2,1)S(1)}, bf16[256,128]{1,0:T(8,128)(2,1)S(1)}, u32[]{:S(2)}, u32[]{:S(2)}) collective-permute-start(bf16[256,128]{1,0:T(8,128)(2,1)S(1)} %get-tuple-element.76), channel_id=1, source_target_pairs={{0,29},{1,30},{2,31},{3,28},{4,1},{5,2},{6,3},{7,0},{8,5},{9,6},{1... | collective-permute-start | bytes 196616 | tf_op jit(solution)/shard_map/ppermute | solution.py:411
  86.4 6.9 %collective-permute-start.21 = (bf16[64,1024]{1,0:T(8,128)(2,1)S(1)}, bf16[64,1024]{1,0:T(8,128)(2,1)S(1)}, u32[]{:S(2)}, u32[]{:S(2)}) collective-permute-start(bf16[64,1024]{1,0:T(8,128)(2,1)S(1)} %get-tuple-element.84), channel_id=1, source_target_pairs={{0,3},{1,0},{2,1},{3,2},{4,7},{5,4},{6,5},{7,6},{8,11},{9,8},{10,9... | collective-permute-start | bytes 393224 | tf_op jit(solution)/shard_map/ppermute | solution.py:397
  87.1 12.7 %collective-permute-start.22 = (bf16[64,1024]{1,0:T(8,128)(2,1)S(1)}, bf16[64,1024]{1,0:T(8,128)(2,1)S(1)}, u32[]{:S(2)}, u32[]{:S(2)}) collective-permute-start(bf16[64,1024]{1,0:T(8,128)(2,1)S(1)} %get-tuple-element.85), channel_id=1, source_target_pairs={{0,2},{1,3},{2,0},{3,1},{4,6},{5,7},{6,4},{7,5},{8,10},{9,11},{10,... | collective-permute-start | bytes 393224 | tf_op jit(solution)/shard_map/ppermute | solution.py:397
  87.8 12.0 %collective-permute-start.23 = (bf16[64,1024]{1,0:T(8,128)(2,1)S(1)}, bf16[64,1024]{1,0:T(8,128)(2,1)S(1)}, u32[]{:S(2)}, u32[]{:S(2)}) collective-permute-start(bf16[64,1024]{1,0:T(8,128)(2,1)S(1)} %get-tuple-element.86), channel_id=1, source_target_pairs={{0,1},{1,2},{2,3},{3,0},{4,5},{5,6},{6,7},{7,4},{8,9},{9,10},{10,1... | collective-permute-start | bytes 393224 | tf_op jit(solution)/shard_map/ppermute | solution.py:397

commit v4 on v3

--- a/solution.py
+++ b/solution.py
@@ -474,30 +474,37 @@
     )
     later_sent = after(tuple(later_sent), other)
     later = [shift(later_sent[j], j) for j in others]
-    later_mine, later_other = later_partials(later, project, me)
-    total = add_two(after(mine, later_other, below), exchanged(other, 1))
+    early = [later[j] for j in [2] if j < count]
+    total = add_two(after(mine, below, *early), exchanged(other, 1))
     if moved is not None:
         blocks = join_pieces(after(blocks, total), moved)
     tops = [owner_to_first(blocks, run) for run in range(pipe // count)]
-    later_total = add_two(after(later_mine, total), exchanged(later_other, 1))
+    later_mine, later_other = later_partials(later, after(project, total), me)
     step = 2
     while step < count:
         received = exchanged(total, step)
-        total = add_two(after(total, later_total), received)
+        total = add_two(after(total, later_other), received)
         step *= 2
     halves = [total, exchanged(total, 1)]
-    step = 2
+    later_total = add_two(later_mine, exchanged(later_other, 1))
+    halves[0] = after(halves[0], later_total)
+    later_parts, step = [later_total], 2
     while step < count:
-        received = exchanged(later_total, step)
-        later_total = add_two(after(later_total, total), received)
+        later_parts = [later_total, exchanged(later_total, step)]
+        later_total = add_two(*later_parts)
         step *= 2
-    halves[0] = after(halves[0], later_total)
-    later_halves = [later_total, exchanged(later_total, 1)]
 
     first_grads = first_attention(halves, seq, half, head, ticks, width)
     passed, heads = middle_step(
-        [first_grads[0], first_grads[2]], pieces, tops, project, below, me, first
-    )
+        [after(first_grads[0], later_parts[-1]), first_grads[2]],
+        pieces,
+        tops,
+        project,
+        below,
+        me,
+        first,
+    )
+    later_halves = [later_total, exchanged(later_total, 1)]
     heads = [down(heads, j) for j in others[1:]]
     received = down(passed)
     later_grads = later_attention(

time: 101 us -> 97.1 us (0.961)
  waiting for transfers between devices: 50 us -> 40.9 us
  starting transfers between devices: 34.8 us -> 40.1 us
    ppermute x9, waiting for transfers between devices: 17.8 us -> 5.88 us  [shift(): lax.ppermute(value, 'dp', [(i, (i + steps) % count) for i in range(count)])]
    ppermute x2, waiting for transfers between devices: 15.3 us -> 18.8 us  [toward_owner(): return lax.ppermute(blocks, BOTH, pairs)]
    ppermute x6, starting transfers between devices: 5.32 us -> 8.16 us  [exchanged(): return lax.ppermute(value, 'dp', [(i, i ^ step) for i in range(count)])]
    ppermute x9, starting transfers between devices: 19.3 us -> 21.4 us  [shift(): lax.ppermute(value, 'dp', [(i, (i + steps) % count) for i in range(count)])]
    ppermute x6, waiting for transfers between devices: 12.1 us -> 10.2 us  [exchanged(): return lax.ppermute(value, 'dp', [(i, i ^ step) for i in range(count)])]
    ppermute x4, waiting for transfers between devices: 4.74 us -> 5.95 us  [down(): return lax.ppermute(value, BOTH, pairs)]
  transfers between devices with their start and end apart: 24 -> 24, of which waited for: 8 -> 9; matrix products, arithmetic and copies ran while one was open for 0% -> 0% of each run, Pallas kernels for 7% -> 7%
where the time goes in v4:
time: 97.1 us; the launch traced here: 96.8 us
  waiting for transfers between devices  40.9 us (42%)
  starting transfers between devices  40.1 us (41%)
  Pallas kernels  12.7 us (13%)
  local copies, waits for them, and re-layouts  2.34 us (2%)
    ppermute x9, starting transfers between devices, shift(): lax.ppermute(value, 'dp', [(i, (i + steps) % count) for i in range(count)])  21.4 us
    ppermute x2, waiting for transfers between devices, toward_owner(): return lax.ppermute(blocks, BOTH, pairs)  18.8 us
    pallas_call x16, Pallas kernels, kernel_call(): pl.pallas_call(body, out_shape=tuple(outs), in_specs=[pl.BlockSpec(memory...  12.7 us
    ppermute x6, waiting for transfers between devices, exchanged(): return lax.ppermute(value, 'dp', [(i, i ^ step) for i in range(count)])  10.2 us
    ppermute x6, starting transfers between devices, exchanged(): return lax.ppermute(value, 'dp', [(i, i ^ step) for i in range(count)])  8.16 us
    ppermute x4, waiting for transfers between devices, down(): return lax.ppermute(value, BOTH, pairs)  5.95 us
    ppermute x9, waiting for transfers between devices, shift(): lax.ppermute(value, 'dp', [(i, (i + steps) % count) for i in range(count)])  5.88 us
    ppermute x4, starting transfers between devices, down(): return lax.ppermute(value, BOTH, pairs)  5.19 us
  transfers between devices with their start and end apart: 24, of which 9 were waited for; matrix products, arithmetic and copies ran while one was open for 0% of the time, Pallas kernels for 7%

profile of v4, /device:TPU:0, one launch (start us, length us, event | category | flops | bytes accessed | tf_op | source)
XLA Modules:
  0.0 96.8 jit_solution(18286859580675801366)
XLA Ops:
  0.7 1.3 %copy-done.1 = bf16[1,2,64,4096]{3,2,1,0:T(8,128)(2,1)S(1)} copy-done((bf16[1,2,64,4096]{3,2,1,0:T(8,128)(2,1)S(1)}, bf16[1,2,64,4096]{3,2,1,0:T(8,128)(2,1)}, u32[]{:S(2)}) %copy-start.1) | copy-done | bytes 1048600
  1.9 1.0 %copy-done.2 = bf16[1,64,4096]{2,1,0:T(8,128)(2,1)S(1)} copy-done((bf16[1,64,4096]{2,1,0:T(8,128)(2,1)S(1)}, bf16[1,64,4096]{2,1,0:T(8,128)(2,1)}, u32[]{:S(2)}) %copy-start.2) | copy-done | bytes 524312
  3.0 0.4 shard_map.76
  3.4 3.1 %collective-permute-start = (bf16[2,64,1024]{2,1,0:T(8,128)(2,1)S(1)}, bf16[2,64,1024]{2,1,0:T(8,128)(2,1)S(1)}, u32[]{:S(2)}, u32[]{:S(2)}) collective-permute-start(bf16[2,64,1024]{2,1,0:T(8,128)(2,1)S(1)} %get-tuple-element.46), channel_id=1, source_target_pairs={{0,1},{1,2},{2,3},{3,0},{4,5},{5,6},{6,7},{7,4},{8,9},{9,10},{10,1... | collective-permute-start | bytes 786440 | tf_op jit(solution)/shard_map/ppermute | solution.py:397
  6.5 2.6 %collective-permute-start.1 = (bf16[2,64,1024]{2,1,0:T(8,128)(2,1)S(1)}, bf16[2,64,1024]{2,1,0:T(8,128)(2,1)S(1)}, u32[]{:S(2)}, u32[]{:S(2)}) collective-permute-start(bf16[2,64,1024]{2,1,0:T(8,128)(2,1)S(1)} %get-tuple-element.47), channel_id=1, source_target_pairs={{0,2},{1,3},{2,0},{3,1},{4,6},{5,7},{6,4},{7,5},{8,10},{9,11},{10,... | collective-permute-start | bytes 786440 | tf_op jit(solution)/shard_map/ppermute | solution.py:397
  9.1 1.3 %collective-permute-start.2 = (bf16[2,64,1024]{2,1,0:T(8,128)(2,1)S(1)}, bf16[2,64,1024]{2,1,0:T(8,128)(2,1)S(1)}, u32[]{:S(2)}, u32[]{:S(2)}) collective-permute-start(bf16[2,64,1024]{2,1,0:T(8,128)(2,1)S(1)} %get-tuple-element.48), channel_id=1, source_target_pairs={{0,3},{1,0},{2,1},{3,2},{4,7},{5,4},{6,5},{7,6},{8,11},{9,8},{10,9... | collective-permute-start | bytes 786440 | tf_op jit(solution)/shard_map/ppermute | solution.py:397
  10.4 1.3 %collective-permute-start.3 = (bf16[1,64,512]{2,1,0:T(8,128)(2,1)S(1)}, bf16[1,64,512]{2,1,0:T(8,128)(2,1)S(1)}, u32[]{:S(2)}, u32[]{:S(2)}) collective-permute-start(bf16[1,64,512]{2,1,0:T(8,128)(2,1)S(1)} %copy-done.4), channel_id=1, source_target_pairs={{1,0},{3,2},{5,4},{7,6},{8,9},{10,11},{12,13},{14,15},{17,16},{19,... | collective-permute-start | bytes 196616 | tf_op jit(solution)/shard_map/ppermute | solution.py:434
  11.7 0.4 shard_map.77
  12.1 15.3 %collective-permute-done.3.right_ref = bf16[1,64,512]{2,1,0:T(8,128)(2,1)S(1)} collective-permute-done((bf16[1,64,512]{2,1,0:T(8,128)(2,1)S(1)}, bf16[1,64,512]{2,1,0:T(8,128)(2,1)S(1)}, u32[]{:S(2)}, u32[]{:S(2)}) %collective-permute-start.3) | collective-permute-done | bytes 65568 | tf_op jit(solution)/shard_map/ppermute | solution.py:434
  27.5 0.0 collective-permute-done.1.refs_2_
  27.5 0.8 shard_map.79
  28.3 0.1 collective-permute-start.7
  28.4 3.8 %collective-permute-start.5 = (bf16[64,1024]{1,0:T(8,128)(2,1)S(1)}, bf16[64,1024]{1,0:T(8,128)(2,1)S(1)}, u32[]{:S(2)}, u32[]{:S(2)}) collective-permute-start(bf16[64,1024]{1,0:T(8,128)(2,1)S(1)} %get-tuple-element.60), channel_id=1, source_target_pairs={{0,2},{1,3},{2,0},{3,1},{4,6},{5,7},{6,4},{7,5},{8,10},{9,11},{10,... | collective-permute-start | bytes 393224 | tf_op jit(solution)/shard_map/ppermute | solution.py:397
  32.2 2.6 %collective-permute-start.8 = (bf16[144,512]{1,0:T(8,128)(2,1)S(1)}, bf16[144,512]{1,0:T(8,128)(2,1)S(1)}, u32[]{:S(2)}, u32[]{:S(2)}) collective-permute-start(bf16[144,512]{1,0:T(8,128)(2,1)S(1)} %get-tuple-element.57), channel_id=1, source_target_pairs={{0,1},{1,0},{2,3},{3,2},{4,5},{5,4},{6,7},{7,6},{8,9},{9,8},{10,11... | collective-permute-start | bytes 442376 | tf_op jit(solution)/shard_map/ppermute | solution.py:445
  34.8 1.3 %collective-permute-start.9 = (bf16[2,64,512]{2,1,0:T(8,128)(2,1)S(1)}, bf16[2,64,512]{2,1,0:T(8,128)(2,1)S(1)}, u32[]{:S(2)}, u32[]{:S(2)}) collective-permute-start(bf16[2,64,512]{2,1,0:T(8,128)(2,1)S(1)} %shard_map.78.left_ref), channel_id=1, source_target_pairs={{2,0},{6,4},{11,9},{15,13},{16,18},{20,22},{25,27},{29,31}} | collective-permute-start | bytes 393224 | tf_op jit(solution)/shard_map/ppermute | solution.py:434
  36.1 0.1 collective-permute-start.4
  36.2 7.1 %collective-permute-start.6 = (bf16[64,1024]{1,0:T(8,128)(2,1)S(1)}, bf16[64,1024]{1,0:T(8,128)(2,1)S(1)}, u32[]{:S(2)}, u32[]{:S(2)}) collective-permute-start(bf16[64,1024]{1,0:T(8,128)(2,1)S(1)} %get-tuple-element.61), channel_id=1, source_target_pairs={{0,3},{1,0},{2,1},{3,2},{4,7},{5,4},{6,5},{7,6},{8,11},{9,8},{10,9... | collective-permute-start | bytes 393224 | tf_op jit(solution)/shard_map/ppermute | solution.py:397
  43.3 0.1 collective-permute-start.12
  43.4 3.5 %collective-permute-done.9.right_ref = bf16[2,64,512]{2,1,0:T(8,128)(2,1)S(1)} collective-permute-done((bf16[2,64,512]{2,1,0:T(8,128)(2,1)S(1)}, bf16[2,64,512]{2,1,0:T(8,128)(2,1)S(1)}, u32[]{:S(2)}, u32[]{:S(2)}) %collective-permute-start.9) | collective-permute-done | bytes 131104 | tf_op jit(solution)/shard_map/ppermute | solution.py:434
  46.9 1.3 %collective-permute-start.11 = (bf16[4,64,512]{2,1,0:T(8,128)(2,1)S(1)}, bf16[4,64,512]{2,1,0:T(8,128)(2,1)S(1)}, u32[]{:S(2)}, u32[]{:S(2)}) collective-permute-start(bf16[4,64,512]{2,1,0:T(8,128)(2,1)S(1)} %shard_map.81), channel_id=1, source_target_pairs={{4,0},{13,1},{22,2},{31,3}} | collective-permute-start | bytes 786440 | tf_op jit(solution)/shard_map/ppermute | solution.py:440
  48.2 1.3 %collective-permute-start.10 = (bf16[4,64,512]{2,1,0:T(8,128)(2,1)S(1)}, bf16[4,64,512]{2,1,0:T(8,128)(2,1)}, u32[]{:S(2)}, u32[]{:S(2)}) collective-permute-start(bf16[4,64,512]{2,1,0:T(8,128)(2,1)S(1)} %shard_map.81), channel_id=1, source_target_pairs={{0,0},{9,1},{18,2},{27,3}} | collective-permute-start | bytes 786440 | tf_op jit(solution)/shard_map/ppermute | solution.py:440
  49.5 0.0 collective-permute-done.6.refs_3_.refs_7_
  49.6 0.6 shard_map.82
  50.2 3.8 %collective-permute-start.13 = (bf16[128,384]{1,0:T(8,128)(2,1)S(1)}, bf16[128,384]{1,0:T(8,128)(2,1)S(1)}, u32[]{:S(2)}, u32[]{:S(2)}) collective-permute-start(bf16[128,384]{1,0:T(8,128)(2,1)S(1)} %get-tuple-element.67), channel_id=1, source_target_pairs={{0,1},{1,0},{2,3},{3,2},{4,5},{5,4},{6,7},{7,6},{8,9},{9,8},{10,11... | collective-permute-start | bytes 294920 | tf_op jit(solution)/shard_map/ppermute | solution.py:445
  54.0 2.0 %collective-permute-done.12.right_ref = bf16[144,512]{1,0:T(8,128)(2,1)S(1)} collective-permute-done((bf16[144,512]{1,0:T(8,128)(2,1)S(1)}, bf16[144,512]{1,0:T(8,128)(2,1)S(1)}, u32[]{:S(2)}, u32[]{:S(2)}) %collective-permute-start.12) | collective-permute-done | bytes 147488 | tf_op jit(solution)/shard_map/ppermute | solution.py:445
  56.1 0.1 collective-permute-start.14
  56.1 1.9 %collective-permute-done.13.right_ref = bf16[128,384]{1,0:T(8,128)(2,1)S(1)} collective-permute-done((bf16[128,384]{1,0:T(8,128)(2,1)S(1)}, bf16[128,384]{1,0:T(8,128)(2,1)S(1)}, u32[]{:S(2)}, u32[]{:S(2)}) %collective-permute-start.13) | collective-permute-done | bytes 98336 | tf_op jit(solution)/shard_map/ppermute | solution.py:445
  58.1 0.1 collective-permute-start.15
  58.2 3.8 %collective-permute-done.14.refs_1_.refs_3_ = bf16[144,512]{1,0:T(8,128)(2,1)S(1)} collective-permute-done((bf16[144,512]{1,0:T(8,128)(2,1)S(1)}, bf16[144,512]{1,0:T(8,128)(2,1)S(1)}, u32[]{:S(2)}, u32[]{:S(2)}) %collective-permute-start.14) | collective-permute-done | bytes 147488 | tf_op jit(solution)/shard_map/ppermute | solution.py:445
  61.9 1.2 %shard_map.85 = (bf16[256,384]{1,0:T(8,128)(2,1)S(1)}, bf16[256,128]{1,0:T(8,128)(2,1)S(1)}, f32[256,128]{1,0:T(8,128)S(1)}) custom-call(bf16[144,512]{1,0:T(8,128)(2,1)S(1)} %shard_map.83.refs_0_.refs_2_, bf16[144,512]{1,0:T(8,128)(2,1)S(1)} %collective-permute-done.14.refs_1_.refs_3_), custom_call_target="tpu_custom_call" | custom-call | flops 1 | bytes 1 | tf_op jit(solution)/shard_map/pallas_call | solution.py:26
  63.1 2.6 %collective-permute-done.15.right_ref = bf16[128,384]{1,0:T(8,128)(2,1)} collective-permute-done((bf16[128,384]{1,0:T(8,128)(2,1)S(1)}, bf16[128,384]{1,0:T(8,128)(2,1)}, u32[]{:S(2)}, u32[]{:S(2)}) %collective-permute-start.15) | collective-permute-done | bytes 98336 | tf_op jit(solution)/shard_map/ppermute | solution.py:445
  65.7 1.3 %shard_map.86 = (bf16[4,64,1152]{2,1,0:T(8,128)(2,1)S(1)}, bf16[256,128]{1,0:T(8,128)(2,1)S(1)}) custom-call(s32[1]{0:T(128)} %bitcast.me_ref, s32[1]{0:T(128)} %bitcast.5.first_ref, bf16[2,64,1024]{2,1,0:T(8,128)(2,1)S(1)} %get-tuple-element.45.refs_0_, bf16[2,64,1024]{2,1,0:T(8,128)(2,1)S(1)} %collective-permute-done.refs_1_, ...), custom_call_target="tpu_custom_call" | custom-call | flops 1 | bytes 1 | tf_op jit(solution)/shard_map/pallas_call | solution.py:26
  67.0 0.1 collective-permute-start.16
  67.1 0.9 shard_map.87.refs_0_
  68.0 1.5 %collective-permute-start.17 = (bf16[128,384]{1,0:T(8,128)(2,1)S(1)}, bf16[128,384]{1,0:T(8,128)(2,1)S(1)}, u32[]{:S(2)}, u32[]{:S(2)}) collective-permute-start(bf16[128,384]{1,0:T(8,128)(2,1)S(1)} %shard_map.87.refs_0_), channel_id=1, source_target_pairs={{0,1},{1,0},{2,3},{3,2},{4,5},{5,4},{6,7},{7,6},{8,9},{9,8},{10,11... | collective-permute-start | bytes 294920 | tf_op jit(solution)/shard_map/ppermute | solution.py:445
  69.5 3.1 %collective-permute-start.20 = (bf16[256,128]{1,0:T(8,128)(2,1)S(1)}, bf16[256,128]{1,0:T(8,128)(2,1)S(1)}, u32[]{:S(2)}, u32[]{:S(2)}) collective-permute-start(bf16[256,128]{1,0:T(8,128)(2,1)S(1)} %get-tuple-element.76), channel_id=1, source_target_pairs={{0,31},{1,28},{2,29},{3,30},{4,3},{5,0},{6,1},{7,2},{8,7},{9,4},{1... | collective-permute-start | bytes 196616 | tf_op jit(solution)/shard_map/ppermute | solution.py:411
  72.6 0.2 collective-permute-start.19
  72.8 1.8 %collective-permute-start.18 = (bf16[256,128]{1,0:T(8,128)(2,1)S(1)}, bf16[256,128]{1,0:T(8,128)(2,1)S(1)}, u32[]{:S(2)}, u32[]{:S(2)}) collective-permute-start(bf16[256,128]{1,0:T(8,128)(2,1)S(1)} %get-tuple-element.76), channel_id=1, source_target_pairs={{0,29},{1,30},{2,31},{3,28},{4,1},{5,2},{6,3},{7,0},{8,5},{9,6},{1... | collective-permute-start | bytes 196616 | tf_op jit(solution)/shard_map/ppermute | solution.py:411
  74.7 0.4 collective-permute-done.20.refs_6_
  75.1 5.6 %collective-permute-done.19.refs_5_ = bf16[256,128]{1,0:T(8,128)(2,1)S(1)} collective-permute-done((bf16[256,128]{1,0:T(8,128)(2,1)S(1)}, bf16[256,128]{1,0:T(8,128)(2,1)S(1)}, u32[]{:S(2)}, u32[]{:S(2)}) %collective-permute-start.19) | collective-permute-done | bytes 65568 | tf_op jit(solution)/shard_map/ppermute | solution.py:411
  80.6 1.2 %shard_map.88 = (bf16[256,384]{1,0:T(8,128)(2,1)S(1)}, bf16[256,128]{1,0:T(8,128)(2,1)S(1)}, f32[256,128]{1,0:T(8,128)S(1)}) custom-call(s32[1]{0:T(128)} %bitcast.me_ref, bf16[128,384]{1,0:T(8,128)(2,1)S(1)} %shard_map.87.refs_0_, bf16[128,384]{1,0:T(8,128)(2,1)S(1)} %collective-permute-done.17.refs_1_, bf16[144,512]{1,0:T(8,128)(2,1)S(1)} %shard_map.83.refs_0_.refs_2_, ...), custom_call_target="tpu_custom_call" | custom-call | flops 1 | bytes 1 | tf_op jit(solution)/shard_map/pallas_call | solution.py:26
  81.8 1.2 %shard_map.89 = (bf16[64,1024]{1,0:T(8,128)(2,1)S(1)}, bf16[64,1024]{1,0:T(8,128)(2,1)S(1)}, bf16[64,1024]{1,0:T(8,128)(2,1)S(1)}, bf16[64,1024]{1,0:T(8,128)(2,1)S(1)}) custom-call(s32[1]{0:T(128)} %bitcast.me_ref, bf16[64,1024]{1,0:T(8,128)(2,1)S(1)} %get-tuple-element.58.refs_0_.refs_4_, bf16[64,1024]{1,0:T(8,128)(2,1)S(1)} %collective-permute-done.4.refs_1_.refs_5_, ...), custom_call_target="tpu_custom_call" | custom-call | flops 1 | bytes 1 | tf_op jit(solution)/shard_map/pallas_call | solution.py:26
  83.0 0.9 collective-permute-start.21
  83.9 0.6 collective-permute-start.22
  84.5 1.9 %collective-permute-start.23 = (bf16[64,1024]{1,0:T(8,128)(2,1)S(1)}, bf16[64,1024]{1,0:T(8,128)(2,1)S(1)}, u32[]{:S(2)}, u32[]{:S(2)}) collective-permute-start(bf16[64,1024]{1,0:T(8,128)(2,1)S(1)} %get-tuple-element.86), channel_id=1, source_target_pairs={{0,1},{1,2},{2,3},{3,0},{4,5},{5,6},{6,7},{7,4},{8,9},{9,10},{10,1... | collective-permute-start | bytes 393224 | tf_op jit(solution)/shard_map/ppermute | solution.py:397
  86.4 3.7 %shard_map.90 = (f32[1024,384]{1,0:T(8,128)}, f32[1024,128]{1,0:T(8,128)}) custom-call(s32[1]{0:T(128)} %bitcast.me_ref, bf16[2,64,1024]{2,1,0:T(8,128)(2,1)S(1)} %get-tuple-element.45.refs_0_, bf16[2,64,1024]{2,1,0:T(8,128)(2,1)S(1)} %collective-permute-done.refs_1_, bf16[2,64,1024]{2,1,0:T(8,128)(2,1)S(1)} %collective-permute-done.1.refs_2_, ...), custom_call_target="tpu_custom_call" | custom-call | flops 1 | bytes 1 | tf_op jit(solution)/shard_map/pallas_call | solution.py:26
  90.1 5.8 %collective-permute-done.22.refs_2_ = bf16[64,1024]{1,0:T(8,128)(2,1)S(1)} collective-permute-done((bf16[64,1024]{1,0:T(8,128)(2,1)S(1)}, bf16[64,1024]{1,0:T(8,128)(2,1)S(1)}, u32[]{:S(2)}, u32[]{:S(2)}) %collective-permute-start.22) | collective-permute-done | bytes 131104 | tf_op jit(solution)/shard_map/ppermute | solution.py:397
  96.0 0.8 shard_map.91
  (26 shorter events, 0.2 us)
Async XLA Ops:
  0.6 26.9 %copy-start = (bf16[1,1024,384]{2,1,0:T(8,128)(2,1)S(1)}, bf16[1,1024,384]{2,1,0:T(8,128)(2,1)}, u32[]{:S(2)}) copy-start(bf16[1,1024,384]{2,1,0:T(8,128)(2,1)} %param.8) | copy-start | bytes 2359300
  0.6 1.3 %copy-start.1 = (bf16[1,2,64,4096]{3,2,1,0:T(8,128)(2,1)S(1)}, bf16[1,2,64,4096]{3,2,1,0:T(8,128)(2,1)}, u32[]{:S(2)}) copy-start(bf16[1,2,64,4096]{3,2,1,0:T(8,128)(2,1)} %param.5) | copy-start | bytes 3145732
  1.9 1.0 %copy-start.2 = (bf16[1,64,4096]{2,1,0:T(8,128)(2,1)S(1)}, bf16[1,64,4096]{2,1,0:T(8,128)(2,1)}, u32[]{:S(2)}) copy-start(bf16[1,64,4096]{2,1,0:T(8,128)(2,1)} %param.6) | copy-start | bytes 1572868
  3.0 7.4 %copy-start.4 = (bf16[1,64,512]{2,1,0:T(8,128)(2,1)S(1)}, bf16[1,64,512]{2,1,0:T(8,128)(2,1)}, u32[]{:S(2)}) copy-start(bf16[1,64,512]{2,1,0:T(8,128)(2,1)} %left_ref) | copy-start | bytes 196612
  3.0 24.5 %copy-start.3 = (bf16[1,1024,128]{2,1,0:T(8,128)(2,1)S(1)}, bf16[1,1024,128]{2,1,0:T(8,128)(2,1)}, u32[]{:S(2)}) copy-start(bf16[1,1024,128]{2,1,0:T(8,128)(2,1)} %param.9) | copy-start | bytes 786436
  3.4 24.1 %collective-permute-start = (bf16[2,64,1024]{2,1,0:T(8,128)(2,1)S(1)}, bf16[2,64,1024]{2,1,0:T(8,128)(2,1)S(1)}, u32[]{:S(2)}, u32[]{:S(2)}) collective-permute-start(bf16[2,64,1024]{2,1,0:T(8,128)(2,1)S(1)} %get-tuple-element.46), channel_id=1, source_target_pairs={{0,1},{1,2},{2,3},{3,0},{4,5},{5,6},{6,7},{7,4},{8,9},{9,10},{10,1... | collective-permute-start | bytes 786440 | tf_op jit(solution)/shard_map/ppermute | solution.py:397
  6.5 21.0 %collective-permute-start.1 = (bf16[2,64,1024]{2,1,0:T(8,128)(2,1)S(1)}, bf16[2,64,1024]{2,1,0:T(8,128)(2,1)S(1)}, u32[]{:S(2)}, u32[]{:S(2)}) collective-permute-start(bf16[2,64,1024]{2,1,0:T(8,128)(2,1)S(1)} %get-tuple-element.47), channel_id=1, source_target_pairs={{0,2},{1,3},{2,0},{3,1},{4,6},{5,7},{6,4},{7,5},{8,10},{9,11},{10,... | collective-permute-start | bytes 786440 | tf_op jit(solution)/shard_map/ppermute | solution.py:397
  9.1 18.4 %collective-permute-start.2 = (bf16[2,64,1024]{2,1,0:T(8,128)(2,1)S(1)}, bf16[2,64,1024]{2,1,0:T(8,128)(2,1)S(1)}, u32[]{:S(2)}, u32[]{:S(2)}) collective-permute-start(bf16[2,64,1024]{2,1,0:T(8,128)(2,1)S(1)} %get-tuple-element.48), channel_id=1, source_target_pairs={{0,3},{1,0},{2,1},{3,2},{4,7},{5,4},{6,5},{7,6},{8,11},{9,8},{10,9... | collective-permute-start | bytes 786440 | tf_op jit(solution)/shard_map/ppermute | solution.py:397
  10.4 17.0 %collective-permute-start.3 = (bf16[1,64,512]{2,1,0:T(8,128)(2,1)S(1)}, bf16[1,64,512]{2,1,0:T(8,128)(2,1)S(1)}, u32[]{:S(2)}, u32[]{:S(2)}) collective-permute-start(bf16[1,64,512]{2,1,0:T(8,128)(2,1)S(1)} %copy-done.4), channel_id=1, source_target_pairs={{1,0},{3,2},{5,4},{7,6},{8,9},{10,11},{12,13},{14,15},{17,16},{19,... | collective-permute-start | bytes 196616 | tf_op jit(solution)/shard_map/ppermute | solution.py:434
  28.3 14.9 %collective-permute-start.7 = (bf16[1024,128]{1,0:T(8,128)(2,1)S(1)}, bf16[1024,128]{1,0:T(8,128)(2,1)S(1)}, u32[]{:S(2)}, u32[]{:S(2)}) collective-permute-start(bf16[1024,128]{1,0:T(8,128)(2,1)S(1)} %bitcast.17), channel_id=1, source_target_pairs={{0,4},{4,8},{8,12},{12,16},{16,20},{20,24},{24,28},{28,0},{1,5},{5... | collective-permute-start | bytes 786440 | tf_op jit(solution)/shard_map/ppermute | solution.py:472
  28.4 7.8 %collective-permute-start.5 = (bf16[64,1024]{1,0:T(8,128)(2,1)S(1)}, bf16[64,1024]{1,0:T(8,128)(2,1)S(1)}, u32[]{:S(2)}, u32[]{:S(2)}) collective-permute-start(bf16[64,1024]{1,0:T(8,128)(2,1)S(1)} %get-tuple-element.60), channel_id=1, source_target_pairs={{0,2},{1,3},{2,0},{3,1},{4,6},{5,7},{6,4},{7,5},{8,10},{9,11},{10,... | collective-permute-start | bytes 393224 | tf_op jit(solution)/shard_map/ppermute | solution.py:397
  32.2 11.0 %collective-permute-start.8 = (bf16[144,512]{1,0:T(8,128)(2,1)S(1)}, bf16[144,512]{1,0:T(8,128)(2,1)S(1)}, u32[]{:S(2)}, u32[]{:S(2)}) collective-permute-start(bf16[144,512]{1,0:T(8,128)(2,1)S(1)} %get-tuple-element.57), channel_id=1, source_target_pairs={{0,1},{1,0},{2,3},{3,2},{4,5},{5,4},{6,7},{7,6},{8,9},{9,8},{10,11... | collective-permute-start | bytes 442376 | tf_op jit(solution)/shard_map/ppermute | solution.py:445
  34.8 12.1 %collective-permute-start.9 = (bf16[2,64,512]{2,1,0:T(8,128)(2,1)S(1)}, bf16[2,64,512]{2,1,0:T(8,128)(2,1)S(1)}, u32[]{:S(2)}, u32[]{:S(2)}) collective-permute-start(bf16[2,64,512]{2,1,0:T(8,128)(2,1)S(1)} %shard_map.78.left_ref), channel_id=1, source_target_pairs={{2,0},{6,4},{11,9},{15,13},{16,18},{20,22},{25,27},{29,31}} | collective-permute-start | bytes 393224 | tf_op jit(solution)/shard_map/ppermute | solution.py:434
  36.1 13.4 %collective-permute-start.4 = (bf16[64,1024]{1,0:T(8,128)(2,1)S(1)}, bf16[64,1024]{1,0:T(8,128)(2,1)S(1)}, u32[]{:S(2)}, u32[]{:S(2)}) collective-permute-start(bf16[64,1024]{1,0:T(8,128)(2,1)S(1)} %get-tuple-element.59), channel_id=1, source_target_pairs={{0,1},{1,2},{2,3},{3,0},{4,5},{5,6},{6,7},{7,4},{8,9},{9,10},{10,1... | collective-permute-start | bytes 393224 | tf_op jit(solution)/shard_map/ppermute | solution.py:397
  36.2 13.4 %collective-permute-start.6 = (bf16[64,1024]{1,0:T(8,128)(2,1)S(1)}, bf16[64,1024]{1,0:T(8,128)(2,1)S(1)}, u32[]{:S(2)}, u32[]{:S(2)}) collective-permute-start(bf16[64,1024]{1,0:T(8,128)(2,1)S(1)} %get-tuple-element.61), channel_id=1, source_target_pairs={{0,3},{1,0},{2,1},{3,2},{4,7},{5,4},{6,5},{7,6},{8,11},{9,8},{10,9... | collective-permute-start | bytes 393224 | tf_op jit(solution)/shard_map/ppermute | solution.py:397
  43.3 12.7 %collective-permute-start.12 = (bf16[144,512]{1,0:T(8,128)(2,1)S(1)}, bf16[144,512]{1,0:T(8,128)(2,1)S(1)}, u32[]{:S(2)}, u32[]{:S(2)}) collective-permute-start(bf16[144,512]{1,0:T(8,128)(2,1)S(1)} %shard_map.80.left_ref), channel_id=1, source_target_pairs={{0,2},{1,3},{2,0},{3,1},{4,6},{5,7},{6,4},{7,5},{8,10},{9,11},{10,... | collective-permute-start | bytes 442376 | tf_op jit(solution)/shard_map/ppermute | solution.py:445
  46.9 18.8 %collective-permute-start.11 = (bf16[4,64,512]{2,1,0:T(8,128)(2,1)S(1)}, bf16[4,64,512]{2,1,0:T(8,128)(2,1)S(1)}, u32[]{:S(2)}, u32[]{:S(2)}) collective-permute-start(bf16[4,64,512]{2,1,0:T(8,128)(2,1)S(1)} %shard_map.81), channel_id=1, source_target_pairs={{4,0},{13,1},{22,2},{31,3}} | collective-permute-start | bytes 786440 | tf_op jit(solution)/shard_map/ppermute | solution.py:440
  48.2 17.5 %collective-permute-start.10 = (bf16[4,64,512]{2,1,0:T(8,128)(2,1)S(1)}, bf16[4,64,512]{2,1,0:T(8,128)(2,1)}, u32[]{:S(2)}, u32[]{:S(2)}) collective-permute-start(bf16[4,64,512]{2,1,0:T(8,128)(2,1)S(1)} %shard_map.81), channel_id=1, source_target_pairs={{0,0},{9,1},{18,2},{27,3}} | collective-permute-start | bytes 786440 | tf_op jit(solution)/shard_map/ppermute | solution.py:440
  50.2 7.8 %collective-permute-start.13 = (bf16[128,384]{1,0:T(8,128)(2,1)S(1)}, bf16[128,384]{1,0:T(8,128)(2,1)S(1)}, u32[]{:S(2)}, u32[]{:S(2)}) collective-permute-start(bf16[128,384]{1,0:T(8,128)(2,1)S(1)} %get-tuple-element.67), channel_id=1, source_target_pairs={{0,1},{1,0},{2,3},{3,2},{4,5},{5,4},{6,7},{7,6},{8,9},{9,8},{10,11... | collective-permute-start | bytes 294920 | tf_op jit(solution)/shard_map/ppermute | solution.py:445
  56.1 5.9 %collective-permute-start.14 = (bf16[144,512]{1,0:T(8,128)(2,1)S(1)}, bf16[144,512]{1,0:T(8,128)(2,1)S(1)}, u32[]{:S(2)}, u32[]{:S(2)}) collective-permute-start(bf16[144,512]{1,0:T(8,128)(2,1)S(1)} %shard_map.83.refs_0_.refs_2_), channel_id=1, source_target_pairs={{0,1},{1,0},{2,3},{3,2},{4,5},{5,4},{6,7},{7,6},{8,9},{9,8},{10,11... | collective-permute-start | bytes 442376 | tf_op jit(solution)/shard_map/ppermute | solution.py:445
  58.1 7.6 %collective-permute-start.15 = (bf16[128,384]{1,0:T(8,128)(2,1)S(1)}, bf16[128,384]{1,0:T(8,128)(2,1)}, u32[]{:S(2)}, u32[]{:S(2)}) collective-permute-start(bf16[128,384]{1,0:T(8,128)(2,1)S(1)} %shard_map.84.left_ref), channel_id=1, source_target_pairs={{0,2},{1,3},{2,0},{3,1},{4,6},{5,7},{6,4},{7,5},{8,10},{9,11},{10,... | collective-permute-start | bytes 294920 | tf_op jit(solution)/shard_map/ppermute | solution.py:445
  67.0 13.6 %collective-permute-start.16 = (bf16[4,64,1152]{2,1,0:T(8,128)(2,1)S(1)}, bf16[4,64,1152]{2,1,0:T(8,128)(2,1)S(1)}, u32[]{:S(2)}, u32[]{:S(2)}) collective-permute-start(bf16[4,64,1152]{2,1,0:T(8,128)(2,1)S(1)} %get-tuple-element.74), channel_id=1, source_target_pairs={{0,28},{1,29},{2,30},{3,31},{4,0},{5,1},{6,2},{7,3},{8,4},{9,5},{1... | collective-permute-start | bytes 1769480 | tf_op jit(solution)/shard_map/ppermute | solution.py:411
  68.0 6.7 %collective-permute-start.17 = (bf16[128,384]{1,0:T(8,128)(2,1)S(1)}, bf16[128,384]{1,0:T(8,128)(2,1)S(1)}, u32[]{:S(2)}, u32[]{:S(2)}) collective-permute-start(bf16[128,384]{1,0:T(8,128)(2,1)S(1)} %shard_map.87.refs_0_), channel_id=1, source_target_pairs={{0,1},{1,0},{2,3},{3,2},{4,5},{5,4},{6,7},{7,6},{8,9},{9,8},{10,11... | collective-permute-start | bytes 294920 | tf_op jit(solution)/shard_map/ppermute | solution.py:445
  69.5 5.5 %collective-permute-start.20 = (bf16[256,128]{1,0:T(8,128)(2,1)S(1)}, bf16[256,128]{1,0:T(8,128)(2,1)S(1)}, u32[]{:S(2)}, u32[]{:S(2)}) collective-permute-start(bf16[256,128]{1,0:T(8,128)(2,1)S(1)} %get-tuple-element.76), channel_id=1, source_target_pairs={{0,31},{1,28},{2,29},{3,30},{4,3},{5,0},{6,1},{7,2},{8,7},{9,4},{1... | collective-permute-start | bytes 196616 | tf_op jit(solution)/shard_map/ppermute | solution.py:411
  72.6 8.0 %collective-permute-start.19 = (bf16[256,128]{1,0:T(8,128)(2,1)S(1)}, bf16[256,128]{1,0:T(8,128)(2,1)S(1)}, u32[]{:S(2)}, u32[]{:S(2)}) collective-permute-start(bf16[256,128]{1,0:T(8,128)(2,1)S(1)} %get-tuple-element.76), channel_id=1, source_target_pairs={{0,30},{1,31},{2,28},{3,29},{4,2},{5,3},{6,0},{7,1},{8,6},{9,7},{1... | collective-permute-start | bytes 196616 | tf_op jit(solution)/shard_map/ppermute | solution.py:411
  72.8 7.8 %collective-permute-start.18 = (bf16[256,128]{1,0:T(8,128)(2,1)S(1)}, bf16[256,128]{1,0:T(8,128)(2,1)S(1)}, u32[]{:S(2)}, u32[]{:S(2)}) collective-permute-start(bf16[256,128]{1,0:T(8,128)(2,1)S(1)} %get-tuple-element.76), channel_id=1, source_target_pairs={{0,29},{1,30},{2,31},{3,28},{4,1},{5,2},{6,3},{7,0},{8,5},{9,6},{1... | collective-permute-start | bytes 196616 | tf_op jit(solution)/shard_map/ppermute | solution.py:411
  83.0 7.2 %collective-permute-start.21 = (bf16[64,1024]{1,0:T(8,128)(2,1)S(1)}, bf16[64,1024]{1,0:T(8,128)(2,1)S(1)}, u32[]{:S(2)}, u32[]{:S(2)}) collective-permute-start(bf16[64,1024]{1,0:T(8,128)(2,1)S(1)} %get-tuple-element.84), channel_id=1, source_target_pairs={{0,3},{1,0},{2,1},{3,2},{4,7},{5,4},{6,5},{7,6},{8,11},{9,8},{10,9... | collective-permute-start | bytes 393224 | tf_op jit(solution)/shard_map/ppermute | solution.py:397
  83.9 12.1 %collective-permute-start.22 = (bf16[64,1024]{1,0:T(8,128)(2,1)S(1)}, bf16[64,1024]{1,0:T(8,128)(2,1)S(1)}, u32[]{:S(2)}, u32[]{:S(2)}) collective-permute-start(bf16[64,1024]{1,0:T(8,128)(2,1)S(1)} %get-tuple-element.85), channel_id=1, source_target_pairs={{0,2},{1,3},{2,0},{3,1},{4,6},{5,7},{6,4},{7,5},{8,10},{9,11},{10,... | collective-permute-start | bytes 393224 | tf_op jit(solution)/shard_map/ppermute | solution.py:397
  84.5 11.5 %collective-permute-start.23 = (bf16[64,1024]{1,0:T(8,128)(2,1)S(1)}, bf16[64,1024]{1,0:T(8,128)(2,1)S(1)}, u32[]{:S(2)}, u32[]{:S(2)}) collective-permute-start(bf16[64,1024]{1,0:T(8,128)(2,1)S(1)} %get-tuple-element.86), channel_id=1, source_target_pairs={{0,1},{1,2},{2,3},{3,0},{4,5},{5,6},{6,7},{7,4},{8,9},{9,10},{10,1... | collective-permute-start | bytes 393224 | tf_op jit(solution)/shard_map/ppermute | solution.py:397

commit v5 on v4

--- a/solution.py
+++ b/solution.py
@@ -22,17 +22,18 @@
     return jax.ShapeDtypeStruct(dims, kind)
 
 
-def kernel_call(body, outs, scalars, arrays, scratch=()):
+def kernel_call(body, outs, scalars, arrays, scratch=(), far=(), cost=1):
     return pl.pallas_call(
         body,
         out_shape=tuple(outs),
         in_specs=[pl.BlockSpec(memory_space=pltpu.SMEM)] * len(scalars)
+        + [pl.BlockSpec(memory_space=pl.ANY)] * len(far)
         + [pl.BlockSpec(memory_space=pltpu.VMEM)] * len(arrays),
         out_specs=tuple(pl.BlockSpec(memory_space=pltpu.VMEM) for _ in outs),
         scratch_shapes=list(scratch),
         compiler_params=pltpu.CompilerParams(vmem_limit_bytes=24 * 1024 * 1024),
-        cost_estimate=pl.CostEstimate(flops=1, bytes_accessed=1, transcendentals=0),
-    )(*[s.reshape(1).astype(jnp.int32) for s in scalars], *arrays)
+        cost_estimate=pl.CostEstimate(flops=1, bytes_accessed=cost, transcendentals=0),
+    )(*[s.reshape(1).astype(jnp.int32) for s in scalars], *far, *arrays)
 
 
 def dot(left, right, contract=(((1,), (0,)), ((), ()))):
@@ -216,6 +217,7 @@
     slope = scale * (jnp.sum(spread * projected, axis=-1, keepdims=True) / width)
     lane = lax.broadcasted_iota(jnp.int32, (rows, LANES), 1)
     numbers_ref[...] = jnp.where(lane == 0, scale, jnp.where(lane == 1, offset, slope))
+    return proj_grad, offset, slope
 
 
 def all_rows(half_refs, seq, half, columns):
@@ -236,42 +238,96 @@
     return [shape(rows, 3 * head), shape(rows, head), shape(rows, LANES, kind=F32)]
 
 
-def first_attention(halves, seq, half, head, ticks, width):
-    rows, wide = 2 * half * seq, 3 * head
-
-    def body(*refs):
-        mine = refs[:2]
-        attention_back(
+def below_parts(pieces, project, below, me):
+    count, (_, seq, part) = len(pieces), pieces[0].shape
+    wide, head = project.shape[1], below.shape[1]
+
+    def body(me_ref, *refs):
+        piece_refs, refs = refs[:count], refs[count:]
+        project_ref, below_ref, rows_ref, product_ref, sums_ref = refs
+        below = below_ref[...]
+        for j in range(count):
+            rows = block_rows(me_ref, j, count, seq)
+            rows_ref[rows, :head] = dot(piece_refs[j][1], below)
+            rows_ref[rows, head:] = dot(piece_refs[j][0], below)
+        product_ref[...] = dot(project_ref[...], below, CONTRACT_FIRST).astype(BF16)
+        sums = jnp.sum(below.astype(F32), axis=0, keepdims=True)
+        sums_ref[...] = jnp.broadcast_to(sums, sums_ref.shape)
+
+    outs = [
+        shape(count * seq, 2 * head, kind=F32),
+        shape(wide, head),
+        shape(8, head, kind=F32),
+    ]
+    return kernel_call(body, outs, [me], [*pieces, project, below])
+
+
+def first_attention(halves, parts, tops, below, seq, half, head, ticks, me, first, width):
+    rows, wide, count, runs = 2 * half * seq, 3 * head, 2 * half, len(tops)
+    run = below.shape[0] // runs
+
+    def body(me_ref, first_ref, *refs):
+        mine, (rows_ref, product_ref, sums_ref), refs = refs[:2], refs[2:5], refs[5:]
+        top_refs, (below_ref, *outs, head_ref) = refs[:runs], refs[runs:]
+        scale = scale_column(mine, 0, ticks, seq, half)
+        proj_grad, offset, slope = attention_back(
             all_rows(mine, seq, half, slice(0, wide)),
             all_rows(mine, seq, half, slice(wide, wide + head)).astype(BF16),
-            refs[0][half * seq :, LANES:].astype(F32)[:1],
-            scale_column(mine, 0, ticks, seq, half),
+            mine[0][half * seq :, LANES:].astype(F32)[:1],
+            scale,
             seq,
-            refs[2:],
+            outs,
             width,
         )
-
-    return kernel_call(body, attention_outs(rows, head), [], halves)
-
-
-def later_attention(halves, facts, heads, received, seq, half, head, ticks, me, width):
-    rows, count = 2 * half * seq, 2 * half
-    part = received.shape[2] - head
-
-    def body(me_ref, *refs):
-        mine, facts, refs = refs[:2], refs[2:4], refs[4:]
-        head_refs, (received_ref, *outs) = refs[: len(heads)], refs[len(heads) :]
-        blocks = []
+        across = dot(proj_grad, product_ref[...])
+        change = scale * across - offset * sums_ref[:1, :] - slope * rows_ref[:, head:]
+        heads = (rows_ref[:, :head] + change).astype(BF16)
+        for parity in range(2):
+            for block in range(half):
+                replica = 2 * block + lax.rem(me_ref[0] + parity, 2)
+                start = (parity * half + block) * seq
+                place = pl.ds(pl.multiple_of(replica * seq, seq), seq)
+                head_ref[place, :] = heads[start : start + seq]
+
+        @pl.when(first_ref[0] == 1)
+        def _():
+            for block in range(count):
+                replica = lax.bitwise_xor(me_ref[0], block)
+                place = pl.ds(pl.multiple_of(replica * seq, seq), seq)
+                head_ref[place, :] = sum(
+                    dot(top_refs[a][block], below_ref[a * run : (a + 1) * run, :])
+                    for a in range(runs)
+                ).astype(BF16)
+
+    outs = [*attention_outs(rows, head), shape(rows, head)]
+    arrays = [*halves, *parts, *tops, below]
+    return kernel_call(body, outs, [me, first], arrays)
+
+
+def sum_heads(heads, seq, me):
+    rows, head = heads[0].shape
+    half = rows // seq // 2
+
+    def body(me_ref, *refs):
         for parity in range(2):
             for block in range(half):
                 replica = 2 * block + lax.rem(me_ref[0] + parity, 2)
                 place = pl.ds(pl.multiple_of(replica * seq, seq), seq)
-                total = sum(ref[place, :].astype(F32) for ref in head_refs)
-                piece = lax.rem(me_ref[0] + count - replica, count)
-                blocks.append(total + received_ref[piece, :, part:].astype(F32))
+                total = sum(ref[place, :].astype(F32) for ref in refs[:-1])
+                start = (parity * half + block) * seq
+                refs[-1][start : start + seq, :] = total.astype(BF16)
+
+    return kernel_call(body, [shape(rows, head)], [me], heads, cost=1)[0]
+
+
+def later_attention(halves, facts, head_half, seq, half, head, ticks, width):
+    rows = 2 * half * seq
+
+    def body(*refs):
+        mine, facts, (head_ref, *outs) = refs[:2], refs[2:4], refs[4:]
         attention_back(
             all_rows(mine, seq, half, slice(None)),
-            jnp.concatenate(blocks, axis=0).astype(BF16),
+            head_ref[...],
             facts[0][half * seq :, LANES:].astype(F32)[:1],
             scale_column(facts, 1, ticks, seq, half),
             seq,
@@ -279,8 +335,8 @@
             width,
         )
 
-    arrays = [*halves, *facts, *heads, received]
-    return kernel_call(body, attention_outs(rows, head), [me], arrays)
+    arrays = [*halves, *facts, head_half]
+    return kernel_call(body, attention_outs(rows, head), [], arrays, cost=1)
 
 
 def input_gradient(grad, numbers, incoming, hidden, project):
@@ -290,42 +346,43 @@
     return (incoming.astype(F32) + change).astype(BF16)
 
 
-def middle_step(grads, pieces, tops, project, below, me, first):
+def middle_step(grads, pieces, tops, project, me, first):
     count, (_, seq, part) = len(pieces), pieces[0].shape
-    head, runs = below.shape[1], len(tops)
+    runs = len(tops)
     run = part // runs
 
     def body(me_ref, first_ref, *refs):
-        refs = list(refs)
-        piece_refs = [refs.pop(0) for _ in range(count)]
-        top_refs = [refs.pop(0) for _ in range(runs)]
-        grad_ref, numbers_ref, project_ref, below_ref, passed_ref, head_ref = refs
+        top_refs, piece_refs, refs = refs[:runs], refs[runs : runs + count], refs[runs + count :]
+        grad_ref, numbers_ref, project_ref, passed_ref, sems = refs
         is_first = first_ref[0] == 1
 
         @pl.when(is_first)
         def _():
+            copies = []
             for j in range(count):
                 block = lax.bitwise_xor(me_ref[0], replica_of(me_ref, j, count))
                 for a in range(runs):
-                    passed_ref[j, :, a * run : (a + 1) * run] = top_refs[a][block]
+                    place = passed_ref.at[j, :, pl.ds(a * run, run)]
+                    copies.append(
+                        pltpu.make_async_copy(top_refs[a].at[block], place, sems.at[j, a])
+                    )
+                    copies[-1].start()
+            for copy in copies:
+                copy.wait()
 
         @pl.when(jnp.logical_not(is_first))
         def _():
             for j in range(count):
                 rows = block_rows(me_ref, j, count, seq)
                 hidden, incoming = piece_refs[j][0], piece_refs[j][1]
-                passed_ref[j, :, :part] = input_gradient(
+                passed_ref[j] = input_gradient(
                     grad_ref[rows, :], numbers_ref[rows, :], incoming, hidden, project_ref[...]
                 )
 
-        for j in range(count):
-            value = dot(passed_ref[j, :, :part], below_ref[...]).astype(BF16)
-            passed_ref[j, :, part:] = value
-            replica = replica_of(me_ref, j, count)
-            head_ref[pl.ds(pl.multiple_of(replica * seq, seq), seq), :] = value
-
-    outs = [shape(count, seq, part + head), shape(count * seq, head)]
-    return kernel_call(body, outs, [me, first], [*pieces, *tops, *grads, project, below])
+    scratch = [pltpu.SemaphoreType.DMA((count, runs))]
+    arrays = [*pieces, *grads, project]
+    outs = [shape(count, seq, part)]
+    return kernel_call(body, outs, [me, first], arrays, scratch, far=tops)[0]
 
 
 def last_step(grads, received, pieces, project, me):
@@ -341,7 +398,7 @@
             outs[j][...] = input_gradient(
                 grad_ref[rows, :],
                 numbers_ref[rows, :],
-                received_ref[j, :, :part],
+                received_ref[j],
                 piece_refs[j][...],
                 project_ref[...],
             )
@@ -480,6 +537,7 @@
         blocks = join_pieces(after(blocks, total), moved)
     tops = [owner_to_first(blocks, run) for run in range(pipe // count)]
     later_mine, later_other = later_partials(later, after(project, total), me)
+    parts = below_parts(pieces, project, below, me)
     step = 2
     while step < count:
         received = exchanged(total, step)
@@ -494,21 +552,16 @@
         later_total = add_two(*later_parts)
         step *= 2
 
-    first_grads = first_attention(halves, seq, half, head, ticks, width)
-    passed, heads = middle_step(
-        [after(first_grads[0], later_parts[-1]), first_grads[2]],
-        pieces,
-        tops,
-        project,
-        below,
-        me,
-        first,
-    )
+    *first_grads, heads = first_attention(
+        halves, parts, tops, below, seq, half, head, ticks, me, first, width
+    )
+    heads = [down(heads, j) for j in others]
     later_halves = [later_total, exchanged(later_total, 1)]
-    heads = [down(heads, j) for j in others[1:]]
-    received = down(passed)
+    passed = middle_step([first_grads[0], first_grads[2]], pieces, tops, project, me, first)
+    received = down(after(passed, later_parts[-1]))
+    head_half = sum_heads(heads, seq, me)
     later_grads = later_attention(
-        later_halves, halves, heads, received, seq, half, head, ticks, me, width
+        later_halves, halves, head_half, seq, half, head, ticks, width
     )
     back = last_step([later_grads[0], later_grads[2]], received, later, project, me)
     mixed = after(later_grads[1], back[0])

time: 97.1 us -> 95 us (0.978)
  starting transfers between devices: 40.1 us -> 37.4 us
    ppermute x6, starting transfers between devices: 8.16 us -> 5.77 us  [exchanged(): return lax.ppermute(value, 'dp', [(i, i ^ step) for i in range(count)])]
    ppermute x9, waiting for transfers between devices: 5.88 us -> 7.44 us  [shift(): lax.ppermute(value, 'dp', [(i, (i + steps) % count) for i in range(count)])]
    ppermute x6, waiting for transfers between devices: 10.2 us -> 8.77 us  [exchanged(): return lax.ppermute(value, 'dp', [(i, i ^ step) for i in range(count)])]
    ppermute x9, starting transfers between devices: 21.4 us -> 20.1 us  [shift(): lax.ppermute(value, 'dp', [(i, (i + steps) % count) for i in range(count)])]
    ppermute x4 -> x5, starting transfers between devices: 5.19 us -> 6.01 us  [down(): return lax.ppermute(value, BOTH, pairs)]
    pallas_call x16 -> x18, Pallas kernels: 12.7 us -> 13.3 us  [kernel_call(): pl.pallas_call(body, out_shape=tuple(outs), in_specs=[pl.BlockSpec(memory...]
    ppermute x4 -> x5, waiting for transfers between devices: 5.95 us -> 5.78 us  [down(): return lax.ppermute(value, BOTH, pairs)]
  transfers between devices with their start and end apart: 24 -> 25, of which waited for: 9 -> 10; matrix products, arithmetic and copies ran while one was open for 0% -> 0% of each run, Pallas kernels for 7% -> 11%
where the time goes in v5:
time: 95 us; the launch traced here: 94.8 us
  waiting for transfers between devices  40.8 us (43%)
  starting transfers between devices  37.4 us (39%)
  Pallas kernels  13.3 us (14%)
  local copies, waits for them, and re-layouts  2.34 us (2%)
    ppermute x9, starting transfers between devices, shift(): lax.ppermute(value, 'dp', [(i, (i + steps) % count) for i in range(count)])  20.1 us
    ppermute x2, waiting for transfers between devices, toward_owner(): return lax.ppermute(blocks, BOTH, pairs)  18.8 us
    pallas_call x18, Pallas kernels, kernel_call(): pl.pallas_call(body, out_shape=tuple(outs), in_specs=[pl.BlockSpec(memory...  13.3 us
    ppermute x6, waiting for transfers between devices, exchanged(): return lax.ppermute(value, 'dp', [(i, i ^ step) for i in range(count)])  8.77 us
    ppermute x9, waiting for transfers between devices, shift(): lax.ppermute(value, 'dp', [(i, (i + steps) % count) for i in range(count)])  7.44 us
    ppermute x5, starting transfers between devices, down(): return lax.ppermute(value, BOTH, pairs)  6.01 us
    ppermute x5, waiting for transfers between devices, down(): return lax.ppermute(value, BOTH, pairs)  5.78 us
    ppermute x6, starting transfers between devices, exchanged(): return lax.ppermute(value, 'dp', [(i, i ^ step) for i in range(count)])  5.77 us
  transfers between devices with their start and end apart: 25, of which 10 were waited for; matrix products, arithmetic and copies ran while one was open for 0% of the time, Pallas kernels for 11%

profile of v5, /device:TPU:0, one launch (start us, length us, event | category | flops | bytes accessed | tf_op | source)
XLA Modules:
  0.0 94.8 jit_solution(1210511224745307689)
XLA Ops:
  0.7 1.3 %copy-done.1 = bf16[1,2,64,4096]{3,2,1,0:T(8,128)(2,1)S(1)} copy-done((bf16[1,2,64,4096]{3,2,1,0:T(8,128)(2,1)S(1)}, bf16[1,2,64,4096]{3,2,1,0:T(8,128)(2,1)}, u32[]{:S(2)}) %copy-start.1) | copy-done | bytes 1048600
  1.9 1.0 %copy-done.2 = bf16[1,64,4096]{2,1,0:T(8,128)(2,1)S(1)} copy-done((bf16[1,64,4096]{2,1,0:T(8,128)(2,1)S(1)}, bf16[1,64,4096]{2,1,0:T(8,128)(2,1)}, u32[]{:S(2)}) %copy-start.2) | copy-done | bytes 524312
  3.0 0.4 shard_map.76
  3.4 3.1 %collective-permute-start = (bf16[2,64,1024]{2,1,0:T(8,128)(2,1)S(1)}, bf16[2,64,1024]{2,1,0:T(8,128)(2,1)S(1)}, u32[]{:S(2)}, u32[]{:S(2)}) collective-permute-start(bf16[2,64,1024]{2,1,0:T(8,128)(2,1)S(1)} %get-tuple-element.48), channel_id=1, source_target_pairs={{0,1},{1,2},{2,3},{3,0},{4,5},{5,6},{6,7},{7,4},{8,9},{9,10},{10,1... | collective-permute-start | bytes 786440 | tf_op jit(solution)/shard_map/ppermute | solution.py:454
  6.5 2.6 %collective-permute-start.1 = (bf16[2,64,1024]{2,1,0:T(8,128)(2,1)S(1)}, bf16[2,64,1024]{2,1,0:T(8,128)(2,1)S(1)}, u32[]{:S(2)}, u32[]{:S(2)}) collective-permute-start(bf16[2,64,1024]{2,1,0:T(8,128)(2,1)S(1)} %get-tuple-element.49), channel_id=1, source_target_pairs={{0,2},{1,3},{2,0},{3,1},{4,6},{5,7},{6,4},{7,5},{8,10},{9,11},{10,... | collective-permute-start | bytes 786440 | tf_op jit(solution)/shard_map/ppermute | solution.py:454
  9.1 1.3 %collective-permute-start.2 = (bf16[2,64,1024]{2,1,0:T(8,128)(2,1)S(1)}, bf16[2,64,1024]{2,1,0:T(8,128)(2,1)S(1)}, u32[]{:S(2)}, u32[]{:S(2)}) collective-permute-start(bf16[2,64,1024]{2,1,0:T(8,128)(2,1)S(1)} %get-tuple-element.50), channel_id=1, source_target_pairs={{0,3},{1,0},{2,1},{3,2},{4,7},{5,4},{6,5},{7,6},{8,11},{9,8},{10,9... | collective-permute-start | bytes 786440 | tf_op jit(solution)/shard_map/ppermute | solution.py:454
  10.4 1.3 %collective-permute-start.3 = (bf16[1,64,512]{2,1,0:T(8,128)(2,1)S(1)}, bf16[1,64,512]{2,1,0:T(8,128)(2,1)S(1)}, u32[]{:S(2)}, u32[]{:S(2)}) collective-permute-start(bf16[1,64,512]{2,1,0:T(8,128)(2,1)S(1)} %copy-done.4), channel_id=1, source_target_pairs={{1,0},{3,2},{5,4},{7,6},{8,9},{10,11},{12,13},{14,15},{17,16},{19,... | collective-permute-start | bytes 196616 | tf_op jit(solution)/shard_map/ppermute | solution.py:491
  11.7 0.4 shard_map.77
  12.1 15.3 %collective-permute-done.3.right_ref = bf16[1,64,512]{2,1,0:T(8,128)(2,1)S(1)} collective-permute-done((bf16[1,64,512]{2,1,0:T(8,128)(2,1)S(1)}, bf16[1,64,512]{2,1,0:T(8,128)(2,1)S(1)}, u32[]{:S(2)}, u32[]{:S(2)}) %collective-permute-start.3) | collective-permute-done | bytes 65568 | tf_op jit(solution)/shard_map/ppermute | solution.py:491
  27.5 0.8 shard_map.79
  28.3 0.1 collective-permute-start.7
  28.4 3.8 %collective-permute-start.5 = (bf16[64,1024]{1,0:T(8,128)(2,1)S(1)}, bf16[64,1024]{1,0:T(8,128)(2,1)S(1)}, u32[]{:S(2)}, u32[]{:S(2)}) collective-permute-start(bf16[64,1024]{1,0:T(8,128)(2,1)S(1)} %get-tuple-element.62), channel_id=1, source_target_pairs={{0,2},{1,3},{2,0},{3,1},{4,6},{5,7},{6,4},{7,5},{8,10},{9,11},{10,... | collective-permute-start | bytes 393224 | tf_op jit(solution)/shard_map/ppermute | solution.py:454
  32.2 2.6 %collective-permute-start.8 = (bf16[144,512]{1,0:T(8,128)(2,1)S(1)}, bf16[144,512]{1,0:T(8,128)(2,1)S(1)}, u32[]{:S(2)}, u32[]{:S(2)}) collective-permute-start(bf16[144,512]{1,0:T(8,128)(2,1)S(1)} %get-tuple-element.59), channel_id=1, source_target_pairs={{0,1},{1,0},{2,3},{3,2},{4,5},{5,4},{6,7},{7,6},{8,9},{9,8},{10,11... | collective-permute-start | bytes 442376 | tf_op jit(solution)/shard_map/ppermute | solution.py:502
  34.8 1.3 %collective-permute-start.9 = (bf16[2,64,512]{2,1,0:T(8,128)(2,1)S(1)}, bf16[2,64,512]{2,1,0:T(8,128)(2,1)S(1)}, u32[]{:S(2)}, u32[]{:S(2)}) collective-permute-start(bf16[2,64,512]{2,1,0:T(8,128)(2,1)S(1)} %shard_map.78.left_ref), channel_id=1, source_target_pairs={{2,0},{6,4},{11,9},{15,13},{16,18},{20,22},{25,27},{29,31}} | collective-permute-start | bytes 393224 | tf_op jit(solution)/shard_map/ppermute | solution.py:491
  36.1 0.1 collective-permute-start.4
  36.2 7.1 %collective-permute-start.6 = (bf16[64,1024]{1,0:T(8,128)(2,1)S(1)}, bf16[64,1024]{1,0:T(8,128)(2,1)S(1)}, u32[]{:S(2)}, u32[]{:S(2)}) collective-permute-start(bf16[64,1024]{1,0:T(8,128)(2,1)S(1)} %get-tuple-element.63), channel_id=1, source_target_pairs={{0,3},{1,0},{2,1},{3,2},{4,7},{5,4},{6,5},{7,6},{8,11},{9,8},{10,9... | collective-permute-start | bytes 393224 | tf_op jit(solution)/shard_map/ppermute | solution.py:454
  43.3 0.1 collective-permute-start.12
  43.4 3.5 %collective-permute-done.9.right_ref = bf16[2,64,512]{2,1,0:T(8,128)(2,1)S(1)} collective-permute-done((bf16[2,64,512]{2,1,0:T(8,128)(2,1)S(1)}, bf16[2,64,512]{2,1,0:T(8,128)(2,1)S(1)}, u32[]{:S(2)}, u32[]{:S(2)}) %collective-permute-start.9) | collective-permute-done | bytes 131104 | tf_op jit(solution)/shard_map/ppermute | solution.py:491
  46.9 0.7 shard_map.81
  47.6 1.3 %collective-permute-start.11 = (bf16[4,64,512]{2,1,0:T(8,128)(2,1)}, bf16[4,64,512]{2,1,0:T(8,128)(2,1)S(1)}, u32[]{:S(2)}, u32[]{:S(2)}) collective-permute-start(bf16[4,64,512]{2,1,0:T(8,128)(2,1)} %shard_map.81), channel_id=1, source_target_pairs={{4,0},{13,1},{22,2},{31,3}} | collective-permute-start | bytes 786440 | tf_op jit(solution)/shard_map/ppermute | solution.py:497
  48.9 1.6 %collective-permute-start.10 = (bf16[4,64,512]{2,1,0:T(8,128)(2,1)}, bf16[4,64,512]{2,1,0:T(8,128)(2,1)S(1)}, u32[]{:S(2)}, u32[]{:S(2)}) collective-permute-start(bf16[4,64,512]{2,1,0:T(8,128)(2,1)} %shard_map.81), channel_id=1, source_target_pairs={{0,0},{9,1},{18,2},{27,3}} | collective-permute-start | bytes 786440 | tf_op jit(solution)/shard_map/ppermute | solution.py:497
  50.5 0.6 shard_map.82
  51.1 2.9 %collective-permute-start.13 = (bf16[128,384]{1,0:T(8,128)(2,1)S(1)}, bf16[128,384]{1,0:T(8,128)(2,1)S(1)}, u32[]{:S(2)}, u32[]{:S(2)}) collective-permute-start(bf16[128,384]{1,0:T(8,128)(2,1)S(1)} %get-tuple-element.69), channel_id=1, source_target_pairs={{0,1},{1,0},{2,3},{3,2},{4,5},{5,4},{6,7},{7,6},{8,9},{9,8},{10,11... | collective-permute-start | bytes 294920 | tf_op jit(solution)/shard_map/ppermute | solution.py:502
  54.0 2.0 %collective-permute-done.12.right_ref = bf16[144,512]{1,0:T(8,128)(2,1)S(1)} collective-permute-done((bf16[144,512]{1,0:T(8,128)(2,1)S(1)}, bf16[144,512]{1,0:T(8,128)(2,1)S(1)}, u32[]{:S(2)}, u32[]{:S(2)}) %collective-permute-start.12) | collective-permute-done | bytes 147488 | tf_op jit(solution)/shard_map/ppermute | solution.py:502
  56.1 0.1 collective-permute-start.14
  56.2 1.9 %collective-permute-done.13.right_ref = bf16[128,384]{1,0:T(8,128)(2,1)S(1)} collective-permute-done((bf16[128,384]{1,0:T(8,128)(2,1)S(1)}, bf16[128,384]{1,0:T(8,128)(2,1)S(1)}, u32[]{:S(2)}, u32[]{:S(2)}) %collective-permute-start.13) | collective-permute-done | bytes 98336 | tf_op jit(solution)/shard_map/ppermute | solution.py:502
  58.1 0.1 collective-permute-start.15
  58.2 0.7 shard_map.85
  58.9 3.1 %collective-permute-done.14.refs_1_.refs_3_ = bf16[144,512]{1,0:T(8,128)(2,1)S(1)} collective-permute-done((bf16[144,512]{1,0:T(8,128)(2,1)S(1)}, bf16[144,512]{1,0:T(8,128)(2,1)S(1)}, u32[]{:S(2)}, u32[]{:S(2)}) %collective-permute-start.14) | collective-permute-done | bytes 147488 | tf_op jit(solution)/shard_map/ppermute | solution.py:502
  61.9 1.5 %shard_map.86 = (bf16[256,384]{1,0:T(8,128)(2,1)S(1)}, bf16[256,128]{1,0:T(8,128)(2,1)S(1)}, f32[256,128]{1,0:T(8,128)S(1)}, bf16[256,128]{1,0:T(8,128)(2,1)S(1)}) custom-call(s32[1]{0:T(128)} %bitcast.me_ref, s32[1]{0:T(128)} %bitcast.5.first_ref, bf16[144,512]{1,0:T(8,128)(2,1)S(1)} %shard_map.83.refs_0_.refs_2_, ...), custom_call_target="tpu_custom_call" | custom-call | flops 1 | bytes 1 | tf_op jit(solution)/shard_map/pallas_call | solution.py:26
  63.4 0.2 shard_map.87
  63.7 1.8 %collective-permute-done.15.right_ref = bf16[128,384]{1,0:T(8,128)(2,1)} collective-permute-done((bf16[128,384]{1,0:T(8,128)(2,1)S(1)}, bf16[128,384]{1,0:T(8,128)(2,1)}, u32[]{:S(2)}, u32[]{:S(2)}) %collective-permute-start.15) | collective-permute-done | bytes 98336 | tf_op jit(solution)/shard_map/ppermute | solution.py:502
  65.5 3.6 %collective-permute-start.21 = (bf16[256,128]{1,0:T(8,128)(2,1)S(1)}, bf16[256,128]{1,0:T(8,128)(2,1)S(1)}, u32[]{:S(2)}, u32[]{:S(2)}) collective-permute-start(bf16[256,128]{1,0:T(8,128)(2,1)S(1)} %get-tuple-element.80), channel_id=1, source_target_pairs={{0,31},{1,28},{2,29},{3,30},{4,3},{5,0},{6,1},{7,2},{8,7},{9,4},{1... | collective-permute-start | bytes 196616 | tf_op jit(solution)/shard_map/ppermute | solution.py:468
  69.1 0.9 shard_map.88.refs_0_
  70.0 0.1 collective-permute-start.17
  70.1 0.3 collective-permute-start.20
  70.4 1.1 %collective-permute-start.19 = (bf16[256,128]{1,0:T(8,128)(2,1)S(1)}, bf16[256,128]{1,0:T(8,128)(2,1)S(1)}, u32[]{:S(2)}, u32[]{:S(2)}) collective-permute-start(bf16[256,128]{1,0:T(8,128)(2,1)S(1)} %get-tuple-element.80), channel_id=1, source_target_pairs={{0,29},{1,30},{2,31},{3,28},{4,1},{5,2},{6,3},{7,0},{8,5},{9,6},{1... | collective-permute-start | bytes 196616 | tf_op jit(solution)/shard_map/ppermute | solution.py:468
  71.5 1.0 %collective-permute-start.18 = (bf16[256,128]{1,0:T(8,128)(2,1)S(1)}, bf16[256,128]{1,0:T(8,128)(2,1)S(1)}, u32[]{:S(2)}, u32[]{:S(2)}) collective-permute-start(bf16[256,128]{1,0:T(8,128)(2,1)S(1)} %get-tuple-element.80), channel_id=1, source_target_pairs={{0,28},{1,29},{2,30},{3,31},{4,0},{5,1},{6,2},{7,3},{8,4},{9,5},{1... | collective-permute-start | bytes 196616 | tf_op jit(solution)/shard_map/ppermute | solution.py:468
  72.5 2.9 %collective-permute-done.20.refs_2_ = bf16[256,128]{1,0:T(8,128)(2,1)S(1)} collective-permute-done((bf16[256,128]{1,0:T(8,128)(2,1)S(1)}, bf16[256,128]{1,0:T(8,128)(2,1)S(1)}, u32[]{:S(2)}, u32[]{:S(2)}) %collective-permute-start.20) | collective-permute-done | bytes 65568 | tf_op jit(solution)/shard_map/ppermute | solution.py:468
  75.4 2.9 %collective-permute-done.19.refs_1_ = bf16[256,128]{1,0:T(8,128)(2,1)S(1)} collective-permute-done((bf16[256,128]{1,0:T(8,128)(2,1)S(1)}, bf16[256,128]{1,0:T(8,128)(2,1)S(1)}, u32[]{:S(2)}, u32[]{:S(2)}) %collective-permute-start.19) | collective-permute-done | bytes 65568 | tf_op jit(solution)/shard_map/ppermute | solution.py:468
  78.3 1.2 %shard_map.90 = (bf16[256,384]{1,0:T(8,128)(2,1)S(1)}, bf16[256,128]{1,0:T(8,128)(2,1)S(1)}, f32[256,128]{1,0:T(8,128)S(1)}) custom-call(bf16[128,384]{1,0:T(8,128)(2,1)S(1)} %shard_map.88.refs_0_, bf16[128,384]{1,0:T(8,128)(2,1)S(1)} %collective-permute-done.17.refs_1_, bf16[144,512]{1,0:T(8,128)(2,1)S(1)} %shard_map.83.refs_0_.refs_2_, ...), custom_call_target="tpu_custom_call" | custom-call | flops 1 | bytes 1 | tf_op jit(solution)/shard_map/pallas_call | solution.py:26
  79.5 1.1 %shard_map.91 = (bf16[64,1024]{1,0:T(8,128)(2,1)S(1)}, bf16[64,1024]{1,0:T(8,128)(2,1)S(1)}, bf16[64,1024]{1,0:T(8,128)(2,1)S(1)}, bf16[64,1024]{1,0:T(8,128)(2,1)S(1)}) custom-call(s32[1]{0:T(128)} %bitcast.me_ref, bf16[64,1024]{1,0:T(8,128)(2,1)S(1)} %get-tuple-element.60.refs_0_.refs_4_, bf16[64,1024]{1,0:T(8,128)(2,1)S(1)} %collective-permute-done.4.refs_1_.refs_5_, ...), custom_call_target="tpu_custom_call" | custom-call | flops 1 | bytes 1 | tf_op jit(solution)/shard_map/pallas_call | solution.py:26
  80.7 1.1 %collective-permute-start.22 = (bf16[64,1024]{1,0:T(8,128)(2,1)S(1)}, bf16[64,1024]{1,0:T(8,128)(2,1)S(1)}, u32[]{:S(2)}, u32[]{:S(2)}) collective-permute-start(bf16[64,1024]{1,0:T(8,128)(2,1)S(1)} %get-tuple-element.88), channel_id=1, source_target_pairs={{0,3},{1,0},{2,1},{3,2},{4,7},{5,4},{6,5},{7,6},{8,11},{9,8},{10,9... | collective-permute-start | bytes 393224 | tf_op jit(solution)/shard_map/ppermute | solution.py:454
  81.8 1.0 %collective-permute-start.24 = (bf16[64,1024]{1,0:T(8,128)(2,1)S(1)}, bf16[64,1024]{1,0:T(8,128)(2,1)S(1)}, u32[]{:S(2)}, u32[]{:S(2)}) collective-permute-start(bf16[64,1024]{1,0:T(8,128)(2,1)S(1)} %get-tuple-element.90), channel_id=1, source_target_pairs={{0,1},{1,2},{2,3},{3,0},{4,5},{5,6},{6,7},{7,4},{8,9},{9,10},{10,1... | collective-permute-start | bytes 393224 | tf_op jit(solution)/shard_map/ppermute | solution.py:454
  82.8 3.7 %shard_map.92 = (f32[1024,384]{1,0:T(8,128)}, f32[1024,128]{1,0:T(8,128)}) custom-call(s32[1]{0:T(128)} %bitcast.me_ref, bf16[2,64,1024]{2,1,0:T(8,128)(2,1)S(1)} %get-tuple-element.47.refs_0_.refs_2_, bf16[2,64,1024]{2,1,0:T(8,128)(2,1)S(1)} %collective-permute-done.refs_1_.refs_3_, bf16[2,64,1024]{2,1,0:T(8,128)(2,1)S(1)} %collective-permute-done.1.refs_2_.refs_4_, ...), custom_call_target="tpu_custom_call" | custom-call | flops 1 | bytes 1 | tf_op jit(solution)/shard_map/pallas_call | solution.py:26
  86.5 0.5 collective-permute-done.22.refs_1_
  87.0 7.0 %collective-permute-done.23.refs_2_ = bf16[64,1024]{1,0:T(8,128)(2,1)S(1)} collective-permute-done((bf16[64,1024]{1,0:T(8,128)(2,1)S(1)}, bf16[64,1024]{1,0:T(8,128)(2,1)S(1)}, u32[]{:S(2)}, u32[]{:S(2)}) %collective-permute-start.23) | collective-permute-done | bytes 131104 | tf_op jit(solution)/shard_map/ppermute | solution.py:454
  93.9 0.8 shard_map.93
  (30 shorter events, 0.2 us)
Async XLA Ops:
  0.6 26.9 %copy-start = (bf16[1,1024,384]{2,1,0:T(8,128)(2,1)S(1)}, bf16[1,1024,384]{2,1,0:T(8,128)(2,1)}, u32[]{:S(2)}) copy-start(bf16[1,1024,384]{2,1,0:T(8,128)(2,1)} %param.8) | copy-start | bytes 2359300
  0.6 1.3 %copy-start.1 = (bf16[1,2,64,4096]{3,2,1,0:T(8,128)(2,1)S(1)}, bf16[1,2,64,4096]{3,2,1,0:T(8,128)(2,1)}, u32[]{:S(2)}) copy-start(bf16[1,2,64,4096]{3,2,1,0:T(8,128)(2,1)} %param.5) | copy-start | bytes 3145732
  1.9 1.0 %copy-start.2 = (bf16[1,64,4096]{2,1,0:T(8,128)(2,1)S(1)}, bf16[1,64,4096]{2,1,0:T(8,128)(2,1)}, u32[]{:S(2)}) copy-start(bf16[1,64,4096]{2,1,0:T(8,128)(2,1)} %param.6) | copy-start | bytes 1572868
  3.0 7.4 %copy-start.4 = (bf16[1,64,512]{2,1,0:T(8,128)(2,1)S(1)}, bf16[1,64,512]{2,1,0:T(8,128)(2,1)}, u32[]{:S(2)}) copy-start(bf16[1,64,512]{2,1,0:T(8,128)(2,1)} %left_ref) | copy-start | bytes 196612
  3.0 24.5 %copy-start.3 = (bf16[1,1024,128]{2,1,0:T(8,128)(2,1)S(1)}, bf16[1,1024,128]{2,1,0:T(8,128)(2,1)}, u32[]{:S(2)}) copy-start(bf16[1,1024,128]{2,1,0:T(8,128)(2,1)} %param.9) | copy-start | bytes 786436
  3.4 24.1 %collective-permute-start = (bf16[2,64,1024]{2,1,0:T(8,128)(2,1)S(1)}, bf16[2,64,1024]{2,1,0:T(8,128)(2,1)S(1)}, u32[]{:S(2)}, u32[]{:S(2)}) collective-permute-start(bf16[2,64,1024]{2,1,0:T(8,128)(2,1)S(1)} %get-tuple-element.48), channel_id=1, source_target_pairs={{0,1},{1,2},{2,3},{3,0},{4,5},{5,6},{6,7},{7,4},{8,9},{9,10},{10,1... | collective-permute-start | bytes 786440 | tf_op jit(solution)/shard_map/ppermute | solution.py:454
  6.5 21.0 %collective-permute-start.1 = (bf16[2,64,1024]{2,1,0:T(8,128)(2,1)S(1)}, bf16[2,64,1024]{2,1,0:T(8,128)(2,1)S(1)}, u32[]{:S(2)}, u32[]{:S(2)}) collective-permute-start(bf16[2,64,1024]{2,1,0:T(8,128)(2,1)S(1)} %get-tuple-element.49), channel_id=1, source_target_pairs={{0,2},{1,3},{2,0},{3,1},{4,6},{5,7},{6,4},{7,5},{8,10},{9,11},{10,... | collective-permute-start | bytes 786440 | tf_op jit(solution)/shard_map/ppermute | solution.py:454
  9.1 18.4 %collective-permute-start.2 = (bf16[2,64,1024]{2,1,0:T(8,128)(2,1)S(1)}, bf16[2,64,1024]{2,1,0:T(8,128)(2,1)S(1)}, u32[]{:S(2)}, u32[]{:S(2)}) collective-permute-start(bf16[2,64,1024]{2,1,0:T(8,128)(2,1)S(1)} %get-tuple-element.50), channel_id=1, source_target_pairs={{0,3},{1,0},{2,1},{3,2},{4,7},{5,4},{6,5},{7,6},{8,11},{9,8},{10,9... | collective-permute-start | bytes 786440 | tf_op jit(solution)/shard_map/ppermute | solution.py:454
  10.4 17.0 %collective-permute-start.3 = (bf16[1,64,512]{2,1,0:T(8,128)(2,1)S(1)}, bf16[1,64,512]{2,1,0:T(8,128)(2,1)S(1)}, u32[]{:S(2)}, u32[]{:S(2)}) collective-permute-start(bf16[1,64,512]{2,1,0:T(8,128)(2,1)S(1)} %copy-done.4), channel_id=1, source_target_pairs={{1,0},{3,2},{5,4},{7,6},{8,9},{10,11},{12,13},{14,15},{17,16},{19,... | collective-permute-start | bytes 196616 | tf_op jit(solution)/shard_map/ppermute | solution.py:491
  28.3 14.9 %collective-permute-start.7 = (bf16[1024,128]{1,0:T(8,128)(2,1)S(1)}, bf16[1024,128]{1,0:T(8,128)(2,1)S(1)}, u32[]{:S(2)}, u32[]{:S(2)}) collective-permute-start(bf16[1024,128]{1,0:T(8,128)(2,1)S(1)} %bitcast.18), channel_id=1, source_target_pairs={{0,4},{4,8},{8,12},{12,16},{16,20},{20,24},{24,28},{28,0},{1,5},{5... | collective-permute-start | bytes 786440 | tf_op jit(solution)/shard_map/ppermute | solution.py:529
  28.4 7.8 %collective-permute-start.5 = (bf16[64,1024]{1,0:T(8,128)(2,1)S(1)}, bf16[64,1024]{1,0:T(8,128)(2,1)S(1)}, u32[]{:S(2)}, u32[]{:S(2)}) collective-permute-start(bf16[64,1024]{1,0:T(8,128)(2,1)S(1)} %get-tuple-element.62), channel_id=1, source_target_pairs={{0,2},{1,3},{2,0},{3,1},{4,6},{5,7},{6,4},{7,5},{8,10},{9,11},{10,... | collective-permute-start | bytes 393224 | tf_op jit(solution)/shard_map/ppermute | solution.py:454
  32.2 11.0 %collective-permute-start.8 = (bf16[144,512]{1,0:T(8,128)(2,1)S(1)}, bf16[144,512]{1,0:T(8,128)(2,1)S(1)}, u32[]{:S(2)}, u32[]{:S(2)}) collective-permute-start(bf16[144,512]{1,0:T(8,128)(2,1)S(1)} %get-tuple-element.59), channel_id=1, source_target_pairs={{0,1},{1,0},{2,3},{3,2},{4,5},{5,4},{6,7},{7,6},{8,9},{9,8},{10,11... | collective-permute-start | bytes 442376 | tf_op jit(solution)/shard_map/ppermute | solution.py:502
  34.8 12.1 %collective-permute-start.9 = (bf16[2,64,512]{2,1,0:T(8,128)(2,1)S(1)}, bf16[2,64,512]{2,1,0:T(8,128)(2,1)S(1)}, u32[]{:S(2)}, u32[]{:S(2)}) collective-permute-start(bf16[2,64,512]{2,1,0:T(8,128)(2,1)S(1)} %shard_map.78.left_ref), channel_id=1, source_target_pairs={{2,0},{6,4},{11,9},{15,13},{16,18},{20,22},{25,27},{29,31}} | collective-permute-start | bytes 393224 | tf_op jit(solution)/shard_map/ppermute | solution.py:491
  36.1 14.4 %collective-permute-start.4 = (bf16[64,1024]{1,0:T(8,128)(2,1)S(1)}, bf16[64,1024]{1,0:T(8,128)(2,1)S(1)}, u32[]{:S(2)}, u32[]{:S(2)}) collective-permute-start(bf16[64,1024]{1,0:T(8,128)(2,1)S(1)} %get-tuple-element.61), channel_id=1, source_target_pairs={{0,1},{1,2},{2,3},{3,0},{4,5},{5,6},{6,7},{7,4},{8,9},{9,10},{10,1... | collective-permute-start | bytes 393224 | tf_op jit(solution)/shard_map/ppermute | solution.py:454
  36.2 14.3 %collective-permute-start.6 = (bf16[64,1024]{1,0:T(8,128)(2,1)S(1)}, bf16[64,1024]{1,0:T(8,128)(2,1)S(1)}, u32[]{:S(2)}, u32[]{:S(2)}) collective-permute-start(bf16[64,1024]{1,0:T(8,128)(2,1)S(1)} %get-tuple-element.63), channel_id=1, source_target_pairs={{0,3},{1,0},{2,1},{3,2},{4,7},{5,4},{6,5},{7,6},{8,11},{9,8},{10,9... | collective-permute-start | bytes 393224 | tf_op jit(solution)/shard_map/ppermute | solution.py:454
  43.3 12.7 %collective-permute-start.12 = (bf16[144,512]{1,0:T(8,128)(2,1)S(1)}, bf16[144,512]{1,0:T(8,128)(2,1)S(1)}, u32[]{:S(2)}, u32[]{:S(2)}) collective-permute-start(bf16[144,512]{1,0:T(8,128)(2,1)S(1)} %shard_map.80.left_ref), channel_id=1, source_target_pairs={{0,2},{1,3},{2,0},{3,1},{4,6},{5,7},{6,4},{7,5},{8,10},{9,11},{10,... | collective-permute-start | bytes 442376 | tf_op jit(solution)/shard_map/ppermute | solution.py:502
  47.6 11.3 %collective-permute-start.11 = (bf16[4,64,512]{2,1,0:T(8,128)(2,1)}, bf16[4,64,512]{2,1,0:T(8,128)(2,1)S(1)}, u32[]{:S(2)}, u32[]{:S(2)}) collective-permute-start(bf16[4,64,512]{2,1,0:T(8,128)(2,1)} %shard_map.81), channel_id=1, source_target_pairs={{4,0},{13,1},{22,2},{31,3}} | collective-permute-start | bytes 786440 | tf_op jit(solution)/shard_map/ppermute | solution.py:497
  48.9 10.0 %collective-permute-start.10 = (bf16[4,64,512]{2,1,0:T(8,128)(2,1)}, bf16[4,64,512]{2,1,0:T(8,128)(2,1)S(1)}, u32[]{:S(2)}, u32[]{:S(2)}) collective-permute-start(bf16[4,64,512]{2,1,0:T(8,128)(2,1)} %shard_map.81), channel_id=1, source_target_pairs={{0,0},{9,1},{18,2},{27,3}} | collective-permute-start | bytes 786440 | tf_op jit(solution)/shard_map/ppermute | solution.py:497
  51.1 6.9 %collective-permute-start.13 = (bf16[128,384]{1,0:T(8,128)(2,1)S(1)}, bf16[128,384]{1,0:T(8,128)(2,1)S(1)}, u32[]{:S(2)}, u32[]{:S(2)}) collective-permute-start(bf16[128,384]{1,0:T(8,128)(2,1)S(1)} %get-tuple-element.69), channel_id=1, source_target_pairs={{0,1},{1,0},{2,3},{3,2},{4,5},{5,4},{6,7},{7,6},{8,9},{9,8},{10,11... | collective-permute-start | bytes 294920 | tf_op jit(solution)/shard_map/ppermute | solution.py:502
  56.1 5.9 %collective-permute-start.14 = (bf16[144,512]{1,0:T(8,128)(2,1)S(1)}, bf16[144,512]{1,0:T(8,128)(2,1)S(1)}, u32[]{:S(2)}, u32[]{:S(2)}) collective-permute-start(bf16[144,512]{1,0:T(8,128)(2,1)S(1)} %shard_map.83.refs_0_.refs_2_), channel_id=1, source_target_pairs={{0,1},{1,0},{2,3},{3,2},{4,5},{5,4},{6,7},{7,6},{8,9},{9,8},{10,11... | collective-permute-start | bytes 442376 | tf_op jit(solution)/shard_map/ppermute | solution.py:502
  58.1 7.4 %collective-permute-start.15 = (bf16[128,384]{1,0:T(8,128)(2,1)S(1)}, bf16[128,384]{1,0:T(8,128)(2,1)}, u32[]{:S(2)}, u32[]{:S(2)}) collective-permute-start(bf16[128,384]{1,0:T(8,128)(2,1)S(1)} %shard_map.84.left_ref), channel_id=1, source_target_pairs={{0,2},{1,3},{2,0},{3,1},{4,6},{5,7},{6,4},{7,5},{8,10},{9,11},{10,... | collective-permute-start | bytes 294920 | tf_op jit(solution)/shard_map/ppermute | solution.py:502
  65.5 14.0 %collective-permute-start.16 = (bf16[4,64,1024]{2,1,0:T(8,128)(2,1)S(1)}, bf16[4,64,1024]{2,1,0:T(8,128)(2,1)S(1)}, u32[]{:S(2)}, u32[]{:S(2)}) collective-permute-start(bf16[4,64,1024]{2,1,0:T(8,128)(2,1)S(1)} %shard_map.87), channel_id=1, source_target_pairs={{0,28},{1,29},{2,30},{3,31},{4,0},{5,1},{6,2},{7,3},{8,4},{9,5},{1... | collective-permute-start | bytes 1572872 | tf_op jit(solution)/shard_map/ppermute | solution.py:468
  65.5 6.0 %collective-permute-start.21 = (bf16[256,128]{1,0:T(8,128)(2,1)S(1)}, bf16[256,128]{1,0:T(8,128)(2,1)S(1)}, u32[]{:S(2)}, u32[]{:S(2)}) collective-permute-start(bf16[256,128]{1,0:T(8,128)(2,1)S(1)} %get-tuple-element.80), channel_id=1, source_target_pairs={{0,31},{1,28},{2,29},{3,30},{4,3},{5,0},{6,1},{7,2},{8,7},{9,4},{1... | collective-permute-start | bytes 196616 | tf_op jit(solution)/shard_map/ppermute | solution.py:468
  70.0 8.3 %collective-permute-start.17 = (bf16[128,384]{1,0:T(8,128)(2,1)S(1)}, bf16[128,384]{1,0:T(8,128)(2,1)S(1)}, u32[]{:S(2)}, u32[]{:S(2)}) collective-permute-start(bf16[128,384]{1,0:T(8,128)(2,1)S(1)} %shard_map.88.refs_0_), channel_id=1, source_target_pairs={{0,1},{1,0},{2,3},{3,2},{4,5},{5,4},{6,7},{7,6},{8,9},{9,8},{10,11... | collective-permute-start | bytes 294920 | tf_op jit(solution)/shard_map/ppermute | solution.py:502
  70.1 5.3 %collective-permute-start.20 = (bf16[256,128]{1,0:T(8,128)(2,1)S(1)}, bf16[256,128]{1,0:T(8,128)(2,1)S(1)}, u32[]{:S(2)}, u32[]{:S(2)}) collective-permute-start(bf16[256,128]{1,0:T(8,128)(2,1)S(1)} %get-tuple-element.80), channel_id=1, source_target_pairs={{0,30},{1,31},{2,28},{3,29},{4,2},{5,3},{6,0},{7,1},{8,6},{9,7},{1... | collective-permute-start | bytes 196616 | tf_op jit(solution)/shard_map/ppermute | solution.py:468
  70.4 7.9 %collective-permute-start.19 = (bf16[256,128]{1,0:T(8,128)(2,1)S(1)}, bf16[256,128]{1,0:T(8,128)(2,1)S(1)}, u32[]{:S(2)}, u32[]{:S(2)}) collective-permute-start(bf16[256,128]{1,0:T(8,128)(2,1)S(1)} %get-tuple-element.80), channel_id=1, source_target_pairs={{0,29},{1,30},{2,31},{3,28},{4,1},{5,2},{6,3},{7,0},{8,5},{9,6},{1... | collective-permute-start | bytes 196616 | tf_op jit(solution)/shard_map/ppermute | solution.py:468
  71.5 6.8 %collective-permute-start.18 = (bf16[256,128]{1,0:T(8,128)(2,1)S(1)}, bf16[256,128]{1,0:T(8,128)(2,1)S(1)}, u32[]{:S(2)}, u32[]{:S(2)}) collective-permute-start(bf16[256,128]{1,0:T(8,128)(2,1)S(1)} %get-tuple-element.80), channel_id=1, source_target_pairs={{0,28},{1,29},{2,30},{3,31},{4,0},{5,1},{6,2},{7,3},{8,4},{9,5},{1... | collective-permute-start | bytes 196616 | tf_op jit(solution)/shard_map/ppermute | solution.py:468
  80.7 6.3 %collective-permute-start.22 = (bf16[64,1024]{1,0:T(8,128)(2,1)S(1)}, bf16[64,1024]{1,0:T(8,128)(2,1)S(1)}, u32[]{:S(2)}, u32[]{:S(2)}) collective-permute-start(bf16[64,1024]{1,0:T(8,128)(2,1)S(1)} %get-tuple-element.88), channel_id=1, source_target_pairs={{0,3},{1,0},{2,1},{3,2},{4,7},{5,4},{6,5},{7,6},{8,11},{9,8},{10,9... | collective-permute-start | bytes 393224 | tf_op jit(solution)/shard_map/ppermute | solution.py:454
  81.8 12.1 %collective-permute-start.23 = (bf16[64,1024]{1,0:T(8,128)(2,1)S(1)}, bf16[64,1024]{1,0:T(8,128)(2,1)S(1)}, u32[]{:S(2)}, u32[]{:S(2)}) collective-permute-start(bf16[64,1024]{1,0:T(8,128)(2,1)S(1)} %get-tuple-element.89), channel_id=1, source_target_pairs={{0,2},{1,3},{2,0},{3,1},{4,6},{5,7},{6,4},{7,5},{8,10},{9,11},{10,... | collective-permute-start | bytes 393224 | tf_op jit(solution)/shard_map/ppermute | solution.py:454
  81.8 12.1 %collective-permute-start.24 = (bf16[64,1024]{1,0:T(8,128)(2,1)S(1)}, bf16[64,1024]{1,0:T(8,128)(2,1)S(1)}, u32[]{:S(2)}, u32[]{:S(2)}) collective-permute-start(bf16[64,1024]{1,0:T(8,128)(2,1)S(1)} %get-tuple-element.90), channel_id=1, source_target_pairs={{0,1},{1,2},{2,3},{3,0},{4,5},{5,6},{6,7},{7,4},{8,9},{9,10},{10,1... | collective-permute-start | bytes 393224 | tf_op jit(solution)/shard_map/ppermute | solution.py:454

commit v6 on v5

--- a/solution.py
+++ b/solution.py
@@ -132,10 +132,15 @@
         piece_refs, refs = refs[:count], refs[count:]
         scale_refs, (project_ref, output_ref, *outs) = refs[:ticks], refs[ticks:]
         project = project_ref[...]
+        hidden = jnp.concatenate([ref[0] for ref in piece_refs], axis=0)
+        projected = dot(hidden, project).astype(BF16)
+        incoming = jnp.concatenate([ref[1] for ref in piece_refs], axis=0)
+        heads = dot(incoming, output_ref[...]).astype(BF16)
         for j in range(count):
             out_ref, rows = outs[j % 2], half_rows(me_ref, j, count, seq)
-            out_ref[rows, :wide] = dot(piece_refs[j][0], project).astype(BF16)
-            out_ref[rows, wide:] = dot(piece_refs[j][1], output_ref[...]).astype(BF16)
+            place = slice(j * seq, (j + 1) * seq)
+            out_ref[rows, :wide] = projected[place]
+            out_ref[rows, wide:] = heads[place]
         sums = jnp.sum(project.astype(F32), axis=0, keepdims=True) / width
         place = lax.broadcasted_iota(jnp.int32, (extra, LANES), 0) - 2 * ticks * (me_ref[0] // 2)
         facts = jnp.zeros((extra, LANES), F32)
@@ -162,9 +167,11 @@
 
     def body(me_ref, *refs):
         piece_refs, (project_ref, *outs) = refs[:count], refs[count:]
-        for j in range(count):
-            value = dot(piece_refs[j][...], project_ref[...])
-            outs[j % 2][half_rows(me_ref, j, count, seq), :] = value.astype(BF16)
+        hidden = jnp.concatenate([ref[...] for ref in piece_refs], axis=0)
+        value = dot(hidden, project_ref[...]).astype(BF16)
+        for j in range(count):
+            rows = half_rows(me_ref, j, count, seq)
+            outs[j % 2][rows, :] = value[j * seq : (j + 1) * seq]
 
     return kernel_call(body, [shape(count // 2 * seq, wide)] * 2, [me], [*pieces, project])
 
@@ -339,9 +346,8 @@
     return kernel_call(body, attention_outs(rows, head), [], arrays, cost=1)
 
 
-def input_gradient(grad, numbers, incoming, hidden, project):
+def input_gradient(hidden_grad, numbers, incoming, hidden):
     scale, offset, slope = (numbers[:, i : i + 1] for i in range(3))
-    hidden_grad = dot(grad, project, CONTRACT_LAST)
     change = scale * hidden_grad - offset - slope * hidden.astype(F32)
     return (incoming.astype(F32) + change).astype(BF16)
 
@@ -353,7 +359,7 @@
 
     def body(me_ref, first_ref, *refs):
         top_refs, piece_refs, refs = refs[:runs], refs[runs : runs + count], refs[runs + count :]
-        grad_ref, numbers_ref, project_ref, passed_ref, sems = refs
+        grad_ref, numbers_ref, project_ref, passed_ref, sems, wide_ref = refs
         is_first = first_ref[0] == 1
 
         @pl.when(is_first)
@@ -372,14 +378,18 @@
 
         @pl.when(jnp.logical_not(is_first))
         def _():
+            wide_ref[...] = dot(grad_ref[...], project_ref[...], CONTRACT_LAST)
             for j in range(count):
                 rows = block_rows(me_ref, j, count, seq)
                 hidden, incoming = piece_refs[j][0], piece_refs[j][1]
                 passed_ref[j] = input_gradient(
-                    grad_ref[rows, :], numbers_ref[rows, :], incoming, hidden, project_ref[...]
+                    wide_ref[rows, :], numbers_ref[rows, :], incoming, hidden
                 )
 
-    scratch = [pltpu.SemaphoreType.DMA((count, runs))]
+    scratch = [
+        pltpu.SemaphoreType.DMA((count, runs)),
+        pltpu.VMEM((count * seq, part), F32),
+    ]
     arrays = [*pieces, *grads, project]
     outs = [shape(count, seq, part)]
     return kernel_call(body, outs, [me, first], arrays, scratch, far=tops)[0]
@@ -389,22 +399,18 @@
     count, (seq, part) = len(pieces), pieces[0].shape
 
     def body(me_ref, *refs):
-        piece_refs, (grad_ref, numbers_ref, received_ref, project_ref, *outs) = (
-            refs[:count],
-            refs[count:],
-        )
+        piece_refs, refs = refs[:count], refs[count:]
+        grad_ref, numbers_ref, received_ref, project_ref, *outs, wide_ref = refs
+        wide_ref[...] = dot(grad_ref[...], project_ref[...], CONTRACT_LAST)
         for j in range(count):
             rows = block_rows(me_ref, j, count, seq)
             outs[j][...] = input_gradient(
-                grad_ref[rows, :],
-                numbers_ref[rows, :],
-                received_ref[j],
-                piece_refs[j][...],
-                project_ref[...],
+                wide_ref[rows, :], numbers_ref[rows, :], received_ref[j], piece_refs[j][...]
             )
 
     arrays = [*pieces, *grads, received, project]
-    return list(kernel_call(body, [shape(seq, part)] * count, [me], arrays))
+    scratch = [pltpu.VMEM((count * seq, part), F32)]
+    return list(kernel_call(body, [shape(seq, part)] * count, [me], arrays, scratch))
 
 
 def weight_gradients(pieces, later, received, first_grads, later_grads, me):

time: 95 us -> 94.5 us (level)
  transfers between devices with their start and end apart: 25 -> 25, of which waited for: 10 -> 10; matrix products, arithmetic and copies ran while one was open for 0% -> 0% of each run, Pallas kernels for 11% -> 10%
where the time goes in v6:
time: 94.5 us; the launch traced here: 94.3 us
  waiting for transfers between devices  41.1 us (43%)
  starting transfers between devices  37.5 us (40%)
  Pallas kernels  12.5 us (13%)
  local copies, waits for them, and re-layouts  2.34 us (2%)
    ppermute x9, starting transfers between devices, shift(): lax.ppermute(value, 'dp', [(i, (i + steps) % count) for i in range(count)])  20.1 us
    ppermute x2, waiting for transfers between devices, toward_owner(): return lax.ppermute(blocks, BOTH, pairs)  18.8 us
    pallas_call x18, Pallas kernels, kernel_call(): pl.pallas_call(body, out_shape=tuple(outs), in_specs=[pl.BlockSpec(memory...  12.5 us
    ppermute x6, waiting for transfers between devices, exchanged(): return lax.ppermute(value, 'dp', [(i, i ^ step) for i in range(count)])  8.93 us
    ppermute x9, waiting for transfers between devices, shift(): lax.ppermute(value, 'dp', [(i, (i + steps) % count) for i in range(count)])  7.53 us
    ppermute x5, starting transfers between devices, down(): return lax.ppermute(value, BOTH, pairs)  6.04 us
    ppermute x5, waiting for transfers between devices, down(): return lax.ppermute(value, BOTH, pairs)  5.79 us
    ppermute x6, starting transfers between devices, exchanged(): return lax.ppermute(value, 'dp', [(i, i ^ step) for i in range(count)])  5.76 us
  transfers between devices with their start and end apart: 25, of which 10 were waited for; matrix products, arithmetic and copies ran while one was open for 0% of the time, Pallas kernels for 10%

profile of v6, /device:TPU:0, one launch (start us, length us, event | category | flops | bytes accessed | tf_op | source)
XLA Modules:
  0.0 94.3 jit_solution(6270097321164017550)
XLA Ops:
  0.7 1.3 %copy-done.1 = bf16[1,2,64,4096]{3,2,1,0:T(8,128)(2,1)S(1)} copy-done((bf16[1,2,64,4096]{3,2,1,0:T(8,128)(2,1)S(1)}, bf16[1,2,64,4096]{3,2,1,0:T(8,128)(2,1)}, u32[]{:S(2)}) %copy-start.1) | copy-done | bytes 1048600
  1.9 1.0 %copy-done.2 = bf16[1,64,4096]{2,1,0:T(8,128)(2,1)S(1)} copy-done((bf16[1,64,4096]{2,1,0:T(8,128)(2,1)S(1)}, bf16[1,64,4096]{2,1,0:T(8,128)(2,1)}, u32[]{:S(2)}) %copy-start.2) | copy-done | bytes 524312
  3.0 0.4 shard_map.76
  3.4 3.1 %collective-permute-start = (bf16[2,64,1024]{2,1,0:T(8,128)(2,1)S(1)}, bf16[2,64,1024]{2,1,0:T(8,128)(2,1)S(1)}, u32[]{:S(2)}, u32[]{:S(2)}) collective-permute-start(bf16[2,64,1024]{2,1,0:T(8,128)(2,1)S(1)} %get-tuple-element.48), channel_id=1, source_target_pairs={{0,1},{1,2},{2,3},{3,0},{4,5},{5,6},{6,7},{7,4},{8,9},{9,10},{10,1... | collective-permute-start | bytes 786440 | tf_op jit(solution)/shard_map/ppermute | solution.py:460
  6.5 2.6 %collective-permute-start.1 = (bf16[2,64,1024]{2,1,0:T(8,128)(2,1)S(1)}, bf16[2,64,1024]{2,1,0:T(8,128)(2,1)S(1)}, u32[]{:S(2)}, u32[]{:S(2)}) collective-permute-start(bf16[2,64,1024]{2,1,0:T(8,128)(2,1)S(1)} %get-tuple-element.49), channel_id=1, source_target_pairs={{0,2},{1,3},{2,0},{3,1},{4,6},{5,7},{6,4},{7,5},{8,10},{9,11},{10,... | collective-permute-start | bytes 786440 | tf_op jit(solution)/shard_map/ppermute | solution.py:460
  9.1 1.3 %collective-permute-start.2 = (bf16[2,64,1024]{2,1,0:T(8,128)(2,1)S(1)}, bf16[2,64,1024]{2,1,0:T(8,128)(2,1)S(1)}, u32[]{:S(2)}, u32[]{:S(2)}) collective-permute-start(bf16[2,64,1024]{2,1,0:T(8,128)(2,1)S(1)} %get-tuple-element.50), channel_id=1, source_target_pairs={{0,3},{1,0},{2,1},{3,2},{4,7},{5,4},{6,5},{7,6},{8,11},{9,8},{10,9... | collective-permute-start | bytes 786440 | tf_op jit(solution)/shard_map/ppermute | solution.py:460
  10.4 1.3 %collective-permute-start.3 = (bf16[1,64,512]{2,1,0:T(8,128)(2,1)S(1)}, bf16[1,64,512]{2,1,0:T(8,128)(2,1)S(1)}, u32[]{:S(2)}, u32[]{:S(2)}) collective-permute-start(bf16[1,64,512]{2,1,0:T(8,128)(2,1)S(1)} %copy-done.4), channel_id=1, source_target_pairs={{1,0},{3,2},{5,4},{7,6},{8,9},{10,11},{12,13},{14,15},{17,16},{19,... | collective-permute-start | bytes 196616 | tf_op jit(solution)/shard_map/ppermute | solution.py:497
  11.7 0.4 shard_map.77
  12.1 15.3 %collective-permute-done.3.right_ref = bf16[1,64,512]{2,1,0:T(8,128)(2,1)S(1)} collective-permute-done((bf16[1,64,512]{2,1,0:T(8,128)(2,1)S(1)}, bf16[1,64,512]{2,1,0:T(8,128)(2,1)S(1)}, u32[]{:S(2)}, u32[]{:S(2)}) %collective-permute-start.3) | collective-permute-done | bytes 65568 | tf_op jit(solution)/shard_map/ppermute | solution.py:497
  27.5 0.6 shard_map.79
  28.1 0.1 collective-permute-start.7
  28.2 3.8 %collective-permute-start.5 = (bf16[64,1024]{1,0:T(8,128)(2,1)S(1)}, bf16[64,1024]{1,0:T(8,128)(2,1)S(1)}, u32[]{:S(2)}, u32[]{:S(2)}) collective-permute-start(bf16[64,1024]{1,0:T(8,128)(2,1)S(1)} %get-tuple-element.62), channel_id=1, source_target_pairs={{0,2},{1,3},{2,0},{3,1},{4,6},{5,7},{6,4},{7,5},{8,10},{9,11},{10,... | collective-permute-start | bytes 393224 | tf_op jit(solution)/shard_map/ppermute | solution.py:460
  32.0 2.6 %collective-permute-start.8 = (bf16[144,512]{1,0:T(8,128)(2,1)S(1)}, bf16[144,512]{1,0:T(8,128)(2,1)S(1)}, u32[]{:S(2)}, u32[]{:S(2)}) collective-permute-start(bf16[144,512]{1,0:T(8,128)(2,1)S(1)} %get-tuple-element.59), channel_id=1, source_target_pairs={{0,1},{1,0},{2,3},{3,2},{4,5},{5,4},{6,7},{7,6},{8,9},{9,8},{10,11... | collective-permute-start | bytes 442376 | tf_op jit(solution)/shard_map/ppermute | solution.py:508
  34.6 1.3 %collective-permute-start.9 = (bf16[2,64,512]{2,1,0:T(8,128)(2,1)S(1)}, bf16[2,64,512]{2,1,0:T(8,128)(2,1)S(1)}, u32[]{:S(2)}, u32[]{:S(2)}) collective-permute-start(bf16[2,64,512]{2,1,0:T(8,128)(2,1)S(1)} %shard_map.78.left_ref), channel_id=1, source_target_pairs={{2,0},{6,4},{11,9},{15,13},{16,18},{20,22},{25,27},{29,31}} | collective-permute-start | bytes 393224 | tf_op jit(solution)/shard_map/ppermute | solution.py:497
  35.9 0.1 collective-permute-start.4
  35.9 7.1 %collective-permute-start.6 = (bf16[64,1024]{1,0:T(8,128)(2,1)S(1)}, bf16[64,1024]{1,0:T(8,128)(2,1)S(1)}, u32[]{:S(2)}, u32[]{:S(2)}) collective-permute-start(bf16[64,1024]{1,0:T(8,128)(2,1)S(1)} %get-tuple-element.63), channel_id=1, source_target_pairs={{0,3},{1,0},{2,1},{3,2},{4,7},{5,4},{6,5},{7,6},{8,11},{9,8},{10,9... | collective-permute-start | bytes 393224 | tf_op jit(solution)/shard_map/ppermute | solution.py:460
  43.1 0.1 collective-permute-start.12
  43.2 3.5 %collective-permute-done.9.right_ref = bf16[2,64,512]{2,1,0:T(8,128)(2,1)S(1)} collective-permute-done((bf16[2,64,512]{2,1,0:T(8,128)(2,1)S(1)}, bf16[2,64,512]{2,1,0:T(8,128)(2,1)S(1)}, u32[]{:S(2)}, u32[]{:S(2)}) %collective-permute-start.9) | collective-permute-done | bytes 131104 | tf_op jit(solution)/shard_map/ppermute | solution.py:497
  46.6 0.7 shard_map.81
  47.4 1.3 %collective-permute-start.11 = (bf16[4,64,512]{2,1,0:T(8,128)(2,1)}, bf16[4,64,512]{2,1,0:T(8,128)(2,1)S(1)}, u32[]{:S(2)}, u32[]{:S(2)}) collective-permute-start(bf16[4,64,512]{2,1,0:T(8,128)(2,1)} %shard_map.81), channel_id=1, source_target_pairs={{4,0},{13,1},{22,2},{31,3}} | collective-permute-start | bytes 786440 | tf_op jit(solution)/shard_map/ppermute | solution.py:503
  48.7 1.6 %collective-permute-start.10 = (bf16[4,64,512]{2,1,0:T(8,128)(2,1)}, bf16[4,64,512]{2,1,0:T(8,128)(2,1)S(1)}, u32[]{:S(2)}, u32[]{:S(2)}) collective-permute-start(bf16[4,64,512]{2,1,0:T(8,128)(2,1)} %shard_map.81), channel_id=1, source_target_pairs={{0,0},{9,1},{18,2},{27,3}} | collective-permute-start | bytes 786440 | tf_op jit(solution)/shard_map/ppermute | solution.py:503
  50.3 0.4 shard_map.82
  50.7 2.9 %collective-permute-start.13 = (bf16[128,384]{1,0:T(8,128)(2,1)S(1)}, bf16[128,384]{1,0:T(8,128)(2,1)S(1)}, u32[]{:S(2)}, u32[]{:S(2)}) collective-permute-start(bf16[128,384]{1,0:T(8,128)(2,1)S(1)} %get-tuple-element.69), channel_id=1, source_target_pairs={{0,1},{1,0},{2,3},{3,2},{4,5},{5,4},{6,7},{7,6},{8,9},{9,8},{10,11... | collective-permute-start | bytes 294920 | tf_op jit(solution)/shard_map/ppermute | solution.py:508
  53.6 2.2 %collective-permute-done.12.right_ref = bf16[144,512]{1,0:T(8,128)(2,1)S(1)} collective-permute-done((bf16[144,512]{1,0:T(8,128)(2,1)S(1)}, bf16[144,512]{1,0:T(8,128)(2,1)S(1)}, u32[]{:S(2)}, u32[]{:S(2)}) %collective-permute-start.12) | collective-permute-done | bytes 147488 | tf_op jit(solution)/shard_map/ppermute | solution.py:508
  55.9 0.1 collective-permute-start.14
  55.9 1.9 %collective-permute-done.13.right_ref = bf16[128,384]{1,0:T(8,128)(2,1)S(1)} collective-permute-done((bf16[128,384]{1,0:T(8,128)(2,1)S(1)}, bf16[128,384]{1,0:T(8,128)(2,1)S(1)}, u32[]{:S(2)}, u32[]{:S(2)}) %collective-permute-start.13) | collective-permute-done | bytes 98336 | tf_op jit(solution)/shard_map/ppermute | solution.py:508
  57.8 0.1 collective-permute-start.15
  57.9 0.7 shard_map.85
  58.6 3.1 %collective-permute-done.14.refs_1_.refs_3_ = bf16[144,512]{1,0:T(8,128)(2,1)S(1)} collective-permute-done((bf16[144,512]{1,0:T(8,128)(2,1)S(1)}, bf16[144,512]{1,0:T(8,128)(2,1)S(1)}, u32[]{:S(2)}, u32[]{:S(2)}) %collective-permute-start.14) | collective-permute-done | bytes 147488 | tf_op jit(solution)/shard_map/ppermute | solution.py:508
  61.7 1.5 %shard_map.86 = (bf16[256,384]{1,0:T(8,128)(2,1)S(1)}, bf16[256,128]{1,0:T(8,128)(2,1)S(1)}, f32[256,128]{1,0:T(8,128)S(1)}, bf16[256,128]{1,0:T(8,128)(2,1)S(1)}) custom-call(s32[1]{0:T(128)} %bitcast.me_ref, s32[1]{0:T(128)} %bitcast.5.first_ref, bf16[144,512]{1,0:T(8,128)(2,1)S(1)} %shard_map.83.refs_0_.refs_2_, ...), custom_call_target="tpu_custom_call" | custom-call | flops 1 | bytes 1 | tf_op jit(solution)/shard_map/pallas_call | solution.py:26
  63.2 0.2 shard_map.87
  63.4 1.8 %collective-permute-done.15.right_ref = bf16[128,384]{1,0:T(8,128)(2,1)} collective-permute-done((bf16[128,384]{1,0:T(8,128)(2,1)S(1)}, bf16[128,384]{1,0:T(8,128)(2,1)}, u32[]{:S(2)}, u32[]{:S(2)}) %collective-permute-start.15) | collective-permute-done | bytes 98336 | tf_op jit(solution)/shard_map/ppermute | solution.py:508
  65.2 3.7 %collective-permute-start.21 = (bf16[256,128]{1,0:T(8,128)(2,1)S(1)}, bf16[256,128]{1,0:T(8,128)(2,1)S(1)}, u32[]{:S(2)}, u32[]{:S(2)}) collective-permute-start(bf16[256,128]{1,0:T(8,128)(2,1)S(1)} %get-tuple-element.80), channel_id=1, source_target_pairs={{0,31},{1,28},{2,29},{3,30},{4,3},{5,0},{6,1},{7,2},{8,7},{9,4},{1... | collective-permute-start | bytes 196616 | tf_op jit(solution)/shard_map/ppermute | solution.py:474
  68.9 0.9 shard_map.88.refs_0_
  69.8 0.1 collective-permute-start.17
  69.9 0.3 collective-permute-start.20
  70.2 1.1 %collective-permute-start.19 = (bf16[256,128]{1,0:T(8,128)(2,1)S(1)}, bf16[256,128]{1,0:T(8,128)(2,1)S(1)}, u32[]{:S(2)}, u32[]{:S(2)}) collective-permute-start(bf16[256,128]{1,0:T(8,128)(2,1)S(1)} %get-tuple-element.80), channel_id=1, source_target_pairs={{0,29},{1,30},{2,31},{3,28},{4,1},{5,2},{6,3},{7,0},{8,5},{9,6},{1... | collective-permute-start | bytes 196616 | tf_op jit(solution)/shard_map/ppermute | solution.py:474
  71.2 1.0 %collective-permute-start.18 = (bf16[256,128]{1,0:T(8,128)(2,1)S(1)}, bf16[256,128]{1,0:T(8,128)(2,1)S(1)}, u32[]{:S(2)}, u32[]{:S(2)}) collective-permute-start(bf16[256,128]{1,0:T(8,128)(2,1)S(1)} %get-tuple-element.80), channel_id=1, source_target_pairs={{0,28},{1,29},{2,30},{3,31},{4,0},{5,1},{6,2},{7,3},{8,4},{9,5},{1... | collective-permute-start | bytes 196616 | tf_op jit(solution)/shard_map/ppermute | solution.py:474
  72.3 2.9 %collective-permute-done.20.refs_2_ = bf16[256,128]{1,0:T(8,128)(2,1)S(1)} collective-permute-done((bf16[256,128]{1,0:T(8,128)(2,1)S(1)}, bf16[256,128]{1,0:T(8,128)(2,1)S(1)}, u32[]{:S(2)}, u32[]{:S(2)}) %collective-permute-start.20) | collective-permute-done | bytes 65568 | tf_op jit(solution)/shard_map/ppermute | solution.py:474
  75.1 2.9 %collective-permute-done.19.refs_1_ = bf16[256,128]{1,0:T(8,128)(2,1)S(1)} collective-permute-done((bf16[256,128]{1,0:T(8,128)(2,1)S(1)}, bf16[256,128]{1,0:T(8,128)(2,1)S(1)}, u32[]{:S(2)}, u32[]{:S(2)}) %collective-permute-start.19) | collective-permute-done | bytes 65568 | tf_op jit(solution)/shard_map/ppermute | solution.py:474
  78.1 1.2 %shard_map.90 = (bf16[256,384]{1,0:T(8,128)(2,1)S(1)}, bf16[256,128]{1,0:T(8,128)(2,1)S(1)}, f32[256,128]{1,0:T(8,128)S(1)}) custom-call(bf16[128,384]{1,0:T(8,128)(2,1)S(1)} %shard_map.88.refs_0_, bf16[128,384]{1,0:T(8,128)(2,1)S(1)} %collective-permute-done.17.refs_1_, bf16[144,512]{1,0:T(8,128)(2,1)S(1)} %shard_map.83.refs_0_.refs_2_, ...), custom_call_target="tpu_custom_call" | custom-call | flops 1 | bytes 1 | tf_op jit(solution)/shard_map/pallas_call | solution.py:26
  79.3 0.8 shard_map.91
  80.1 1.1 %collective-permute-start.22 = (bf16[64,1024]{1,0:T(8,128)(2,1)S(1)}, bf16[64,1024]{1,0:T(8,128)(2,1)S(1)}, u32[]{:S(2)}, u32[]{:S(2)}) collective-permute-start(bf16[64,1024]{1,0:T(8,128)(2,1)S(1)} %get-tuple-element.88), channel_id=1, source_target_pairs={{0,3},{1,0},{2,1},{3,2},{4,7},{5,4},{6,5},{7,6},{8,11},{9,8},{10,9... | collective-permute-start | bytes 393224 | tf_op jit(solution)/shard_map/ppermute | solution.py:460
  81.2 1.0 %collective-permute-start.24 = (bf16[64,1024]{1,0:T(8,128)(2,1)S(1)}, bf16[64,1024]{1,0:T(8,128)(2,1)S(1)}, u32[]{:S(2)}, u32[]{:S(2)}) collective-permute-start(bf16[64,1024]{1,0:T(8,128)(2,1)S(1)} %get-tuple-element.90), channel_id=1, source_target_pairs={{0,1},{1,2},{2,3},{3,0},{4,5},{5,6},{6,7},{7,4},{8,9},{9,10},{10,1... | collective-permute-start | bytes 393224 | tf_op jit(solution)/shard_map/ppermute | solution.py:460
  82.2 3.7 %shard_map.92 = (f32[1024,384]{1,0:T(8,128)}, f32[1024,128]{1,0:T(8,128)}) custom-call(s32[1]{0:T(128)} %bitcast.me_ref, bf16[2,64,1024]{2,1,0:T(8,128)(2,1)S(1)} %get-tuple-element.47.refs_0_.refs_2_, bf16[2,64,1024]{2,1,0:T(8,128)(2,1)S(1)} %collective-permute-done.refs_1_.refs_3_, bf16[2,64,1024]{2,1,0:T(8,128)(2,1)S(1)} %collective-permute-done.1.refs_2_.refs_4_, ...), custom_call_target="tpu_custom_call" | custom-call | flops 1 | bytes 1 | tf_op jit(solution)/shard_map/pallas_call | solution.py:26
  85.9 0.4 collective-permute-done.22.refs_1_
  86.3 7.1 %collective-permute-done.23.refs_2_ = bf16[64,1024]{1,0:T(8,128)(2,1)S(1)} collective-permute-done((bf16[64,1024]{1,0:T(8,128)(2,1)S(1)}, bf16[64,1024]{1,0:T(8,128)(2,1)S(1)}, u32[]{:S(2)}, u32[]{:S(2)}) %collective-permute-start.23) | collective-permute-done | bytes 131104 | tf_op jit(solution)/shard_map/ppermute | solution.py:460
  93.4 0.8 shard_map.93
  (30 shorter events, 0.2 us)
Async XLA Ops:
  0.6 26.9 %copy-start = (bf16[1,1024,384]{2,1,0:T(8,128)(2,1)S(1)}, bf16[1,1024,384]{2,1,0:T(8,128)(2,1)}, u32[]{:S(2)}) copy-start(bf16[1,1024,384]{2,1,0:T(8,128)(2,1)} %param.8) | copy-start | bytes 2359300
  0.6 1.3 %copy-start.1 = (bf16[1,2,64,4096]{3,2,1,0:T(8,128)(2,1)S(1)}, bf16[1,2,64,4096]{3,2,1,0:T(8,128)(2,1)}, u32[]{:S(2)}) copy-start(bf16[1,2,64,4096]{3,2,1,0:T(8,128)(2,1)} %param.5) | copy-start | bytes 3145732
  1.9 1.0 %copy-start.2 = (bf16[1,64,4096]{2,1,0:T(8,128)(2,1)S(1)}, bf16[1,64,4096]{2,1,0:T(8,128)(2,1)}, u32[]{:S(2)}) copy-start(bf16[1,64,4096]{2,1,0:T(8,128)(2,1)} %param.6) | copy-start | bytes 1572868
  3.0 7.4 %copy-start.4 = (bf16[1,64,512]{2,1,0:T(8,128)(2,1)S(1)}, bf16[1,64,512]{2,1,0:T(8,128)(2,1)}, u32[]{:S(2)}) copy-start(bf16[1,64,512]{2,1,0:T(8,128)(2,1)} %left_ref) | copy-start | bytes 196612
  3.0 24.5 %copy-start.3 = (bf16[1,1024,128]{2,1,0:T(8,128)(2,1)S(1)}, bf16[1,1024,128]{2,1,0:T(8,128)(2,1)}, u32[]{:S(2)}) copy-start(bf16[1,1024,128]{2,1,0:T(8,128)(2,1)} %param.9) | copy-start | bytes 786436
  3.4 24.1 %collective-permute-start = (bf16[2,64,1024]{2,1,0:T(8,128)(2,1)S(1)}, bf16[2,64,1024]{2,1,0:T(8,128)(2,1)S(1)}, u32[]{:S(2)}, u32[]{:S(2)}) collective-permute-start(bf16[2,64,1024]{2,1,0:T(8,128)(2,1)S(1)} %get-tuple-element.48), channel_id=1, source_target_pairs={{0,1},{1,2},{2,3},{3,0},{4,5},{5,6},{6,7},{7,4},{8,9},{9,10},{10,1... | collective-permute-start | bytes 786440 | tf_op jit(solution)/shard_map/ppermute | solution.py:460
  6.5 21.0 %collective-permute-start.1 = (bf16[2,64,1024]{2,1,0:T(8,128)(2,1)S(1)}, bf16[2,64,1024]{2,1,0:T(8,128)(2,1)S(1)}, u32[]{:S(2)}, u32[]{:S(2)}) collective-permute-start(bf16[2,64,1024]{2,1,0:T(8,128)(2,1)S(1)} %get-tuple-element.49), channel_id=1, source_target_pairs={{0,2},{1,3},{2,0},{3,1},{4,6},{5,7},{6,4},{7,5},{8,10},{9,11},{10,... | collective-permute-start | bytes 786440 | tf_op jit(solution)/shard_map/ppermute | solution.py:460
  9.1 18.4 %collective-permute-start.2 = (bf16[2,64,1024]{2,1,0:T(8,128)(2,1)S(1)}, bf16[2,64,1024]{2,1,0:T(8,128)(2,1)S(1)}, u32[]{:S(2)}, u32[]{:S(2)}) collective-permute-start(bf16[2,64,1024]{2,1,0:T(8,128)(2,1)S(1)} %get-tuple-element.50), channel_id=1, source_target_pairs={{0,3},{1,0},{2,1},{3,2},{4,7},{5,4},{6,5},{7,6},{8,11},{9,8},{10,9... | collective-permute-start | bytes 786440 | tf_op jit(solution)/shard_map/ppermute | solution.py:460
  10.4 17.0 %collective-permute-start.3 = (bf16[1,64,512]{2,1,0:T(8,128)(2,1)S(1)}, bf16[1,64,512]{2,1,0:T(8,128)(2,1)S(1)}, u32[]{:S(2)}, u32[]{:S(2)}) collective-permute-start(bf16[1,64,512]{2,1,0:T(8,128)(2,1)S(1)} %copy-done.4), channel_id=1, source_target_pairs={{1,0},{3,2},{5,4},{7,6},{8,9},{10,11},{12,13},{14,15},{17,16},{19,... | collective-permute-start | bytes 196616 | tf_op jit(solution)/shard_map/ppermute | solution.py:497
  28.1 14.9 %collective-permute-start.7 = (bf16[1024,128]{1,0:T(8,128)(2,1)S(1)}, bf16[1024,128]{1,0:T(8,128)(2,1)S(1)}, u32[]{:S(2)}, u32[]{:S(2)}) collective-permute-start(bf16[1024,128]{1,0:T(8,128)(2,1)S(1)} %bitcast.18), channel_id=1, source_target_pairs={{0,4},{4,8},{8,12},{12,16},{16,20},{20,24},{24,28},{28,0},{1,5},{5... | collective-permute-start | bytes 786440 | tf_op jit(solution)/shard_map/ppermute | solution.py:535
  28.2 7.8 %collective-permute-start.5 = (bf16[64,1024]{1,0:T(8,128)(2,1)S(1)}, bf16[64,1024]{1,0:T(8,128)(2,1)S(1)}, u32[]{:S(2)}, u32[]{:S(2)}) collective-permute-start(bf16[64,1024]{1,0:T(8,128)(2,1)S(1)} %get-tuple-element.62), channel_id=1, source_target_pairs={{0,2},{1,3},{2,0},{3,1},{4,6},{5,7},{6,4},{7,5},{8,10},{9,11},{10,... | collective-permute-start | bytes 393224 | tf_op jit(solution)/shard_map/ppermute | solution.py:460
  32.0 11.0 %collective-permute-start.8 = (bf16[144,512]{1,0:T(8,128)(2,1)S(1)}, bf16[144,512]{1,0:T(8,128)(2,1)S(1)}, u32[]{:S(2)}, u32[]{:S(2)}) collective-permute-start(bf16[144,512]{1,0:T(8,128)(2,1)S(1)} %get-tuple-element.59), channel_id=1, source_target_pairs={{0,1},{1,0},{2,3},{3,2},{4,5},{5,4},{6,7},{7,6},{8,9},{9,8},{10,11... | collective-permute-start | bytes 442376 | tf_op jit(solution)/shard_map/ppermute | solution.py:508
  34.6 12.1 %collective-permute-start.9 = (bf16[2,64,512]{2,1,0:T(8,128)(2,1)S(1)}, bf16[2,64,512]{2,1,0:T(8,128)(2,1)S(1)}, u32[]{:S(2)}, u32[]{:S(2)}) collective-permute-start(bf16[2,64,512]{2,1,0:T(8,128)(2,1)S(1)} %shard_map.78.left_ref), channel_id=1, source_target_pairs={{2,0},{6,4},{11,9},{15,13},{16,18},{20,22},{25,27},{29,31}} | collective-permute-start | bytes 393224 | tf_op jit(solution)/shard_map/ppermute | solution.py:497
  35.9 14.4 %collective-permute-start.4 = (bf16[64,1024]{1,0:T(8,128)(2,1)S(1)}, bf16[64,1024]{1,0:T(8,128)(2,1)S(1)}, u32[]{:S(2)}, u32[]{:S(2)}) collective-permute-start(bf16[64,1024]{1,0:T(8,128)(2,1)S(1)} %get-tuple-element.61), channel_id=1, source_target_pairs={{0,1},{1,2},{2,3},{3,0},{4,5},{5,6},{6,7},{7,4},{8,9},{9,10},{10,1... | collective-permute-start | bytes 393224 | tf_op jit(solution)/shard_map/ppermute | solution.py:460
  35.9 14.3 %collective-permute-start.6 = (bf16[64,1024]{1,0:T(8,128)(2,1)S(1)}, bf16[64,1024]{1,0:T(8,128)(2,1)S(1)}, u32[]{:S(2)}, u32[]{:S(2)}) collective-permute-start(bf16[64,1024]{1,0:T(8,128)(2,1)S(1)} %get-tuple-element.63), channel_id=1, source_target_pairs={{0,3},{1,0},{2,1},{3,2},{4,7},{5,4},{6,5},{7,6},{8,11},{9,8},{10,9... | collective-permute-start | bytes 393224 | tf_op jit(solution)/shard_map/ppermute | solution.py:460
  43.1 12.7 %collective-permute-start.12 = (bf16[144,512]{1,0:T(8,128)(2,1)S(1)}, bf16[144,512]{1,0:T(8,128)(2,1)S(1)}, u32[]{:S(2)}, u32[]{:S(2)}) collective-permute-start(bf16[144,512]{1,0:T(8,128)(2,1)S(1)} %shard_map.80.left_ref), channel_id=1, source_target_pairs={{0,2},{1,3},{2,0},{3,1},{4,6},{5,7},{6,4},{7,5},{8,10},{9,11},{10,... | collective-permute-start | bytes 442376 | tf_op jit(solution)/shard_map/ppermute | solution.py:508
  47.4 11.3 %collective-permute-start.11 = (bf16[4,64,512]{2,1,0:T(8,128)(2,1)}, bf16[4,64,512]{2,1,0:T(8,128)(2,1)S(1)}, u32[]{:S(2)}, u32[]{:S(2)}) collective-permute-start(bf16[4,64,512]{2,1,0:T(8,128)(2,1)} %shard_map.81), channel_id=1, source_target_pairs={{4,0},{13,1},{22,2},{31,3}} | collective-permute-start | bytes 786440 | tf_op jit(solution)/shard_map/ppermute | solution.py:503
  48.7 10.0 %collective-permute-start.10 = (bf16[4,64,512]{2,1,0:T(8,128)(2,1)}, bf16[4,64,512]{2,1,0:T(8,128)(2,1)S(1)}, u32[]{:S(2)}, u32[]{:S(2)}) collective-permute-start(bf16[4,64,512]{2,1,0:T(8,128)(2,1)} %shard_map.81), channel_id=1, source_target_pairs={{0,0},{9,1},{18,2},{27,3}} | collective-permute-start | bytes 786440 | tf_op jit(solution)/shard_map/ppermute | solution.py:503
  50.7 7.1 %collective-permute-start.13 = (bf16[128,384]{1,0:T(8,128)(2,1)S(1)}, bf16[128,384]{1,0:T(8,128)(2,1)S(1)}, u32[]{:S(2)}, u32[]{:S(2)}) collective-permute-start(bf16[128,384]{1,0:T(8,128)(2,1)S(1)} %get-tuple-element.69), channel_id=1, source_target_pairs={{0,1},{1,0},{2,3},{3,2},{4,5},{5,4},{6,7},{7,6},{8,9},{9,8},{10,11... | collective-permute-start | bytes 294920 | tf_op jit(solution)/shard_map/ppermute | solution.py:508
  55.9 5.8 %collective-permute-start.14 = (bf16[144,512]{1,0:T(8,128)(2,1)S(1)}, bf16[144,512]{1,0:T(8,128)(2,1)S(1)}, u32[]{:S(2)}, u32[]{:S(2)}) collective-permute-start(bf16[144,512]{1,0:T(8,128)(2,1)S(1)} %shard_map.83.refs_0_.refs_2_), channel_id=1, source_target_pairs={{0,1},{1,0},{2,3},{3,2},{4,5},{5,4},{6,7},{7,6},{8,9},{9,8},{10,11... | collective-permute-start | bytes 442376 | tf_op jit(solution)/shard_map/ppermute | solution.py:508
  57.8 7.4 %collective-permute-start.15 = (bf16[128,384]{1,0:T(8,128)(2,1)S(1)}, bf16[128,384]{1,0:T(8,128)(2,1)}, u32[]{:S(2)}, u32[]{:S(2)}) collective-permute-start(bf16[128,384]{1,0:T(8,128)(2,1)S(1)} %shard_map.84.left_ref), channel_id=1, source_target_pairs={{0,2},{1,3},{2,0},{3,1},{4,6},{5,7},{6,4},{7,5},{8,10},{9,11},{10,... | collective-permute-start | bytes 294920 | tf_op jit(solution)/shard_map/ppermute | solution.py:508
  65.2 14.1 %collective-permute-start.16 = (bf16[4,64,1024]{2,1,0:T(8,128)(2,1)S(1)}, bf16[4,64,1024]{2,1,0:T(8,128)(2,1)S(1)}, u32[]{:S(2)}, u32[]{:S(2)}) collective-permute-start(bf16[4,64,1024]{2,1,0:T(8,128)(2,1)S(1)} %shard_map.87), channel_id=1, source_target_pairs={{0,28},{1,29},{2,30},{3,31},{4,0},{5,1},{6,2},{7,3},{8,4},{9,5},{1... | collective-permute-start | bytes 1572872 | tf_op jit(solution)/shard_map/ppermute | solution.py:474
  65.2 6.0 %collective-permute-start.21 = (bf16[256,128]{1,0:T(8,128)(2,1)S(1)}, bf16[256,128]{1,0:T(8,128)(2,1)S(1)}, u32[]{:S(2)}, u32[]{:S(2)}) collective-permute-start(bf16[256,128]{1,0:T(8,128)(2,1)S(1)} %get-tuple-element.80), channel_id=1, source_target_pairs={{0,31},{1,28},{2,29},{3,30},{4,3},{5,0},{6,1},{7,2},{8,7},{9,4},{1... | collective-permute-start | bytes 196616 | tf_op jit(solution)/shard_map/ppermute | solution.py:474
  69.8 8.3 %collective-permute-start.17 = (bf16[128,384]{1,0:T(8,128)(2,1)S(1)}, bf16[128,384]{1,0:T(8,128)(2,1)S(1)}, u32[]{:S(2)}, u32[]{:S(2)}) collective-permute-start(bf16[128,384]{1,0:T(8,128)(2,1)S(1)} %shard_map.88.refs_0_), channel_id=1, source_target_pairs={{0,1},{1,0},{2,3},{3,2},{4,5},{5,4},{6,7},{7,6},{8,9},{9,8},{10,11... | collective-permute-start | bytes 294920 | tf_op jit(solution)/shard_map/ppermute | solution.py:508
  69.9 5.3 %collective-permute-start.20 = (bf16[256,128]{1,0:T(8,128)(2,1)S(1)}, bf16[256,128]{1,0:T(8,128)(2,1)S(1)}, u32[]{:S(2)}, u32[]{:S(2)}) collective-permute-start(bf16[256,128]{1,0:T(8,128)(2,1)S(1)} %get-tuple-element.80), channel_id=1, source_target_pairs={{0,30},{1,31},{2,28},{3,29},{4,2},{5,3},{6,0},{7,1},{8,6},{9,7},{1... | collective-permute-start | bytes 196616 | tf_op jit(solution)/shard_map/ppermute | solution.py:474
  70.2 7.9 %collective-permute-start.19 = (bf16[256,128]{1,0:T(8,128)(2,1)S(1)}, bf16[256,128]{1,0:T(8,128)(2,1)S(1)}, u32[]{:S(2)}, u32[]{:S(2)}) collective-permute-start(bf16[256,128]{1,0:T(8,128)(2,1)S(1)} %get-tuple-element.80), channel_id=1, source_target_pairs={{0,29},{1,30},{2,31},{3,28},{4,1},{5,2},{6,3},{7,0},{8,5},{9,6},{1... | collective-permute-start | bytes 196616 | tf_op jit(solution)/shard_map/ppermute | solution.py:474
  71.2 6.8 %collective-permute-start.18 = (bf16[256,128]{1,0:T(8,128)(2,1)S(1)}, bf16[256,128]{1,0:T(8,128)(2,1)S(1)}, u32[]{:S(2)}, u32[]{:S(2)}) collective-permute-start(bf16[256,128]{1,0:T(8,128)(2,1)S(1)} %get-tuple-element.80), channel_id=1, source_target_pairs={{0,28},{1,29},{2,30},{3,31},{4,0},{5,1},{6,2},{7,3},{8,4},{9,5},{1... | collective-permute-start | bytes 196616 | tf_op jit(solution)/shard_map/ppermute | solution.py:474
  80.1 6.2 %collective-permute-start.22 = (bf16[64,1024]{1,0:T(8,128)(2,1)S(1)}, bf16[64,1024]{1,0:T(8,128)(2,1)S(1)}, u32[]{:S(2)}, u32[]{:S(2)}) collective-permute-start(bf16[64,1024]{1,0:T(8,128)(2,1)S(1)} %get-tuple-element.88), channel_id=1, source_target_pairs={{0,3},{1,0},{2,1},{3,2},{4,7},{5,4},{6,5},{7,6},{8,11},{9,8},{10,9... | collective-permute-start | bytes 393224 | tf_op jit(solution)/shard_map/ppermute | solution.py:460
  81.2 12.2 %collective-permute-start.23 = (bf16[64,1024]{1,0:T(8,128)(2,1)S(1)}, bf16[64,1024]{1,0:T(8,128)(2,1)S(1)}, u32[]{:S(2)}, u32[]{:S(2)}) collective-permute-start(bf16[64,1024]{1,0:T(8,128)(2,1)S(1)} %get-tuple-element.89), channel_id=1, source_target_pairs={{0,2},{1,3},{2,0},{3,1},{4,6},{5,7},{6,4},{7,5},{8,10},{9,11},{10,... | collective-permute-start | bytes 393224 | tf_op jit(solution)/shard_map/ppermute | solution.py:460
  81.2 12.2 %collective-permute-start.24 = (bf16[64,1024]{1,0:T(8,128)(2,1)S(1)}, bf16[64,1024]{1,0:T(8,128)(2,1)S(1)}, u32[]{:S(2)}, u32[]{:S(2)}) collective-permute-start(bf16[64,1024]{1,0:T(8,128)(2,1)S(1)} %get-tuple-element.90), channel_id=1, source_target_pairs={{0,1},{1,2},{2,3},{3,0},{4,5},{5,6},{6,7},{7,4},{8,9},{9,10},{10,1... | collective-permute-start | bytes 393224 | tf_op jit(solution)/shard_map/ppermute | solution.py:460

commit v7 on v6

--- a/solution.py
+++ b/solution.py
@@ -149,7 +149,7 @@
                 facts = jnp.where(place == 2 * t + index, value, facts)
         for out_ref, lanes in zip(outs, (facts, jnp.zeros((extra, LANES), F32))):
             out_ref[half * seq :, :LANES] = lanes.astype(BF16)
-            out_ref[half * seq :, LANES:] = jnp.broadcast_to(sums, (extra, wide)).astype(BF16)
+            out_ref[half * seq :, LANES:] = two_terms(sums, extra)
 
     outs = [shape(half * seq + extra, wide + head)] * 2
     return kernel_call(body, outs, [me], [*pieces, *scales, project, output])
@@ -176,9 +176,19 @@
     return kernel_call(body, [shape(count // 2 * seq, wide)] * 2, [me], [*pieces, project])
 
 
-def add_two(left, right):
+def two_terms(row, rows):
+    high, low = split_two(row)
+    place = lax.broadcasted_iota(jnp.int32, (rows, row.shape[1]), 0)
+    return jnp.where(place % 2 == 0, high, low).astype(BF16)
+
+
+def add_two(left, right, tail=None):
     def body(left_ref, right_ref, out_ref):
-        out_ref[...] = (left_ref[...].astype(F32) + right_ref[...].astype(F32)).astype(BF16)
+        total = left_ref[...].astype(F32) + right_ref[...].astype(F32)
+        out_ref[...] = total.astype(BF16)
+        if tail is not None:
+            means = total[tail : tail + 1, LANES:] + total[tail + 1 : tail + 2, LANES:]
+            out_ref[tail:, LANES:] = two_terms(means, left.shape[0] - tail)
 
     return kernel_call(body, [shape(*left.shape)], [], [left, right])[0]
 
@@ -224,7 +234,7 @@
     slope = scale * (jnp.sum(spread * projected, axis=-1, keepdims=True) / width)
     lane = lax.broadcasted_iota(jnp.int32, (rows, LANES), 1)
     numbers_ref[...] = jnp.where(lane == 0, scale, jnp.where(lane == 1, offset, slope))
-    return proj_grad, offset, slope
+    return proj_grad, slope
 
 
 def all_rows(half_refs, seq, half, columns):
@@ -241,6 +251,11 @@
     return jnp.concatenate(columns, axis=0)
 
 
+def row_means(half_refs, seq, half):
+    facts = half_refs[0][half * seq :, LANES:].astype(F32)
+    return facts[:1] + facts[1:2]
+
+
 def attention_outs(rows, head):
     return [shape(rows, 3 * head), shape(rows, head), shape(rows, LANES, kind=F32)]
 
@@ -257,13 +272,13 @@
             rows = block_rows(me_ref, j, count, seq)
             rows_ref[rows, :head] = dot(piece_refs[j][1], below)
             rows_ref[rows, head:] = dot(piece_refs[j][0], below)
-        product_ref[...] = dot(project_ref[...], below, CONTRACT_FIRST).astype(BF16)
+        product_ref[...] = dot(project_ref[...], below, CONTRACT_FIRST)
         sums = jnp.sum(below.astype(F32), axis=0, keepdims=True)
         sums_ref[...] = jnp.broadcast_to(sums, sums_ref.shape)
 
     outs = [
         shape(count * seq, 2 * head, kind=F32),
-        shape(wide, head),
+        shape(wide, head, kind=F32),
         shape(8, head, kind=F32),
     ]
     return kernel_call(body, outs, [me], [*pieces, project, below])
@@ -277,17 +292,23 @@
         mine, (rows_ref, product_ref, sums_ref), refs = refs[:2], refs[2:5], refs[5:]
         top_refs, (below_ref, *outs, head_ref) = refs[:runs], refs[runs:]
         scale = scale_column(mine, 0, ticks, seq, half)
-        proj_grad, offset, slope = attention_back(
+        row_mean = row_means(mine, seq, half)
+        proj_grad, slope = attention_back(
             all_rows(mine, seq, half, slice(0, wide)),
             all_rows(mine, seq, half, slice(wide, wide + head)).astype(BF16),
-            mine[0][half * seq :, LANES:].astype(F32)[:1],
+            row_mean,
             scale,
             seq,
             outs,
             width,
         )
-        across = dot(proj_grad, product_ref[...])
-        change = scale * across - offset * sums_ref[:1, :] - slope * rows_ref[:, head:]
+        centered = [
+            product_ref[start : start + LANES, :]
+            - column(row_mean[:, start : start + LANES])[:, :1] * sums_ref[:1, :]
+            for start in range(0, wide, LANES)
+        ]
+        across = dot(proj_grad, jnp.concatenate(centered, axis=0).astype(BF16))
+        change = scale * across - slope * rows_ref[:, head:]
         heads = (rows_ref[:, :head] + change).astype(BF16)
         for parity in range(2):
             for block in range(half):
@@ -335,7 +356,7 @@
         attention_back(
             all_rows(mine, seq, half, slice(None)),
             head_ref[...],
-            facts[0][half * seq :, LANES:].astype(F32)[:1],
+            row_means(facts, seq, half),
             scale_column(facts, 1, ticks, seq, half),
             seq,
             outs,
@@ -538,7 +559,7 @@
     later_sent = after(tuple(later_sent), other)
     later = [shift(later_sent[j], j) for j in others]
     early = [later[j] for j in [2] if j < count]
-    total = add_two(after(mine, below, *early), exchanged(other, 1))
+    total = add_two(after(mine, below, *early), exchanged(other, 1), half * seq)
     if moved is not None:
         blocks = join_pieces(after(blocks, total), moved)
     tops = [owner_to_first(blocks, run) for run in range(pipe // count)]
@@ -547,7 +568,7 @@
     step = 2
     while step < count:
         received = exchanged(total, step)
-        total = add_two(after(total, later_other), received)
+        total = add_two(after(total, later_other), received, half * seq)
         step *= 2
     halves = [total, exchanged(total, 1)]
     later_total = add_two(later_mine, exchanged(later_other, 1))

time: 94.5 us -> 94.5 us (level)
  transfers between devices with their start and end apart: 25 -> 25, of which waited for: 10 -> 10; matrix products, arithmetic and copies ran while one was open for 0% -> 0% of each run, Pallas kernels for 10% -> 11%
where the time goes in v7:
time: 94.5 us; the launch traced here: 94.2 us
  waiting for transfers between devices  40.9 us (43%)
  starting transfers between devices  37.4 us (40%)
  Pallas kernels  12.6 us (13%)
  local copies, waits for them, and re-layouts  2.34 us (2%)
    ppermute x9, starting transfers between devices, shift(): lax.ppermute(value, 'dp', [(i, (i + steps) % count) for i in range(count)])  20.1 us
    ppermute x2, waiting for transfers between devices, toward_owner(): return lax.ppermute(blocks, BOTH, pairs)  18.8 us
    pallas_call x18, Pallas kernels, kernel_call(): pl.pallas_call(body, out_shape=tuple(outs), in_specs=[pl.BlockSpec(memory...  12.6 us
    ppermute x6, waiting for transfers between devices, exchanged(): return lax.ppermute(value, 'dp', [(i, i ^ step) for i in range(count)])  8.83 us
    ppermute x9, waiting for transfers between devices, shift(): lax.ppermute(value, 'dp', [(i, (i + steps) % count) for i in range(count)])  7.45 us
    ppermute x5, starting transfers between devices, down(): return lax.ppermute(value, BOTH, pairs)  6.05 us
    ppermute x5, waiting for transfers between devices, down(): return lax.ppermute(value, BOTH, pairs)  5.77 us
    ppermute x6, starting transfers between devices, exchanged(): return lax.ppermute(value, 'dp', [(i, i ^ step) for i in range(count)])  5.76 us
  transfers between devices with their start and end apart: 25, of which 10 were waited for; matrix products, arithmetic and copies ran while one was open for 0% of the time, Pallas kernels for 11%

profile of v7, /device:TPU:0, one launch (start us, length us, event | category | flops | bytes accessed | tf_op | source)
XLA Modules:
  0.0 94.2 jit_solution(7799804880778194493)
XLA Ops:
  0.7 1.3 %copy-done.1 = bf16[1,2,64,4096]{3,2,1,0:T(8,128)(2,1)S(1)} copy-done((bf16[1,2,64,4096]{3,2,1,0:T(8,128)(2,1)S(1)}, bf16[1,2,64,4096]{3,2,1,0:T(8,128)(2,1)}, u32[]{:S(2)}) %copy-start.1) | copy-done | bytes 1048600
  1.9 1.0 %copy-done.2 = bf16[1,64,4096]{2,1,0:T(8,128)(2,1)S(1)} copy-done((bf16[1,64,4096]{2,1,0:T(8,128)(2,1)S(1)}, bf16[1,64,4096]{2,1,0:T(8,128)(2,1)}, u32[]{:S(2)}) %copy-start.2) | copy-done | bytes 524312
  3.0 0.4 shard_map.76
  3.4 3.1 %collective-permute-start = (bf16[2,64,1024]{2,1,0:T(8,128)(2,1)S(1)}, bf16[2,64,1024]{2,1,0:T(8,128)(2,1)S(1)}, u32[]{:S(2)}, u32[]{:S(2)}) collective-permute-start(bf16[2,64,1024]{2,1,0:T(8,128)(2,1)S(1)} %get-tuple-element.48), channel_id=1, source_target_pairs={{0,1},{1,2},{2,3},{3,0},{4,5},{5,6},{6,7},{7,4},{8,9},{9,10},{10,1... | collective-permute-start | bytes 786440 | tf_op jit(solution)/shard_map/ppermute | solution.py:481
  6.5 2.6 %collective-permute-start.1 = (bf16[2,64,1024]{2,1,0:T(8,128)(2,1)S(1)}, bf16[2,64,1024]{2,1,0:T(8,128)(2,1)S(1)}, u32[]{:S(2)}, u32[]{:S(2)}) collective-permute-start(bf16[2,64,1024]{2,1,0:T(8,128)(2,1)S(1)} %get-tuple-element.49), channel_id=1, source_target_pairs={{0,2},{1,3},{2,0},{3,1},{4,6},{5,7},{6,4},{7,5},{8,10},{9,11},{10,... | collective-permute-start | bytes 786440 | tf_op jit(solution)/shard_map/ppermute | solution.py:481
  9.1 1.3 %collective-permute-start.2 = (bf16[2,64,1024]{2,1,0:T(8,128)(2,1)S(1)}, bf16[2,64,1024]{2,1,0:T(8,128)(2,1)S(1)}, u32[]{:S(2)}, u32[]{:S(2)}) collective-permute-start(bf16[2,64,1024]{2,1,0:T(8,128)(2,1)S(1)} %get-tuple-element.50), channel_id=1, source_target_pairs={{0,3},{1,0},{2,1},{3,2},{4,7},{5,4},{6,5},{7,6},{8,11},{9,8},{10,9... | collective-permute-start | bytes 786440 | tf_op jit(solution)/shard_map/ppermute | solution.py:481
  10.4 1.3 %collective-permute-start.3 = (bf16[1,64,512]{2,1,0:T(8,128)(2,1)S(1)}, bf16[1,64,512]{2,1,0:T(8,128)(2,1)S(1)}, u32[]{:S(2)}, u32[]{:S(2)}) collective-permute-start(bf16[1,64,512]{2,1,0:T(8,128)(2,1)S(1)} %copy-done.4), channel_id=1, source_target_pairs={{1,0},{3,2},{5,4},{7,6},{8,9},{10,11},{12,13},{14,15},{17,16},{19,... | collective-permute-start | bytes 196616 | tf_op jit(solution)/shard_map/ppermute | solution.py:518
  11.7 0.4 shard_map.77
  12.1 15.3 %collective-permute-done.3.right_ref = bf16[1,64,512]{2,1,0:T(8,128)(2,1)S(1)} collective-permute-done((bf16[1,64,512]{2,1,0:T(8,128)(2,1)S(1)}, bf16[1,64,512]{2,1,0:T(8,128)(2,1)S(1)}, u32[]{:S(2)}, u32[]{:S(2)}) %collective-permute-start.3) | collective-permute-done | bytes 65568 | tf_op jit(solution)/shard_map/ppermute | solution.py:518
  27.5 0.6 shard_map.79
  28.1 0.1 collective-permute-start.7
  28.2 3.8 %collective-permute-start.5 = (bf16[64,1024]{1,0:T(8,128)(2,1)S(1)}, bf16[64,1024]{1,0:T(8,128)(2,1)S(1)}, u32[]{:S(2)}, u32[]{:S(2)}) collective-permute-start(bf16[64,1024]{1,0:T(8,128)(2,1)S(1)} %get-tuple-element.62), channel_id=1, source_target_pairs={{0,2},{1,3},{2,0},{3,1},{4,6},{5,7},{6,4},{7,5},{8,10},{9,11},{10,... | collective-permute-start | bytes 393224 | tf_op jit(solution)/shard_map/ppermute | solution.py:481
  32.0 2.6 %collective-permute-start.8 = (bf16[144,512]{1,0:T(8,128)(2,1)S(1)}, bf16[144,512]{1,0:T(8,128)(2,1)S(1)}, u32[]{:S(2)}, u32[]{:S(2)}) collective-permute-start(bf16[144,512]{1,0:T(8,128)(2,1)S(1)} %get-tuple-element.59), channel_id=1, source_target_pairs={{0,1},{1,0},{2,3},{3,2},{4,5},{5,4},{6,7},{7,6},{8,9},{9,8},{10,11... | collective-permute-start | bytes 442376 | tf_op jit(solution)/shard_map/ppermute | solution.py:529
  34.6 1.3 %collective-permute-start.9 = (bf16[2,64,512]{2,1,0:T(8,128)(2,1)S(1)}, bf16[2,64,512]{2,1,0:T(8,128)(2,1)S(1)}, u32[]{:S(2)}, u32[]{:S(2)}) collective-permute-start(bf16[2,64,512]{2,1,0:T(8,128)(2,1)S(1)} %shard_map.78.left_ref), channel_id=1, source_target_pairs={{2,0},{6,4},{11,9},{15,13},{16,18},{20,22},{25,27},{29,31}} | collective-permute-start | bytes 393224 | tf_op jit(solution)/shard_map/ppermute | solution.py:518
  35.9 0.1 collective-permute-start.4
  35.9 7.1 %collective-permute-start.6 = (bf16[64,1024]{1,0:T(8,128)(2,1)S(1)}, bf16[64,1024]{1,0:T(8,128)(2,1)S(1)}, u32[]{:S(2)}, u32[]{:S(2)}) collective-permute-start(bf16[64,1024]{1,0:T(8,128)(2,1)S(1)} %get-tuple-element.63), channel_id=1, source_target_pairs={{0,3},{1,0},{2,1},{3,2},{4,7},{5,4},{6,5},{7,6},{8,11},{9,8},{10,9... | collective-permute-start | bytes 393224 | tf_op jit(solution)/shard_map/ppermute | solution.py:481
  43.1 0.1 collective-permute-start.12
  43.2 3.5 %collective-permute-done.9.right_ref = bf16[2,64,512]{2,1,0:T(8,128)(2,1)S(1)} collective-permute-done((bf16[2,64,512]{2,1,0:T(8,128)(2,1)S(1)}, bf16[2,64,512]{2,1,0:T(8,128)(2,1)S(1)}, u32[]{:S(2)}, u32[]{:S(2)}) %collective-permute-start.9) | collective-permute-done | bytes 131104 | tf_op jit(solution)/shard_map/ppermute | solution.py:518
  46.6 0.7 shard_map.81
  47.4 1.3 %collective-permute-start.11 = (bf16[4,64,512]{2,1,0:T(8,128)(2,1)}, bf16[4,64,512]{2,1,0:T(8,128)(2,1)S(1)}, u32[]{:S(2)}, u32[]{:S(2)}) collective-permute-start(bf16[4,64,512]{2,1,0:T(8,128)(2,1)} %shard_map.81), channel_id=1, source_target_pairs={{4,0},{13,1},{22,2},{31,3}} | collective-permute-start | bytes 786440 | tf_op jit(solution)/shard_map/ppermute | solution.py:524
  48.7 1.6 %collective-permute-start.10 = (bf16[4,64,512]{2,1,0:T(8,128)(2,1)}, bf16[4,64,512]{2,1,0:T(8,128)(2,1)S(1)}, u32[]{:S(2)}, u32[]{:S(2)}) collective-permute-start(bf16[4,64,512]{2,1,0:T(8,128)(2,1)} %shard_map.81), channel_id=1, source_target_pairs={{0,0},{9,1},{18,2},{27,3}} | collective-permute-start | bytes 786440 | tf_op jit(solution)/shard_map/ppermute | solution.py:524
  50.3 0.4 shard_map.82
  50.7 2.9 %collective-permute-start.13 = (bf16[128,384]{1,0:T(8,128)(2,1)S(1)}, bf16[128,384]{1,0:T(8,128)(2,1)S(1)}, u32[]{:S(2)}, u32[]{:S(2)}) collective-permute-start(bf16[128,384]{1,0:T(8,128)(2,1)S(1)} %get-tuple-element.69), channel_id=1, source_target_pairs={{0,1},{1,0},{2,3},{3,2},{4,5},{5,4},{6,7},{7,6},{8,9},{9,8},{10,11... | collective-permute-start | bytes 294920 | tf_op jit(solution)/shard_map/ppermute | solution.py:529
  53.6 2.2 %collective-permute-done.12.right_ref = bf16[144,512]{1,0:T(8,128)(2,1)S(1)} collective-permute-done((bf16[144,512]{1,0:T(8,128)(2,1)S(1)}, bf16[144,512]{1,0:T(8,128)(2,1)S(1)}, u32[]{:S(2)}, u32[]{:S(2)}) %collective-permute-start.12) | collective-permute-done | bytes 147488 | tf_op jit(solution)/shard_map/ppermute | solution.py:529
  55.9 0.1 collective-permute-start.14
  55.9 1.9 %collective-permute-done.13.right_ref = bf16[128,384]{1,0:T(8,128)(2,1)S(1)} collective-permute-done((bf16[128,384]{1,0:T(8,128)(2,1)S(1)}, bf16[128,384]{1,0:T(8,128)(2,1)S(1)}, u32[]{:S(2)}, u32[]{:S(2)}) %collective-permute-start.13) | collective-permute-done | bytes 98336 | tf_op jit(solution)/shard_map/ppermute | solution.py:529
  57.8 0.1 collective-permute-start.15
  57.9 0.7 shard_map.85
  58.6 3.1 %collective-permute-done.14.refs_1_.refs_3_ = bf16[144,512]{1,0:T(8,128)(2,1)S(1)} collective-permute-done((bf16[144,512]{1,0:T(8,128)(2,1)S(1)}, bf16[144,512]{1,0:T(8,128)(2,1)S(1)}, u32[]{:S(2)}, u32[]{:S(2)}) %collective-permute-start.14) | collective-permute-done | bytes 147488 | tf_op jit(solution)/shard_map/ppermute | solution.py:529
  61.7 1.6 %shard_map.86 = (bf16[256,384]{1,0:T(8,128)(2,1)S(1)}, bf16[256,128]{1,0:T(8,128)(2,1)S(1)}, f32[256,128]{1,0:T(8,128)S(1)}, bf16[256,128]{1,0:T(8,128)(2,1)S(1)}) custom-call(s32[1]{0:T(128)} %bitcast.me_ref, s32[1]{0:T(128)} %bitcast.5.first_ref, bf16[144,512]{1,0:T(8,128)(2,1)S(1)} %shard_map.83.refs_0_.refs_2_, ...), custom_call_target="tpu_custom_call" | custom-call | flops 1 | bytes 1 | tf_op jit(solution)/shard_map/pallas_call | solution.py:26
  63.3 0.2 shard_map.87
  63.5 1.7 %collective-permute-done.15.right_ref = bf16[128,384]{1,0:T(8,128)(2,1)} collective-permute-done((bf16[128,384]{1,0:T(8,128)(2,1)S(1)}, bf16[128,384]{1,0:T(8,128)(2,1)}, u32[]{:S(2)}, u32[]{:S(2)}) %collective-permute-start.15) | collective-permute-done | bytes 98336 | tf_op jit(solution)/shard_map/ppermute | solution.py:529
  65.2 3.7 %collective-permute-start.21 = (bf16[256,128]{1,0:T(8,128)(2,1)S(1)}, bf16[256,128]{1,0:T(8,128)(2,1)S(1)}, u32[]{:S(2)}, u32[]{:S(2)}) collective-permute-start(bf16[256,128]{1,0:T(8,128)(2,1)S(1)} %get-tuple-element.80), channel_id=1, source_target_pairs={{0,31},{1,28},{2,29},{3,30},{4,3},{5,0},{6,1},{7,2},{8,7},{9,4},{1... | collective-permute-start | bytes 196616 | tf_op jit(solution)/shard_map/ppermute | solution.py:495
  68.9 0.9 shard_map.88.refs_0_
  69.8 0.1 collective-permute-start.17
  69.9 0.3 collective-permute-start.20
  70.2 1.1 %collective-permute-start.19 = (bf16[256,128]{1,0:T(8,128)(2,1)S(1)}, bf16[256,128]{1,0:T(8,128)(2,1)S(1)}, u32[]{:S(2)}, u32[]{:S(2)}) collective-permute-start(bf16[256,128]{1,0:T(8,128)(2,1)S(1)} %get-tuple-element.80), channel_id=1, source_target_pairs={{0,29},{1,30},{2,31},{3,28},{4,1},{5,2},{6,3},{7,0},{8,5},{9,6},{1... | collective-permute-start | bytes 196616 | tf_op jit(solution)/shard_map/ppermute | solution.py:495
  71.2 1.0 %collective-permute-start.18 = (bf16[256,128]{1,0:T(8,128)(2,1)S(1)}, bf16[256,128]{1,0:T(8,128)(2,1)S(1)}, u32[]{:S(2)}, u32[]{:S(2)}) collective-permute-start(bf16[256,128]{1,0:T(8,128)(2,1)S(1)} %get-tuple-element.80), channel_id=1, source_target_pairs={{0,28},{1,29},{2,30},{3,31},{4,0},{5,1},{6,2},{7,3},{8,4},{9,5},{1... | collective-permute-start | bytes 196616 | tf_op jit(solution)/shard_map/ppermute | solution.py:495
  72.3 2.9 %collective-permute-done.20.refs_2_ = bf16[256,128]{1,0:T(8,128)(2,1)S(1)} collective-permute-done((bf16[256,128]{1,0:T(8,128)(2,1)S(1)}, bf16[256,128]{1,0:T(8,128)(2,1)S(1)}, u32[]{:S(2)}, u32[]{:S(2)}) %collective-permute-start.20) | collective-permute-done | bytes 65568 | tf_op jit(solution)/shard_map/ppermute | solution.py:495
  75.1 2.9 %collective-permute-done.19.refs_1_ = bf16[256,128]{1,0:T(8,128)(2,1)S(1)} collective-permute-done((bf16[256,128]{1,0:T(8,128)(2,1)S(1)}, bf16[256,128]{1,0:T(8,128)(2,1)S(1)}, u32[]{:S(2)}, u32[]{:S(2)}) %collective-permute-start.19) | collective-permute-done | bytes 65568 | tf_op jit(solution)/shard_map/ppermute | solution.py:495
  78.1 1.2 %shard_map.90 = (bf16[256,384]{1,0:T(8,128)(2,1)S(1)}, bf16[256,128]{1,0:T(8,128)(2,1)S(1)}, f32[256,128]{1,0:T(8,128)S(1)}) custom-call(bf16[128,384]{1,0:T(8,128)(2,1)S(1)} %shard_map.88.refs_0_, bf16[128,384]{1,0:T(8,128)(2,1)S(1)} %collective-permute-done.17.refs_1_, bf16[144,512]{1,0:T(8,128)(2,1)S(1)} %shard_map.83.refs_0_.refs_2_, ...), custom_call_target="tpu_custom_call" | custom-call | flops 1 | bytes 1 | tf_op jit(solution)/shard_map/pallas_call | solution.py:26
  79.3 0.8 shard_map.91
  80.1 1.1 %collective-permute-start.22 = (bf16[64,1024]{1,0:T(8,128)(2,1)S(1)}, bf16[64,1024]{1,0:T(8,128)(2,1)S(1)}, u32[]{:S(2)}, u32[]{:S(2)}) collective-permute-start(bf16[64,1024]{1,0:T(8,128)(2,1)S(1)} %get-tuple-element.88), channel_id=1, source_target_pairs={{0,3},{1,0},{2,1},{3,2},{4,7},{5,4},{6,5},{7,6},{8,11},{9,8},{10,9... | collective-permute-start | bytes 393224 | tf_op jit(solution)/shard_map/ppermute | solution.py:481
  81.2 1.0 %collective-permute-start.24 = (bf16[64,1024]{1,0:T(8,128)(2,1)S(1)}, bf16[64,1024]{1,0:T(8,128)(2,1)S(1)}, u32[]{:S(2)}, u32[]{:S(2)}) collective-permute-start(bf16[64,1024]{1,0:T(8,128)(2,1)S(1)} %get-tuple-element.90), channel_id=1, source_target_pairs={{0,1},{1,2},{2,3},{3,0},{4,5},{5,6},{6,7},{7,4},{8,9},{9,10},{10,1... | collective-permute-start | bytes 393224 | tf_op jit(solution)/shard_map/ppermute | solution.py:481
  82.2 3.7 %shard_map.92 = (f32[1024,384]{1,0:T(8,128)}, f32[1024,128]{1,0:T(8,128)}) custom-call(s32[1]{0:T(128)} %bitcast.me_ref, bf16[2,64,1024]{2,1,0:T(8,128)(2,1)S(1)} %get-tuple-element.47.refs_0_.refs_2_, bf16[2,64,1024]{2,1,0:T(8,128)(2,1)S(1)} %collective-permute-done.refs_1_.refs_3_, bf16[2,64,1024]{2,1,0:T(8,128)(2,1)S(1)} %collective-permute-done.1.refs_2_.refs_4_, ...), custom_call_target="tpu_custom_call" | custom-call | flops 1 | bytes 1 | tf_op jit(solution)/shard_map/pallas_call | solution.py:26
  85.9 0.5 collective-permute-done.22.refs_1_
  86.4 6.9 %collective-permute-done.23.refs_2_ = bf16[64,1024]{1,0:T(8,128)(2,1)S(1)} collective-permute-done((bf16[64,1024]{1,0:T(8,128)(2,1)S(1)}, bf16[64,1024]{1,0:T(8,128)(2,1)S(1)}, u32[]{:S(2)}, u32[]{:S(2)}) %collective-permute-start.23) | collective-permute-done | bytes 131104 | tf_op jit(solution)/shard_map/ppermute | solution.py:481
  93.3 0.8 shard_map.93
  (30 shorter events, 0.2 us)
Async XLA Ops:
  0.6 26.9 %copy-start = (bf16[1,1024,384]{2,1,0:T(8,128)(2,1)S(1)}, bf16[1,1024,384]{2,1,0:T(8,128)(2,1)}, u32[]{:S(2)}) copy-start(bf16[1,1024,384]{2,1,0:T(8,128)(2,1)} %param.8) | copy-start | bytes 2359300
  0.6 1.3 %copy-start.1 = (bf16[1,2,64,4096]{3,2,1,0:T(8,128)(2,1)S(1)}, bf16[1,2,64,4096]{3,2,1,0:T(8,128)(2,1)}, u32[]{:S(2)}) copy-start(bf16[1,2,64,4096]{3,2,1,0:T(8,128)(2,1)} %param.5) | copy-start | bytes 3145732
  1.9 1.0 %copy-start.2 = (bf16[1,64,4096]{2,1,0:T(8,128)(2,1)S(1)}, bf16[1,64,4096]{2,1,0:T(8,128)(2,1)}, u32[]{:S(2)}) copy-start(bf16[1,64,4096]{2,1,0:T(8,128)(2,1)} %param.6) | copy-start | bytes 1572868
  3.0 7.4 %copy-start.4 = (bf16[1,64,512]{2,1,0:T(8,128)(2,1)S(1)}, bf16[1,64,512]{2,1,0:T(8,128)(2,1)}, u32[]{:S(2)}) copy-start(bf16[1,64,512]{2,1,0:T(8,128)(2,1)} %left_ref) | copy-start | bytes 196612
  3.0 24.5 %copy-start.3 = (bf16[1,1024,128]{2,1,0:T(8,128)(2,1)S(1)}, bf16[1,1024,128]{2,1,0:T(8,128)(2,1)}, u32[]{:S(2)}) copy-start(bf16[1,1024,128]{2,1,0:T(8,128)(2,1)} %param.9) | copy-start | bytes 786436
  3.4 24.1 %collective-permute-start = (bf16[2,64,1024]{2,1,0:T(8,128)(2,1)S(1)}, bf16[2,64,1024]{2,1,0:T(8,128)(2,1)S(1)}, u32[]{:S(2)}, u32[]{:S(2)}) collective-permute-start(bf16[2,64,1024]{2,1,0:T(8,128)(2,1)S(1)} %get-tuple-element.48), channel_id=1, source_target_pairs={{0,1},{1,2},{2,3},{3,0},{4,5},{5,6},{6,7},{7,4},{8,9},{9,10},{10,1... | collective-permute-start | bytes 786440 | tf_op jit(solution)/shard_map/ppermute | solution.py:481
  6.5 21.0 %collective-permute-start.1 = (bf16[2,64,1024]{2,1,0:T(8,128)(2,1)S(1)}, bf16[2,64,1024]{2,1,0:T(8,128)(2,1)S(1)}, u32[]{:S(2)}, u32[]{:S(2)}) collective-permute-start(bf16[2,64,1024]{2,1,0:T(8,128)(2,1)S(1)} %get-tuple-element.49), channel_id=1, source_target_pairs={{0,2},{1,3},{2,0},{3,1},{4,6},{5,7},{6,4},{7,5},{8,10},{9,11},{10,... | collective-permute-start | bytes 786440 | tf_op jit(solution)/shard_map/ppermute | solution.py:481
  9.1 18.4 %collective-permute-start.2 = (bf16[2,64,1024]{2,1,0:T(8,128)(2,1)S(1)}, bf16[2,64,1024]{2,1,0:T(8,128)(2,1)S(1)}, u32[]{:S(2)}, u32[]{:S(2)}) collective-permute-start(bf16[2,64,1024]{2,1,0:T(8,128)(2,1)S(1)} %get-tuple-element.50), channel_id=1, source_target_pairs={{0,3},{1,0},{2,1},{3,2},{4,7},{5,4},{6,5},{7,6},{8,11},{9,8},{10,9... | collective-permute-start | bytes 786440 | tf_op jit(solution)/shard_map/ppermute | solution.py:481
  10.4 17.0 %collective-permute-start.3 = (bf16[1,64,512]{2,1,0:T(8,128)(2,1)S(1)}, bf16[1,64,512]{2,1,0:T(8,128)(2,1)S(1)}, u32[]{:S(2)}, u32[]{:S(2)}) collective-permute-start(bf16[1,64,512]{2,1,0:T(8,128)(2,1)S(1)} %copy-done.4), channel_id=1, source_target_pairs={{1,0},{3,2},{5,4},{7,6},{8,9},{10,11},{12,13},{14,15},{17,16},{19,... | collective-permute-start | bytes 196616 | tf_op jit(solution)/shard_map/ppermute | solution.py:518
  28.1 14.9 %collective-permute-start.7 = (bf16[1024,128]{1,0:T(8,128)(2,1)S(1)}, bf16[1024,128]{1,0:T(8,128)(2,1)S(1)}, u32[]{:S(2)}, u32[]{:S(2)}) collective-permute-start(bf16[1024,128]{1,0:T(8,128)(2,1)S(1)} %bitcast.18), channel_id=1, source_target_pairs={{0,4},{4,8},{8,12},{12,16},{16,20},{20,24},{24,28},{28,0},{1,5},{5... | collective-permute-start | bytes 786440 | tf_op jit(solution)/shard_map/ppermute | solution.py:556
  28.2 7.8 %collective-permute-start.5 = (bf16[64,1024]{1,0:T(8,128)(2,1)S(1)}, bf16[64,1024]{1,0:T(8,128)(2,1)S(1)}, u32[]{:S(2)}, u32[]{:S(2)}) collective-permute-start(bf16[64,1024]{1,0:T(8,128)(2,1)S(1)} %get-tuple-element.62), channel_id=1, source_target_pairs={{0,2},{1,3},{2,0},{3,1},{4,6},{5,7},{6,4},{7,5},{8,10},{9,11},{10,... | collective-permute-start | bytes 393224 | tf_op jit(solution)/shard_map/ppermute | solution.py:481
  32.0 11.0 %collective-permute-start.8 = (bf16[144,512]{1,0:T(8,128)(2,1)S(1)}, bf16[144,512]{1,0:T(8,128)(2,1)S(1)}, u32[]{:S(2)}, u32[]{:S(2)}) collective-permute-start(bf16[144,512]{1,0:T(8,128)(2,1)S(1)} %get-tuple-element.59), channel_id=1, source_target_pairs={{0,1},{1,0},{2,3},{3,2},{4,5},{5,4},{6,7},{7,6},{8,9},{9,8},{10,11... | collective-permute-start | bytes 442376 | tf_op jit(solution)/shard_map/ppermute | solution.py:529
  34.6 12.1 %collective-permute-start.9 = (bf16[2,64,512]{2,1,0:T(8,128)(2,1)S(1)}, bf16[2,64,512]{2,1,0:T(8,128)(2,1)S(1)}, u32[]{:S(2)}, u32[]{:S(2)}) collective-permute-start(bf16[2,64,512]{2,1,0:T(8,128)(2,1)S(1)} %shard_map.78.left_ref), channel_id=1, source_target_pairs={{2,0},{6,4},{11,9},{15,13},{16,18},{20,22},{25,27},{29,31}} | collective-permute-start | bytes 393224 | tf_op jit(solution)/shard_map/ppermute | solution.py:518
  35.9 14.4 %collective-permute-start.4 = (bf16[64,1024]{1,0:T(8,128)(2,1)S(1)}, bf16[64,1024]{1,0:T(8,128)(2,1)S(1)}, u32[]{:S(2)}, u32[]{:S(2)}) collective-permute-start(bf16[64,1024]{1,0:T(8,128)(2,1)S(1)} %get-tuple-element.61), channel_id=1, source_target_pairs={{0,1},{1,2},{2,3},{3,0},{4,5},{5,6},{6,7},{7,4},{8,9},{9,10},{10,1... | collective-permute-start | bytes 393224 | tf_op jit(solution)/shard_map/ppermute | solution.py:481
  35.9 14.3 %collective-permute-start.6 = (bf16[64,1024]{1,0:T(8,128)(2,1)S(1)}, bf16[64,1024]{1,0:T(8,128)(2,1)S(1)}, u32[]{:S(2)}, u32[]{:S(2)}) collective-permute-start(bf16[64,1024]{1,0:T(8,128)(2,1)S(1)} %get-tuple-element.63), channel_id=1, source_target_pairs={{0,3},{1,0},{2,1},{3,2},{4,7},{5,4},{6,5},{7,6},{8,11},{9,8},{10,9... | collective-permute-start | bytes 393224 | tf_op jit(solution)/shard_map/ppermute | solution.py:481
  43.1 12.7 %collective-permute-start.12 = (bf16[144,512]{1,0:T(8,128)(2,1)S(1)}, bf16[144,512]{1,0:T(8,128)(2,1)S(1)}, u32[]{:S(2)}, u32[]{:S(2)}) collective-permute-start(bf16[144,512]{1,0:T(8,128)(2,1)S(1)} %shard_map.80.left_ref), channel_id=1, source_target_pairs={{0,2},{1,3},{2,0},{3,1},{4,6},{5,7},{6,4},{7,5},{8,10},{9,11},{10,... | collective-permute-start | bytes 442376 | tf_op jit(solution)/shard_map/ppermute | solution.py:529
  47.4 11.3 %collective-permute-start.11 = (bf16[4,64,512]{2,1,0:T(8,128)(2,1)}, bf16[4,64,512]{2,1,0:T(8,128)(2,1)S(1)}, u32[]{:S(2)}, u32[]{:S(2)}) collective-permute-start(bf16[4,64,512]{2,1,0:T(8,128)(2,1)} %shard_map.81), channel_id=1, source_target_pairs={{4,0},{13,1},{22,2},{31,3}} | collective-permute-start | bytes 786440 | tf_op jit(solution)/shard_map/ppermute | solution.py:524
  48.7 10.0 %collective-permute-start.10 = (bf16[4,64,512]{2,1,0:T(8,128)(2,1)}, bf16[4,64,512]{2,1,0:T(8,128)(2,1)S(1)}, u32[]{:S(2)}, u32[]{:S(2)}) collective-permute-start(bf16[4,64,512]{2,1,0:T(8,128)(2,1)} %shard_map.81), channel_id=1, source_target_pairs={{0,0},{9,1},{18,2},{27,3}} | collective-permute-start | bytes 786440 | tf_op jit(solution)/shard_map/ppermute | solution.py:524
  50.7 7.1 %collective-permute-start.13 = (bf16[128,384]{1,0:T(8,128)(2,1)S(1)}, bf16[128,384]{1,0:T(8,128)(2,1)S(1)}, u32[]{:S(2)}, u32[]{:S(2)}) collective-permute-start(bf16[128,384]{1,0:T(8,128)(2,1)S(1)} %get-tuple-element.69), channel_id=1, source_target_pairs={{0,1},{1,0},{2,3},{3,2},{4,5},{5,4},{6,7},{7,6},{8,9},{9,8},{10,11... | collective-permute-start | bytes 294920 | tf_op jit(solution)/shard_map/ppermute | solution.py:529
  55.9 5.8 %collective-permute-start.14 = (bf16[144,512]{1,0:T(8,128)(2,1)S(1)}, bf16[144,512]{1,0:T(8,128)(2,1)S(1)}, u32[]{:S(2)}, u32[]{:S(2)}) collective-permute-start(bf16[144,512]{1,0:T(8,128)(2,1)S(1)} %shard_map.83.refs_0_.refs_2_), channel_id=1, source_target_pairs={{0,1},{1,0},{2,3},{3,2},{4,5},{5,4},{6,7},{7,6},{8,9},{9,8},{10,11... | collective-permute-start | bytes 442376 | tf_op jit(solution)/shard_map/ppermute | solution.py:529
  57.8 7.4 %collective-permute-start.15 = (bf16[128,384]{1,0:T(8,128)(2,1)S(1)}, bf16[128,384]{1,0:T(8,128)(2,1)}, u32[]{:S(2)}, u32[]{:S(2)}) collective-permute-start(bf16[128,384]{1,0:T(8,128)(2,1)S(1)} %shard_map.84.left_ref), channel_id=1, source_target_pairs={{0,2},{1,3},{2,0},{3,1},{4,6},{5,7},{6,4},{7,5},{8,10},{9,11},{10,... | collective-permute-start | bytes 294920 | tf_op jit(solution)/shard_map/ppermute | solution.py:529
  65.2 14.1 %collective-permute-start.16 = (bf16[4,64,1024]{2,1,0:T(8,128)(2,1)S(1)}, bf16[4,64,1024]{2,1,0:T(8,128)(2,1)S(1)}, u32[]{:S(2)}, u32[]{:S(2)}) collective-permute-start(bf16[4,64,1024]{2,1,0:T(8,128)(2,1)S(1)} %shard_map.87), channel_id=1, source_target_pairs={{0,28},{1,29},{2,30},{3,31},{4,0},{5,1},{6,2},{7,3},{8,4},{9,5},{1... | collective-permute-start | bytes 1572872 | tf_op jit(solution)/shard_map/ppermute | solution.py:495
  65.2 6.0 %collective-permute-start.21 = (bf16[256,128]{1,0:T(8,128)(2,1)S(1)}, bf16[256,128]{1,0:T(8,128)(2,1)S(1)}, u32[]{:S(2)}, u32[]{:S(2)}) collective-permute-start(bf16[256,128]{1,0:T(8,128)(2,1)S(1)} %get-tuple-element.80), channel_id=1, source_target_pairs={{0,31},{1,28},{2,29},{3,30},{4,3},{5,0},{6,1},{7,2},{8,7},{9,4},{1... | collective-permute-start | bytes 196616 | tf_op jit(solution)/shard_map/ppermute | solution.py:495
  69.8 8.3 %collective-permute-start.17 = (bf16[128,384]{1,0:T(8,128)(2,1)S(1)}, bf16[128,384]{1,0:T(8,128)(2,1)S(1)}, u32[]{:S(2)}, u32[]{:S(2)}) collective-permute-start(bf16[128,384]{1,0:T(8,128)(2,1)S(1)} %shard_map.88.refs_0_), channel_id=1, source_target_pairs={{0,1},{1,0},{2,3},{3,2},{4,5},{5,4},{6,7},{7,6},{8,9},{9,8},{10,11... | collective-permute-start | bytes 294920 | tf_op jit(solution)/shard_map/ppermute | solution.py:529
  69.9 5.3 %collective-permute-start.20 = (bf16[256,128]{1,0:T(8,128)(2,1)S(1)}, bf16[256,128]{1,0:T(8,128)(2,1)S(1)}, u32[]{:S(2)}, u32[]{:S(2)}) collective-permute-start(bf16[256,128]{1,0:T(8,128)(2,1)S(1)} %get-tuple-element.80), channel_id=1, source_target_pairs={{0,30},{1,31},{2,28},{3,29},{4,2},{5,3},{6,0},{7,1},{8,6},{9,7},{1... | collective-permute-start | bytes 196616 | tf_op jit(solution)/shard_map/ppermute | solution.py:495
  70.2 7.9 %collective-permute-start.19 = (bf16[256,128]{1,0:T(8,128)(2,1)S(1)}, bf16[256,128]{1,0:T(8,128)(2,1)S(1)}, u32[]{:S(2)}, u32[]{:S(2)}) collective-permute-start(bf16[256,128]{1,0:T(8,128)(2,1)S(1)} %get-tuple-element.80), channel_id=1, source_target_pairs={{0,29},{1,30},{2,31},{3,28},{4,1},{5,2},{6,3},{7,0},{8,5},{9,6},{1... | collective-permute-start | bytes 196616 | tf_op jit(solution)/shard_map/ppermute | solution.py:495
  71.2 6.8 %collective-permute-start.18 = (bf16[256,128]{1,0:T(8,128)(2,1)S(1)}, bf16[256,128]{1,0:T(8,128)(2,1)S(1)}, u32[]{:S(2)}, u32[]{:S(2)}) collective-permute-start(bf16[256,128]{1,0:T(8,128)(2,1)S(1)} %get-tuple-element.80), channel_id=1, source_target_pairs={{0,28},{1,29},{2,30},{3,31},{4,0},{5,1},{6,2},{7,3},{8,4},{9,5},{1... | collective-permute-start | bytes 196616 | tf_op jit(solution)/shard_map/ppermute | solution.py:495
  80.1 6.3 %collective-permute-start.22 = (bf16[64,1024]{1,0:T(8,128)(2,1)S(1)}, bf16[64,1024]{1,0:T(8,128)(2,1)S(1)}, u32[]{:S(2)}, u32[]{:S(2)}) collective-permute-start(bf16[64,1024]{1,0:T(8,128)(2,1)S(1)} %get-tuple-element.88), channel_id=1, source_target_pairs={{0,3},{1,0},{2,1},{3,2},{4,7},{5,4},{6,5},{7,6},{8,11},{9,8},{10,9... | collective-permute-start | bytes 393224 | tf_op jit(solution)/shard_map/ppermute | solution.py:481
  81.2 12.1 %collective-permute-start.23 = (bf16[64,1024]{1,0:T(8,128)(2,1)S(1)}, bf16[64,1024]{1,0:T(8,128)(2,1)S(1)}, u32[]{:S(2)}, u32[]{:S(2)}) collective-permute-start(bf16[64,1024]{1,0:T(8,128)(2,1)S(1)} %get-tuple-element.89), channel_id=1, source_target_pairs={{0,2},{1,3},{2,0},{3,1},{4,6},{5,7},{6,4},{7,5},{8,10},{9,11},{10,... | collective-permute-start | bytes 393224 | tf_op jit(solution)/shard_map/ppermute | solution.py:481
  81.2 12.1 %collective-permute-start.24 = (bf16[64,1024]{1,0:T(8,128)(2,1)S(1)}, bf16[64,1024]{1,0:T(8,128)(2,1)S(1)}, u32[]{:S(2)}, u32[]{:S(2)}) collective-permute-start(bf16[64,1024]{1,0:T(8,128)(2,1)S(1)} %get-tuple-element.90), channel_id=1, source_target_pairs={{0,1},{1,2},{2,3},{3,0},{4,5},{5,6},{6,7},{7,4},{8,9},{9,10},{10,1... | collective-permute-start | bytes 393224 | tf_op jit(solution)/shard_map/ppermute | solution.py:481

commit v8 on v7

--- a/solution.py
+++ b/solution.py
@@ -193,38 +193,45 @@
     return kernel_call(body, [shape(*left.shape)], [], [left, right])[0]
 
 
-def attention_back(projected, head_half, row_mean, scale, seq, outs, width):
-    grad_ref, mixed_ref, numbers_ref = outs
-    rows, head = head_half.shape
-    count = rows // seq
-    root = math.sqrt(head)
+def each(function, seq, *values):
+    count = values[0].shape[0] // seq
+    return jnp.concatenate(
+        [function(*(v[r * seq : (r + 1) * seq] for v in values)) for r in range(count)], axis=0
+    )
+
+
+def dot_last(left, right):
+    return dot(left, right, CONTRACT_LAST)
+
+
+def dot_first(left, right):
+    return dot(left, right, CONTRACT_FIRST)
+
+
+def attention_front(projected, seq, mixed_ref):
+    head = projected.shape[1] // 3
     query, query_scale = normalize(projected[:, :head])
     key, key_scale = normalize(projected[:, head : 2 * head])
-    query_half, key_half = query.astype(BF16), key.astype(BF16)
     value_half = projected[:, 2 * head :].astype(BF16)
-
-    def each(function, *values):
-        return jnp.concatenate(
-            [function(*(v[r * seq : (r + 1) * seq] for v in values)) for r in range(count)], axis=0
-        )
-
-    def last(left, right):
-        return dot(left, right, CONTRACT_LAST)
-
-    def leading(left, right):
-        return dot(left, right, CONTRACT_FIRST)
-
-    powered = jnp.exp(each(last, query_half, key_half) / root)
+    scores = each(dot_last, seq, query.astype(BF16), key.astype(BF16))
+    powered = jnp.exp(scores / math.sqrt(head))
     attention = powered / jnp.sum(powered, axis=-1, keepdims=True)
-    attention_half = attention.astype(BF16)
-    mixed_ref[...] = each(dot, attention_half, value_half).astype(BF16)
-    prob_grad = each(last, head_half, value_half)
-    value_grad = each(leading, attention_half, head_half).astype(BF16)
+    mixed_ref[...] = each(dot, seq, attention.astype(BF16), value_half).astype(BF16)
+    return query, key, attention, value_half, query_scale, key_scale
+
+
+def attention_back(projected, front, head_half, row_mean, scale, seq, outs, width):
+    query, key, attention, value_half, query_scale, key_scale = front
+    grad_ref, numbers_ref = outs
+    rows, head = head_half.shape
+    root = math.sqrt(head)
+    prob_grad = each(dot_last, seq, head_half, value_half)
+    value_grad = each(dot_first, seq, attention.astype(BF16), head_half).astype(BF16)
     score_grad = (
         attention * (prob_grad - jnp.sum(attention * prob_grad, axis=-1, keepdims=True)) / root
     ).astype(BF16)
-    query_grad = norm_back(each(dot, score_grad, key_half), query, query_scale)
-    key_grad = norm_back(each(leading, score_grad, query_half), key, key_scale)
+    query_grad = norm_back(each(dot, seq, score_grad, key.astype(BF16)), query, query_scale)
+    key_grad = norm_back(each(dot_first, seq, score_grad, query.astype(BF16)), key, key_scale)
     proj_grad = jnp.concatenate(
         [query_grad.astype(BF16), key_grad.astype(BF16), value_grad], axis=1
     )
@@ -293,13 +300,16 @@
         top_refs, (below_ref, *outs, head_ref) = refs[:runs], refs[runs:]
         scale = scale_column(mine, 0, ticks, seq, half)
         row_mean = row_means(mine, seq, half)
+        projected = all_rows(mine, seq, half, slice(0, wide))
+        grad_ref, mixed_ref, numbers_ref = outs
         proj_grad, slope = attention_back(
-            all_rows(mine, seq, half, slice(0, wide)),
+            projected,
+            attention_front(projected, seq, mixed_ref),
             all_rows(mine, seq, half, slice(wide, wide + head)).astype(BF16),
             row_mean,
             scale,
             seq,
-            outs,
+            (grad_ref, numbers_ref),
             width,
         )
         centered = [
@@ -332,39 +342,75 @@
     return kernel_call(body, outs, [me, first], arrays)
 
 
-def sum_heads(heads, seq, me):
+def sum_heads(heads, received, seq, me):
     rows, head = heads[0].shape
-    half = rows // seq // 2
+    count = rows // seq
+    half, part = count // 2, received.shape[2] - head
 
     def body(me_ref, *refs):
+        *head_refs, received_ref, out_ref = refs
         for parity in range(2):
             for block in range(half):
                 replica = 2 * block + lax.rem(me_ref[0] + parity, 2)
                 place = pl.ds(pl.multiple_of(replica * seq, seq), seq)
-                total = sum(ref[place, :].astype(F32) for ref in refs[:-1])
+                total = sum(ref[place, :].astype(F32) for ref in head_refs)
+                piece = lax.rem(me_ref[0] + count - replica, count)
+                total += received_ref[piece, :, part:].astype(F32)
                 start = (parity * half + block) * seq
-                refs[-1][start : start + seq, :] = total.astype(BF16)
-
-    return kernel_call(body, [shape(rows, head)], [me], heads, cost=1)[0]
-
-
-def later_attention(halves, facts, head_half, seq, half, head, ticks, width):
+                out_ref[start : start + seq, :] = total.astype(BF16)
+
+    return kernel_call(body, [shape(rows, head)], [me], [*heads, received])[0]
+
+
+def later_front(halves, facts, seq, half, head, ticks):
     rows = 2 * half * seq
 
     def body(*refs):
-        mine, facts, (head_ref, *outs) = refs[:2], refs[2:4], refs[4:]
+        mine, facts, outs = refs[:2], refs[2:4], refs[4:]
+        mixed_ref, projected_ref, query_ref, key_ref, attention_ref, value_ref, scales_ref = outs
+        projected = all_rows(mine, seq, half, slice(None))
+        query, key, attention, value_half, *scales = attention_front(projected, seq, mixed_ref)
+        projected_ref[...] = projected
+        query_ref[...], key_ref[...] = query, key
+        attention_ref[...], value_ref[...] = attention, value_half
+        scales.append(scale_column(facts, 1, ticks, seq, half))
+        for place, scale in enumerate(scales):
+            scales_ref[place] = jnp.broadcast_to(scale, (rows, LANES))
+
+    outs = [
+        shape(rows, head),
+        shape(rows, 3 * head, kind=F32),
+        shape(rows, head, kind=F32),
+        shape(rows, head, kind=F32),
+        shape(rows, seq, kind=F32),
+        shape(rows, head),
+        shape(3, rows, LANES, kind=F32),
+    ]
+    return kernel_call(body, outs, [], [*halves, *facts])
+
+
+def later_attention(front, facts, head_half, seq, half, head, width):
+    rows = 2 * half * seq
+
+    def body(*refs):
+        projected_ref, query_ref, key_ref, attention_ref, value_ref, scales_ref = refs[:6]
+        facts, (head_ref, *outs) = refs[6:8], refs[8:]
+        scales = [scales_ref[place, :, :1] for place in range(3)]
+        front = [query_ref[...], key_ref[...], attention_ref[...], value_ref[...], *scales[:2]]
         attention_back(
-            all_rows(mine, seq, half, slice(None)),
+            projected_ref[...],
+            front,
             head_ref[...],
             row_means(facts, seq, half),
-            scale_column(facts, 1, ticks, seq, half),
+            scales[2],
             seq,
             outs,
             width,
         )
 
-    arrays = [*halves, *facts, head_half]
-    return kernel_call(body, attention_outs(rows, head), [], arrays, cost=1)
+    arrays = [*front, *facts, head_half]
+    outs = [shape(rows, 3 * head), shape(rows, LANES, kind=F32)]
+    return kernel_call(body, outs, [], arrays)
 
 
 def input_gradient(hidden_grad, numbers, incoming, hidden):
@@ -373,15 +419,18 @@
     return (incoming.astype(F32) + change).astype(BF16)
 
 
-def middle_step(grads, pieces, tops, project, me, first):
+def middle_step(grads, heads, pieces, tops, project, me, first):
     count, (_, seq, part) = len(pieces), pieces[0].shape
     runs = len(tops)
     run = part // runs
 
     def body(me_ref, first_ref, *refs):
         top_refs, piece_refs, refs = refs[:runs], refs[runs : runs + count], refs[runs + count :]
-        grad_ref, numbers_ref, project_ref, passed_ref, sems, wide_ref = refs
+        grad_ref, numbers_ref, head_ref, project_ref, passed_ref, sems, wide_ref = refs
         is_first = first_ref[0] == 1
+        for j in range(count):
+            place = pl.ds(pl.multiple_of(replica_of(me_ref, j, count) * seq, seq), seq)
+            passed_ref[j, :, part:] = head_ref[place, :]
 
         @pl.when(is_first)
         def _():
@@ -403,7 +452,7 @@
             for j in range(count):
                 rows = block_rows(me_ref, j, count, seq)
                 hidden, incoming = piece_refs[j][0], piece_refs[j][1]
-                passed_ref[j] = input_gradient(
+                passed_ref[j, :, :part] = input_gradient(
                     wide_ref[rows, :], numbers_ref[rows, :], incoming, hidden
                 )
 
@@ -411,8 +460,8 @@
         pltpu.SemaphoreType.DMA((count, runs)),
         pltpu.VMEM((count * seq, part), F32),
     ]
-    arrays = [*pieces, *grads, project]
-    outs = [shape(count, seq, part)]
+    arrays = [*pieces, *grads, heads, project]
+    outs = [shape(count, seq, part + heads.shape[1])]
     return kernel_call(body, outs, [me, first], arrays, scratch, far=tops)[0]
 
 
@@ -426,7 +475,7 @@
         for j in range(count):
             rows = block_rows(me_ref, j, count, seq)
             outs[j][...] = input_gradient(
-                wide_ref[rows, :], numbers_ref[rows, :], received_ref[j], piece_refs[j][...]
+                wide_ref[rows, :], numbers_ref[rows, :], received_ref[j, :, :part], piece_refs[j][...]
             )
 
     arrays = [*pieces, *grads, received, project]
@@ -582,16 +631,18 @@
     *first_grads, heads = first_attention(
         halves, parts, tops, below, seq, half, head, ticks, me, first, width
     )
-    heads = [down(heads, j) for j in others]
+    moved_heads = [down(heads, j) for j in others[1:]]
     later_halves = [later_total, exchanged(later_total, 1)]
-    passed = middle_step([first_grads[0], first_grads[2]], pieces, tops, project, me, first)
+    passed = middle_step(
+        [first_grads[0], first_grads[2]], heads, pieces, tops, project, me, first
+    )
     received = down(after(passed, later_parts[-1]))
-    head_half = sum_heads(heads, seq, me)
-    later_grads = later_attention(
-        later_halves, halves, head_half, seq, half, head, ticks, width
-    )
-    back = last_step([later_grads[0], later_grads[2]], received, later, project, me)
-    mixed = after(later_grads[1], back[0])
+    mixed, *front = later_front(later_halves, halves, seq, half, head, ticks)
+    moved_heads[0] = after(moved_heads[0], mixed)
+    head_half = sum_heads(moved_heads, received, seq, me)
+    later_grads = later_attention(front, halves, head_half, seq, half, head, width)
+    back = last_step(later_grads, received, later, project, me)
+    mixed = after(mixed, back[0])
     back = [shift(back[j], -j) for j in others]
     project_grads, output_grads = weight_gradients(
         pieces, later, received, first_grads[:2], [later_grads[0], mixed], me

time: 94.5 us -> 94.8 us (level)
    ppermute x5 -> x4, starting transfers between devices: 6.05 us -> 5.18 us  [down(): return lax.ppermute(value, BOTH, pairs)]
    ppermute x5 -> x4, waiting for transfers between devices: 5.77 us -> 5.22 us  [down(): return lax.ppermute(value, BOTH, pairs)]
    pallas_call x18 -> x19, Pallas kernels: 12.6 us -> 12.8 us  [kernel_call(): pl.pallas_call(body, out_shape=tuple(outs), in_specs=[pl.BlockSpec(memory...]
  transfers between devices with their start and end apart: 25 -> 24, of which waited for: 10 -> 11; matrix products, arithmetic and copies ran while one was open for 0% -> 0% of each run, Pallas kernels for 11% -> 10%
where the time goes in v8:
time: 94.8 us; the launch traced here: 94.6 us
  waiting for transfers between devices  41.2 us (43%)
  starting transfers between devices  37.3 us (39%)
  Pallas kernels  12.8 us (14%)
  local copies, waits for them, and re-layouts  2.34 us (2%)
    ppermute x9, starting transfers between devices, shift(): lax.ppermute(value, 'dp', [(i, (i + steps) % count) for i in range(count)])  20.3 us
    ppermute x2, waiting for transfers between devices, toward_owner(): return lax.ppermute(blocks, BOTH, pairs)  18.8 us
    pallas_call x19, Pallas kernels, kernel_call(): pl.pallas_call(body, out_shape=tuple(outs), in_specs=[pl.BlockSpec(memory...  12.8 us
    ppermute x6, waiting for transfers between devices, exchanged(): return lax.ppermute(value, 'dp', [(i, i ^ step) for i in range(count)])  8.81 us
    ppermute x9, waiting for transfers between devices, shift(): lax.ppermute(value, 'dp', [(i, (i + steps) % count) for i in range(count)])  8.34 us
    ppermute x6, starting transfers between devices, exchanged(): return lax.ppermute(value, 'dp', [(i, i ^ step) for i in range(count)])  6.36 us
    ppermute x4, waiting for transfers between devices, down(): return lax.ppermute(value, BOTH, pairs)  5.22 us
    ppermute x4, starting transfers between devices, down(): return lax.ppermute(value, BOTH, pairs)  5.18 us
  transfers between devices with their start and end apart: 24, of which 11 were waited for; matrix products, arithmetic and copies ran while one was open for 0% of the time, Pallas kernels for 10%

profile of v8, /device:TPU:0, one launch (start us, length us, event | category | flops | bytes accessed | tf_op | source)
XLA Modules:
  0.0 94.6 jit_solution(4452096151041526080)
XLA Ops:
  0.7 1.3 %copy-done.1 = bf16[1,2,64,4096]{3,2,1,0:T(8,128)(2,1)S(1)} copy-done((bf16[1,2,64,4096]{3,2,1,0:T(8,128)(2,1)S(1)}, bf16[1,2,64,4096]{3,2,1,0:T(8,128)(2,1)}, u32[]{:S(2)}) %copy-start.1) | copy-done | bytes 1048600
  1.9 1.0 %copy-done.2 = bf16[1,64,4096]{2,1,0:T(8,128)(2,1)S(1)} copy-done((bf16[1,64,4096]{2,1,0:T(8,128)(2,1)S(1)}, bf16[1,64,4096]{2,1,0:T(8,128)(2,1)}, u32[]{:S(2)}) %copy-start.2) | copy-done | bytes 524312
  3.0 0.4 shard_map.76
  3.4 3.1 %collective-permute-start = (bf16[2,64,1024]{2,1,0:T(8,128)(2,1)S(1)}, bf16[2,64,1024]{2,1,0:T(8,128)(2,1)S(1)}, u32[]{:S(2)}, u32[]{:S(2)}) collective-permute-start(bf16[2,64,1024]{2,1,0:T(8,128)(2,1)S(1)} %get-tuple-element.55), channel_id=1, source_target_pairs={{0,1},{1,2},{2,3},{3,0},{4,5},{5,6},{6,7},{7,4},{8,9},{9,10},{10,1... | collective-permute-start | bytes 786440 | tf_op jit(solution)/shard_map/ppermute | solution.py:530
  6.5 2.6 %collective-permute-start.1 = (bf16[2,64,1024]{2,1,0:T(8,128)(2,1)S(1)}, bf16[2,64,1024]{2,1,0:T(8,128)(2,1)S(1)}, u32[]{:S(2)}, u32[]{:S(2)}) collective-permute-start(bf16[2,64,1024]{2,1,0:T(8,128)(2,1)S(1)} %get-tuple-element.56), channel_id=1, source_target_pairs={{0,2},{1,3},{2,0},{3,1},{4,6},{5,7},{6,4},{7,5},{8,10},{9,11},{10,... | collective-permute-start | bytes 786440 | tf_op jit(solution)/shard_map/ppermute | solution.py:530
  9.1 1.3 %collective-permute-start.2 = (bf16[2,64,1024]{2,1,0:T(8,128)(2,1)S(1)}, bf16[2,64,1024]{2,1,0:T(8,128)(2,1)S(1)}, u32[]{:S(2)}, u32[]{:S(2)}) collective-permute-start(bf16[2,64,1024]{2,1,0:T(8,128)(2,1)S(1)} %get-tuple-element.57), channel_id=1, source_target_pairs={{0,3},{1,0},{2,1},{3,2},{4,7},{5,4},{6,5},{7,6},{8,11},{9,8},{10,9... | collective-permute-start | bytes 786440 | tf_op jit(solution)/shard_map/ppermute | solution.py:530
  10.4 1.3 %collective-permute-start.3 = (bf16[1,64,512]{2,1,0:T(8,128)(2,1)S(1)}, bf16[1,64,512]{2,1,0:T(8,128)(2,1)S(1)}, u32[]{:S(2)}, u32[]{:S(2)}) collective-permute-start(bf16[1,64,512]{2,1,0:T(8,128)(2,1)S(1)} %copy-done.4), channel_id=1, source_target_pairs={{1,0},{3,2},{5,4},{7,6},{8,9},{10,11},{12,13},{14,15},{17,16},{19,... | collective-permute-start | bytes 196616 | tf_op jit(solution)/shard_map/ppermute | solution.py:567
  11.7 0.4 shard_map.77
  12.1 15.3 %collective-permute-done.3.right_ref = bf16[1,64,512]{2,1,0:T(8,128)(2,1)S(1)} collective-permute-done((bf16[1,64,512]{2,1,0:T(8,128)(2,1)S(1)}, bf16[1,64,512]{2,1,0:T(8,128)(2,1)S(1)}, u32[]{:S(2)}, u32[]{:S(2)}) %collective-permute-start.3) | collective-permute-done | bytes 65568 | tf_op jit(solution)/shard_map/ppermute | solution.py:567
  27.5 0.6 shard_map.79
  28.1 0.1 collective-permute-start.7
  28.2 3.8 %collective-permute-start.5 = (bf16[64,1024]{1,0:T(8,128)(2,1)S(1)}, bf16[64,1024]{1,0:T(8,128)(2,1)S(1)}, u32[]{:S(2)}, u32[]{:S(2)}) collective-permute-start(bf16[64,1024]{1,0:T(8,128)(2,1)S(1)} %get-tuple-element.69), channel_id=1, source_target_pairs={{0,2},{1,3},{2,0},{3,1},{4,6},{5,7},{6,4},{7,5},{8,10},{9,11},{10,... | collective-permute-start | bytes 393224 | tf_op jit(solution)/shard_map/ppermute | solution.py:530
  32.0 2.6 %collective-permute-start.8 = (bf16[144,512]{1,0:T(8,128)(2,1)S(1)}, bf16[144,512]{1,0:T(8,128)(2,1)S(1)}, u32[]{:S(2)}, u32[]{:S(2)}) collective-permute-start(bf16[144,512]{1,0:T(8,128)(2,1)S(1)} %get-tuple-element.66), channel_id=1, source_target_pairs={{0,1},{1,0},{2,3},{3,2},{4,5},{5,4},{6,7},{7,6},{8,9},{9,8},{10,11... | collective-permute-start | bytes 442376 | tf_op jit(solution)/shard_map/ppermute | solution.py:578
  34.6 1.3 %collective-permute-start.9 = (bf16[2,64,512]{2,1,0:T(8,128)(2,1)S(1)}, bf16[2,64,512]{2,1,0:T(8,128)(2,1)S(1)}, u32[]{:S(2)}, u32[]{:S(2)}) collective-permute-start(bf16[2,64,512]{2,1,0:T(8,128)(2,1)S(1)} %shard_map.78.left_ref), channel_id=1, source_target_pairs={{2,0},{6,4},{11,9},{15,13},{16,18},{20,22},{25,27},{29,31}} | collective-permute-start | bytes 393224 | tf_op jit(solution)/shard_map/ppermute | solution.py:567
  35.9 7.1 %collective-permute-start.6 = (bf16[64,1024]{1,0:T(8,128)(2,1)S(1)}, bf16[64,1024]{1,0:T(8,128)(2,1)S(1)}, u32[]{:S(2)}, u32[]{:S(2)}) collective-permute-start(bf16[64,1024]{1,0:T(8,128)(2,1)S(1)} %get-tuple-element.70), channel_id=1, source_target_pairs={{0,3},{1,0},{2,1},{3,2},{4,7},{5,4},{6,5},{7,6},{8,11},{9,8},{10,9... | collective-permute-start | bytes 393224 | tf_op jit(solution)/shard_map/ppermute | solution.py:530
  43.1 0.1 collective-permute-start.12
  43.2 3.5 %collective-permute-done.9.right_ref = bf16[2,64,512]{2,1,0:T(8,128)(2,1)S(1)} collective-permute-done((bf16[2,64,512]{2,1,0:T(8,128)(2,1)S(1)}, bf16[2,64,512]{2,1,0:T(8,128)(2,1)S(1)}, u32[]{:S(2)}, u32[]{:S(2)}) %collective-permute-start.9) | collective-permute-done | bytes 131104 | tf_op jit(solution)/shard_map/ppermute | solution.py:567
  46.6 0.7 shard_map.81
  47.4 1.3 %collective-permute-start.11 = (bf16[4,64,512]{2,1,0:T(8,128)(2,1)}, bf16[4,64,512]{2,1,0:T(8,128)(2,1)S(1)}, u32[]{:S(2)}, u32[]{:S(2)}) collective-permute-start(bf16[4,64,512]{2,1,0:T(8,128)(2,1)} %shard_map.81), channel_id=1, source_target_pairs={{4,0},{13,1},{22,2},{31,3}} | collective-permute-start | bytes 786440 | tf_op jit(solution)/shard_map/ppermute | solution.py:573
  48.7 1.6 %collective-permute-start.10 = (bf16[4,64,512]{2,1,0:T(8,128)(2,1)}, bf16[4,64,512]{2,1,0:T(8,128)(2,1)S(1)}, u32[]{:S(2)}, u32[]{:S(2)}) collective-permute-start(bf16[4,64,512]{2,1,0:T(8,128)(2,1)} %shard_map.81), channel_id=1, source_target_pairs={{0,0},{9,1},{18,2},{27,3}} | collective-permute-start | bytes 786440 | tf_op jit(solution)/shard_map/ppermute | solution.py:573
  50.3 0.4 shard_map.82
  50.7 2.9 %collective-permute-start.13 = (bf16[128,384]{1,0:T(8,128)(2,1)S(1)}, bf16[128,384]{1,0:T(8,128)(2,1)S(1)}, u32[]{:S(2)}, u32[]{:S(2)}) collective-permute-start(bf16[128,384]{1,0:T(8,128)(2,1)S(1)} %get-tuple-element.76), channel_id=1, source_target_pairs={{0,1},{1,0},{2,3},{3,2},{4,5},{5,4},{6,7},{7,6},{8,9},{9,8},{10,11... | collective-permute-start | bytes 294920 | tf_op jit(solution)/shard_map/ppermute | solution.py:578
  53.6 2.2 %collective-permute-done.12.right_ref = bf16[144,512]{1,0:T(8,128)(2,1)S(1)} collective-permute-done((bf16[144,512]{1,0:T(8,128)(2,1)S(1)}, bf16[144,512]{1,0:T(8,128)(2,1)S(1)}, u32[]{:S(2)}, u32[]{:S(2)}) %collective-permute-start.12) | collective-permute-done | bytes 147488 | tf_op jit(solution)/shard_map/ppermute | solution.py:578
  55.9 0.1 collective-permute-start.14
  55.9 1.9 %collective-permute-done.13.right_ref = bf16[128,384]{1,0:T(8,128)(2,1)S(1)} collective-permute-done((bf16[128,384]{1,0:T(8,128)(2,1)S(1)}, bf16[128,384]{1,0:T(8,128)(2,1)S(1)}, u32[]{:S(2)}, u32[]{:S(2)}) %collective-permute-start.13) | collective-permute-done | bytes 98336 | tf_op jit(solution)/shard_map/ppermute | solution.py:578
  57.8 0.1 collective-permute-start.15
  57.9 0.7 shard_map.85
  58.6 3.1 %collective-permute-done.14.refs_1_.refs_3_.refs_7_ = bf16[144,512]{1,0:T(8,128)(2,1)S(1)} collective-permute-done((bf16[144,512]{1,0:T(8,128)(2,1)S(1)}, bf16[144,512]{1,0:T(8,128)(2,1)S(1)}, u32[]{:S(2)}, u32[]{:S(2)}) %collective-permute-start.14) | collective-permute-done | bytes 147488 | tf_op jit(solution)/shard_map/ppermute | solution.py:578
  61.7 1.6 %shard_map.86 = (bf16[256,384]{1,0:T(8,128)(2,1)S(1)}, bf16[256,128]{1,0:T(8,128)(2,1)S(1)}, f32[256,128]{1,0:T(8,128)S(1)}, bf16[256,128]{1,0:T(8,128)(2,1)S(1)}) custom-call(s32[1]{0:T(128)} %bitcast.me_ref, s32[1]{0:T(128)} %bitcast.5.first_ref, bf16[144,512]{1,0:T(8,128)(2,1)S(1)} %shard_map.83.refs_0_.refs_2_.refs_6_, ...), custom_call_target="tpu_custom_call" | custom-call | flops 1 | bytes 1 | tf_op jit(solution)/shard_map/pallas_call | solution.py:26
  63.3 0.2 shard_map.87
  63.5 1.7 %collective-permute-done.15.right_ref = bf16[128,384]{1,0:T(8,128)(2,1)} collective-permute-done((bf16[128,384]{1,0:T(8,128)(2,1)S(1)}, bf16[128,384]{1,0:T(8,128)(2,1)}, u32[]{:S(2)}, u32[]{:S(2)}) %collective-permute-start.15) | collective-permute-done | bytes 98336 | tf_op jit(solution)/shard_map/ppermute | solution.py:578
  65.2 0.9 shard_map.88.refs_0_
  66.1 0.7 collective-permute-start.17
  66.8 1.0 %collective-permute-start.18 = (bf16[256,128]{1,0:T(8,128)(2,1)S(1)}, bf16[256,128]{1,0:T(8,128)(2,1)S(1)}, u32[]{:S(2)}, u32[]{:S(2)}) collective-permute-start(bf16[256,128]{1,0:T(8,128)(2,1)S(1)} %get-tuple-element.85.refs_8_), channel_id=1, source_target_pairs={{0,29},{1,30},{2,31},{3,28},{4,1},{5,2},{6,3},{7,0},{8,5},{9,6},{1... | collective-permute-start | bytes 196616 | tf_op jit(solution)/shard_map/ppermute | solution.py:544
  67.8 3.3 %collective-permute-start.20 = (bf16[256,128]{1,0:T(8,128)(2,1)S(1)}, bf16[256,128]{1,0:T(8,128)(2,1)S(1)}, u32[]{:S(2)}, u32[]{:S(2)}) collective-permute-start(bf16[256,128]{1,0:T(8,128)(2,1)S(1)} %get-tuple-element.85.refs_8_), channel_id=1, source_target_pairs={{0,31},{1,28},{2,29},{3,30},{4,3},{5,0},{6,1},{7,2},{8,7},{9,4},{1... | collective-permute-start | bytes 196616 | tf_op jit(solution)/shard_map/ppermute | solution.py:544
  71.1 0.9 collective-permute-start.19
  72.0 0.6 shard_map.89
  72.6 0.4 collective-permute-done.18.refs_0_
  73.0 1.1 %collective-permute-done.20.refs_2_ = bf16[256,128]{1,0:T(8,128)(2,1)S(1)} collective-permute-done((bf16[256,128]{1,0:T(8,128)(2,1)S(1)}, bf16[256,128]{1,0:T(8,128)(2,1)S(1)}, u32[]{:S(2)}, u32[]{:S(2)}) %collective-permute-start.20) | collective-permute-done | bytes 65568 | tf_op jit(solution)/shard_map/ppermute | solution.py:544
  74.1 3.7 %collective-permute-done.19.refs_1_ = bf16[256,128]{1,0:T(8,128)(2,1)S(1)} collective-permute-done((bf16[256,128]{1,0:T(8,128)(2,1)S(1)}, bf16[256,128]{1,0:T(8,128)(2,1)S(1)}, u32[]{:S(2)}, u32[]{:S(2)}) %collective-permute-start.19) | collective-permute-done | bytes 65568 | tf_op jit(solution)/shard_map/ppermute | solution.py:544
  77.8 0.8 shard_map.91
  78.6 0.8 shard_map.92
  79.4 1.6 %collective-permute-start.21 = (bf16[64,1024]{1,0:T(8,128)(2,1)S(1)}, bf16[64,1024]{1,0:T(8,128)(2,1)S(1)}, u32[]{:S(2)}, u32[]{:S(2)}) collective-permute-start(bf16[64,1024]{1,0:T(8,128)(2,1)S(1)} %get-tuple-element.102), channel_id=1, source_target_pairs={{0,3},{1,0},{2,1},{3,2},{4,7},{5,4},{6,5},{7,6},{8,11},{9,8},{10,9... | collective-permute-start | bytes 393224 | tf_op jit(solution)/shard_map/ppermute | solution.py:530
  81.0 0.6 collective-permute-start.23
  81.7 3.7 %shard_map.93 = (f32[1024,384]{1,0:T(8,128)}, f32[1024,128]{1,0:T(8,128)}) custom-call(s32[1]{0:T(128)} %bitcast.me_ref, bf16[2,64,1024]{2,1,0:T(8,128)(2,1)S(1)} %get-tuple-element.54.refs_0_.refs_2_, bf16[2,64,1024]{2,1,0:T(8,128)(2,1)S(1)} %collective-permute-done.refs_1_.refs_3_, bf16[2,64,1024]{2,1,0:T(8,128)(2,1)S(1)} %collective-permute-done.1.refs_2_.refs_4_, ...), custom_call_target="tpu_custom_call" | custom-call | flops 1 | bytes 1 | tf_op jit(solution)/shard_map/pallas_call | solution.py:26
  85.4 0.3 collective-permute-done.21.refs_1_
  85.7 8.0 %collective-permute-done.22.refs_2_ = bf16[64,1024]{1,0:T(8,128)(2,1)S(1)} collective-permute-done((bf16[64,1024]{1,0:T(8,128)(2,1)S(1)}, bf16[64,1024]{1,0:T(8,128)(2,1)S(1)}, u32[]{:S(2)}, u32[]{:S(2)}) %collective-permute-start.22) | collective-permute-done | bytes 131104 | tf_op jit(solution)/shard_map/ppermute | solution.py:530
  93.7 0.8 shard_map.94
  (29 shorter events, 0.3 us)
Async XLA Ops:
  0.6 26.9 %copy-start = (bf16[1,1024,384]{2,1,0:T(8,128)(2,1)S(1)}, bf16[1,1024,384]{2,1,0:T(8,128)(2,1)}, u32[]{:S(2)}) copy-start(bf16[1,1024,384]{2,1,0:T(8,128)(2,1)} %param.8) | copy-start | bytes 2359300
  0.6 1.3 %copy-start.1 = (bf16[1,2,64,4096]{3,2,1,0:T(8,128)(2,1)S(1)}, bf16[1,2,64,4096]{3,2,1,0:T(8,128)(2,1)}, u32[]{:S(2)}) copy-start(bf16[1,2,64,4096]{3,2,1,0:T(8,128)(2,1)} %param.5) | copy-start | bytes 3145732
  1.9 1.0 %copy-start.2 = (bf16[1,64,4096]{2,1,0:T(8,128)(2,1)S(1)}, bf16[1,64,4096]{2,1,0:T(8,128)(2,1)}, u32[]{:S(2)}) copy-start(bf16[1,64,4096]{2,1,0:T(8,128)(2,1)} %param.6) | copy-start | bytes 1572868
  3.0 7.4 %copy-start.4 = (bf16[1,64,512]{2,1,0:T(8,128)(2,1)S(1)}, bf16[1,64,512]{2,1,0:T(8,128)(2,1)}, u32[]{:S(2)}) copy-start(bf16[1,64,512]{2,1,0:T(8,128)(2,1)} %left_ref) | copy-start | bytes 196612
  3.0 24.5 %copy-start.3 = (bf16[1,1024,128]{2,1,0:T(8,128)(2,1)S(1)}, bf16[1,1024,128]{2,1,0:T(8,128)(2,1)}, u32[]{:S(2)}) copy-start(bf16[1,1024,128]{2,1,0:T(8,128)(2,1)} %param.9) | copy-start | bytes 786436
  3.4 24.1 %collective-permute-start = (bf16[2,64,1024]{2,1,0:T(8,128)(2,1)S(1)}, bf16[2,64,1024]{2,1,0:T(8,128)(2,1)S(1)}, u32[]{:S(2)}, u32[]{:S(2)}) collective-permute-start(bf16[2,64,1024]{2,1,0:T(8,128)(2,1)S(1)} %get-tuple-element.55), channel_id=1, source_target_pairs={{0,1},{1,2},{2,3},{3,0},{4,5},{5,6},{6,7},{7,4},{8,9},{9,10},{10,1... | collective-permute-start | bytes 786440 | tf_op jit(solution)/shard_map/ppermute | solution.py:530
  6.5 21.0 %collective-permute-start.1 = (bf16[2,64,1024]{2,1,0:T(8,128)(2,1)S(1)}, bf16[2,64,1024]{2,1,0:T(8,128)(2,1)S(1)}, u32[]{:S(2)}, u32[]{:S(2)}) collective-permute-start(bf16[2,64,1024]{2,1,0:T(8,128)(2,1)S(1)} %get-tuple-element.56), channel_id=1, source_target_pairs={{0,2},{1,3},{2,0},{3,1},{4,6},{5,7},{6,4},{7,5},{8,10},{9,11},{10,... | collective-permute-start | bytes 786440 | tf_op jit(solution)/shard_map/ppermute | solution.py:530
  9.1 18.4 %collective-permute-start.2 = (bf16[2,64,1024]{2,1,0:T(8,128)(2,1)S(1)}, bf16[2,64,1024]{2,1,0:T(8,128)(2,1)S(1)}, u32[]{:S(2)}, u32[]{:S(2)}) collective-permute-start(bf16[2,64,1024]{2,1,0:T(8,128)(2,1)S(1)} %get-tuple-element.57), channel_id=1, source_target_pairs={{0,3},{1,0},{2,1},{3,2},{4,7},{5,4},{6,5},{7,6},{8,11},{9,8},{10,9... | collective-permute-start | bytes 786440 | tf_op jit(solution)/shard_map/ppermute | solution.py:530
  10.4 17.0 %collective-permute-start.3 = (bf16[1,64,512]{2,1,0:T(8,128)(2,1)S(1)}, bf16[1,64,512]{2,1,0:T(8,128)(2,1)S(1)}, u32[]{:S(2)}, u32[]{:S(2)}) collective-permute-start(bf16[1,64,512]{2,1,0:T(8,128)(2,1)S(1)} %copy-done.4), channel_id=1, source_target_pairs={{1,0},{3,2},{5,4},{7,6},{8,9},{10,11},{12,13},{14,15},{17,16},{19,... | collective-permute-start | bytes 196616 | tf_op jit(solution)/shard_map/ppermute | solution.py:567
  28.1 14.9 %collective-permute-start.7 = (bf16[1024,128]{1,0:T(8,128)(2,1)S(1)}, bf16[1024,128]{1,0:T(8,128)(2,1)S(1)}, u32[]{:S(2)}, u32[]{:S(2)}) collective-permute-start(bf16[1024,128]{1,0:T(8,128)(2,1)S(1)} %bitcast.18), channel_id=1, source_target_pairs={{0,4},{4,8},{8,12},{12,16},{16,20},{20,24},{24,28},{28,0},{1,5},{5... | collective-permute-start | bytes 786440 | tf_op jit(solution)/shard_map/ppermute | solution.py:605
  28.2 7.8 %collective-permute-start.5 = (bf16[64,1024]{1,0:T(8,128)(2,1)S(1)}, bf16[64,1024]{1,0:T(8,128)(2,1)S(1)}, u32[]{:S(2)}, u32[]{:S(2)}) collective-permute-start(bf16[64,1024]{1,0:T(8,128)(2,1)S(1)} %get-tuple-element.69), channel_id=1, source_target_pairs={{0,2},{1,3},{2,0},{3,1},{4,6},{5,7},{6,4},{7,5},{8,10},{9,11},{10,... | collective-permute-start | bytes 393224 | tf_op jit(solution)/shard_map/ppermute | solution.py:530
  32.0 11.0 %collective-permute-start.8 = (bf16[144,512]{1,0:T(8,128)(2,1)S(1)}, bf16[144,512]{1,0:T(8,128)(2,1)S(1)}, u32[]{:S(2)}, u32[]{:S(2)}) collective-permute-start(bf16[144,512]{1,0:T(8,128)(2,1)S(1)} %get-tuple-element.66), channel_id=1, source_target_pairs={{0,1},{1,0},{2,3},{3,2},{4,5},{5,4},{6,7},{7,6},{8,9},{9,8},{10,11... | collective-permute-start | bytes 442376 | tf_op jit(solution)/shard_map/ppermute | solution.py:578
  34.6 12.1 %collective-permute-start.9 = (bf16[2,64,512]{2,1,0:T(8,128)(2,1)S(1)}, bf16[2,64,512]{2,1,0:T(8,128)(2,1)S(1)}, u32[]{:S(2)}, u32[]{:S(2)}) collective-permute-start(bf16[2,64,512]{2,1,0:T(8,128)(2,1)S(1)} %shard_map.78.left_ref), channel_id=1, source_target_pairs={{2,0},{6,4},{11,9},{15,13},{16,18},{20,22},{25,27},{29,31}} | collective-permute-start | bytes 393224 | tf_op jit(solution)/shard_map/ppermute | solution.py:567
  35.9 14.4 %collective-permute-start.4 = (bf16[64,1024]{1,0:T(8,128)(2,1)S(1)}, bf16[64,1024]{1,0:T(8,128)(2,1)S(1)}, u32[]{:S(2)}, u32[]{:S(2)}) collective-permute-start(bf16[64,1024]{1,0:T(8,128)(2,1)S(1)} %get-tuple-element.68), channel_id=1, source_target_pairs={{0,1},{1,2},{2,3},{3,0},{4,5},{5,6},{6,7},{7,4},{8,9},{9,10},{10,1... | collective-permute-start | bytes 393224 | tf_op jit(solution)/shard_map/ppermute | solution.py:530
  35.9 14.3 %collective-permute-start.6 = (bf16[64,1024]{1,0:T(8,128)(2,1)S(1)}, bf16[64,1024]{1,0:T(8,128)(2,1)S(1)}, u32[]{:S(2)}, u32[]{:S(2)}) collective-permute-start(bf16[64,1024]{1,0:T(8,128)(2,1)S(1)} %get-tuple-element.70), channel_id=1, source_target_pairs={{0,3},{1,0},{2,1},{3,2},{4,7},{5,4},{6,5},{7,6},{8,11},{9,8},{10,9... | collective-permute-start | bytes 393224 | tf_op jit(solution)/shard_map/ppermute | solution.py:530
  43.1 12.7 %collective-permute-start.12 = (bf16[144,512]{1,0:T(8,128)(2,1)S(1)}, bf16[144,512]{1,0:T(8,128)(2,1)S(1)}, u32[]{:S(2)}, u32[]{:S(2)}) collective-permute-start(bf16[144,512]{1,0:T(8,128)(2,1)S(1)} %shard_map.80.left_ref), channel_id=1, source_target_pairs={{0,2},{1,3},{2,0},{3,1},{4,6},{5,7},{6,4},{7,5},{8,10},{9,11},{10,... | collective-permute-start | bytes 442376 | tf_op jit(solution)/shard_map/ppermute | solution.py:578
  47.4 11.3 %collective-permute-start.11 = (bf16[4,64,512]{2,1,0:T(8,128)(2,1)}, bf16[4,64,512]{2,1,0:T(8,128)(2,1)S(1)}, u32[]{:S(2)}, u32[]{:S(2)}) collective-permute-start(bf16[4,64,512]{2,1,0:T(8,128)(2,1)} %shard_map.81), channel_id=1, source_target_pairs={{4,0},{13,1},{22,2},{31,3}} | collective-permute-start | bytes 786440 | tf_op jit(solution)/shard_map/ppermute | solution.py:573
  48.7 10.0 %collective-permute-start.10 = (bf16[4,64,512]{2,1,0:T(8,128)(2,1)}, bf16[4,64,512]{2,1,0:T(8,128)(2,1)S(1)}, u32[]{:S(2)}, u32[]{:S(2)}) collective-permute-start(bf16[4,64,512]{2,1,0:T(8,128)(2,1)} %shard_map.81), channel_id=1, source_target_pairs={{0,0},{9,1},{18,2},{27,3}} | collective-permute-start | bytes 786440 | tf_op jit(solution)/shard_map/ppermute | solution.py:573
  50.7 7.1 %collective-permute-start.13 = (bf16[128,384]{1,0:T(8,128)(2,1)S(1)}, bf16[128,384]{1,0:T(8,128)(2,1)S(1)}, u32[]{:S(2)}, u32[]{:S(2)}) collective-permute-start(bf16[128,384]{1,0:T(8,128)(2,1)S(1)} %get-tuple-element.76), channel_id=1, source_target_pairs={{0,1},{1,0},{2,3},{3,2},{4,5},{5,4},{6,7},{7,6},{8,9},{9,8},{10,11... | collective-permute-start | bytes 294920 | tf_op jit(solution)/shard_map/ppermute | solution.py:578
  55.9 5.8 %collective-permute-start.14 = (bf16[144,512]{1,0:T(8,128)(2,1)S(1)}, bf16[144,512]{1,0:T(8,128)(2,1)S(1)}, u32[]{:S(2)}, u32[]{:S(2)}) collective-permute-start(bf16[144,512]{1,0:T(8,128)(2,1)S(1)} %shard_map.83.refs_0_.refs_2_.refs_6_), channel_id=1, source_target_pairs={{0,1},{1,0},{2,3},{3,2},{4,5},{5,4},{6,7},{7,6},{8,9},{9,8},{10,11... | collective-permute-start | bytes 442376 | tf_op jit(solution)/shard_map/ppermute | solution.py:578
  57.8 7.4 %collective-permute-start.15 = (bf16[128,384]{1,0:T(8,128)(2,1)S(1)}, bf16[128,384]{1,0:T(8,128)(2,1)}, u32[]{:S(2)}, u32[]{:S(2)}) collective-permute-start(bf16[128,384]{1,0:T(8,128)(2,1)S(1)} %shard_map.84.left_ref), channel_id=1, source_target_pairs={{0,2},{1,3},{2,0},{3,1},{4,6},{5,7},{6,4},{7,5},{8,10},{9,11},{10,... | collective-permute-start | bytes 294920 | tf_op jit(solution)/shard_map/ppermute | solution.py:578
  65.2 12.6 %collective-permute-start.16 = (bf16[4,64,1152]{2,1,0:T(8,128)(2,1)S(1)}, bf16[4,64,1152]{2,1,0:T(8,128)(2,1)S(1)}, u32[]{:S(2)}, u32[]{:S(2)}) collective-permute-start(bf16[4,64,1152]{2,1,0:T(8,128)(2,1)S(1)} %shard_map.87), channel_id=1, source_target_pairs={{0,28},{1,29},{2,30},{3,31},{4,0},{5,1},{6,2},{7,3},{8,4},{9,5},{1... | collective-permute-start | bytes 1769480 | tf_op jit(solution)/shard_map/ppermute | solution.py:544
  66.1 5.8 %collective-permute-start.17 = (bf16[128,384]{1,0:T(8,128)(2,1)S(1)}, bf16[128,384]{1,0:T(8,128)(2,1)S(1)}, u32[]{:S(2)}, u32[]{:S(2)}) collective-permute-start(bf16[128,384]{1,0:T(8,128)(2,1)S(1)} %shard_map.88.refs_0_), channel_id=1, source_target_pairs={{0,1},{1,0},{2,3},{3,2},{4,5},{5,4},{6,7},{7,6},{8,9},{9,8},{10,11... | collective-permute-start | bytes 294920 | tf_op jit(solution)/shard_map/ppermute | solution.py:578
  66.8 6.2 %collective-permute-start.18 = (bf16[256,128]{1,0:T(8,128)(2,1)S(1)}, bf16[256,128]{1,0:T(8,128)(2,1)S(1)}, u32[]{:S(2)}, u32[]{:S(2)}) collective-permute-start(bf16[256,128]{1,0:T(8,128)(2,1)S(1)} %get-tuple-element.85.refs_8_), channel_id=1, source_target_pairs={{0,29},{1,30},{2,31},{3,28},{4,1},{5,2},{6,3},{7,0},{8,5},{9,6},{1... | collective-permute-start | bytes 196616 | tf_op jit(solution)/shard_map/ppermute | solution.py:544
  67.8 6.3 %collective-permute-start.20 = (bf16[256,128]{1,0:T(8,128)(2,1)S(1)}, bf16[256,128]{1,0:T(8,128)(2,1)S(1)}, u32[]{:S(2)}, u32[]{:S(2)}) collective-permute-start(bf16[256,128]{1,0:T(8,128)(2,1)S(1)} %get-tuple-element.85.refs_8_), channel_id=1, source_target_pairs={{0,31},{1,28},{2,29},{3,30},{4,3},{5,0},{6,1},{7,2},{8,7},{9,4},{1... | collective-permute-start | bytes 196616 | tf_op jit(solution)/shard_map/ppermute | solution.py:544
  71.1 6.7 %collective-permute-start.19 = (bf16[256,128]{1,0:T(8,128)(2,1)S(1)}, bf16[256,128]{1,0:T(8,128)(2,1)S(1)}, u32[]{:S(2)}, u32[]{:S(2)}) collective-permute-start(bf16[256,128]{1,0:T(8,128)(2,1)S(1)} %get-tuple-element.85.refs_8_), channel_id=1, source_target_pairs={{0,30},{1,31},{2,28},{3,29},{4,2},{5,3},{6,0},{7,1},{8,6},{9,7},{1... | collective-permute-start | bytes 196616 | tf_op jit(solution)/shard_map/ppermute | solution.py:544
  79.4 6.3 %collective-permute-start.21 = (bf16[64,1024]{1,0:T(8,128)(2,1)S(1)}, bf16[64,1024]{1,0:T(8,128)(2,1)S(1)}, u32[]{:S(2)}, u32[]{:S(2)}) collective-permute-start(bf16[64,1024]{1,0:T(8,128)(2,1)S(1)} %get-tuple-element.102), channel_id=1, source_target_pairs={{0,3},{1,0},{2,1},{3,2},{4,7},{5,4},{6,5},{7,6},{8,11},{9,8},{10,9... | collective-permute-start | bytes 393224 | tf_op jit(solution)/shard_map/ppermute | solution.py:530
  81.0 12.7 %collective-permute-start.22 = (bf16[64,1024]{1,0:T(8,128)(2,1)S(1)}, bf16[64,1024]{1,0:T(8,128)(2,1)S(1)}, u32[]{:S(2)}, u32[]{:S(2)}) collective-permute-start(bf16[64,1024]{1,0:T(8,128)(2,1)S(1)} %get-tuple-element.103), channel_id=1, source_target_pairs={{0,2},{1,3},{2,0},{3,1},{4,6},{5,7},{6,4},{7,5},{8,10},{9,11},{10,... | collective-permute-start | bytes 393224 | tf_op jit(solution)/shard_map/ppermute | solution.py:530
  81.0 12.7 %collective-permute-start.23 = (bf16[64,1024]{1,0:T(8,128)(2,1)S(1)}, bf16[64,1024]{1,0:T(8,128)(2,1)S(1)}, u32[]{:S(2)}, u32[]{:S(2)}) collective-permute-start(bf16[64,1024]{1,0:T(8,128)(2,1)S(1)} %get-tuple-element.104), channel_id=1, source_target_pairs={{0,1},{1,2},{2,3},{3,0},{4,5},{5,6},{6,7},{7,4},{8,9},{9,10},{10,1... | collective-permute-start | bytes 393224 | tf_op jit(solution)/shard_map/ppermute | solution.py:530

commit v9 on v7

--- a/solution.py
+++ b/solution.py
@@ -543,7 +543,7 @@
     sent, scale = first_pieces(section_inputs[0], arriving[0], me, count)
     pieces = [shift(sent[j], j) for j in others]
     later_sent, later_scale = later_pieces(section_inputs[0], me, count)
-    blocks = join_pieces(after(blocks, later_scale), moved)
+    blocks = join_pieces(after(blocks, scale), moved)
     bit = 2
     while bit < count // 2:
         blocks = join_pieces(blocks, toward_owner(blocks, bit))
@@ -563,7 +563,7 @@
     if moved is not None:
         blocks = join_pieces(after(blocks, total), moved)
     tops = [owner_to_first(blocks, run) for run in range(pipe // count)]
-    later_mine, later_other = later_partials(later, after(project, total), me)
+    later_mine, later_other = later_partials(later, project, me)
     parts = below_parts(pieces, project, below, me)
     step = 2
     while step < count:

time: 94.5 us -> 94.5 us (level)
  no operation moved by 1% of the time
where the time goes in v9:
time: 94.5 us; the launch traced here: 94.2 us
  waiting for transfers between devices  40.9 us (43%)
  starting transfers between devices  37.4 us (40%)
  Pallas kernels  12.6 us (13%)
  local copies, waits for them, and re-layouts  2.34 us (2%)
    ppermute x9, starting transfers between devices, shift(): lax.ppermute(value, 'dp', [(i, (i + steps) % count) for i in range(count)])  20.1 us
    ppermute x2, waiting for transfers between devices, toward_owner(): return lax.ppermute(blocks, BOTH, pairs)  18.8 us
    pallas_call x18, Pallas kernels, kernel_call(): pl.pallas_call(body, out_shape=tuple(outs), in_specs=[pl.BlockSpec(memory...  12.6 us
    ppermute x6, waiting for transfers between devices, exchanged(): return lax.ppermute(value, 'dp', [(i, i ^ step) for i in range(count)])  8.83 us
    ppermute x9, waiting for transfers between devices, shift(): lax.ppermute(value, 'dp', [(i, (i + steps) % count) for i in range(count)])  7.45 us
    ppermute x5, starting transfers between devices, down(): return lax.ppermute(value, BOTH, pairs)  6.05 us
    ppermute x5, waiting for transfers between devices, down(): return lax.ppermute(value, BOTH, pairs)  5.77 us
    ppermute x6, starting transfers between devices, exchanged(): return lax.ppermute(value, 'dp', [(i, i ^ step) for i in range(count)])  5.76 us
  transfers between devices with their start and end apart: 25, of which 10 were waited for; matrix products, arithmetic and copies ran while one was open for 0% of the time, Pallas kernels for 11%

profile of v9, /device:TPU:0, one launch (start us, length us, event | category | flops | bytes accessed | tf_op | source)
XLA Modules:
  0.0 94.2 jit_solution(7799804880778194493)
XLA Ops:
  0.7 1.3 %copy-done.1 = bf16[1,2,64,4096]{3,2,1,0:T(8,128)(2,1)S(1)} copy-done((bf16[1,2,64,4096]{3,2,1,0:T(8,128)(2,1)S(1)}, bf16[1,2,64,4096]{3,2,1,0:T(8,128)(2,1)}, u32[]{:S(2)}) %copy-start.1) | copy-done | bytes 1048600
  1.9 1.0 %copy-done.2 = bf16[1,64,4096]{2,1,0:T(8,128)(2,1)S(1)} copy-done((bf16[1,64,4096]{2,1,0:T(8,128)(2,1)S(1)}, bf16[1,64,4096]{2,1,0:T(8,128)(2,1)}, u32[]{:S(2)}) %copy-start.2) | copy-done | bytes 524312
  3.0 0.4 shard_map.76
  3.4 3.1 %collective-permute-start = (bf16[2,64,1024]{2,1,0:T(8,128)(2,1)S(1)}, bf16[2,64,1024]{2,1,0:T(8,128)(2,1)S(1)}, u32[]{:S(2)}, u32[]{:S(2)}) collective-permute-start(bf16[2,64,1024]{2,1,0:T(8,128)(2,1)S(1)} %get-tuple-element.47), channel_id=1, source_target_pairs={{0,1},{1,2},{2,3},{3,0},{4,5},{5,6},{6,7},{7,4},{8,9},{9,10},{10,1... | collective-permute-start | bytes 786440 | tf_op jit(solution)/shard_map/ppermute | solution.py:481
  6.5 2.6 %collective-permute-start.1 = (bf16[2,64,1024]{2,1,0:T(8,128)(2,1)S(1)}, bf16[2,64,1024]{2,1,0:T(8,128)(2,1)S(1)}, u32[]{:S(2)}, u32[]{:S(2)}) collective-permute-start(bf16[2,64,1024]{2,1,0:T(8,128)(2,1)S(1)} %get-tuple-element.48), channel_id=1, source_target_pairs={{0,2},{1,3},{2,0},{3,1},{4,6},{5,7},{6,4},{7,5},{8,10},{9,11},{10,... | collective-permute-start | bytes 786440 | tf_op jit(solution)/shard_map/ppermute | solution.py:481
  9.1 1.3 %collective-permute-start.2 = (bf16[2,64,1024]{2,1,0:T(8,128)(2,1)S(1)}, bf16[2,64,1024]{2,1,0:T(8,128)(2,1)S(1)}, u32[]{:S(2)}, u32[]{:S(2)}) collective-permute-start(bf16[2,64,1024]{2,1,0:T(8,128)(2,1)S(1)} %get-tuple-element.49), channel_id=1, source_target_pairs={{0,3},{1,0},{2,1},{3,2},{4,7},{5,4},{6,5},{7,6},{8,11},{9,8},{10,9... | collective-permute-start | bytes 786440 | tf_op jit(solution)/shard_map/ppermute | solution.py:481
  10.4 1.3 %collective-permute-start.3 = (bf16[1,64,512]{2,1,0:T(8,128)(2,1)S(1)}, bf16[1,64,512]{2,1,0:T(8,128)(2,1)S(1)}, u32[]{:S(2)}, u32[]{:S(2)}) collective-permute-start(bf16[1,64,512]{2,1,0:T(8,128)(2,1)S(1)} %copy-done.4), channel_id=1, source_target_pairs={{1,0},{3,2},{5,4},{7,6},{8,9},{10,11},{12,13},{14,15},{17,16},{19,... | collective-permute-start | bytes 196616 | tf_op jit(solution)/shard_map/ppermute | solution.py:518
  11.7 0.4 shard_map.77
  12.1 15.3 %collective-permute-done.3.right_ref = bf16[1,64,512]{2,1,0:T(8,128)(2,1)S(1)} collective-permute-done((bf16[1,64,512]{2,1,0:T(8,128)(2,1)S(1)}, bf16[1,64,512]{2,1,0:T(8,128)(2,1)S(1)}, u32[]{:S(2)}, u32[]{:S(2)}) %collective-permute-start.3) | collective-permute-done | bytes 65568 | tf_op jit(solution)/shard_map/ppermute | solution.py:518
  27.5 0.6 shard_map.79
  28.1 0.1 collective-permute-start.7
  28.2 3.8 %collective-permute-start.5 = (bf16[64,1024]{1,0:T(8,128)(2,1)S(1)}, bf16[64,1024]{1,0:T(8,128)(2,1)S(1)}, u32[]{:S(2)}, u32[]{:S(2)}) collective-permute-start(bf16[64,1024]{1,0:T(8,128)(2,1)S(1)} %get-tuple-element.61), channel_id=1, source_target_pairs={{0,2},{1,3},{2,0},{3,1},{4,6},{5,7},{6,4},{7,5},{8,10},{9,11},{10,... | collective-permute-start | bytes 393224 | tf_op jit(solution)/shard_map/ppermute | solution.py:481
  32.0 2.6 %collective-permute-start.8 = (bf16[144,512]{1,0:T(8,128)(2,1)S(1)}, bf16[144,512]{1,0:T(8,128)(2,1)S(1)}, u32[]{:S(2)}, u32[]{:S(2)}) collective-permute-start(bf16[144,512]{1,0:T(8,128)(2,1)S(1)} %get-tuple-element.58), channel_id=1, source_target_pairs={{0,1},{1,0},{2,3},{3,2},{4,5},{5,4},{6,7},{7,6},{8,9},{9,8},{10,11... | collective-permute-start | bytes 442376 | tf_op jit(solution)/shard_map/ppermute | solution.py:529
  34.6 1.3 %collective-permute-start.9 = (bf16[2,64,512]{2,1,0:T(8,128)(2,1)S(1)}, bf16[2,64,512]{2,1,0:T(8,128)(2,1)S(1)}, u32[]{:S(2)}, u32[]{:S(2)}) collective-permute-start(bf16[2,64,512]{2,1,0:T(8,128)(2,1)S(1)} %shard_map.78.left_ref), channel_id=1, source_target_pairs={{2,0},{6,4},{11,9},{15,13},{16,18},{20,22},{25,27},{29,31}} | collective-permute-start | bytes 393224 | tf_op jit(solution)/shard_map/ppermute | solution.py:518
  35.9 0.1 collective-permute-start.4
  35.9 7.1 %collective-permute-start.6 = (bf16[64,1024]{1,0:T(8,128)(2,1)S(1)}, bf16[64,1024]{1,0:T(8,128)(2,1)S(1)}, u32[]{:S(2)}, u32[]{:S(2)}) collective-permute-start(bf16[64,1024]{1,0:T(8,128)(2,1)S(1)} %get-tuple-element.62), channel_id=1, source_target_pairs={{0,3},{1,0},{2,1},{3,2},{4,7},{5,4},{6,5},{7,6},{8,11},{9,8},{10,9... | collective-permute-start | bytes 393224 | tf_op jit(solution)/shard_map/ppermute | solution.py:481
  43.1 0.1 collective-permute-start.12
  43.2 3.5 %collective-permute-done.9.right_ref = bf16[2,64,512]{2,1,0:T(8,128)(2,1)S(1)} collective-permute-done((bf16[2,64,512]{2,1,0:T(8,128)(2,1)S(1)}, bf16[2,64,512]{2,1,0:T(8,128)(2,1)S(1)}, u32[]{:S(2)}, u32[]{:S(2)}) %collective-permute-start.9) | collective-permute-done | bytes 131104 | tf_op jit(solution)/shard_map/ppermute | solution.py:518
  46.6 0.7 shard_map.81
  47.4 1.3 %collective-permute-start.11 = (bf16[4,64,512]{2,1,0:T(8,128)(2,1)}, bf16[4,64,512]{2,1,0:T(8,128)(2,1)S(1)}, u32[]{:S(2)}, u32[]{:S(2)}) collective-permute-start(bf16[4,64,512]{2,1,0:T(8,128)(2,1)} %shard_map.81), channel_id=1, source_target_pairs={{4,0},{13,1},{22,2},{31,3}} | collective-permute-start | bytes 786440 | tf_op jit(solution)/shard_map/ppermute | solution.py:524
  48.7 1.6 %collective-permute-start.10 = (bf16[4,64,512]{2,1,0:T(8,128)(2,1)}, bf16[4,64,512]{2,1,0:T(8,128)(2,1)S(1)}, u32[]{:S(2)}, u32[]{:S(2)}) collective-permute-start(bf16[4,64,512]{2,1,0:T(8,128)(2,1)} %shard_map.81), channel_id=1, source_target_pairs={{0,0},{9,1},{18,2},{27,3}} | collective-permute-start | bytes 786440 | tf_op jit(solution)/shard_map/ppermute | solution.py:524
  50.3 0.4 shard_map.82
  50.7 2.9 %collective-permute-start.13 = (bf16[128,384]{1,0:T(8,128)(2,1)S(1)}, bf16[128,384]{1,0:T(8,128)(2,1)S(1)}, u32[]{:S(2)}, u32[]{:S(2)}) collective-permute-start(bf16[128,384]{1,0:T(8,128)(2,1)S(1)} %get-tuple-element.67), channel_id=1, source_target_pairs={{0,1},{1,0},{2,3},{3,2},{4,5},{5,4},{6,7},{7,6},{8,9},{9,8},{10,11... | collective-permute-start | bytes 294920 | tf_op jit(solution)/shard_map/ppermute | solution.py:529
  53.6 2.2 %collective-permute-done.12.right_ref = bf16[144,512]{1,0:T(8,128)(2,1)S(1)} collective-permute-done((bf16[144,512]{1,0:T(8,128)(2,1)S(1)}, bf16[144,512]{1,0:T(8,128)(2,1)S(1)}, u32[]{:S(2)}, u32[]{:S(2)}) %collective-permute-start.12) | collective-permute-done | bytes 147488 | tf_op jit(solution)/shard_map/ppermute | solution.py:529
  55.9 0.1 collective-permute-start.14
  55.9 1.9 %collective-permute-done.13.right_ref = bf16[128,384]{1,0:T(8,128)(2,1)S(1)} collective-permute-done((bf16[128,384]{1,0:T(8,128)(2,1)S(1)}, bf16[128,384]{1,0:T(8,128)(2,1)S(1)}, u32[]{:S(2)}, u32[]{:S(2)}) %collective-permute-start.13) | collective-permute-done | bytes 98336 | tf_op jit(solution)/shard_map/ppermute | solution.py:529
  57.8 0.1 collective-permute-start.15
  57.9 0.7 shard_map.85
  58.6 3.1 %collective-permute-done.14.refs_1_.refs_3_ = bf16[144,512]{1,0:T(8,128)(2,1)S(1)} collective-permute-done((bf16[144,512]{1,0:T(8,128)(2,1)S(1)}, bf16[144,512]{1,0:T(8,128)(2,1)S(1)}, u32[]{:S(2)}, u32[]{:S(2)}) %collective-permute-start.14) | collective-permute-done | bytes 147488 | tf_op jit(solution)/shard_map/ppermute | solution.py:529
  61.7 1.6 %shard_map.86 = (bf16[256,384]{1,0:T(8,128)(2,1)S(1)}, bf16[256,128]{1,0:T(8,128)(2,1)S(1)}, f32[256,128]{1,0:T(8,128)S(1)}, bf16[256,128]{1,0:T(8,128)(2,1)S(1)}) custom-call(s32[1]{0:T(128)} %bitcast.me_ref, s32[1]{0:T(128)} %bitcast.5.first_ref, bf16[144,512]{1,0:T(8,128)(2,1)S(1)} %shard_map.83.refs_0_.refs_2_, ...), custom_call_target="tpu_custom_call" | custom-call | flops 1 | bytes 1 | tf_op jit(solution)/shard_map/pallas_call | solution.py:26
  63.3 0.2 shard_map.87
  63.5 1.7 %collective-permute-done.15.right_ref = bf16[128,384]{1,0:T(8,128)(2,1)} collective-permute-done((bf16[128,384]{1,0:T(8,128)(2,1)S(1)}, bf16[128,384]{1,0:T(8,128)(2,1)}, u32[]{:S(2)}, u32[]{:S(2)}) %collective-permute-start.15) | collective-permute-done | bytes 98336 | tf_op jit(solution)/shard_map/ppermute | solution.py:529
  65.2 3.7 %collective-permute-start.21 = (bf16[256,128]{1,0:T(8,128)(2,1)S(1)}, bf16[256,128]{1,0:T(8,128)(2,1)S(1)}, u32[]{:S(2)}, u32[]{:S(2)}) collective-permute-start(bf16[256,128]{1,0:T(8,128)(2,1)S(1)} %get-tuple-element.78), channel_id=1, source_target_pairs={{0,31},{1,28},{2,29},{3,30},{4,3},{5,0},{6,1},{7,2},{8,7},{9,4},{1... | collective-permute-start | bytes 196616 | tf_op jit(solution)/shard_map/ppermute | solution.py:495
  68.9 0.9 shard_map.88.refs_0_
  69.8 0.1 collective-permute-start.17
  69.9 0.3 collective-permute-start.20
  70.2 1.1 %collective-permute-start.19 = (bf16[256,128]{1,0:T(8,128)(2,1)S(1)}, bf16[256,128]{1,0:T(8,128)(2,1)S(1)}, u32[]{:S(2)}, u32[]{:S(2)}) collective-permute-start(bf16[256,128]{1,0:T(8,128)(2,1)S(1)} %get-tuple-element.78), channel_id=1, source_target_pairs={{0,29},{1,30},{2,31},{3,28},{4,1},{5,2},{6,3},{7,0},{8,5},{9,6},{1... | collective-permute-start | bytes 196616 | tf_op jit(solution)/shard_map/ppermute | solution.py:495
  71.2 1.0 %collective-permute-start.18 = (bf16[256,128]{1,0:T(8,128)(2,1)S(1)}, bf16[256,128]{1,0:T(8,128)(2,1)S(1)}, u32[]{:S(2)}, u32[]{:S(2)}) collective-permute-start(bf16[256,128]{1,0:T(8,128)(2,1)S(1)} %get-tuple-element.78), channel_id=1, source_target_pairs={{0,28},{1,29},{2,30},{3,31},{4,0},{5,1},{6,2},{7,3},{8,4},{9,5},{1... | collective-permute-start | bytes 196616 | tf_op jit(solution)/shard_map/ppermute | solution.py:495
  72.3 2.9 %collective-permute-done.20.refs_2_ = bf16[256,128]{1,0:T(8,128)(2,1)S(1)} collective-permute-done((bf16[256,128]{1,0:T(8,128)(2,1)S(1)}, bf16[256,128]{1,0:T(8,128)(2,1)S(1)}, u32[]{:S(2)}, u32[]{:S(2)}) %collective-permute-start.20) | collective-permute-done | bytes 65568 | tf_op jit(solution)/shard_map/ppermute | solution.py:495
  75.1 2.9 %collective-permute-done.19.refs_1_ = bf16[256,128]{1,0:T(8,128)(2,1)S(1)} collective-permute-done((bf16[256,128]{1,0:T(8,128)(2,1)S(1)}, bf16[256,128]{1,0:T(8,128)(2,1)S(1)}, u32[]{:S(2)}, u32[]{:S(2)}) %collective-permute-start.19) | collective-permute-done | bytes 65568 | tf_op jit(solution)/shard_map/ppermute | solution.py:495
  78.1 1.2 %shard_map.90 = (bf16[256,384]{1,0:T(8,128)(2,1)S(1)}, bf16[256,128]{1,0:T(8,128)(2,1)S(1)}, f32[256,128]{1,0:T(8,128)S(1)}) custom-call(bf16[128,384]{1,0:T(8,128)(2,1)S(1)} %shard_map.88.refs_0_, bf16[128,384]{1,0:T(8,128)(2,1)S(1)} %collective-permute-done.17.refs_1_, bf16[144,512]{1,0:T(8,128)(2,1)S(1)} %shard_map.83.refs_0_.refs_2_, ...), custom_call_target="tpu_custom_call" | custom-call | flops 1 | bytes 1 | tf_op jit(solution)/shard_map/pallas_call | solution.py:26
  79.3 0.8 shard_map.91
  80.1 1.1 %collective-permute-start.22 = (bf16[64,1024]{1,0:T(8,128)(2,1)S(1)}, bf16[64,1024]{1,0:T(8,128)(2,1)S(1)}, u32[]{:S(2)}, u32[]{:S(2)}) collective-permute-start(bf16[64,1024]{1,0:T(8,128)(2,1)S(1)} %get-tuple-element.86), channel_id=1, source_target_pairs={{0,3},{1,0},{2,1},{3,2},{4,7},{5,4},{6,5},{7,6},{8,11},{9,8},{10,9... | collective-permute-start | bytes 393224 | tf_op jit(solution)/shard_map/ppermute | solution.py:481
  81.2 1.0 %collective-permute-start.24 = (bf16[64,1024]{1,0:T(8,128)(2,1)S(1)}, bf16[64,1024]{1,0:T(8,128)(2,1)S(1)}, u32[]{:S(2)}, u32[]{:S(2)}) collective-permute-start(bf16[64,1024]{1,0:T(8,128)(2,1)S(1)} %get-tuple-element.88), channel_id=1, source_target_pairs={{0,1},{1,2},{2,3},{3,0},{4,5},{5,6},{6,7},{7,4},{8,9},{9,10},{10,1... | collective-permute-start | bytes 393224 | tf_op jit(solution)/shard_map/ppermute | solution.py:481
  82.2 3.7 %shard_map.92 = (f32[1024,384]{1,0:T(8,128)}, f32[1024,128]{1,0:T(8,128)}) custom-call(s32[1]{0:T(128)} %bitcast.me_ref, bf16[2,64,1024]{2,1,0:T(8,128)(2,1)S(1)} %get-tuple-element.46.refs_0_.refs_2_, bf16[2,64,1024]{2,1,0:T(8,128)(2,1)S(1)} %collective-permute-done.refs_1_.refs_3_, bf16[2,64,1024]{2,1,0:T(8,128)(2,1)S(1)} %collective-permute-done.1.refs_2_.refs_4_, ...), custom_call_target="tpu_custom_call" | custom-call | flops 1 | bytes 1 | tf_op jit(solution)/shard_map/pallas_call | solution.py:26
  85.9 0.5 collective-permute-done.22.refs_1_
  86.4 6.9 %collective-permute-done.23.refs_2_ = bf16[64,1024]{1,0:T(8,128)(2,1)S(1)} collective-permute-done((bf16[64,1024]{1,0:T(8,128)(2,1)S(1)}, bf16[64,1024]{1,0:T(8,128)(2,1)S(1)}, u32[]{:S(2)}, u32[]{:S(2)}) %collective-permute-start.23) | collective-permute-done | bytes 131104 | tf_op jit(solution)/shard_map/ppermute | solution.py:481
  93.3 0.8 shard_map.93
  (30 shorter events, 0.2 us)
Async XLA Ops:
  0.6 26.9 %copy-start = (bf16[1,1024,384]{2,1,0:T(8,128)(2,1)S(1)}, bf16[1,1024,384]{2,1,0:T(8,128)(2,1)}, u32[]{:S(2)}) copy-start(bf16[1,1024,384]{2,1,0:T(8,128)(2,1)} %param.8) | copy-start | bytes 2359300
  0.6 1.3 %copy-start.1 = (bf16[1,2,64,4096]{3,2,1,0:T(8,128)(2,1)S(1)}, bf16[1,2,64,4096]{3,2,1,0:T(8,128)(2,1)}, u32[]{:S(2)}) copy-start(bf16[1,2,64,4096]{3,2,1,0:T(8,128)(2,1)} %param.5) | copy-start | bytes 3145732
  1.9 1.0 %copy-start.2 = (bf16[1,64,4096]{2,1,0:T(8,128)(2,1)S(1)}, bf16[1,64,4096]{2,1,0:T(8,128)(2,1)}, u32[]{:S(2)}) copy-start(bf16[1,64,4096]{2,1,0:T(8,128)(2,1)} %param.6) | copy-start | bytes 1572868
  3.0 7.4 %copy-start.4 = (bf16[1,64,512]{2,1,0:T(8,128)(2,1)S(1)}, bf16[1,64,512]{2,1,0:T(8,128)(2,1)}, u32[]{:S(2)}) copy-start(bf16[1,64,512]{2,1,0:T(8,128)(2,1)} %left_ref) | copy-start | bytes 196612
  3.0 24.5 %copy-start.3 = (bf16[1,1024,128]{2,1,0:T(8,128)(2,1)S(1)}, bf16[1,1024,128]{2,1,0:T(8,128)(2,1)}, u32[]{:S(2)}) copy-start(bf16[1,1024,128]{2,1,0:T(8,128)(2,1)} %param.9) | copy-start | bytes 786436
  3.4 24.1 %collective-permute-start = (bf16[2,64,1024]{2,1,0:T(8,128)(2,1)S(1)}, bf16[2,64,1024]{2,1,0:T(8,128)(2,1)S(1)}, u32[]{:S(2)}, u32[]{:S(2)}) collective-permute-start(bf16[2,64,1024]{2,1,0:T(8,128)(2,1)S(1)} %get-tuple-element.47), channel_id=1, source_target_pairs={{0,1},{1,2},{2,3},{3,0},{4,5},{5,6},{6,7},{7,4},{8,9},{9,10},{10,1... | collective-permute-start | bytes 786440 | tf_op jit(solution)/shard_map/ppermute | solution.py:481
  6.5 21.0 %collective-permute-start.1 = (bf16[2,64,1024]{2,1,0:T(8,128)(2,1)S(1)}, bf16[2,64,1024]{2,1,0:T(8,128)(2,1)S(1)}, u32[]{:S(2)}, u32[]{:S(2)}) collective-permute-start(bf16[2,64,1024]{2,1,0:T(8,128)(2,1)S(1)} %get-tuple-element.48), channel_id=1, source_target_pairs={{0,2},{1,3},{2,0},{3,1},{4,6},{5,7},{6,4},{7,5},{8,10},{9,11},{10,... | collective-permute-start | bytes 786440 | tf_op jit(solution)/shard_map/ppermute | solution.py:481
  9.1 18.4 %collective-permute-start.2 = (bf16[2,64,1024]{2,1,0:T(8,128)(2,1)S(1)}, bf16[2,64,1024]{2,1,0:T(8,128)(2,1)S(1)}, u32[]{:S(2)}, u32[]{:S(2)}) collective-permute-start(bf16[2,64,1024]{2,1,0:T(8,128)(2,1)S(1)} %get-tuple-element.49), channel_id=1, source_target_pairs={{0,3},{1,0},{2,1},{3,2},{4,7},{5,4},{6,5},{7,6},{8,11},{9,8},{10,9... | collective-permute-start | bytes 786440 | tf_op jit(solution)/shard_map/ppermute | solution.py:481
  10.4 17.0 %collective-permute-start.3 = (bf16[1,64,512]{2,1,0:T(8,128)(2,1)S(1)}, bf16[1,64,512]{2,1,0:T(8,128)(2,1)S(1)}, u32[]{:S(2)}, u32[]{:S(2)}) collective-permute-start(bf16[1,64,512]{2,1,0:T(8,128)(2,1)S(1)} %copy-done.4), channel_id=1, source_target_pairs={{1,0},{3,2},{5,4},{7,6},{8,9},{10,11},{12,13},{14,15},{17,16},{19,... | collective-permute-start | bytes 196616 | tf_op jit(solution)/shard_map/ppermute | solution.py:518
  28.1 14.9 %collective-permute-start.7 = (bf16[1024,128]{1,0:T(8,128)(2,1)S(1)}, bf16[1024,128]{1,0:T(8,128)(2,1)S(1)}, u32[]{:S(2)}, u32[]{:S(2)}) collective-permute-start(bf16[1024,128]{1,0:T(8,128)(2,1)S(1)} %bitcast.18), channel_id=1, source_target_pairs={{0,4},{4,8},{8,12},{12,16},{16,20},{20,24},{24,28},{28,0},{1,5},{5... | collective-permute-start | bytes 786440 | tf_op jit(solution)/shard_map/ppermute | solution.py:556
  28.2 7.8 %collective-permute-start.5 = (bf16[64,1024]{1,0:T(8,128)(2,1)S(1)}, bf16[64,1024]{1,0:T(8,128)(2,1)S(1)}, u32[]{:S(2)}, u32[]{:S(2)}) collective-permute-start(bf16[64,1024]{1,0:T(8,128)(2,1)S(1)} %get-tuple-element.61), channel_id=1, source_target_pairs={{0,2},{1,3},{2,0},{3,1},{4,6},{5,7},{6,4},{7,5},{8,10},{9,11},{10,... | collective-permute-start | bytes 393224 | tf_op jit(solution)/shard_map/ppermute | solution.py:481
  32.0 11.0 %collective-permute-start.8 = (bf16[144,512]{1,0:T(8,128)(2,1)S(1)}, bf16[144,512]{1,0:T(8,128)(2,1)S(1)}, u32[]{:S(2)}, u32[]{:S(2)}) collective-permute-start(bf16[144,512]{1,0:T(8,128)(2,1)S(1)} %get-tuple-element.58), channel_id=1, source_target_pairs={{0,1},{1,0},{2,3},{3,2},{4,5},{5,4},{6,7},{7,6},{8,9},{9,8},{10,11... | collective-permute-start | bytes 442376 | tf_op jit(solution)/shard_map/ppermute | solution.py:529
  34.6 12.1 %collective-permute-start.9 = (bf16[2,64,512]{2,1,0:T(8,128)(2,1)S(1)}, bf16[2,64,512]{2,1,0:T(8,128)(2,1)S(1)}, u32[]{:S(2)}, u32[]{:S(2)}) collective-permute-start(bf16[2,64,512]{2,1,0:T(8,128)(2,1)S(1)} %shard_map.78.left_ref), channel_id=1, source_target_pairs={{2,0},{6,4},{11,9},{15,13},{16,18},{20,22},{25,27},{29,31}} | collective-permute-start | bytes 393224 | tf_op jit(solution)/shard_map/ppermute | solution.py:518
  35.9 14.4 %collective-permute-start.4 = (bf16[64,1024]{1,0:T(8,128)(2,1)S(1)}, bf16[64,1024]{1,0:T(8,128)(2,1)S(1)}, u32[]{:S(2)}, u32[]{:S(2)}) collective-permute-start(bf16[64,1024]{1,0:T(8,128)(2,1)S(1)} %get-tuple-element.60), channel_id=1, source_target_pairs={{0,1},{1,2},{2,3},{3,0},{4,5},{5,6},{6,7},{7,4},{8,9},{9,10},{10,1... | collective-permute-start | bytes 393224 | tf_op jit(solution)/shard_map/ppermute | solution.py:481
  35.9 14.3 %collective-permute-start.6 = (bf16[64,1024]{1,0:T(8,128)(2,1)S(1)}, bf16[64,1024]{1,0:T(8,128)(2,1)S(1)}, u32[]{:S(2)}, u32[]{:S(2)}) collective-permute-start(bf16[64,1024]{1,0:T(8,128)(2,1)S(1)} %get-tuple-element.62), channel_id=1, source_target_pairs={{0,3},{1,0},{2,1},{3,2},{4,7},{5,4},{6,5},{7,6},{8,11},{9,8},{10,9... | collective-permute-start | bytes 393224 | tf_op jit(solution)/shard_map/ppermute | solution.py:481
  43.1 12.7 %collective-permute-start.12 = (bf16[144,512]{1,0:T(8,128)(2,1)S(1)}, bf16[144,512]{1,0:T(8,128)(2,1)S(1)}, u32[]{:S(2)}, u32[]{:S(2)}) collective-permute-start(bf16[144,512]{1,0:T(8,128)(2,1)S(1)} %shard_map.80.left_ref), channel_id=1, source_target_pairs={{0,2},{1,3},{2,0},{3,1},{4,6},{5,7},{6,4},{7,5},{8,10},{9,11},{10,... | collective-permute-start | bytes 442376 | tf_op jit(solution)/shard_map/ppermute | solution.py:529
  47.4 11.3 %collective-permute-start.11 = (bf16[4,64,512]{2,1,0:T(8,128)(2,1)}, bf16[4,64,512]{2,1,0:T(8,128)(2,1)S(1)}, u32[]{:S(2)}, u32[]{:S(2)}) collective-permute-start(bf16[4,64,512]{2,1,0:T(8,128)(2,1)} %shard_map.81), channel_id=1, source_target_pairs={{4,0},{13,1},{22,2},{31,3}} | collective-permute-start | bytes 786440 | tf_op jit(solution)/shard_map/ppermute | solution.py:524
  48.7 10.0 %collective-permute-start.10 = (bf16[4,64,512]{2,1,0:T(8,128)(2,1)}, bf16[4,64,512]{2,1,0:T(8,128)(2,1)S(1)}, u32[]{:S(2)}, u32[]{:S(2)}) collective-permute-start(bf16[4,64,512]{2,1,0:T(8,128)(2,1)} %shard_map.81), channel_id=1, source_target_pairs={{0,0},{9,1},{18,2},{27,3}} | collective-permute-start | bytes 786440 | tf_op jit(solution)/shard_map/ppermute | solution.py:524
  50.7 7.1 %collective-permute-start.13 = (bf16[128,384]{1,0:T(8,128)(2,1)S(1)}, bf16[128,384]{1,0:T(8,128)(2,1)S(1)}, u32[]{:S(2)}, u32[]{:S(2)}) collective-permute-start(bf16[128,384]{1,0:T(8,128)(2,1)S(1)} %get-tuple-element.67), channel_id=1, source_target_pairs={{0,1},{1,0},{2,3},{3,2},{4,5},{5,4},{6,7},{7,6},{8,9},{9,8},{10,11... | collective-permute-start | bytes 294920 | tf_op jit(solution)/shard_map/ppermute | solution.py:529
  55.9 5.8 %collective-permute-start.14 = (bf16[144,512]{1,0:T(8,128)(2,1)S(1)}, bf16[144,512]{1,0:T(8,128)(2,1)S(1)}, u32[]{:S(2)}, u32[]{:S(2)}) collective-permute-start(bf16[144,512]{1,0:T(8,128)(2,1)S(1)} %shard_map.83.refs_0_.refs_2_), channel_id=1, source_target_pairs={{0,1},{1,0},{2,3},{3,2},{4,5},{5,4},{6,7},{7,6},{8,9},{9,8},{10,11... | collective-permute-start | bytes 442376 | tf_op jit(solution)/shard_map/ppermute | solution.py:529
  57.8 7.4 %collective-permute-start.15 = (bf16[128,384]{1,0:T(8,128)(2,1)S(1)}, bf16[128,384]{1,0:T(8,128)(2,1)}, u32[]{:S(2)}, u32[]{:S(2)}) collective-permute-start(bf16[128,384]{1,0:T(8,128)(2,1)S(1)} %shard_map.84.left_ref), channel_id=1, source_target_pairs={{0,2},{1,3},{2,0},{3,1},{4,6},{5,7},{6,4},{7,5},{8,10},{9,11},{10,... | collective-permute-start | bytes 294920 | tf_op jit(solution)/shard_map/ppermute | solution.py:529
  65.2 14.1 %collective-permute-start.16 = (bf16[4,64,1024]{2,1,0:T(8,128)(2,1)S(1)}, bf16[4,64,1024]{2,1,0:T(8,128)(2,1)S(1)}, u32[]{:S(2)}, u32[]{:S(2)}) collective-permute-start(bf16[4,64,1024]{2,1,0:T(8,128)(2,1)S(1)} %shard_map.87), channel_id=1, source_target_pairs={{0,28},{1,29},{2,30},{3,31},{4,0},{5,1},{6,2},{7,3},{8,4},{9,5},{1... | collective-permute-start | bytes 1572872 | tf_op jit(solution)/shard_map/ppermute | solution.py:495
  65.2 6.0 %collective-permute-start.21 = (bf16[256,128]{1,0:T(8,128)(2,1)S(1)}, bf16[256,128]{1,0:T(8,128)(2,1)S(1)}, u32[]{:S(2)}, u32[]{:S(2)}) collective-permute-start(bf16[256,128]{1,0:T(8,128)(2,1)S(1)} %get-tuple-element.78), channel_id=1, source_target_pairs={{0,31},{1,28},{2,29},{3,30},{4,3},{5,0},{6,1},{7,2},{8,7},{9,4},{1... | collective-permute-start | bytes 196616 | tf_op jit(solution)/shard_map/ppermute | solution.py:495
  69.8 8.3 %collective-permute-start.17 = (bf16[128,384]{1,0:T(8,128)(2,1)S(1)}, bf16[128,384]{1,0:T(8,128)(2,1)S(1)}, u32[]{:S(2)}, u32[]{:S(2)}) collective-permute-start(bf16[128,384]{1,0:T(8,128)(2,1)S(1)} %shard_map.88.refs_0_), channel_id=1, source_target_pairs={{0,1},{1,0},{2,3},{3,2},{4,5},{5,4},{6,7},{7,6},{8,9},{9,8},{10,11... | collective-permute-start | bytes 294920 | tf_op jit(solution)/shard_map/ppermute | solution.py:529
  69.9 5.3 %collective-permute-start.20 = (bf16[256,128]{1,0:T(8,128)(2,1)S(1)}, bf16[256,128]{1,0:T(8,128)(2,1)S(1)}, u32[]{:S(2)}, u32[]{:S(2)}) collective-permute-start(bf16[256,128]{1,0:T(8,128)(2,1)S(1)} %get-tuple-element.78), channel_id=1, source_target_pairs={{0,30},{1,31},{2,28},{3,29},{4,2},{5,3},{6,0},{7,1},{8,6},{9,7},{1... | collective-permute-start | bytes 196616 | tf_op jit(solution)/shard_map/ppermute | solution.py:495
  70.2 7.9 %collective-permute-start.19 = (bf16[256,128]{1,0:T(8,128)(2,1)S(1)}, bf16[256,128]{1,0:T(8,128)(2,1)S(1)}, u32[]{:S(2)}, u32[]{:S(2)}) collective-permute-start(bf16[256,128]{1,0:T(8,128)(2,1)S(1)} %get-tuple-element.78), channel_id=1, source_target_pairs={{0,29},{1,30},{2,31},{3,28},{4,1},{5,2},{6,3},{7,0},{8,5},{9,6},{1... | collective-permute-start | bytes 196616 | tf_op jit(solution)/shard_map/ppermute | solution.py:495
  71.2 6.8 %collective-permute-start.18 = (bf16[256,128]{1,0:T(8,128)(2,1)S(1)}, bf16[256,128]{1,0:T(8,128)(2,1)S(1)}, u32[]{:S(2)}, u32[]{:S(2)}) collective-permute-start(bf16[256,128]{1,0:T(8,128)(2,1)S(1)} %get-tuple-element.78), channel_id=1, source_target_pairs={{0,28},{1,29},{2,30},{3,31},{4,0},{5,1},{6,2},{7,3},{8,4},{9,5},{1... | collective-permute-start | bytes 196616 | tf_op jit(solution)/shard_map/ppermute | solution.py:495
  80.1 6.3 %collective-permute-start.22 = (bf16[64,1024]{1,0:T(8,128)(2,1)S(1)}, bf16[64,1024]{1,0:T(8,128)(2,1)S(1)}, u32[]{:S(2)}, u32[]{:S(2)}) collective-permute-start(bf16[64,1024]{1,0:T(8,128)(2,1)S(1)} %get-tuple-element.86), channel_id=1, source_target_pairs={{0,3},{1,0},{2,1},{3,2},{4,7},{5,4},{6,5},{7,6},{8,11},{9,8},{10,9... | collective-permute-start | bytes 393224 | tf_op jit(solution)/shard_map/ppermute | solution.py:481
  81.2 12.1 %collective-permute-start.23 = (bf16[64,1024]{1,0:T(8,128)(2,1)S(1)}, bf16[64,1024]{1,0:T(8,128)(2,1)S(1)}, u32[]{:S(2)}, u32[]{:S(2)}) collective-permute-start(bf16[64,1024]{1,0:T(8,128)(2,1)S(1)} %get-tuple-element.87), channel_id=1, source_target_pairs={{0,2},{1,3},{2,0},{3,1},{4,6},{5,7},{6,4},{7,5},{8,10},{9,11},{10,... | collective-permute-start | bytes 393224 | tf_op jit(solution)/shard_map/ppermute | solution.py:481
  81.2 12.1 %collective-permute-start.24 = (bf16[64,1024]{1,0:T(8,128)(2,1)S(1)}, bf16[64,1024]{1,0:T(8,128)(2,1)S(1)}, u32[]{:S(2)}, u32[]{:S(2)}) collective-permute-start(bf16[64,1024]{1,0:T(8,128)(2,1)S(1)} %get-tuple-element.88), channel_id=1, source_target_pairs={{0,1},{1,2},{2,3},{3,0},{4,5},{5,6},{6,7},{7,4},{8,9},{9,10},{10,1... | collective-permute-start | bytes 393224 | tf_op jit(solution)/shard_map/ppermute | solution.py:481
